TPU v7x, 128 devices: a whole 4x4x4 slice. The times are simulated.
128 devices in a mesh: section: 2 (over z_hi), shard: 16 (over x, z_lo, core), replica: 4 (over y).
Axes of the slice: x: 4, y: 4, z: 4 (z_hi: 2, z_lo: 2; z = z_hi * 2 + z_lo), core: 2. Of those that a mesh axis runs over, the one named last changes fastest.
Arguments:
- edge_inputs: bfloat16 [2, 2, 64, 128, 1024], P('section', None, ('shard', 'replica')), may hold values from -6 to 6
- image_counts: int32 [2], replicated, may hold values from 32 to 64, as said below
- w_qkv: bfloat16 [2, 1024, 3072], P('section', 'shard'), may hold values from -0.1875 to 0.1875
- w_proj: bfloat16 [2, 1024, 1024], P('section', 'shard'), may hold values from -0.5 to 0.5
- w_fc1: bfloat16 [2, 1024, 4096], P('section', 'shard'), may hold values from -0.1875 to 0.1875
- w_fc2: bfloat16 [2, 4096, 1024], P('section', 'shard'), may hold values from -0.09375 to 0.09375
- vectors: bfloat16 [2, 10, 1024], P('section', None, 'shard'), may hold values from -1.5 to 1.5
- fc1_bias: bfloat16 [2, 4096], P('section', 'shard'), may hold values from -1.75 to 1.75
Outputs:
- edge_values: float32 [2, 2, 64, 128, 1024], P('section', None, ('shard', 'replica'))
- grad_qkv: float32 [2, 1024, 3072], P('section', 'shard')
- grad_proj: float32 [2, 1024, 1024], P('section', 'shard')
- grad_fc1: float32 [2, 1024, 4096], P('section', 'shard')
- grad_fc2: float32 [2, 4096, 1024], P('section', 'shard')
- grad_vectors: float32 [2, 10, 1024], P('section', None, 'shard')
- grad_fc1_bias: float32 [2, 4096], P('section', 'shard')
Inputs may be any that keep to these rules, and one draw needn't show every extreme that they name: micro-batch m holds images 0 to image_counts[m] - 1.
All inputs are finite; a program needn't handle non-finite values.
Results may differ from a plain program's by a relative error of at most 0.022.
Values may be sent and summed in bfloat16 or wider, within the bound.
No kernel may reach another device: no remote copies, remote signals or barrier semaphores. Data moves between devices by JAX's collectives and lax.ppermute only.
A program may use at most 256 MiB of HBM per device.

v0:
```python
import jax
import jax.numpy as jnp
from jax import lax
from jax.sharding import PartitionSpec as P

HEAD_DIM = 64


epsilon = 1e-06


def passed_along(value, axis, steps):
    count = lax.axis_size(axis)
    first, last = (max(0, -steps), min(count, count - steps))
    return lax.ppermute(value, axis, [(source, source + steps) for source in range(first, last)])


def shortened(array):
    return jax.tree.map(lambda a: a.astype(jnp.bfloat16) if a.dtype == jnp.float32 else a, array)


def normalize(values, gain, shift):
    average = jnp.mean(values, axis=-1, keepdims=True)
    centered = values - average
    spread = jnp.mean(centered * centered, axis=-1, keepdims=True)
    return centered * lax.rsqrt(spread + epsilon) * gain + shift


def gelu_exact(values):
    return jax.nn.gelu(values, approximate=False)


def gather_again(local_parts):
    weight_qkv, weight_proj, weight_fc1, weight_fc2, small_params, hidden_bias = local_parts
    attention = (
        lax.all_gather(weight_qkv, "shard", axis=0, tiled=True),
        lax.all_gather(weight_proj, "shard", axis=0, tiled=True),
        lax.all_gather(small_params, "shard", axis=1, tiled=True),
    )
    feedforward = (
        lax.all_gather(weight_fc1, "shard", axis=0, tiled=True),
        lax.all_gather(weight_fc2, "shard", axis=0, tiled=True),
        lax.all_gather(hidden_bias, "shard", axis=0, tiled=True),
    )
    return (
        attention[0],
        attention[1],
        feedforward[0],
        feedforward[1],
        attention[2],
        feedforward[2],
    )


def forward_layer(inputs, layer_weights):
    weight_qkv, weight_proj, weight_fc1, weight_fc2, small_bf, hidden_bf = layer_weights
    small_params = small_bf.astype(jnp.float32)
    hidden_bias = hidden_bf.astype(jnp.float32)
    seq_len, width = inputs.shape
    head_count = width // HEAD_DIM
    scaling = 1.0 / HEAD_DIM**0.5
    normed = normalize(inputs, small_params[0], small_params[1]).astype(jnp.bfloat16)
    qkv_bias = jnp.concatenate([small_params[2], jnp.zeros((width,), jnp.float32), small_params[3]])
    projected = (jnp.dot(normed, weight_qkv, preferred_element_type=jnp.float32) + qkv_bias).astype(
        jnp.bfloat16
    )
    split_heads = projected.reshape(seq_len, 3, head_count, HEAD_DIM)
    queries = split_heads[:, 0]
    keys_all = split_heads[:, 1]
    values_all = split_heads[:, 2]
    scores = (
        jnp.einsum("qhd,khd->hqk", queries, keys_all, preferred_element_type=jnp.float32) * scaling
    )
    soft_weights = jax.nn.softmax(scores, axis=-1)
    soft_low = soft_weights.astype(jnp.bfloat16)
    mixed_heads = jnp.einsum(
        "hqk,khd->qhd", soft_low, values_all, preferred_element_type=jnp.float32
    )
    mixed_rows = mixed_heads.reshape(seq_len, width).astype(jnp.bfloat16)
    branch = jnp.dot(mixed_rows, weight_proj, preferred_element_type=jnp.float32) + small_params[4]
    middle = inputs + small_params[5] * branch
    second = normalize(middle, small_params[6], small_params[7]).astype(jnp.bfloat16)
    hidden = jnp.dot(second, weight_fc1, preferred_element_type=jnp.float32) + hidden_bias
    activated = gelu_exact(hidden).astype(jnp.bfloat16)
    out_branch = (
        jnp.dot(activated, weight_fc2, preferred_element_type=jnp.float32) + small_params[8]
    )
    output = middle + small_params[9] * out_branch
    saved = (
        normed,
        queries,
        keys_all,
        values_all,
        soft_weights,
        soft_low,
        mixed_rows,
        branch,
        middle,
        second,
        hidden,
        activated,
        out_branch,
    )
    return (output, saved)


def backward_layer(inputs, upstream, layer_weights):
    weight_qkv, weight_proj, weight_fc1, weight_fc2, small_bf, hidden_bf = layer_weights
    small_params = small_bf.astype(jnp.float32)
    seq_len, width = inputs.shape
    scaling = 1.0 / HEAD_DIM**0.5
    unused_output, saved = forward_layer(inputs, layer_weights)
    (
        normed,
        queries,
        keys_all,
        values_all,
        soft_weights,
        soft_low,
        mixed_rows,
        branch,
        middle,
        second,
        hidden,
        activated,
        out_branch,
    ) = saved
    d_out_branch = (small_params[9] * upstream).astype(jnp.bfloat16)
    grad_scale_two = jnp.sum(upstream * out_branch, axis=0)
    grad_fc2_bias = jnp.sum(d_out_branch.astype(jnp.float32), axis=0)
    grad_fc2 = jnp.einsum("sf,sd->fd", activated, d_out_branch, preferred_element_type=jnp.float32)
    d_activated = jnp.einsum(
        "sd,fd->sf", d_out_branch, weight_fc2, preferred_element_type=jnp.float32
    )
    unused_gelu, gelu_pull = jax.vjp(gelu_exact, hidden)
    d_hidden = gelu_pull(d_activated)[0].astype(jnp.bfloat16)
    grad_hidden_bias = jnp.sum(d_hidden.astype(jnp.float32), axis=0)
    grad_fc1 = jnp.einsum("sd,sf->df", second, d_hidden, preferred_element_type=jnp.float32)
    d_second = jnp.einsum("sf,df->sd", d_hidden, weight_fc1, preferred_element_type=jnp.float32)
    unused_norm, norm_pull = jax.vjp(normalize, middle, small_params[6], small_params[7])
    d_middle_norm, grad_gain_two, grad_shift_two = norm_pull(d_second)
    d_middle = upstream + d_middle_norm
    grad_scale_one = jnp.sum(d_middle * branch, axis=0)
    d_branch = (small_params[5] * d_middle).astype(jnp.bfloat16)
    grad_proj_bias = jnp.sum(d_branch.astype(jnp.float32), axis=0)
    grad_proj = jnp.einsum("sd,se->de", mixed_rows, d_branch, preferred_element_type=jnp.float32)
    d_mixed = jnp.einsum("se,de->sd", d_branch, weight_proj, preferred_element_type=jnp.float32)
    d_mixed = d_mixed.astype(jnp.bfloat16).reshape(queries.shape)
    grad_values = jnp.einsum("hqk,qhd->khd", soft_low, d_mixed, preferred_element_type=jnp.float32)
    d_soft = jnp.einsum("qhd,khd->hqk", d_mixed, values_all, preferred_element_type=jnp.float32)
    row_terms = jnp.sum(soft_weights * d_soft, axis=-1, keepdims=True)
    d_scores = (soft_weights * (d_soft - row_terms)).astype(jnp.bfloat16)
    grad_queries = (
        jnp.einsum("hqk,khd->qhd", d_scores, keys_all, preferred_element_type=jnp.float32) * scaling
    )
    grad_keys = (
        jnp.einsum("hqk,qhd->khd", d_scores, queries, preferred_element_type=jnp.float32) * scaling
    )
    d_projected = jnp.stack([grad_queries, grad_keys, grad_values], axis=1).reshape(
        seq_len, 3 * width
    )
    d_projected = d_projected.astype(jnp.bfloat16)
    column_sums = jnp.sum(d_projected.astype(jnp.float32), axis=0)
    grad_query_bias = column_sums[:width]
    grad_value_bias = column_sums[2 * width :]
    grad_qkv = jnp.einsum("sd,se->de", normed, d_projected, preferred_element_type=jnp.float32)
    d_normed = jnp.einsum("se,de->sd", d_projected, weight_qkv, preferred_element_type=jnp.float32)
    unused_first, first_pull = jax.vjp(normalize, inputs, small_params[0], small_params[1])
    d_inputs_norm, grad_gain_one, grad_shift_one = first_pull(d_normed)
    d_inputs = d_middle + d_inputs_norm
    grad_small = jnp.stack(
        [
            grad_gain_one,
            grad_shift_one,
            grad_query_bias,
            grad_value_bias,
            grad_proj_bias,
            grad_scale_one,
            grad_gain_two,
            grad_shift_two,
            grad_fc2_bias,
            grad_scale_two,
        ]
    )
    return (d_inputs, (grad_qkv, grad_proj, grad_fc1, grad_fc2, grad_small, grad_hidden_bias))


def scale_tree(tree_value, factor):
    return tuple((member * factor for member in tree_value))


def add_trees(left_tree, right_tree):
    return tuple(
        (left_member + right_member for left_member, right_member in zip(left_tree, right_tree))
    )


def shards(edge_inputs, image_counts, w_qkv, w_proj, w_fc1, w_fc2, vectors, fc1_bias):
    section_index = lax.axis_index("section")
    image_index = lax.axis_index(("shard", "replica"))
    sources = edge_inputs[0, :, 0]
    micro_count = sources.shape[0]
    present = (image_index < image_counts).astype(jnp.float32)
    local_parts = (w_qkv[0], w_proj[0], w_fc1[0], w_fc2[0], vectors[0], fc1_bias[0])
    kept_inputs = jnp.zeros_like(sources)
    outputs = jnp.zeros(sources.shape, jnp.float32)
    received = jnp.zeros(sources.shape[1:], jnp.bfloat16)
    for moment in range(micro_count + 1):
        index_now = moment - section_index
        usable = (index_now >= 0) & (index_now < micro_count)
        slot_index = jnp.clip(index_now, 0, micro_count - 1)
        layer_in = jnp.where(section_index == 0, sources[min(moment, micro_count - 1)], received)
        weights_now = gather_again(local_parts)
        result, unused_saved = forward_layer(layer_in.astype(jnp.float32), weights_now)
        kept_inputs = kept_inputs.at[slot_index].set(
            jnp.where(usable, layer_in, kept_inputs[slot_index])
        )
        outputs = outputs.at[slot_index].set(jnp.where(usable, result, outputs[slot_index]))
        if moment < micro_count:
            received = passed_along(result.astype(jnp.bfloat16), "section", 1)
    received_grad = jnp.zeros(sources.shape[1:], jnp.bfloat16)
    input_grads = jnp.zeros(sources.shape, jnp.float32)
    totals = None
    for moment in range(micro_count + 1):
        index_now = moment - 1 + section_index
        usable = (index_now >= 0) & (index_now < micro_count)
        slot_index = jnp.clip(index_now, 0, micro_count - 1)
        pick_index = min(moment, micro_count - 1)
        upstream = jnp.where(
            section_index == 1,
            sources[pick_index].astype(jnp.float32) * present[pick_index],
            received_grad.astype(jnp.float32),
        )
        weights_now = gather_again(local_parts)
        d_inputs, gradients = backward_layer(
            kept_inputs[slot_index].astype(jnp.float32), upstream, weights_now
        )
        gradients = scale_tree(gradients, usable.astype(jnp.float32))
        input_grads = input_grads.at[slot_index].set(
            jnp.where(usable, d_inputs, input_grads[slot_index])
        )
        totals = gradients if totals is None else add_trees(totals, gradients)
        if moment < micro_count:
            received_grad = passed_along(d_inputs.astype(jnp.bfloat16), "section", -1)
    totals = (
        lax.psum_scatter(
            totals[0].astype(jnp.bfloat16), "shard", scatter_dimension=0, tiled=True
        ).astype(jnp.float32),
        lax.psum_scatter(
            totals[1].astype(jnp.bfloat16), "shard", scatter_dimension=0, tiled=True
        ).astype(jnp.float32),
        lax.psum_scatter(
            totals[2].astype(jnp.bfloat16), "shard", scatter_dimension=0, tiled=True
        ).astype(jnp.float32),
        lax.psum_scatter(
            totals[3].astype(jnp.bfloat16), "shard", scatter_dimension=0, tiled=True
        ).astype(jnp.float32),
        lax.psum_scatter(
            totals[4].astype(jnp.bfloat16), "shard", scatter_dimension=1, tiled=True
        ).astype(jnp.float32),
        lax.psum_scatter(
            totals[5].astype(jnp.bfloat16), "shard", scatter_dimension=0, tiled=True
        ).astype(jnp.float32),
    )
    totals = jax.tree.map(
        lambda part: part.astype(jnp.float32), lax.psum(shortened(totals), "replica")
    )
    section_values = jnp.where(section_index == 0, input_grads, outputs)
    edge_values = section_values[None, :, None]
    return (
        edge_values,
        totals[0][None],
        totals[1][None],
        totals[2][None],
        totals[3][None],
        totals[4][None],
        totals[5][None],
    )


def solution(mesh):
    placed = (
        P("section", None, ("shard", "replica"), None, None),
        P(),
        P("section", "shard", None),
        P("section", "shard", None),
        P("section", "shard", None),
        P("section", "shard", None),
        P("section", None, "shard"),
        P("section", "shard"),
    )
    return jax.shard_map(
        shards,
        mesh=mesh,
        in_specs=placed,
        out_specs=(
            P("section", None, ("shard", "replica"), None, None),
            P("section", "shard", None),
            P("section", "shard", None),
            P("section", "shard", None),
            P("section", "shard", None),
            P("section", None, "shard"),
            P("section", "shard"),
        ),
        check_vma=False,
    )
```

profile of v0, /device:TPU:0, one launch (start us, length us, event | category | flops | bytes accessed | tf_op | source)
XLA Modules:
  0.0 874.3 jit_solution(15679831654919766782)
XLA Ops:
  10.8 21.8 %all-gather = bf16[1,10,1024]{1,0,2:T(2,128)(2,1)S(1)} all-gather(bf16[1,10,64]{1,0,2:T(2,128)(2,1)S(1)} %copy.107), channel_id=2, replica_groups=mesh['section'=2,'shard'=16,'replica'=4] {'shard'}, dimensions={2}, use_global_device_ids=true | all-gather | bytes 21760 | tf_op jit(solution)/shard_map/all_gather | solution.py:38
  33.2 16.3 %all-gather.4 = bf16[1,4096]{1,0:T(2,128)(2,1)S(1)} all-gather(bf16[1,256]{1,0:T(2,128)(2,1)S(1)} %copy-done.113), channel_id=6, replica_groups=mesh['section'=2,'shard'=16,'replica'=4] {'shard'}, dimensions={1}, use_global_device_ids=true | all-gather | bytes 8704 | tf_op jit(solution)/shard_map/all_gather | solution.py:43
  50.2 34.1 %slice_reduce_fusion.3 = (f32[1024]{0:T(1024)S(1)}, f32[1024]{0:T(1024)S(1)}, f32[1024]{0:T(1024)S(1)}, f32[1024]{0:T(1024)S(1)}, f32[1024]{0:T(1024)S(1)}, /*in...) fusion(f32[1,10,1024]{1,0,2:T(1,128)S(1)} %convert_element_type.530), kind=kLoop, calls=%fused_computation.487 | loop fusion | bytes 81920 | tf_op jit(solution)/shard_map/slice | solution.py:88
  94.9 51.6 %all-gather.17.cloned.1.call-done = bf16[1,4096,1024]{2,1,0:T(8,128)(2,1)} async-done(((bf16[1,256,1024]{2,1,0:T(8,128)(2,1)}), bf16[1,4096,1024]{2,1,0:T(8,128)(2,1)}) %all-gather.17.cloned.1.call-update) | async-done | bytes 8388624 | tf_op jit(solution)/shard_map/all_gather | solution.py:42
  146.5 54.6 %all-gather.15.cloned.1.call-done = bf16[1,1024,4096]{2,1,0:T(8,128)(2,1)} async-done(((bf16[1,64,4096]{2,1,0:T(8,128)(2,1)}), bf16[1,1024,4096]{2,1,0:T(8,128)(2,1)}) %all-gather.15.cloned.1.call-update) | async-done | bytes 8388624 | tf_op jit(solution)/shard_map/all_gather | solution.py:41
  201.0 12.2 %fusion.728 = (bf16[128,1024]{1,0:T(8,128)(2,1)S(1)}, f32[128,1024]{1,0:T(8,128)}) fusion(f32[128,1024]{1,0:T(8,128)S(1)} %get-tuple-element.248, f32[1024]{0:T(1024)S(1)} %get-tuple-element.178, bf16[1,4096,1024]{2,1,0:T(8,128)(2,1)} %all-gather.17.cloned.1.call-done, f32[4096]{0:T(1024)S(1)} %bitcast.815, ...), kind=kOutput, calls=%fused_computation.849 | convolution fusion | flops 2183266304 | bytes 18121728 | tf_op jit(solution)/shard_map/dot_general | solution.py:86
  236.3 14.3 %fusion.733 = (bf16[128,1024]{1,0:T(8,128)(2,1)}, f32[128,1024]{1,0:T(8,128)}) fusion(f32[128,1024]{1,0:T(8,128)} %copy-done.48, f32[1024]{0:T(1024)S(1)} %get-tuple-element.178, bf16[1,4096,1024]{2,1,0:T(8,128)(2,1)} %all-gather.17.cloned.1.call-done, f32[4096]{0:T(1024)S(1)} %bitcast.816, bf16[1,1024,4096]{2,1,0:T(8,128)(2,1)} %all-gather.15.cloned.1.call-done, ...), kind=kOutput, calls=%fused_computation.852 | convolution fusion | flops 2183266304 | bytes 18121728 | tf_op jit(solution)/shard_map/dot_general | solution.py:86
  281.6 8.7 convert_reduce_fusion.2
  348.3 8.3 convert_reduce_fusion.1
  387.0 8.3 convert_reduce_fusion
  427.2 13.0 %add_convert_fusion.2 = bf16[1024,3072]{1,0:T(8,128)(2,1)} fusion(f32[1024,3072]{1,0:T(8,128)} %fusion.497, f32[1024,3072]{1,0:T(8,128)} %fusion.500, bf16[128,3072]{0,1:T(8,128)(2,1)S(1)} %bitcast.766, f32[]{:T(128)S(6)} %convert_element_type.508, f32[]{:T(128)S(6)} %convert_element_type.505, f32[]{:T(128)S(6)} %convert_element_type.502, ...), kind=kOutput, calls=%fused_computation.8 | convolution fusion | flops 824967168 | bytes 32515088 | tf_op jit(solution)/shard_map/sd,se->de/dot_general | solution.py:166
  440.3 9.7 %fusion.708 = f32[1024,4096]{1,0:T(8,128)} fusion(bf16[128,4096]{1,0:T(8,128)(2,1)} %copy-done.29, f32[128,1024]{1,0:T(8,128)} %copy-done.4, f32[128]{0:T(128)S(1)} %fusion.600, f32[128]{0:T(128)S(1)} %broadcast_multiply_fusion.6, f32[1024]{0:T(1024)S(1)} %get-tuple-element.170, f32[1024]{0:T(1024)S(1)} %get-tuple-element.171), kind=kOutput, calls=%fused_computation.832 | convolution fusion | flops 1074397184 | bytes 18359296 | tf_op jit(solution)/shard_map/sd,sf->df/dot_general | solution.py:138
  458.1 15.1 %add_convert_fusion.1 = bf16[1024,4096]{1,0:T(8,128)(2,1)} fusion(f32[1024,4096]{1,0:T(8,128)} %fusion.709, f32[1024,4096]{1,0:T(8,128)} %fusion.708, bf16[128,4096]{1,0:T(8,128)(2,1)} %copy-done.32, f32[]{:T(128)S(6)} %convert_element_type.508, f32[]{:T(128)S(6)} %convert_element_type.505, f32[]{:T(128)S(6)} %convert_element_type.502, ...), kind=kOutput, calls=%fused_computation.7 | convolution fusion | flops 1099563008 | bytes 43525132 | tf_op jit(solution)/shard_map/sd,sf->df/dot_general | solution.py:138
  473.3 12.0 %fusion.587 = f32[4096,1024]{1,0:T(8,128)} fusion(f32[1024]{0:T(1024)S(1)} %get-tuple-element.169, f32[]{:T(128)} %bitcast.1, pred[]{:T(512)S(6)} %eq.5, bf16[1,2,1,128,1024]{4,3,2,1,0:T(8,128)(2,1)S(1)} %copy-done.1, f32[128,4096]{1,0:T(8,128)} %copy-done.41), kind=kOutput, calls=%fused_computation.652 | convolution fusion | flops 1108475904 | bytes 19140612 | tf_op jit(solution)/shard_map/sf,sd->fd/dot_general | solution.py:131
  493.4 18.6 %add_convert_fusion = bf16[4096,1024]{1,0:T(8,128)(2,1)} fusion(f32[4096,1024]{1,0:T(8,128)} %fusion.743, f32[4096,1024]{1,0:T(8,128)} %fusion.587, bf16[128,1024]{1,0:T(8,128)(2,1)} %copy-done.67, f32[]{:T(128)S(6)} %convert_element_type.508, f32[]{:T(128)S(6)} %convert_element_type.505, f32[]{:T(128)S(6)} %convert_element_type.502, f32[128,4096]{1,0:T(8,128)} %fusion.72), kind=kOutput, calls=%fused_computation.6 | convolution fusion | flops 1132986368 | bytes 44302348 | tf_op jit(solution)/shard_map/sf,sd->fd/dot_general | solution.py:131
  526.0 10.7 %fusion.312 = f32[1024]{0:T(1024)} fusion(bf16[1,4096,1024]{2,1,0:T(8,128)(2,1)} %all-gather.17.cloned.1.call-done, f32[1024]{0:T(1024)S(1)} %copy-done.101, f32[]{:T(128)} %bitcast.1, pred[]{:T(512)S(6)} %eq.5, bf16[1,2,1,128,1024]{4,3,2,1,0:T(8,128)(2,1)S(1)} %copy-done.1, f32[128,4096]{1,0:T(8,128)} %copy-done.41), kind=kOutput, calls=%fused_computation.292 | convolution fusion | flops 1108605952 | bytes 10756101 | tf_op jit(solution)/shard_map/dot_general | solution.py:86
  562.9 9.5 %fusion.306 = f32[1024]{0:T(1024)} fusion(bf16[1,4096,1024]{2,1,0:T(8,128)(2,1)} %all-gather.17.cloned.1.call-done, bf16[128,1024]{1,0:T(8,128)(2,1)S(1)} %copy-done.54, f32[]{:T(128)} %bitcast.47, f32[1024]{0:T(1024)S(1)} %copy-done.101, pred[]{:T(512)S(6)} %eq.5, bf16[1,2,1,128,1024]{4,3,2,1,0:T(8,128)(2,1)S(1)} %copy-done.1, f32[128,4096]{1,0:T(8,128)S(1)} %copy-done.43), kind=kOutput, calls=%fused_computation.290 | convolution fusion | flops 1108737024 | bytes 11018245 | tf_op jit(solution)/shard_map/dot_general | solution.py:86
  575.0 11.8 %fusion.303 = f32[2,128,1024]{2,1,0:T(8,128)S(1)} fusion(f32[2,128,1024]{2,1,0:T(8,128)S(1)} %copy-done.10, s32[]{:T(128)} %min.37, f32[1,128,1024]{2,1,0:T(8,128)S(1)} %copy-done.66, f32[128,1024]{1,0:T(8,128)S(1)} %copy-done.47, bf16[1,4096,1024]{2,1,0:T(8,128)(2,1)} %all-gather.17.cloned.1.call-done, ...), kind=kOutput, calls=%fused_computation.289 | convolution fusion | flops 2183397376 | bytes 18908166 | tf_op jit(solution)/shard_map/dot_general | solution.py:86
  586.8 55.0 %reduce-scatter.12.cloned.1.call-done = bf16[64,4096]{1,0:T(8,128)(2,1)} async-done(((bf16[1024,4096]{1,0:T(8,128)(2,1)}), bf16[64,4096]{1,0:T(8,128)(2,1)}) %reduce-scatter.12.cloned.1.call-update) | async-done | bytes 524304 | tf_op jit(solution)/shard_map/reduce_scatter | solution.py:252
  641.9 100.0 %reduce-scatter.14.cloned.1.call-done = bf16[256,1024]{1,0:T(8,128)(2,1)} async-done(((bf16[4096,1024]{1,0:T(8,128)(2,1)}), bf16[256,1024]{1,0:T(8,128)(2,1)}) %reduce-scatter.14.cloned.1.call-update) | async-done | bytes 524304 | tf_op jit(solution)/shard_map/reduce_scatter | solution.py:255
  746.7 31.0 %all-reduce = bf16[4096]{0:T(1024)(128)(2,1)S(1)} all-reduce(bf16[4096]{0:T(1024)(128)(2,1)S(1)} %add_convert_fusion.20), channel_id=13, replica_groups=mesh['section'=2,'shard'=16,'replica'=4] {'shard'}, use_global_device_ids=true, to_apply=%region_97.98.clone | all-reduce | flops 4096 | bytes 16384
  781.1 27.1 %reduce-scatter.16.cloned.1.call-done = bf16[64,10]{1,0:T(8,128)(2,1)} async-done(((bf16[1024,10]{1,0:T(8,128)(2,1)}), bf16[64,10]{1,0:T(8,128)(2,1)}) %reduce-scatter.16.cloned.1.call-update) | async-done | bytes 1296
  809.0 10.7 %all-reduce.1 = (bf16[1,10,64]{2,1,0:T(8,128)(2,1)S(1)}, bf16[1,256]{1,0:T(2,128)(2,1)S(1)}) all-reduce(bf16[1,10,64]{2,1,0:T(8,128)(2,1)S(1)} %bitcast.841, bf16[1,256]{1,0:T(2,128)(2,1)S(1)} %broadcast_in_dim.82), channel_id=1, replica_groups=mesh['section'=2,'shard'=16,'replica'=4] {'replica'}, use_global_device_ids=true, to_apply=%region_93.94 | all-reduce | flops 896 | bytes 3584 | tf_op jit(solution)/shard_map/psum | solution.py:266
  820.8 39.4 %all-reduce.5.cloned.1.call-done = (bf16[1,64,3072]{2,1,0:T(8,128)(2,1)}, bf16[1,64,1024]{2,1,0:T(8,128)(2,1)}, bf16[1,64,4096]{2,1,0:T(8,128)(2,1)}, bf16[1,256,1024]{2,1,0:T(8,128)(2,1)}) async-done(((bf16[1,64,3072]{2,1,0:T(8,128)(2,1)}, bf16[1,64,1024]{2,1,0:T(8,128)(2,1)}, bf16[1,64,4096]{2,1,0:T(8,128)(2,1)}, bf16[1,256,1024]{2,1,0:T(8,128)(2,1)}), (bf16[1,64,3072]{2,1,0:T(8,128)(2,1)}, ...) | async-done | bytes 1572880 | tf_op jit(solution)/shard_map/psum | solution.py:266
  (503 shorter events, 263.5 us)
Async XLA Ops:
  7.2 42.3 %copy-start.117 = (s32[2]{0:T(128)S(1)}, s32[2]{0:T(128)}, u32[]{:S(2)}) copy-start(s32[2]{0:T(128)} %param.27) | copy-start | bytes 28
  7.2 79.6 %all-gather.11.cloned.1.call-start = ((), (), s32[]{:S(2)}) async-start(), calls=%async_computation.9 | async-start | bytes 6684672 | tf_op jit(solution)/shard_map/all_gather | solution.py:36
  7.9 84.6 %all-gather.13.cloned.1.call-start = ((), (), s32[]{:S(2)}) async-start(), calls=%async_computation.10 | async-start | bytes 2228224 | tf_op jit(solution)/shard_map/all_gather | solution.py:37
  8.7 137.8 %all-gather.17.cloned.1.call-start = ((), (), s32[]{:S(2)}) async-start(), calls=%async_computation.12 | async-start | bytes 8912896 | tf_op jit(solution)/shard_map/all_gather | solution.py:42
  9.4 191.6 %all-gather.15.cloned.1.call-start = ((), (), s32[]{:S(2)}) async-start(), calls=%async_computation.11 | async-start | bytes 8912896 | tf_op jit(solution)/shard_map/all_gather | solution.py:41
  10.0 576.8 %reduce-scatter.10.cloned.1.call-start = ((), (), s32[]{:S(2)}) async-start(), calls=%async_computation.6 | async-start | bytes 2228224 | tf_op jit(solution)/shard_map/reduce_scatter | solution.py:249
  49.5 291.9 %copy-start.74 = (f32[1,4096]{1,0:T(1,128)}, f32[1,4096]{1,0:T(1,128)S(1)}, u32[]{:S(2)}) copy-start(f32[1,4096]{1,0:T(1,128)S(1)} %convert_element_type.531) | copy-start | bytes 49156
  50.2 35.0 %copy-start.1 = (bf16[1,2,1,128,1024]{4,3,2,1,0:T(8,128)(2,1)S(1)}, bf16[1,2,1,128,1024]{4,3,2,1,0:T(8,128)(2,1)}, u32[]{:S(2)}) copy-start(bf16[1,2,1,128,1024]{4,3,2,1,0:T(8,128)(2,1)} %param.26) | copy-start | bytes 1572868
  84.3 152.0 %copy-start.100 = (f32[1024]{0:T(1024)}, f32[1024]{0:T(1024)S(1)}, u32[]{:S(2)}) copy-start(f32[1024]{0:T(1024)S(1)} %get-tuple-element.178) | copy-start | bytes 12292
  84.4 243.5 %copy-start.72 = (f32[1024]{0:T(1024)}, f32[1024]{0:T(1024)S(1)}, u32[]{:S(2)}) copy-start(f32[1024]{0:T(1024)S(1)} %get-tuple-element.172) | copy-start | bytes 12292
  84.4 230.3 %copy-start.76 = (f32[3072]{0:T(1024)}, f32[3072]{0:T(1024)S(1)}, u32[]{:S(2)}) copy-start(f32[3072]{0:T(1024)S(1)} %pad_maximum_fusion) | copy-start | bytes 36868
  213.2 10.8 %collective-permute-start = (bf16[128,1024]{1,0:T(8,128)(2,1)S(1)}, bf16[128,1024]{1,0:T(8,128)(2,1)S(1)}, u32[]{:S(2)}, u32[]{:S(2)}) collective-permute-start(bf16[128,1024]{1,0:T(8,128)(2,1)S(1)} %get-tuple-element.249), channel_id=1, source_target_pairs={{0,64},{1,65},{2,66},{3,67},{4,68},{5,69},{6,70},{7,71},{8,72},{9,... | collective-permute-start | bytes 786440 | tf_op jit(solution)/shard_map/ppermute | solution.py:15
  250.6 11.3 %collective-permute-start.1 = (bf16[128,1024]{1,0:T(8,128)(2,1)}, bf16[128,1024]{1,0:T(8,128)(2,1)S(1)}, u32[]{:S(2)}, u32[]{:S(2)}) collective-permute-start(bf16[128,1024]{1,0:T(8,128)(2,1)} %get-tuple-element.253), channel_id=1, source_target_pairs={{0,64},{1,65},{2,66},{3,67},{4,68},{5,69},{6,70},{7,71},{8,72},{9,... | collective-permute-start | bytes 786440 | tf_op jit(solution)/shard_map/ppermute | solution.py:15
  294.2 36.5 %copy-start.102 = (f32[128]{0:T(128)}, f32[128]{0:T(128)S(1)}, u32[]{:S(2)}) copy-start(f32[128]{0:T(128)S(1)} %negate_multiply_fusion.11) | copy-start | bytes 1540
  314.7 111.6 %copy-start.104 = (f32[128]{0:T(128)}, f32[128]{0:T(128)S(1)}, u32[]{:S(2)}) copy-start(f32[128]{0:T(128)S(1)} %fusion.603) | copy-start | bytes 1540
  333.0 13.9 %collective-permute-start.2 = (bf16[128,1024]{1,0:T(8,128)(2,1)S(1)}, bf16[128,1024]{1,0:T(8,128)(2,1)S(1)}, u32[]{:S(2)}, u32[]{:S(2)}) collective-permute-start(bf16[128,1024]{1,0:T(8,128)(2,1)S(1)} %get-tuple-element.232), channel_id=1, source_target_pairs={{64,0},{65,1},{66,2},{67,3},{68,4},{69,5},{70,6},{71,7},{72,8},{73... | collective-permute-start | bytes 786440 | tf_op jit(solution)/shard_map/ppermute | solution.py:15
  375.1 10.5 %collective-permute-start.3 = (bf16[128,1024]{1,0:T(8,128)(2,1)S(1)}, bf16[128,1024]{1,0:T(8,128)(2,1)S(1)}, u32[]{:S(2)}, u32[]{:S(2)}) collective-permute-start(bf16[128,1024]{1,0:T(8,128)(2,1)S(1)} %fusion.580), channel_id=1, source_target_pairs={{64,0},{65,1},{66,2},{67,3},{68,4},{69,5},{70,6},{71,7},{72,8},{73... | collective-permute-start | bytes 786440 | tf_op jit(solution)/shard_map/ppermute | solution.py:15
  404.7 182.1 %reduce-scatter.8.cloned.1.call-start = ((), (), s32[]{:S(2)}) async-start(), calls=%async_computation.5 | async-start | bytes 6684672 | tf_op jit(solution)/shard_map/reduce_scatter | solution.py:246
  440.2 201.7 %reduce-scatter.12.cloned.1.call-start = ((), (), s32[]{:S(2)}) async-start(), calls=%async_computation.7 | async-start | bytes 8912896 | tf_op jit(solution)/shard_map/reduce_scatter | solution.py:252
  473.2 268.6 %reduce-scatter.14.cloned.1.call-start = ((), (), s32[]{:S(2)}) async-start(), calls=%async_computation.8 | async-start | bytes 8912896 | tf_op jit(solution)/shard_map/reduce_scatter | solution.py:255
  512.0 296.3 %reduce-scatter.16.cloned.1.call-start = ((), (), s32[]{:S(2)}) async-start(), calls=%async_computation.13 | async-start | bytes 278528
  574.9 285.4 %all-reduce.5.cloned.1.call-start = ((), (), s32[]{:S(2)}) async-start(), calls=%async_computation.14 | async-start | bytes 3145728 | tf_op jit(solution)/shard_map/psum | solution.py:266
  586.8 155.3 %copy-start.103 = (f32[128]{0:T(128)S(1)}, f32[128]{0:T(128)}, u32[]{:S(2)}) copy-start(f32[128]{0:T(128)} %copy-done.102) | copy-start | bytes 1540
  586.8 155.3 %copy-start.107 = (f32[128]{0:T(128)S(1)}, f32[128]{0:T(128)}, u32[]{:S(2)}) copy-start(f32[128]{0:T(128)} %copy-done.106) | copy-start | bytes 1540
  (127 other events, 889.4 us)
Sparse Core Ops, SparseCore 0:
  9.7 46.9 all-gather.10
  58.4 34.0 all-gather.12
  94.2 52.1 all-gather.16
  148.0 52.9 all-gather.14
  404.9 62.3 reduce-scatter.9
  469.5 74.5 reduce-scatter.7
  546.5 95.2 reduce-scatter.11
  644.3 97.5 reduce-scatter.13
  744.8 63.3 reduce-scatter.15
  810.8 49.3 all-reduce.4
where the time goes:
time: 885 us; the launch traced here: 874 us
  waiting for transfers between devices  344 us (39%)
  matrix products  304 us (34%)
  blocking collectives  79.8 us (9%)
  local copies, waits for them, and re-layouts  69.9 us (8%)
  other arithmetic  44.7 us (5%)
  between operations  17.2 us (2%)
  starting transfers between devices  14.4 us (2%)
    reduce_scatter x1, waiting for transfers between devices, shards(): lax.psum_scatter(totals[3].astype(jnp.bfloat16), 'shard', scatter_dimensi...  100 us
    dot_general x6, matrix products, forward_layer(): jnp.dot(activated, weight_fc2, preferred_element_type=jnp.float32)  64.2 us
    reduce_scatter x1, waiting for transfers between devices, shards(): lax.psum_scatter(totals[2].astype(jnp.bfloat16), 'shard', scatter_dimensi...  55 us
    all_gather x1, waiting for transfers between devices, gather_again(): lax.all_gather(weight_fc1, 'shard', axis=0, tiled=True)  54.6 us
    all_gather x1, waiting for transfers between devices, gather_again(): lax.all_gather(weight_fc2, 'shard', axis=0, tiled=True)  51.6 us
    psum x1, waiting for transfers between devices, shards(): lax.psum(shortened(totals), 'replica')  39.4 us
    dot_general x3, matrix products, backward_layer(): jnp.einsum('sf,sd->fd', activated, d_out_branch, preferred_element_type=j...  38.6 us
    slice x1, local copies, waits for them, and re-layouts, forward_layer(): output = middle + small_params[9] * out_branch  34.1 us
  transfers between devices with their start and end apart: 14, of which 10 were waited for; matrix products, arithmetic and copies ran while one was open for 29% of the time, Pallas kernels for 0%

commit v1 on v0

v1 whole, which is shorter than its diff:
```python
import jax
import jax.numpy as jnp
from jax import lax
from jax.sharding import PartitionSpec as P

HEAD_DIM = 64
XS, ZS, CS, YS = 4, 2, 2, 4
epsilon = 1e-06
bf16, f32 = jnp.bfloat16, jnp.float32


def shard_of(x, z, c):
    return (x % XS) * 4 + (z % ZS) * 2 + (c % CS)


def from_shard(value, dx=0, dz=0, dc=0):
    pairs = [
        (shard_of(x + dx, z + dz, c + dc), shard_of(x, z, c))
        for x in range(XS)
        for z in range(ZS)
        for c in range(CS)
    ]
    return lax.ppermute(value, "shard", pairs)


def from_replica(value, dy):
    return lax.ppermute(value, "replica", [((y + dy) % YS, y) for y in range(YS)])


def passed_along(value, steps):
    pairs = [(0, 1)] if steps == 1 else [(1, 0)]
    return lax.ppermute(value, "section", pairs)


def pick(array, index, axis, keep=False):
    return lax.dynamic_index_in_dim(array, index, axis, keepdims=keep)


def rolled(array, shift, axis):
    n = array.shape[axis]
    twice = jnp.concatenate([array, array], axis=axis)
    return lax.dynamic_slice_in_dim(twice, shift, n, axis)


def normalize(values, gain, shift):
    average = jnp.mean(values, axis=-1, keepdims=True)
    centered = values - average
    spread = jnp.mean(centered * centered, axis=-1, keepdims=True)
    return centered * lax.rsqrt(spread + epsilon) * gain + shift


def gelu_exact(values):
    return jax.nn.gelu(values, approximate=False)


def gather_columns(unit):
    other = from_shard(unit, dz=1)
    pair = jnp.stack([unit, other])
    plus = from_shard(pair, dx=1)
    minus = from_shard(pair, dx=3)
    far_a = from_shard(plus[0], dx=1)
    far_b = from_shard(minus[1], dx=3)
    mine = [pair, plus, jnp.stack([far_a, far_b]), minus]
    theirs = [
        from_shard(pair, dc=1),
        from_shard(plus, dc=1),
        jnp.stack([from_shard(far_a, dc=1), from_shard(far_b, dc=1)]),
        from_shard(minus, dc=1),
    ]
    return jnp.stack([jnp.stack(mine), jnp.stack(theirs)])


def gather_rows(piece):
    near = [piece if (dx, dz) == (0, 0) else from_shard(piece, dx=dx, dz=dz) for dx in range(XS) for dz in range(ZS)]
    here = jnp.stack(near)
    plus = from_replica(here, 1)
    minus = from_replica(here, 3)
    far_a = from_replica(plus[:, :64], 1)
    far_b = from_replica(minus[:, 64:], 3)
    mine = [here, plus, jnp.concatenate([far_a, far_b], axis=1), minus]
    theirs = [
        from_shard(here, dc=1),
        from_shard(plus, dc=1),
        jnp.concatenate([from_shard(far_a, dc=1), from_shard(far_b, dc=1)], axis=1),
        from_shard(minus, dc=1),
    ]
    both = jnp.stack([jnp.stack(mine), jnp.stack(theirs)])
    return both.reshape(CS, YS, XS, ZS, 96, 1024)


def gather_all(w_qkv, w_proj, w_fc1, w_fc2, vectors, fc1_bias, place):
    x, z, c, y = place
    small = jnp.concatenate([vectors, fc1_bias.reshape(4, 64)], axis=0).T
    small = jnp.pad(small, ((0, 0), (0, 114)))
    unit = jnp.concatenate([w_qkv, w_proj, w_fc2[128:192], w_fc2[192:], small], axis=1)
    piece = jnp.concatenate(
        [
            lax.dynamic_slice(w_fc1, (0, y * 1024), (64, 1024)),
            lax.dynamic_slice(w_fc2, (y * 32, 0), (32, 1024)),
        ],
        axis=0,
    )
    columns = gather_columns(unit)
    rows = gather_rows(piece)
    back = lambda v, i, axis: rolled(v, (v.shape[axis] - i) % v.shape[axis], axis)
    columns = back(back(back(columns, c, 0), x, 1), z, 2)
    columns = columns.transpose(1, 2, 0, 3, 4)
    rows = back(back(back(back(rows, c, 0), y, 1), x, 2), z, 3)
    qkv = columns[..., :3072].reshape(1024, 3072)
    proj = columns[..., 3072:4096].reshape(1024, 1024)
    fc2_b = columns[..., 4096:6144].reshape(XS, ZS, CS, 64, 2, 1024).transpose(0, 1, 2, 4, 3, 5)
    fc2_b = fc2_b.reshape(16, 128, 1024)
    small = columns[..., 6144:6158].reshape(16, 64, 14)
    fc1 = rows[..., :64, :].transpose(2, 3, 0, 4, 1, 5).reshape(1024, 4096)
    fc2_a = rows[..., 64:, :].transpose(2, 3, 0, 1, 4, 5).reshape(16, 128, 1024)
    fc2 = jnp.concatenate([fc2_a, fc2_b], axis=1).reshape(4096, 1024)
    vec = small[:, :, :10].transpose(2, 0, 1).reshape(10, 1024).astype(f32)
    bias = small[:, :, 10:].transpose(0, 2, 1).reshape(4096).astype(f32)
    return qkv, proj, fc1, fc2, vec, bias


def forward_layer(inputs, layer_weights):
    qkv, proj, fc1, fc2, vec, bias = layer_weights
    rows, width = inputs.shape
    images, heads = rows // 128, width // HEAD_DIM
    normed = normalize(inputs, vec[0], vec[1]).astype(bf16)
    qkv_bias = jnp.concatenate([vec[2], jnp.zeros((width,), f32), vec[3]])
    projected = (jnp.dot(normed, qkv, preferred_element_type=f32) + qkv_bias).astype(bf16)
    split = projected.reshape(images, 128, 3, heads, HEAD_DIM).transpose(2, 0, 3, 1, 4)
    queries, keys, values = split[0], split[1], split[2]
    scores = jnp.einsum("ihqd,ihkd->ihqk", queries, keys, preferred_element_type=f32) * 0.125
    soft = jax.nn.softmax(scores, axis=-1)
    mixed = jnp.einsum("ihqk,ihkd->ihqd", soft.astype(bf16), values, preferred_element_type=f32)
    mixed = mixed.astype(bf16).transpose(0, 2, 1, 3).reshape(rows, width)
    branch = jnp.dot(mixed, proj, preferred_element_type=f32) + vec[4]
    middle = inputs + vec[5] * branch
    second = normalize(middle, vec[6], vec[7]).astype(bf16)
    hidden = jnp.dot(second, fc1, preferred_element_type=f32) + bias
    activated = gelu_exact(hidden).astype(bf16)
    out_branch = jnp.dot(activated, fc2, preferred_element_type=f32) + vec[8]
    output = middle + vec[9] * out_branch
    return output, (normed, queries, keys, values, soft, mixed, branch, middle, second, hidden, activated, out_branch)


def backward_layer(inputs, upstream, saved, layer_weights):
    qkv, proj, fc1, fc2, vec, bias = layer_weights
    normed, queries, keys, values, soft, mixed, branch, middle, second, hidden, activated, out_branch = saved
    rows, width = inputs.shape
    d_out = (vec[9] * upstream).astype(bf16)
    g9 = jnp.sum(upstream * out_branch, axis=0)
    g8 = jnp.sum(d_out.astype(f32), axis=0)
    d_act = jnp.einsum("sd,fd->sf", d_out, fc2, preferred_element_type=f32)
    _, gelu_pull = jax.vjp(gelu_exact, hidden)
    d_hidden = gelu_pull(d_act)[0].astype(bf16)
    g_bias = jnp.sum(d_hidden.astype(f32), axis=0)
    d_second = jnp.einsum("sf,df->sd", d_hidden, fc1, preferred_element_type=f32)
    _, norm_pull = jax.vjp(normalize, middle, vec[6], vec[7])
    d_norm, g6, g7 = norm_pull(d_second)
    d_middle = upstream + d_norm
    g5 = jnp.sum(d_middle * branch, axis=0)
    d_branch = (vec[5] * d_middle).astype(bf16)
    g4 = jnp.sum(d_branch.astype(f32), axis=0)
    d_mixed = jnp.einsum("se,de->sd", d_branch, proj, preferred_element_type=f32).astype(bf16)
    images, heads = rows // 128, width // HEAD_DIM
    d_mixed = d_mixed.reshape(images, 128, heads, HEAD_DIM).transpose(0, 2, 1, 3)
    d_values = jnp.einsum("ihqk,ihqd->ihkd", soft.astype(bf16), d_mixed, preferred_element_type=f32)
    d_soft = jnp.einsum("ihqd,ihkd->ihqk", d_mixed, values, preferred_element_type=f32)
    row_terms = jnp.sum(soft * d_soft, axis=-1, keepdims=True)
    d_scores = (soft * (d_soft - row_terms)).astype(bf16)
    d_queries = jnp.einsum("ihqk,ihkd->ihqd", d_scores, keys, preferred_element_type=f32) * 0.125
    d_keys = jnp.einsum("ihqk,ihqd->ihkd", d_scores, queries, preferred_element_type=f32) * 0.125
    d_proj = jnp.stack([d_queries, d_keys, d_values]).astype(bf16)
    d_proj = d_proj.transpose(1, 3, 0, 2, 4).reshape(rows, 3 * width)
    sums = jnp.sum(d_proj.astype(f32), axis=0)
    d_normed = jnp.einsum("se,de->sd", d_proj, qkv, preferred_element_type=f32)
    _, first_pull = jax.vjp(normalize, inputs, vec[0], vec[1])
    d_first, g0, g1 = first_pull(d_normed)
    d_inputs = d_middle + d_first
    small = jnp.stack([g0, g1, sums[:width], sums[2 * width :], g4, g5, g6, g7, g8, g9])
    return d_inputs, (d_proj, d_branch, d_hidden, d_out), small, g_bias


def with_twin(acts, c):
    tokens = acts.shape[0]
    parts = acts.T.reshape(XS, ZS, CS, -1, tokens)
    mine = pick(parts, c, 2)
    theirs = from_shard(pick(parts, 1 - c, 2), dc=1)
    return jnp.concatenate([mine, theirs], axis=-1)


def scatter_columns(d_unit):
    first = from_shard(d_unit[2, 0], dx=3)
    second = from_shard(d_unit[2, 1], dx=1)
    to_plus = jnp.stack([d_unit[1, 0].astype(f32) + first.astype(f32), d_unit[1, 1].astype(f32)]).astype(bf16)
    to_minus = jnp.stack([d_unit[3, 0].astype(f32), d_unit[3, 1].astype(f32) + second.astype(f32)]).astype(bf16)
    got_a = from_shard(to_plus, dx=3)
    got_b = from_shard(to_minus, dx=1)
    total = d_unit[0].astype(f32) + got_a.astype(f32) + got_b.astype(f32)
    got = from_shard(total[1].astype(bf16), dz=1)
    return total[0] + got.astype(f32)


def summed_over_replicas(part, y):
    low = part.astype(bf16).reshape(YS, 16, -1)
    mine = pick(part.reshape(YS, 16, -1), y, 0)
    for dy in range(1, YS):
        got = from_replica(pick(low, (y + YS - dy) % YS, 0), dy)
        mine = mine + got.astype(f32)
    mine = mine.astype(bf16)
    parts = [mine] + [from_replica(mine, dy) for dy in range(1, YS)]
    return rolled(jnp.stack(parts), (YS - y) % YS, 0).reshape(part.shape).astype(f32)


def scatter_rows(chunks, y):
    first = from_replica(chunks[2][:, :, :64], 3)
    second = from_replica(chunks[2][:, :, 64:], 1)
    add = lambda a, b: (a.astype(f32) + b.astype(f32)).astype(bf16)
    to_plus = jnp.concatenate([add(chunks[1][:, :, :64], first), chunks[1][:, :, 64:]], axis=2)
    to_minus = jnp.concatenate([chunks[3][:, :, :64], add(chunks[3][:, :, 64:], second)], axis=2)
    got_a = from_replica(to_plus, 3)
    got_b = from_replica(to_minus, 1)
    total = chunks[0].astype(f32) + got_a.astype(f32) + got_b.astype(f32)
    low = total.astype(bf16)
    mine = total[0, 0]
    for dx in range(XS):
        for dz in range(ZS):
            if (dx, dz) != (0, 0):
                mine = mine + from_shard(low[dx, dz], dx=XS - dx, dz=dz).astype(f32)
    mine = mine.astype(bf16)
    parts = [mine] + [from_replica(mine, dy) for dy in range(1, YS)]
    return rolled(jnp.stack(parts), (YS - y) % YS, 0).astype(f32)


def shards(edge_inputs, image_counts, w_qkv, w_proj, w_fc1, w_fc2, vectors, fc1_bias):
    section = lax.axis_index("section")
    shard = lax.axis_index("shard")
    y = lax.axis_index("replica")
    x, z, c = shard // 4, (shard // 2) % 2, shard % 2
    place = (x, z, c, y)
    source = edge_inputs[0, :, 0]
    present = (shard * YS + y < image_counts).astype(f32)
    layer_weights = gather_all(w_qkv[0], w_proj[0], w_fc1[0], w_fc2[0], vectors[0], fc1_bias[0], place)

    own = source.reshape(256, 1024)
    first_out, _ = forward_layer(own.astype(f32), layer_weights)
    received = passed_along(first_out.astype(bf16), 1)
    inputs = jnp.where(section == 0, own, received).astype(f32)
    output, saved = forward_layer(inputs, layer_weights)
    normed, mixed, second, activated = saved[0], saved[5], saved[8], saved[10]
    acts_a = with_twin(normed, c)
    acts_m = with_twin(mixed, c)
    acts_c = with_twin(second, c)
    acts_u = with_twin(activated, c)

    cotangent = (source.astype(f32) * present[:, None, None]).reshape(256, 1024)
    d_first, _, _, _ = backward_layer(inputs, cotangent, saved, layer_weights)
    received_grad = passed_along(d_first.astype(bf16), -1)
    upstream = jnp.where(section == 1, cotangent, received_grad.astype(f32))
    d_inputs, cots, g_small, g_bias = backward_layer(inputs, upstream, saved, layer_weights)
    d_qkv, d_proj, d_fc1, d_fc2 = [
        jnp.concatenate([v, from_shard(v, dc=1)], axis=0) for v in cots
    ]

    relative = lambda v: rolled(rolled(v, x, 0), z, 1)
    acts_a, acts_m, acts_c, acts_u = [relative(v) for v in (acts_a, acts_m, acts_c, acts_u)]
    product = lambda a, b: jnp.einsum("xzrt,tn->xzrn", a, b, preferred_element_type=f32)
    small = jnp.concatenate(
        [g_small.reshape(10, XS, ZS, CS, 64).transpose(1, 2, 3, 4, 0),
         g_bias.reshape(XS, ZS, CS, 4, 64).transpose(0, 1, 2, 4, 3)], axis=-1
    )
    mine = pick(small, c, 2)
    theirs = from_shard(pick(small, 1 - c, 2).astype(bf16), dc=1)
    small = relative(jnp.pad(mine + theirs.astype(f32), ((0, 0),) * 3 + ((0, 114),)))
    d_unit = jnp.concatenate(
        [
            product(acts_a, d_qkv).astype(bf16),
            product(acts_m, d_proj).astype(bf16),
            product(acts_u[:, :, 128:192], d_fc2).astype(bf16),
            product(acts_u[:, :, 192:], d_fc2).astype(bf16),
            small.astype(bf16),
        ],
        axis=-1,
    )
    acts_y = rolled(acts_u[:, :, :128].reshape(XS, ZS, YS, 32, 512), y, 2)
    d_fc1_y = rolled(d_fc1.reshape(512, YS, 1024), y, 1)
    chunks = [
        jnp.concatenate(
            [product(acts_c, d_fc1_y[:, dy]).astype(bf16), product(acts_y[:, :, dy], d_fc2).astype(bf16)],
            axis=2,
        )
        for dy in range(YS)
    ]
    rows = scatter_rows(chunks, y)
    columns = summed_over_replicas(scatter_columns(d_unit), y)
    grad_qkv = columns[:, :3072]
    grad_proj = columns[:, 3072:4096]
    grad_fc1 = rows[:, :64].transpose(1, 0, 2).reshape(64, 4096)
    grad_fc2 = jnp.concatenate(
        [rows[:, 64:].reshape(128, 1024), columns[:, 4096:5120], columns[:, 5120:6144]], axis=0
    )
    grad_vec = columns[:, 6144:6154].T
    grad_bias = columns[:, 6154:6158].T.reshape(256)
    edge_values = jnp.where(section == 0, d_inputs, output).reshape(1, 2, 1, 128, 1024)
    return (
        edge_values,
        grad_qkv[None],
        grad_proj[None],
        grad_fc1[None],
        grad_fc2[None],
        grad_vec[None],
        grad_bias[None],
    )


def solution(mesh):
    placed = (
        P("section", None, ("shard", "replica"), None, None),
        P(),
        P("section", "shard", None),
        P("section", "shard", None),
        P("section", "shard", None),
        P("section", "shard", None),
        P("section", None, "shard"),
        P("section", "shard"),
    )
    return jax.shard_map(
        shards,
        mesh=mesh,
        in_specs=placed,
        out_specs=(placed[0],) + placed[2:],
        check_vma=False,
    )
```

time: 885 us -> 661 us (0.75)
  waiting for transfers between devices: 344 us -> 159 us
  matrix products: 304 us -> 125 us
  local copies, waits for them, and re-layouts: 69.9 us -> 168 us
  other arithmetic: 44.7 us -> 129 us
  blocking collectives: 79.8 us -> 0 us
  starting transfers between devices: 14.4 us -> 66.5 us
  between operations: 17.2 us -> 2.68 us
    dot_general x66 -> x36, matrix products: 294 us -> 118 us  [the longest x2 22.4 us: forward_layer(): out_branch = jnp.dot(activated, fc2, preferred_element_type=f32) + vec[8]]
    reduce_scatter x4 -> x0, waiting for transfers between devices: 155 us -> none  [the longest x1 100 us: shards(): lax.psum_scatter(totals[3].astype(jnp.bfloat16), 'shard', scatter_dimensi...]
    ppermute x4 -> x62, waiting for transfers between devices: 13.4 us -> 159 us  [the longest x43 81.6 us: from_shard(): return lax.ppermute(value, 'shard', pairs)]
    all_gather x4 -> x0, waiting for transfers between devices: 106 us -> none  [the longest x1 54.6 us: gather_again(): lax.all_gather(weight_fc1, 'shard', axis=0, tiled=True)]
    concatenate x1 -> x25, other arithmetic: 0.01 us -> 76.4 us  [the longest x15 66.4 us: rolled(): twice = jnp.concatenate([array, array], axis=axis)]
    ppermute x4 -> x62, starting transfers between devices: 13.8 us -> 66.5 us  [the longest x43 40.4 us: from_shard(): return lax.ppermute(value, 'shard', pairs)]
    reshape x0 -> x12, local copies, waits for them, and re-layouts: none -> 43.2 us  [the longest x4 28.7 us: forward_layer(): projected.reshape(images, 128, 3, heads, HEAD_DIM).transpose(2, 0, 3, 1, 4)]
    psum x1 -> x0, waiting for transfers between devices: 39.4 us -> none  [shards(): lax.psum(shortened(totals), 'replica')]
  transfers between devices with their start and end apart: 14 -> 62, of which waited for: 10 -> 21; matrix products, arithmetic and copies ran while one was open for 29% -> 34% of each run, Pallas kernels for 0% -> 0%
where the time goes in v1:
time: 661 us; the launch traced here: 651 us
  local copies, waits for them, and re-layouts  168 us (25%)
  waiting for transfers between devices  159 us (24%)
  other arithmetic  129 us (20%)
  matrix products  125 us (19%)
  starting transfers between devices  66.5 us (10%)
    ppermute x43, waiting for transfers between devices, from_shard(): return lax.ppermute(value, 'shard', pairs)  81.6 us
    ppermute x17, waiting for transfers between devices, from_replica(): lax.ppermute(value, 'replica', [((y + dy) % YS, y) for y in range(YS)])  66.6 us
    concatenate x15, other arithmetic, rolled(): twice = jnp.concatenate([array, array], axis=axis)  66.4 us
    ppermute x43, starting transfers between devices, from_shard(): return lax.ppermute(value, 'shard', pairs)  40.4 us
    unnamed x120, local copies, waits for them, and re-layouts  38.2 us
    reshape x4, local copies, waits for them, and re-layouts, forward_layer(): projected.reshape(images, 128, 3, heads, HEAD_DIM).transpose(2, 0, 3, 1, 4)  28.7 us
    dot_general x2, matrix products, forward_layer(): out_branch = jnp.dot(activated, fc2, preferred_element_type=f32) + vec[8]  22.4 us
    dynamic_slice x3, local copies, waits for them, and re-layouts, pick(): return lax.dynamic_index_in_dim(array, index, axis, keepdims=keep)  20.2 us
  transfers between devices with their start and end apart: 62, of which 21 were waited for; matrix products, arithmetic and copies ran while one was open for 34% of the time, Pallas kernels for 0%

profile of v1, /device:TPU:0, one launch (start us, length us, event | category | flops | bytes accessed | tf_op | source)
XLA Modules:
  0.0 651.1 jit_solution(4821285194287682968)
XLA Ops:
  27.3 15.5 %collective-permute-done = bf16[64,6272]{1,0:T(8,128)(2,1)S(1)} collective-permute-done((bf16[64,6272]{1,0:T(8,128)(2,1)S(1)}, bf16[64,6272]{1,0:T(8,128)(2,1)S(1)}, u32[]{:S(2)}, u32[]{:S(2)}) %collective-permute-start) | collective-permute-done | bytes 802848 | tf_op jit(solution)/shard_map/ppermute | solution.py:23
  53.4 32.0 %collective-permute-done.17 = bf16[8,96,1024]{2,1,0:T(8,128)(2,1)S(1)} collective-permute-done((bf16[8,96,1024]{2,1,0:T(8,128)(2,1)}, bf16[8,96,1024]{2,1,0:T(8,128)(2,1)S(1)}, u32[]{:S(2)}, u32[]{:S(2)}) %collective-permute-start.17) | collective-permute-done | bytes 1572896 | tf_op jit(solution)/shard_map/ppermute | solution.py:27
  100.4 12.5 %collective-permute-done.20 = bf16[8,32,1024]{2,1,0:T(8,128)(2,1)S(1)} collective-permute-done((bf16[8,32,1024]{2,1,0:T(8,128)(2,1)S(1)}, bf16[8,32,1024]{2,1,0:T(8,128)(2,1)S(1)}, u32[]{:S(2)}, u32[]{:S(2)}) %collective-permute-start.20) | collective-permute-done | bytes 524320 | tf_op jit(solution)/shard_map/ppermute | solution.py:27
  122.8 19.9 %fusion.16 = bf16[2,4,4,2,96,1024]{5,4,1,0,3,2:T(8,128)(2,1)S(1)} fusion(s32[]{:T(128)S(6)} %select_n.152, bf16[1,1,4,2,96,1024]{5,4,1,0,3,2:T(8,128)(2,1)} %bitcast.49, bf16[1,1,4,2,96,1024]{5,4,1,0,3,2:T(8,128)(2,1)S(1)} %bitcast.610, bf16[1,1,4,2,96,1024]{5,4,1,0,3,2:T(8,128)(2,1)S(1)} %bitcast.602, bf16[1,1,4,2,96,1024]{5,4,1,0,3,2:T(8,128)(2,1)} %bitcast.52, ...), kind=kLoop, calls=%fused_computation.46 | loop fusion | flops 94371840 | bytes 25165828 | tf_op jit(solution)/shard_map/concatenate | solution.py:41
  154.7 8.2 %fusion.8 = bf16[2,4,4,2,96,1024]{5,4,1,0,3,2:T(8,128)(2,1)S(1)} fusion(s32[]{:T(128)S(6)} %select_n.159, bf16[2,4,4,2,96,1024]{5,4,1,0,3,2:T(8,128)(2,1)} %fusion.9), kind=kLoop, calls=%fused_computation.38 | loop fusion | flops 6291456 | bytes 25165828 | tf_op jit(solution)/shard_map/concatenate | solution.py:41
  169.9 8.4 %slice_bitcast_fusion = bf16[4,2,2,64,4,1024]{5,3,4,2,1,0:T(8,128)(2,1)} fusion(bf16[2,4,4,2,96,1024]{5,4,1,0,3,2:T(8,128)(2,1)} %copy-done.2), kind=kLoop, calls=%fused_computation.56 | loop fusion | bytes 16777216 | tf_op jit(solution)/shard_map/transpose | solution.py:114
  178.3 11.1 %copy.275 = bf16[4,2,2,64,4,1024]{5,4,3,2,1,0:T(4,128)(2,1)} copy(bf16[4,2,2,64,4,1024]{5,3,4,2,1,0:T(8,128)(2,1)} %slice_bitcast_fusion) | data formatting | bytes 16777216 | tf_op jit(solution)/shard_map/transpose | solution.py:114
  189.4 12.1 %copy.349 = bf16[128,8,4,1024]{3,1,2,0:T(8,128)(2,1)} copy(bf16[128,8,4,1024]{3,2,1,0:T(4,128)(2,1)} %bitcast.558) | data formatting | bytes 16777216
  207.0 9.5 %fusion.7 = bf16[2,4,2,64,6272]{4,3,0,2,1:T(8,128)(2,1)S(1)} fusion(s32[]{:T(128)S(6)} %select_n.152, bf16[1,4,2,64,6272]{4,3,0,2,1:T(8,128)(2,1)S(1)} %bitcast.568, bf16[1,4,2,64,6272]{4,3,0,2,1:T(8,128)(2,1)S(1)} %maximum_bitcast_fusion.1), kind=kLoop, calls=%fused_computation.37 | loop fusion | flops 19267584 | bytes 25690116 | tf_op jit(solution)/shard_map/concatenate | solution.py:41
  216.5 8.2 %fusion.4 = bf16[2,4,2,64,6272]{4,3,0,2,1:T(8,128)(2,1)} fusion(s32[]{:T(128)S(6)} %select_n.155, bf16[2,4,2,64,6272]{4,3,0,2,1:T(8,128)(2,1)S(1)} %fusion.7), kind=kLoop, calls=%fused_computation.34 | loop fusion | flops 6422528 | bytes 25690116 | tf_op jit(solution)/shard_map/concatenate | solution.py:41
  224.7 9.2 %fusion.3 = bf16[4,2,2,64,6272]{4,3,2,1,0:T(8,128)(2,1)S(1)} fusion(s32[]{:T(128)S(6)} %select_n.159, bf16[2,4,2,64,6272]{4,3,0,2,1:T(8,128)(2,1)} %fusion.4), kind=kLoop, calls=%fused_computation.33 | loop fusion | flops 6422528 | bytes 25690116 | tf_op jit(solution)/shard_map/transpose | solution.py:107
  253.2 13.5 %copy.272 = bf16[2,128,3,16,64]{1,4,3,0,2:T(8,128)(2,1)} copy(bf16[2,128,3,16,64]{4,3,2,1,0:T(8,128)(2,1)} %reshape.418) | data formatting | bytes 3145728 | tf_op jit(solution)/shard_map/reshape | solution.py:129
  280.3 8.2 %pad_maximum_fusion = bf16[16,256,1024]{2,1,0:T(8,128)(2,1)} fusion(bf16[16,128,1024]{2,1,0:T(8,128)(2,1)} %bitcast.577, bf16[16,128,1024]{2,1,0:T(8,128)(2,1)} %bitcast.576), kind=kLoop, calls=%fused_computation.57 | loop fusion | flops 16777216 | bytes 16777216 | tf_op jit(solution)/shard_map/concatenate | solution.py:116
  288.5 18.9 %fusion.147 = bf16[256,1024]{1,0:T(8,128)(2,1)S(1)} fusion(f32[256,1024]{1,0:T(8,128)S(1)} %copy-done.19, bf16[4096,1024]{1,0:T(8,128)(2,1)} %bitcast.559, bf16[1024,4096]{1,0:T(8,128)(2,1)} %bitcast.586, f32[4096]{0:T(1024)S(1)} %reshape.406, f32[1024]{0:T(1024)S(1)} %add.381, f32[1024]{0:T(1024)S(1)} %add.372, f32[1024]{0:T(1024)S(1)} %mul.428, ...), kind=kOutput, calls=%fused_computation.282 | convolution fusion | flops 4366532608 | bytes 18384896 | tf_op jit(solution)/shard_map/dot_general | solution.py:140
  312.8 11.1 %collective-permute-done.26 = bf16[256,1024]{1,0:T(8,128)(2,1)S(1)} collective-permute-done((bf16[256,1024]{1,0:T(8,128)(2,1)S(1)}, bf16[256,1024]{1,0:T(8,128)(2,1)S(1)}, u32[]{:S(2)}, u32[]{:S(2)}) %collective-permute-start.26) | collective-permute-done | bytes 524320 | tf_op jit(solution)/shard_map/ppermute | solution.py:32
  348.9 15.6 %fusion.30 = (f32[256,4096]{1,0:T(8,128)}, f32[256,4096]{1,0:T(8,128)}) fusion(f32[4096]{0:T(1024)S(1)} %reshape.406, bf16[1024,4096]{1,0:T(8,128)(2,1)} %bitcast.587, f32[256,1024]{1,0:T(8,128)S(1)} %get-tuple-element.83, f32[256]{0:T(256)S(1)} %fusion.245, f32[256]{0:T(256)S(1)} %broadcast_multiply_fusion, f32[1024]{0:T(1024)S(1)} %add.372, ...), kind=kOutput, calls=%fused_computation.72 | convolution fusion | flops 2214854656 | bytes 17852416 | tf_op jit(solution)/shard_map/dot_general | solution.py:138
  364.5 12.4 %multiply_reduce_fusion.8 = (f32[256]{0:T(256)S(1)}, f32[256,1024]{1,0:T(8,128)}) fusion(f32[256,1024]{1,0:T(8,128)S(1)} %get-tuple-element.83, f32[256]{0:T(256)S(1)} %broadcast_multiply_fusion, f32[1024]{0:T(1024)S(1)} %mul.428, bf16[1024,4096]{1,0:T(8,128)(2,1)} %bitcast.588, f32[256,4096]{1,0:T(8,128)} %get-tuple-element.140, ...), kind=kOutput, calls=%fused_computation.350 | convolution fusion | flops 4310695936 | bytes 27793408 | tf_op jit(solution)/shard_map/sf,df->sd/dot_general | solution.py:156
  390.5 10.0 %fusion.33 = bf16[4096,256]{0,1:T(8,128)(2,1)} fusion(f32[256,4096]{1,0:T(8,128)S(1)} %copy-done.7), kind=kLoop, calls=%fused_computation.75 | loop fusion | flops 68157440 | bytes 6291456 | tf_op jit(solution)/shard_map/convert_element_type | solution.py:139
  411.9 8.6 %constant_dynamic-slice_fusion.1 = (bf16[4,2,1,256,256]{3,2,1,0,4:T(2,128)(2,1)}, bf16[4,2,1,256,256]{3,2,1,0,4:T(2,128)(2,1)}) fusion(bf16[4,2,2,256,256]{3,2,1,0,4:T(2,128)(2,1)} %reshape.398, s32[]{:T(128)S(6)} %select_n.168, s32[]{:T(128)S(6)} %select_n.167), kind=kLoop, calls=%fused_computation.500 | loop fusion | bytes 4194312 | tf_op jit(solution)/shard_map/jit(dynamic_index_in_dim)/dynamic_slice | solution.py:36
  434.8 12.1 %convert_reduce_fusion = (f32[4096]{0:T(1024)S(1)}, bf16[256,4096]{1,0:T(8,128)(2,1)S(1)}) fusion(f32[256,4096]{1,0:T(8,128)} %get-tuple-element.140, f32[256,4096]{1,0:T(8,128)} %get-tuple-element.141, bf16[256,1024]{1,0:T(8,128)(2,1)S(1)} %get-tuple-element.67, bf16[4096,1024]{1,0:T(8,128)(2,1)} %bitcast.561), kind=kOutput, calls=%fused_computation.91 | convolution fusion | flops 2164256768 | bytes 19415040 | tf_op jit(solution)/shard_map/sd,fd->sf/dot_general | solution.py:152
  525.9 14.5 %collective-permute-done.35 = bf16[64,6272]{1,0:T(8,128)(2,1)S(1)} collective-permute-done((bf16[64,6272]{1,0:T(8,128)(2,1)S(1)}, bf16[64,6272]{1,0:T(8,128)(2,1)S(1)}, u32[]{:S(2)}, u32[]{:S(2)}) %collective-permute-start.35) | collective-permute-done | bytes 802848 | tf_op jit(solution)/shard_map/ppermute | solution.py:23
  552.9 24.5 %collective-permute-done.38 = bf16[2,64,6272]{2,1,0:T(8,128)(2,1)S(1)} collective-permute-done((bf16[2,64,6272]{2,1,0:T(8,128)(2,1)S(1)}, bf16[2,64,6272]{2,1,0:T(8,128)(2,1)S(1)}, u32[]{:S(2)}, u32[]{:S(2)}) %collective-permute-start.38) | collective-permute-done | bytes 1605664 | tf_op jit(solution)/shard_map/ppermute | solution.py:23
  595.7 12.2 %collective-permute-done.39 = bf16[64,6272]{1,0:T(8,128)(2,1)S(1)} collective-permute-done((bf16[64,6272]{1,0:T(8,128)(2,1)S(1)}, bf16[64,6272]{1,0:T(8,128)(2,1)S(1)}, u32[]{:S(2)}, u32[]{:S(2)}) %collective-permute-start.39) | collective-permute-done | bytes 802848 | tf_op jit(solution)/shard_map/ppermute | solution.py:23
  620.2 8.2 %collective-permute-done.42 = bf16[16,6272]{1,0:T(8,128)(2,1)S(1)} collective-permute-done((bf16[16,6272]{1,0:T(8,128)(2,1)S(1)}, bf16[16,6272]{1,0:T(8,128)(2,1)S(1)}, u32[]{:S(2)}, u32[]{:S(2)}) %collective-permute-start.42) | collective-permute-done | bytes 200736 | tf_op jit(solution)/shard_map/ppermute | solution.py:27
  (446 shorter events, 331.9 us)
Async XLA Ops:
  19.9 28.1 %collective-permute-start.16 = (bf16[96,1024]{1,0:T(8,128)(2,1)S(1)}, bf16[96,1024]{1,0:T(8,128)(2,1)S(1)}, u32[]{:S(2)}, u32[]{:S(2)}) collective-permute-start(bf16[96,1024]{1,0:T(8,128)(2,1)S(1)} %pad_maximum_fusion.9), channel_id=1, source_target_pairs={{56,0},{60,4},{48,8},{52,12},{8,16},{12,20},{0,24},{4,28},{24,32},... | collective-permute-start | bytes 589832 | tf_op jit(solution)/shard_map/ppermute | solution.py:23
  44.2 47.1 %collective-permute-start.3 = (bf16[2,64,6272]{2,1,0:T(8,128)(2,1)}, bf16[2,64,6272]{2,1,0:T(8,128)(2,1)S(1)}, u32[]{:S(2)}, u32[]{:S(2)}) collective-permute-start(bf16[2,64,6272]{2,1,0:T(8,128)(2,1)} %get-tuple-element.98), channel_id=1, source_target_pairs={{48,0},{52,4},{56,8},{60,12},{0,16},{4,20},{8,24},{12,28},{16,32},... | collective-permute-start | bytes 4816904 | tf_op jit(solution)/shard_map/ppermute | solution.py:23
  48.7 36.8 %collective-permute-start.17 = (bf16[8,96,1024]{2,1,0:T(8,128)(2,1)}, bf16[8,96,1024]{2,1,0:T(8,128)(2,1)S(1)}, u32[]{:S(2)}, u32[]{:S(2)}) collective-permute-start(bf16[8,96,1024]{2,1,0:T(8,128)(2,1)} %bitcast_dynamic-update-slice_fusion.17), channel_id=1, source_target_pairs={{1,0},{2,1},{3,2},{0,3},{5,4},{6,5},{7,6},{4,7},{9,8},{10,9},{11,1... | collective-permute-start | bytes 4718600 | tf_op jit(solution)/shard_map/ppermute | solution.py:27
  51.8 46.9 %collective-permute-start.19 = (bf16[8,96,1024]{2,1,0:T(8,128)(2,1)}, bf16[8,96,1024]{2,1,0:T(8,128)(2,1)}, u32[]{:S(2)}, u32[]{:S(2)}) collective-permute-start(bf16[8,96,1024]{2,1,0:T(8,128)(2,1)} %bitcast_dynamic-update-slice_fusion.17), channel_id=1, source_target_pairs={{3,0},{0,1},{1,2},{2,3},{7,4},{4,5},{5,6},{6,7},{11,8},{8,9},{9,10... | collective-permute-start | bytes 4718600 | tf_op jit(solution)/shard_map/ppermute | solution.py:27
  51.9 41.8 %collective-permute-start.1 = (bf16[2,64,6272]{2,1,0:T(8,128)(2,1)}, bf16[2,64,6272]{2,1,0:T(8,128)(2,1)}, u32[]{:S(2)}, u32[]{:S(2)}) collective-permute-start(bf16[2,64,6272]{2,1,0:T(8,128)(2,1)} %get-tuple-element.98), channel_id=1, source_target_pairs={{16,0},{20,4},{24,8},{28,12},{32,16},{36,20},{40,24},{44,28},{48,3... | collective-permute-start | bytes 4816904 | tf_op jit(solution)/shard_map/ppermute | solution.py:23
  87.7 25.3 %collective-permute-start.18 = (bf16[8,64,1024]{2,1,0:T(8,128)(2,1)}, bf16[8,64,1024]{2,1,0:T(8,128)(2,1)S(1)}, u32[]{:S(2)}, u32[]{:S(2)}) collective-permute-start(bf16[8,64,1024]{2,1,0:T(8,128)(2,1)} %slice.329), channel_id=1, source_target_pairs={{1,0},{2,1},{3,2},{0,3},{5,4},{6,5},{7,6},{4,7},{9,8},{10,9},{11,1... | collective-permute-start | bytes 3145736 | tf_op jit(solution)/shard_map/ppermute | solution.py:27
  100.3 21.3 %collective-permute-start.21 = (bf16[8,96,1024]{2,1,0:T(8,128)(2,1)}, bf16[8,96,1024]{2,1,0:T(8,128)(2,1)S(1)}, u32[]{:S(2)}, u32[]{:S(2)}) collective-permute-start(bf16[8,96,1024]{2,1,0:T(8,128)(2,1)} %bitcast_dynamic-update-slice_fusion.17), channel_id=1, source_target_pairs={{4,0},{0,4},{12,8},{8,12},{20,16},{16,20},{28,24},{24,28},{36,32},... | collective-permute-start | bytes 4718600 | tf_op jit(solution)/shard_map/ppermute | solution.py:23
  120.9 82.3 %collective-permute-start.5 = (bf16[2,64,6272]{2,1,0:T(8,128)(2,1)}, bf16[2,64,6272]{2,1,0:T(8,128)(2,1)S(1)}, u32[]{:S(2)}, u32[]{:S(2)}) collective-permute-start(bf16[2,64,6272]{2,1,0:T(8,128)(2,1)} %get-tuple-element.98), channel_id=1, source_target_pairs={{4,0},{0,4},{12,8},{8,12},{20,16},{16,20},{28,24},{24,28},{36,32},... | collective-permute-start | bytes 4816904 | tf_op jit(solution)/shard_map/ppermute | solution.py:23
  121.4 81.8 %collective-permute-start.9 = (bf16[2,64,6272]{2,1,0:T(8,128)(2,1)S(1)}, bf16[2,64,6272]{2,1,0:T(8,128)(2,1)S(1)}, u32[]{:S(2)}, u32[]{:S(2)}) collective-permute-start(bf16[2,64,6272]{2,1,0:T(8,128)(2,1)S(1)} %copy-done.25), channel_id=1, source_target_pairs={{4,0},{0,4},{12,8},{8,12},{20,16},{16,20},{28,24},{24,28},{36,32},... | collective-permute-start | bytes 4816904 | tf_op jit(solution)/shard_map/ppermute | solution.py:23
  121.6 81.5 %collective-permute-start.6 = (bf16[2,64,6272]{2,1,0:T(8,128)(2,1)}, bf16[2,64,6272]{2,1,0:T(8,128)(2,1)}, u32[]{:S(2)}, u32[]{:S(2)}) collective-permute-start(bf16[2,64,6272]{2,1,0:T(8,128)(2,1)} %collective-permute-done.1), channel_id=1, source_target_pairs={{4,0},{0,4},{12,8},{8,12},{20,16},{16,20},{28,24},{24,28},{36,32},... | collective-permute-start | bytes 4816904 | tf_op jit(solution)/shard_map/ppermute | solution.py:23
  122.1 79.5 %collective-permute-start.8 = (bf16[64,6272]{1,0:T(8,128)(2,1)}, bf16[64,6272]{1,0:T(8,128)(2,1)}, u32[]{:S(2)}, u32[]{:S(2)}) collective-permute-start(bf16[64,6272]{1,0:T(8,128)(2,1)} %collective-permute-done.4), channel_id=1, source_target_pairs={{4,0},{0,4},{12,8},{8,12},{20,16},{16,20},{28,24},{24,28},{36,32},... | collective-permute-start | bytes 2408456 | tf_op jit(solution)/shard_map/ppermute | solution.py:23
  122.2 79.4 %collective-permute-start.7 = (bf16[64,6272]{1,0:T(8,128)(2,1)}, bf16[64,6272]{1,0:T(8,128)(2,1)}, u32[]{:S(2)}, u32[]{:S(2)}) collective-permute-start(bf16[64,6272]{1,0:T(8,128)(2,1)} %collective-permute-done.2), channel_id=1, source_target_pairs={{4,0},{0,4},{12,8},{8,12},{20,16},{16,20},{28,24},{24,28},{36,32},... | collective-permute-start | bytes 2408456 | tf_op jit(solution)/shard_map/ppermute | solution.py:23
  405.3 29.2 %collective-permute-start.27 = (bf16[256,1024]{1,0:T(8,128)(2,1)S(1)}, bf16[256,1024]{1,0:T(8,128)(2,1)S(1)}, u32[]{:S(2)}, u32[]{:S(2)}) collective-permute-start(bf16[256,1024]{1,0:T(8,128)(2,1)S(1)} %add_convert_fusion.6), channel_id=1, source_target_pairs={{64,0},{65,1},{66,2},{67,3},{68,4},{69,5},{70,6},{71,7},{72,8},{73... | collective-permute-start | bytes 1572872 | tf_op jit(solution)/shard_map/ppermute | solution.py:32
  407.4 25.1 %collective-permute-start.30 = (bf16[4,2,64,256]{3,2,1,0:T(8,128)(2,1)}, bf16[4,2,64,256]{3,2,1,0:T(8,128)(2,1)}, u32[]{:S(2)}, u32[]{:S(2)}) collective-permute-start(bf16[4,2,64,256]{3,2,1,0:T(8,128)(2,1)} %get-tuple-element.115), channel_id=1, source_target_pairs={{4,0},{0,4},{12,8},{8,12},{20,16},{16,20},{28,24},{24,28},{36,32},... | collective-permute-start | bytes 786440 | tf_op jit(solution)/shard_map/ppermute | solution.py:23
  432.0 73.2 %collective-permute-start.32 = (bf16[4,2,256,256]{3,2,1,0:T(8,128)(2,1)}, bf16[4,2,256,256]{3,2,1,0:T(8,128)(2,1)}, u32[]{:S(2)}, u32[]{:S(2)}) collective-permute-start(bf16[4,2,256,256]{3,2,1,0:T(8,128)(2,1)} %bitcast.630), channel_id=1, source_target_pairs={{4,0},{0,4},{12,8},{8,12},{20,16},{16,20},{28,24},{24,28},{36,32},... | collective-permute-start | bytes 3145736 | tf_op jit(solution)/shard_map/ppermute | solution.py:23
  477.2 38.3 %collective-permute-start.31 = (bf16[256,1024]{1,0:T(8,128)(2,1)}, bf16[256,1024]{1,0:T(8,128)(2,1)}, u32[]{:S(2)}, u32[]{:S(2)}) collective-permute-start(bf16[256,1024]{1,0:T(8,128)(2,1)} %get-tuple-element.71), channel_id=1, source_target_pairs={{4,0},{0,4},{12,8},{8,12},{20,16},{16,20},{28,24},{24,28},{36,32},... | collective-permute-start | bytes 1572872 | tf_op jit(solution)/shard_map/ppermute | solution.py:23
  480.4 31.9 %collective-permute-start.29 = (bf16[256,3072]{1,0:T(8,128)(2,1)}, bf16[256,3072]{1,0:T(8,128)(2,1)}, u32[]{:S(2)}, u32[]{:S(2)}) collective-permute-start(bf16[256,3072]{1,0:T(8,128)(2,1)} %copy.298), channel_id=1, source_target_pairs={{4,0},{0,4},{12,8},{8,12},{20,16},{16,20},{28,24},{24,28},{36,32},... | collective-permute-start | bytes 4718600 | tf_op jit(solution)/shard_map/ppermute | solution.py:23
  509.2 35.9 %collective-permute-start.50 = (bf16[4,2,32,1024]{3,2,1,0:T(8,128)(2,1)S(1)}, bf16[4,2,32,1024]{3,2,1,0:T(8,128)(2,1)S(1)}, u32[]{:S(2)}, u32[]{:S(2)}) collective-permute-start(bf16[4,2,32,1024]{3,2,1,0:T(8,128)(2,1)S(1)} %convolution_convert_fusion.8), channel_id=1, source_target_pairs={{1,0},{2,1},{3,2},{0,3},{5,4},{6,5},{7,6},{4,7},{9,8},{10,9},{11,1... | collective-permute-start | bytes 1572872 | tf_op jit(solution)/shard_map/ppermute | solution.py:27
  525.8 25.9 %collective-permute-start.48 = (bf16[4,2,64,1024]{3,2,1,0:T(8,128)(2,1)S(1)}, bf16[4,2,64,1024]{3,2,1,0:T(8,128)(2,1)S(1)}, u32[]{:S(2)}, u32[]{:S(2)}) collective-permute-start(bf16[4,2,64,1024]{3,2,1,0:T(8,128)(2,1)S(1)} %convolution_convert_fusion.2), channel_id=1, source_target_pairs={{3,0},{0,1},{1,2},{2,3},{7,4},{4,5},{5,6},{6,7},{11,8},{8,9},{9,10... | collective-permute-start | bytes 3145736 | tf_op jit(solution)/shard_map/ppermute | solution.py:27
  540.9 36.5 %collective-permute-start.38 = (bf16[2,64,6272]{2,1,0:T(8,128)(2,1)S(1)}, bf16[2,64,6272]{2,1,0:T(8,128)(2,1)S(1)}, u32[]{:S(2)}, u32[]{:S(2)}) collective-permute-start(bf16[2,64,6272]{2,1,0:T(8,128)(2,1)S(1)} %pad_maximum_fusion.4), channel_id=1, source_target_pairs={{16,0},{20,4},{24,8},{28,12},{32,16},{36,20},{40,24},{44,28},{48,3... | collective-permute-start | bytes 4816904 | tf_op jit(solution)/shard_map/ppermute | solution.py:23
  544.1 36.9 %collective-permute-start.36 = (bf16[2,64,6272]{2,1,0:T(8,128)(2,1)S(1)}, bf16[2,64,6272]{2,1,0:T(8,128)(2,1)S(1)}, u32[]{:S(2)}, u32[]{:S(2)}) collective-permute-start(bf16[2,64,6272]{2,1,0:T(8,128)(2,1)S(1)} %pad_maximum_fusion.3), channel_id=1, source_target_pairs={{48,0},{52,4},{56,8},{60,12},{0,16},{4,20},{8,24},{12,28},{16,32},... | collective-permute-start | bytes 4816904 | tf_op jit(solution)/shard_map/ppermute | solution.py:23
  546.5 36.4 %collective-permute-start.51 = (bf16[4,2,96,1024]{3,2,1,0:T(8,128)(2,1)S(1)}, bf16[4,2,96,1024]{3,2,1,0:T(8,128)(2,1)S(1)}, u32[]{:S(2)}, u32[]{:S(2)}) collective-permute-start(bf16[4,2,96,1024]{3,2,1,0:T(8,128)(2,1)S(1)} %pad_maximum_fusion.8), channel_id=1, source_target_pairs={{1,0},{2,1},{3,2},{0,3},{5,4},{6,5},{7,6},{4,7},{9,8},{10,9},{11,1... | collective-permute-start | bytes 4718600 | tf_op jit(solution)/shard_map/ppermute | solution.py:27
  552.5 36.4 %collective-permute-start.49 = (bf16[4,2,96,1024]{3,2,1,0:T(8,128)(2,1)S(1)}, bf16[4,2,96,1024]{3,2,1,0:T(8,128)(2,1)S(1)}, u32[]{:S(2)}, u32[]{:S(2)}) collective-permute-start(bf16[4,2,96,1024]{3,2,1,0:T(8,128)(2,1)S(1)} %pad_maximum_fusion.7), channel_id=1, source_target_pairs={{3,0},{0,1},{1,2},{2,3},{7,4},{4,5},{5,6},{6,7},{11,8},{8,9},{9,10... | collective-permute-start | bytes 4718600 | tf_op jit(solution)/shard_map/ppermute | solution.py:27
  581.7 26.2 %collective-permute-start.39 = (bf16[64,6272]{1,0:T(8,128)(2,1)S(1)}, bf16[64,6272]{1,0:T(8,128)(2,1)S(1)}, u32[]{:S(2)}, u32[]{:S(2)}) collective-permute-start(bf16[64,6272]{1,0:T(8,128)(2,1)S(1)} %fusion.183), channel_id=1, source_target_pairs={{8,0},{12,4},{0,8},{4,12},{24,16},{28,20},{16,24},{20,28},{40,32},... | collective-permute-start | bytes 2408456 | tf_op jit(solution)/shard_map/ppermute | solution.py:23
  (86 other events, 894.6 us)

commit v2 on v1

v2 whole, which is shorter than its diff:
```python
import jax
import jax.numpy as jnp
from jax import lax
from jax.experimental import pallas as pl
from jax.experimental.pallas import tpu as pltpu
from jax.sharding import PartitionSpec as P

XS, ZS, CS, YS = 4, 2, 2, 4
T = 256
D, FF = 1024, 4096
UNIT = 6272
QP = 4224
epsilon = 1e-06
bf16, f32 = jnp.bfloat16, jnp.float32
ANY = pl.BlockSpec(memory_space=pl.ANY)
VM = pl.BlockSpec(memory_space=pltpu.VMEM)
NT = (((1,), (1,)), ((), ()))
TN = (((0,), (0,)), ((), ()))


def shard_of(x, z, c):
    return (x % XS) * 4 + (z % ZS) * 2 + (c % CS)


def from_shard(value, dx=0, dz=0, dc=0):
    pairs = [
        (shard_of(x + dx, z + dz, c + dc), shard_of(x, z, c))
        for x in range(XS)
        for z in range(ZS)
        for c in range(CS)
    ]
    return lax.ppermute(value, "shard", pairs)


def from_replica(value, dy):
    return lax.ppermute(value, "replica", [((y + dy) % YS, y) for y in range(YS)])


def passed_along(value, steps):
    return lax.ppermute(value, "section", [(0, 1)] if steps == 1 else [(1, 0)])


def place():
    shard = lax.axis_index("shard")
    x = lax.div(shard, jnp.int32(4))
    z = lax.rem(lax.div(shard, jnp.int32(2)), jnp.int32(2))
    c = lax.rem(shard, jnp.int32(2))
    return x, z, c, lax.axis_index("replica")


def near(base, step, size):
    return lax.rem(base + jnp.int32(step), jnp.int32(size))


def call(kernel, outs, args, kinds, scratch=(), flops=0, moved=0, out_kinds=None, name=None):
    return pl.pallas_call(
        kernel,
        out_shape=[jax.ShapeDtypeStruct(s, d) for s, d in outs],
        in_specs=list(kinds),
        out_specs=list(out_kinds or [VM] * len(outs)),
        scratch_shapes=list(scratch),
        compiler_params=pltpu.CompilerParams(vmem_limit_bytes=56 * 2**20),
        cost_estimate=pl.CostEstimate(flops=flops, bytes_accessed=moved, transcendentals=0),
        name=name,
    )(*args)


def dot(a, b, dims=(((1,), (0,)), ((), ()))):
    return lax.dot_general(a, b, dims, preferred_element_type=f32)


def stats(values):
    average = jnp.mean(values, axis=-1, keepdims=True)
    centered = values - average
    spread = jnp.mean(centered * centered, axis=-1, keepdims=True)
    scale = lax.rsqrt(spread + epsilon)
    return centered * scale, scale


def norm_back(grad, gain, hat, scale):
    d_hat = grad * gain
    d_in = scale * (
        d_hat - jnp.mean(d_hat, axis=-1, keepdims=True) - hat * jnp.mean(d_hat * hat, axis=-1, keepdims=True)
    )
    return d_in, jnp.sum(grad * hat, axis=0, keepdims=True), jnp.sum(grad, axis=0, keepdims=True)


def pack_kernel(qkv, proj, fc1, fc2, vectors, bias, unit, piece, small, sems):
    _, _, _, y = place()
    small[...] = jnp.zeros_like(small)
    small[0:10, 0:64] = vectors[...].astype(f32)
    small[16:18, :] = bias[...].astype(f32)
    low = small[...].astype(bf16)
    copies = [
        pltpu.make_async_copy(fc1.at[:, pl.ds(pl.multiple_of(y * 1024, 1024), 1024)], piece.at[0:64], sems.at[0]),
        pltpu.make_async_copy(fc2.at[pl.ds(pl.multiple_of(y * 32, 32), 32)], piece.at[64:96], sems.at[1]),
        pltpu.make_async_copy(qkv, unit.at[:, 0:3072], sems.at[2]),
        pltpu.make_async_copy(proj, unit.at[:, 3072:4096], sems.at[3]),
        pltpu.make_async_copy(fc2.at[128:192], unit.at[:, 4096:5120], sems.at[4]),
        pltpu.make_async_copy(fc2.at[192:256], unit.at[:, 5120:6144], sems.at[5]),
    ]
    for copy in copies:
        copy.start()
    for copy in copies:
        copy.wait()
    unit[:, 6144:6272] = low


def pack(w_qkv, w_proj, w_fc1, w_fc2, vectors, fc1_bias):
    return call(
        pack_kernel,
        [((64, UNIT), bf16), ((96, 1024), bf16)],
        (w_qkv, w_proj, w_fc1, w_fc2, vectors, fc1_bias.reshape(2, 128)),
        [ANY] * 4 + [VM] * 2,
        scratch=[pltpu.VMEM((64, 128), f32), pltpu.SemaphoreType.DMA((6,))],
        moved=4 * 2**20,
        name="pack_parts",
    )


def halves_kernel(*refs):
    pieces, low, high, sems = refs[:8], refs[8], refs[9], refs[10]
    x, z, _, _ = place()
    waits = []
    for n, piece in enumerate(pieces):
        index = near(x, n // 2, XS) * 2 + near(z, n % 2, ZS)

        @pl.when(index < 4)
        def _(piece=piece, index=index, n=n):
            pltpu.make_async_copy(piece, low.at[index], sems.at[n]).start()

        @pl.when(index >= 4)
        def _(piece=piece, index=index, n=n):
            pltpu.make_async_copy(piece, high.at[index - 4], sems.at[n]).start()

        waits.append(pltpu.make_async_copy(piece, low.at[0], sems.at[n]))
    for copy in waits:
        copy.wait()


def halves(pieces):
    return call(
        halves_kernel,
        [((4, 96, 1024), bf16)] * 2,
        pieces,
        [ANY] * 8,
        scratch=[pltpu.SemaphoreType.DMA((8,))],
        out_kinds=[ANY] * 2,
        moved=4 * 2**20,
        name="place_pieces",
    )


def vectors_kernel(*refs):
    pieces, vec, bias, held, sems = refs[:16], refs[16], refs[17], refs[18], refs[19]
    x, z, c, _ = place()
    copies = []
    for n, piece in enumerate(pieces):
        k, dx, dz = n // 8, (n // 2) % 4, n % 2
        index = near(x, dx, XS) * 4 + near(z, dz, ZS) * 2 + near(c, k, CS)
        copies.append(pltpu.make_async_copy(piece.at[0:32, 6144:6272], held.at[index], sems.at[n]))
        copies[-1].start()
    for copy in copies:
        copy.wait()
    lane = lax.broadcasted_iota(jnp.int32, (16, 128), 1)
    for t in range(8):
        a = held[2 * t, 0:16].astype(f32)
        b = held[2 * t + 1, 0:16].astype(f32)
        vec[:, t * 128 : t * 128 + 128] = jnp.where(lane < 64, a, pltpu.roll(b, 64, 1))
    for s in range(16):
        tail = held[s, 16:32].astype(f32)
        bias[0:1, s * 256 : s * 256 + 128] = tail[0:1]
        bias[0:1, s * 256 + 128 : s * 256 + 256] = tail[1:2]


def gathered_vectors(columns):
    flat = [columns[k][dx][dz] for k in range(CS) for dx in range(XS) for dz in range(ZS)]
    return call(
        vectors_kernel,
        [((16, 1024), f32), ((1, FF), f32)],
        flat,
        [ANY] * 16,
        scratch=[pltpu.VMEM((16, 32, 128), bf16), pltpu.SemaphoreType.DMA((16,))],
        moved=2**20,
        name="gathered_vectors",
    )


def column_copies(pieces, target, low, high, sems):
    x, z, c, _ = place()
    out = []
    for n, piece in enumerate(pieces):
        k, dx, dz = n // 8, (n // 2) % 4, n % 2
        xz = near(x, dx, XS) * 2 + near(z, dz, ZS)
        out.append(pltpu.make_async_copy(piece.at[:, low:high], target(xz, near(c, k, CS)), sems.at[n]))
    return out


def attention_weights(pieces, w_qkv, w_proj, sems):
    a = column_copies(pieces, lambda xz, c: w_qkv.at[xz, c], 0, 3072, sems.at[0])
    b = column_copies(pieces, lambda xz, c: w_proj.at[xz, c], 3072, 4096, sems.at[1])
    return a, b


ATTENTION_SCRATCH = [
    pltpu.VMEM((8, 2, 64, 3072), bf16),
    pltpu.VMEM((8, 2, 64, 1024), bf16),
    pltpu.SemaphoreType.DMA((2, 16)),
]


def feed_weights(columns, rows, w1, w2, sems):
    x, z, c, y = place()
    first, second = [], []
    for n, piece in enumerate(rows):
        k, dy, half = n // 8, (n // 2) % 4, n % 2
        ck, yk = near(c, k, CS), near(y, dy, YS)
        first.append(pltpu.make_async_copy(piece.at[:, 0:64], w1.at[yk, 4 * half : 4 * half + 4, ck], sems.at[0, n]))
        second.append(
            pltpu.make_async_copy(
                piece.at[:, 64:96],
                w2.at[4 * half : 4 * half + 4, ck, pl.ds(pl.multiple_of(yk * 32, 32), 32)],
                sems.at[1, n],
            )
        )
    second += column_copies(columns, lambda xz, c: w2.at[xz, c, 128:192], 4096, 5120, sems.at[2])
    second += column_copies(columns, lambda xz, c: w2.at[xz, c, 192:256], 5120, 6144, sems.at[3])
    return first, second


FEED_SCRATCH = [
    pltpu.VMEM((4, 8, 2, 64, 1024), bf16),
    pltpu.VMEM((8, 2, 256, 1024), bf16),
    pltpu.SemaphoreType.DMA((4, 16)),
]


def start(copies):
    for copy in copies:
        copy.start()


def wait(copies):
    for copy in copies:
        copy.wait()


def stacked_heads(pair, lane):
    zero = jnp.zeros_like(pair)
    return jnp.concatenate([jnp.where(lane, pair, zero), jnp.where(lane, zero, pair)], axis=0)


def attention_forward_kernel(keep, x_ref, vec, *refs):
    pieces, refs = refs[:16], refs[16:]
    if keep:
        a_out, p_out, soft_out, m_out, o_out, x1_out, c_out, w_qkv, w_proj, sems = refs
    else:
        x1_out, c_out, w_qkv, w_proj, sems, p_out, m_out = refs
    first, second = attention_weights(pieces, w_qkv, w_proj, sems)
    start(first)
    start(second)
    x = x_ref[...].astype(f32)
    hat, _ = stats(x)
    a = (hat * vec[0:1, :] + vec[1:2, :]).astype(bf16)
    if keep:
        a_out[...] = a
    wait(first)
    for j in range(6):
        part = dot(a, w_qkv[:, :, :, j * 512 : j * 512 + 512].reshape(D, 512))
        if j < 2:
            part = part + vec[2:3, j * 512 : j * 512 + 512]
        if j >= 4:
            part = part + vec[3:4, j * 512 - 2048 : j * 512 - 1536]
        p_out[:, j * 512 : j * 512 + 512] = part.astype(bf16)
    lane = lax.broadcasted_iota(jnp.int32, (128, 128), 1) < 64

    def unit(u, _):
        i, h = lax.div(u, jnp.int32(8)), lax.rem(u, jnp.int32(8))
        rows = pl.ds(pl.multiple_of(i * 128, 128), 128)
        q, k, v = [p_out[rows, pl.ds(pl.multiple_of(h * 128 + o, 128), 128)] for o in (0, 1024, 2048)]
        s = dot(stacked_heads(q, lane), k, NT) * 0.125
        e = jnp.exp(s - jnp.max(s, axis=-1, keepdims=True))
        soft = e / jnp.sum(e, axis=-1, keepdims=True)
        if keep:
            soft_out[u] = soft
        mixed = dot(soft.astype(bf16), v)
        m_out[rows, pl.ds(pl.multiple_of(h * 128, 128), 128)] = jnp.where(lane, mixed[:128], mixed[128:]).astype(bf16)
        return 0

    lax.fori_loop(0, 16, unit, 0, unroll=4)
    wait(second)
    o = dot(m_out[...], w_proj[...].reshape(D, D)) + vec[4:5, :]
    x1 = x + vec[5:6, :] * o
    if keep:
        o_out[...] = o
    x1_out[...] = x1
    hat, _ = stats(x1)
    c_out[...] = (hat * vec[6:7, :] + vec[7:8, :]).astype(bf16)


def attention_forward(keep, x, vec, columns):
    flat = [columns[k][dx][dz] for k in range(CS) for dx in range(XS) for dz in range(ZS)]
    outs = [((T, D), f32), ((T, D), bf16)]
    scratch = list(ATTENTION_SCRATCH)
    if keep:
        outs = [((T, D), bf16), ((T, 3072), bf16), ((16, 256, 128), f32), ((T, D), bf16), ((T, D), f32)] + outs
    else:
        scratch += [pltpu.VMEM((T, 3072), bf16), pltpu.VMEM((T, D), bf16)]
    return call(
        lambda *refs: attention_forward_kernel(keep, *refs),
        outs,
        [x, vec] + flat,
        [VM, VM] + [ANY] * 16,
        scratch=scratch,
        flops=2 * T * D * 4 * D,
        moved=14 * 2**20,
        name="attention_forward",
    )


def feed_forward_kernel(keep, x1_ref, c_ref, vec, bias, *refs):
    columns, rows, refs = refs[:16], refs[16:32], refs[32:]
    if keep:
        u_out, gp_out, f_out, y_out, w1, w2, sems = refs
    else:
        y_out, w1, w2, sems = refs
    first, second = feed_weights(columns, rows, w1, w2, sems)
    start(first)
    start(second)
    c = c_ref[...]
    total = None
    wait(first)
    for t in range(8):
        y, off = t // 2, (t % 2) * 512
        h = dot(c, w1[y, :, :, :, off : off + 512].reshape(D, 512)) + bias[0:1, t * 512 : t * 512 + 512]
        cdf = 0.5 * (1.0 + lax.erf(h * 0.7071067811865476))
        u = (h * cdf).astype(bf16)
        if keep:
            gp = cdf + h * (jnp.exp(-0.5 * h * h) * 0.3989422804014327)
            u_out[:, t * 512 : t * 512 + 512] = u
            gp_out[:, t * 512 : t * 512 + 512] = gp.astype(bf16)
        if t == 0:
            wait(second)
        part = dot(u, w2[t].reshape(512, D))
        total = part if total is None else total + part
    f = total + vec[8:9, :]
    if keep:
        f_out[...] = f
    y_out[...] = (x1_ref[...] + vec[9:10, :] * f).astype(y_out.dtype)


def feed_forward(keep, x1, c, vec, bias, columns, rows):
    flat = [columns[k][dx][dz] for k in range(CS) for dx in range(XS) for dz in range(ZS)]
    flat += [rows[k][dy][half] for k in range(CS) for dy in range(YS) for half in range(2)]
    outs = [((T, D), f32 if keep else bf16)]
    if keep:
        outs = [((T, FF), bf16), ((T, FF), bf16), ((T, D), f32)] + outs
    return call(
        lambda *refs: feed_forward_kernel(keep, *refs),
        outs,
        [x1, c, vec, bias] + flat,
        [VM] * 4 + [ANY] * 32,
        scratch=FEED_SCRATCH,
        flops=4 * T * D * FF,
        moved=24 * 2**20,
        name="feed_forward",
    )


def feed_backward_kernel(g_ref, f_ref, gp_ref, x1_ref, o_ref, vec, *refs):
    columns, rows, refs = refs[:16], refs[16:32], refs[32:]
    df_out, dh_out, dx1_out, do_out, small, gbias, w1, w2, sems = refs
    first, second = feed_weights(columns, rows, w1, w2, sems)
    start(second)
    start(first)
    g = g_ref[...]
    df = (vec[9:10, :] * g).astype(bf16)
    df_out[...] = df
    small[8:9, :] = jnp.sum(df.astype(f32), axis=0, keepdims=True)
    small[9:10, :] = jnp.sum(g * f_ref[...], axis=0, keepdims=True)
    small[0:4, :] = jnp.zeros((4, D), f32)
    small[10:16, :] = jnp.zeros((6, D), f32)
    wait(second)
    total = None
    for t in range(8):
        y, off = t // 2, (t % 2) * 512
        cols = slice(t * 512, t * 512 + 512)
        du = dot(df, w2[t].reshape(512, D), NT)
        dh = (gp_ref[:, cols].astype(f32) * du).astype(bf16)
        dh_out[:, cols] = dh
        gbias[0:1, cols] = jnp.sum(dh.astype(f32), axis=0, keepdims=True)
        if t == 0:
            wait(first)
        part = dot(dh, w1[y, :, :, :, off : off + 512].reshape(D, 512), NT)
        total = part if total is None else total + part
    hat, scale = stats(x1_ref[...])
    d_norm, small[6:7, :], small[7:8, :] = norm_back(total, vec[6:7, :], hat, scale)
    dx1 = g + d_norm
    dx1_out[...] = dx1
    small[5:6, :] = jnp.sum(dx1 * o_ref[...], axis=0, keepdims=True)
    do = (vec[5:6, :] * dx1).astype(bf16)
    do_out[...] = do
    small[4:5, :] = jnp.sum(do.astype(f32), axis=0, keepdims=True)


def feed_backward(g, f, gp, x1, o, vec, columns, rows):
    flat = [columns[k][dx][dz] for k in range(CS) for dx in range(XS) for dz in range(ZS)]
    flat += [rows[k][dy][half] for k in range(CS) for dy in range(YS) for half in range(2)]
    return call(
        feed_backward_kernel,
        [((T, D), bf16), ((T, FF), bf16), ((T, D), f32), ((T, D), bf16), ((16, D), f32), ((1, FF), f32)],
        [g, f, gp, x1, o, vec] + flat,
        [VM] * 6 + [ANY] * 32,
        scratch=FEED_SCRATCH,
        flops=4 * T * D * FF,
        moved=26 * 2**20,
        name="feed_backward",
    )


def attention_backward_kernel(do_ref, dx1_ref, x_ref, p_ref, soft_ref, vec, *refs):
    pieces, refs = refs[:16], refs[16:]
    dp_out, dx_out, small, w_qkv, w_proj, sems, dm_ref = refs
    first, second = attention_weights(pieces, w_qkv, w_proj, sems)
    start(second)
    start(first)
    wait(second)
    dm_ref[...] = dot(do_ref[...], w_proj[...].reshape(D, D), NT).astype(bf16)
    lane = lax.broadcasted_iota(jnp.int32, (128, 128), 1) < 64

    def unit(u, _):
        i, h = lax.div(u, jnp.int32(8)), lax.rem(u, jnp.int32(8))
        rows = pl.ds(pl.multiple_of(i * 128, 128), 128)
        at = lambda o: pl.ds(pl.multiple_of(h * 128 + o, 128), 128)
        q, k, v = [p_ref[rows, at(o)] for o in (0, 1024, 2048)]
        dm = stacked_heads(dm_ref[rows, at(0)], lane)
        soft = soft_ref[u]
        dp_out[rows, at(2048)] = dot(soft.astype(bf16), dm, TN).astype(bf16)
        dw = dot(dm, v, NT)
        ds = (soft * (dw - jnp.sum(soft * dw, axis=-1, keepdims=True))).astype(bf16)
        dq = dot(ds, k) * 0.125
        dp_out[rows, at(0)] = jnp.where(lane, dq[:128], dq[128:]).astype(bf16)
        dp_out[rows, at(1024)] = (dot(ds, stacked_heads(q, lane), TN) * 0.125).astype(bf16)
        return 0

    lax.fori_loop(0, 16, unit, 0, unroll=4)
    small[2:3, :] = jnp.sum(dp_out[:, 0:1024].astype(f32), axis=0, keepdims=True)
    small[3:4, :] = jnp.sum(dp_out[:, 2048:3072].astype(f32), axis=0, keepdims=True)
    small[4:16, :] = jnp.zeros((12, D), f32)
    wait(first)
    total = None
    for j in range(6):
        cols = slice(j * 512, j * 512 + 512)
        part = dot(dp_out[:, cols], w_qkv[:, :, :, cols].reshape(D, 512), NT)
        total = part if total is None else total + part
    hat, scale = stats(x_ref[...].astype(f32))
    d_norm, small[0:1, :], small[1:2, :] = norm_back(total, vec[0:1, :], hat, scale)
    dx_out[...] = dx1_ref[...] + d_norm


def attention_backward(do, dx1, x, p, soft, vec, columns):
    flat = [columns[k][dx][dz] for k in range(CS) for dx in range(XS) for dz in range(ZS)]
    return call(
        attention_backward_kernel,
        [((T, 3072), bf16), ((T, D), f32), ((16, D), f32)],
        [do, dx1, x, p, soft, vec] + flat,
        [VM] * 6 + [ANY] * 16,
        scratch=list(ATTENTION_SCRATCH) + [pltpu.VMEM((T, D), bf16)],
        flops=2 * T * D * 4 * D,
        moved=18 * 2**20,
        name="attention_backward",
    )


def picked_kernel(a_ref, m_ref, c_ref, u_ref, mine, theirs):
    x, z, c, _ = place()
    row = lax.broadcasted_iota(jnp.int32, (512, D), 0)
    col = lax.broadcasted_iota(jnp.int32, (512, D), 1)
    eye_r = lax.broadcasted_iota(jnp.int32, (256, 256), 0)
    eye = jnp.where(eye_r == lax.broadcasted_iota(jnp.int32, (256, 256), 1), 1.0, 0.0).astype(bf16)
    dx, dz, inner = row >> 7, (row >> 6) & 1, row & 63
    base = (((x + dx) & 3) << 8) + (((z + dz) & 1) << 7) + inner
    for k, out in enumerate((mine, theirs)):
        ck = near(c, k, CS)
        chosen = jnp.where(col == base + ck * 64, 1.0, 0.0).astype(bf16)
        for n, ref in enumerate((a_ref, m_ref, c_ref)):
            out[n * 512 : n * 512 + 512, :] = dot(chosen, ref[...], NT).astype(bf16)
        for j in range(8):
            s = near(x, j // 2, XS) * 4 + near(z, j % 2, ZS) * 2 + ck
            block = u_ref[:, pl.ds(pl.multiple_of(s * 256, 256), 256)]
            out[1536 + j * 256 : 1792 + j * 256, :] = dot(eye, block, NT).astype(bf16)


def picked(a, m, c, u):
    return call(
        picked_kernel,
        [((3584, T), bf16)] * 2,
        [a, m, c, u],
        [VM] * 4,
        flops=2 * 10**9,
        moved=8 * 2**20,
        name="transposed_acts",
    )


def feed_grads_kernel(mine, theirs, dh, dh2, df, df2, *refs):
    outs, acts, dh_all, df_all, rows, tail, sems, out_sems = refs[:16], *refs[16:]
    _, _, _, y = place()
    copies = [
        pltpu.make_async_copy(mine.at[1024:3584], acts.at[:, 0:256], sems.at[0]),
        pltpu.make_async_copy(theirs.at[1024:3584], acts.at[:, 256:512], sems.at[1]),
        pltpu.make_async_copy(df, df_all.at[0:256], sems.at[2]),
        pltpu.make_async_copy(df2, df_all.at[256:512], sems.at[3]),
        pltpu.make_async_copy(dh, dh_all.at[0:256], sems.at[4]),
        pltpu.make_async_copy(dh2, dh_all.at[256:512], sems.at[5]),
    ]
    start(copies)
    wait(copies[:4])
    sends = []
    for j in range(8):
        grad = dot(acts[512 + j * 256 : 768 + j * 256, :], df_all[...]).astype(bf16)
        tail[j, :, 0:1024] = grad[128:192]
        tail[j, :, 1024:2048] = grad[192:256]
        sends.append(pltpu.make_async_copy(tail.at[j], outs[8 + j], out_sems.at[8 + j]))
        sends[-1].start()
        for yk in range(YS):
            dy = near(jnp.int32(yk + YS) - y, 0, YS)
            rows[dy, j // 4, j % 4, 64:96] = grad[yk * 32 : yk * 32 + 32]
    wait(copies[4:])
    for dy in (2, 1, 3, 0):
        start_col = pl.multiple_of(near(y, dy, YS) * 1024, 1024)
        for half in range(2):
            grad = dot(acts[half * 256 : half * 256 + 256, :], dh_all[:, pl.ds(start_col, 1024)]).astype(bf16)
            rows[dy, half, :, 0:64] = grad.reshape(4, 64, 1024)
            sends.append(pltpu.make_async_copy(rows.at[dy, half], outs[dy * 2 + half], out_sems.at[dy * 2 + half]))
            sends[-1].start()
    wait(sends)


def feed_grads(mine, theirs, dh, dh2, df, df2):
    out = call(
        feed_grads_kernel,
        [((4, 96, 1024), bf16)] * 8 + [((64, 2048), bf16)] * 8,
        [mine, theirs, dh, dh2, df, df2],
        [ANY] * 6,
        scratch=[
            pltpu.VMEM((2560, 512), bf16),
            pltpu.VMEM((512, FF), bf16),
            pltpu.VMEM((512, D), bf16),
            pltpu.VMEM((4, 2, 4, 96, 1024), bf16),
            pltpu.VMEM((8, 64, 2048), bf16),
            pltpu.SemaphoreType.DMA((6,)),
            pltpu.SemaphoreType.DMA((16,)),
        ],
        out_kinds=[ANY] * 16,
        flops=8 * T * D * FF,
        moved=24 * 2**20,
        name="feed_grads",
    )
    return [[out[dy * 2], out[dy * 2 + 1]] for dy in range(YS)], out[8:]


def attention_grads_kernel(mine, theirs, dp, dp2, do, do2, s1, s2, s3, s4, b1, b2, *refs):
    outs, acts, dp_all, do_all, held, sems, out_sems = refs[:8], *refs[8:]
    x, z, c, _ = place()
    copies = [
        pltpu.make_async_copy(mine.at[0:1024], acts.at[:, 0:256], sems.at[0]),
        pltpu.make_async_copy(theirs.at[0:1024], acts.at[:, 256:512], sems.at[1]),
        pltpu.make_async_copy(do, do_all.at[0:256], sems.at[2]),
        pltpu.make_async_copy(do2, do_all.at[256:512], sems.at[3]),
        pltpu.make_async_copy(dp, dp_all.at[0:256], sems.at[4]),
        pltpu.make_async_copy(dp2, dp_all.at[256:512], sems.at[5]),
    ]
    start(copies)
    vec = (s1[...] + s2[...] + s3[...] + s4[...]).astype(bf16)
    row = lax.broadcasted_iota(jnp.int32, (D, 128), 0)
    col = lax.broadcasted_iota(jnp.int32, (D, 128), 1)
    for j in range(8):
        s = near(x, j // 2, XS) * 4 + near(z, j % 2, ZS) * 2 + c
        chosen = jnp.where((row == col + s * 64) & (col < 64), 1.0, 0.0).astype(bf16)
        held[j, :, 4096:4224] = jnp.zeros((64, 128), bf16)
        held[j, 0:16, 4096:4224] = dot(vec, chosen).astype(bf16)
        a = b1[0:1, pl.ds(pl.multiple_of(s * 256, 256), 128)] + b2[0:1, pl.ds(pl.multiple_of(s * 256, 256), 128)]
        b = b1[0:1, pl.ds(pl.multiple_of(s * 256 + 128, 128), 128)] + b2[0:1, pl.ds(pl.multiple_of(s * 256 + 128, 128), 128)]
        line = lax.broadcasted_iota(jnp.int32, (16, 128), 0)
        held[j, 16:32, 4096:4224] = jnp.where(line == 0, a, jnp.where(line == 1, b, 0.0)).astype(bf16)
    wait(copies[:4])
    for n in range(2):
        grad = dot(acts[512:1024, :], do_all[:, n * 512 : n * 512 + 512]).astype(bf16)
        held[:, :, 3072 + n * 512 : 3584 + n * 512] = grad.reshape(8, 64, 512)
    wait(copies[4:])
    for n in range(6):
        grad = dot(acts[0:512, :], dp_all[:, n * 512 : n * 512 + 512]).astype(bf16)
        held[:, :, n * 512 : n * 512 + 512] = grad.reshape(8, 64, 512)
    sends = [pltpu.make_async_copy(held.at[j], outs[j], out_sems.at[j]) for j in range(8)]
    start(sends)
    wait(sends)


def attention_grads(mine, theirs, dp, dp2, do, do2, smalls, biases):
    return call(
        attention_grads_kernel,
        [((64, QP), bf16)] * 8,
        [mine, theirs, dp, dp2, do, do2] + smalls + biases,
        [ANY] * 6 + [VM] * 6,
        scratch=[
            pltpu.VMEM((1024, 512), bf16),
            pltpu.VMEM((512, 3072), bf16),
            pltpu.VMEM((512, D), bf16),
            pltpu.VMEM((8, 64, QP), bf16),
            pltpu.SemaphoreType.DMA((6,)),
            pltpu.SemaphoreType.DMA((8,)),
        ],
        out_kinds=[ANY] * 8,
        flops=8 * T * D * 2 * D,
        moved=16 * 2**20,
        name="attention_grads",
    )


def sum_kernel(count, *refs):
    total = refs[0][...].astype(f32)
    for ref in refs[1:count]:
        total = total + ref[...].astype(f32)
    outs = refs[count:]
    if len(outs) == 1:
        outs[0][...] = total.astype(bf16)
    else:
        for n, out in enumerate(outs):
            out[...] = total[n].astype(bf16)


def summed(parts, split=False):
    shape = parts[0].shape
    outs = [(shape[1:], bf16)] * shape[0] if split else [(shape, bf16)]
    size = 1
    for n in shape:
        size *= n
    out = call(
        lambda *refs: sum_kernel(len(parts), *refs),
        outs,
        parts,
        [VM] * len(parts),
        flops=size * len(parts),
        moved=2 * size * (len(parts) + 1),
        name="summed",
    )
    return out if split else out[0]


def scatter_columns(parts):
    far_a = from_shard(parts[4], dx=3)
    far_b = from_shard(parts[5], dx=1)
    plus_b = from_shard(parts[3], dx=3)
    minus_a = from_shard(parts[6], dx=1)
    plus_a = from_shard(summed([parts[2], far_a]), dx=3)
    minus_b = from_shard(summed([parts[7], far_b]), dx=1)
    other = summed([parts[1], plus_b, minus_b])
    got = from_shard(other, dz=1)
    return summed([parts[0], plus_a, minus_a, got])


def scatter_rows(parts):
    far_a = from_replica(parts[2][0], 3)
    far_b = from_replica(parts[2][1], 1)
    plus_b = from_replica(parts[1][1], 3)
    minus_a = from_replica(parts[3][0], 1)
    plus_a = from_replica(summed([parts[1][0], far_a]), 3)
    minus_b = from_replica(summed([parts[3][1], far_b]), 1)
    high = summed([parts[0][1], plus_b, minus_b], split=True)
    low = summed([parts[0][0], plus_a, minus_a], split=True)
    places = low + high
    got = [
        from_shard(places[2 * dx + dz], dx=XS - dx, dz=dz)
        for dx in range(XS)
        for dz in range(ZS)
        if (dx, dz) != (0, 0)
    ]
    return summed([places[0]] + got)


def own_quarter(part, y):
    quarters = part.reshape(YS, 16, -1)
    at = lambda dy: lax.dynamic_index_in_dim(quarters, lax.rem(y + dy, YS), 0, keepdims=False)
    return summed([at(0)] + [from_replica(at(dy), YS - dy) for dy in range(1, YS)])


def results_kernel(*refs):
    rows, columns, tails = refs[0:4], refs[4:8], refs[8:12]
    g_qkv, g_proj, g_fc1, g_fc2, g_vec, g_bias, rows_all, cols_all, tail_all, sems = refs[12:]
    _, _, _, y = place()
    copies = []
    for dy in range(YS):
        yk = near(y, dy, YS)
        copies.append(pltpu.make_async_copy(rows[dy], rows_all.at[yk], sems.at[0, dy]))
        copies.append(pltpu.make_async_copy(columns[dy], cols_all.at[yk], sems.at[1, dy]))
        copies.append(pltpu.make_async_copy(tails[dy], tail_all.at[yk], sems.at[2, dy]))
    start(copies)
    wait(copies)
    for k in range(YS):
        g_fc1[:, k * 1024 : k * 1024 + 1024] = rows_all[k, 0:64].astype(f32)
        g_fc2[k * 32 : k * 32 + 32, :] = rows_all[k, 64:96].astype(f32)
        line = slice(k * 16, k * 16 + 16)
        g_qkv[line, :] = cols_all[k, :, 0:3072].astype(f32)
        g_proj[line, :] = cols_all[k, :, 3072:4096].astype(f32)
        g_fc2[128 + k * 16 : 144 + k * 16, :] = tail_all[k, :, 0:1024].astype(f32)
        g_fc2[192 + k * 16 : 208 + k * 16, :] = tail_all[k, :, 1024:2048].astype(f32)
    g_vec[...] = cols_all[0, :, 4096:4224].astype(f32)
    g_bias[...] = cols_all[1, :, 4096:4224].astype(f32)


def results(rows, columns, tails):
    return call(
        results_kernel,
        [((64, 3072), f32), ((64, 1024), f32), ((64, FF), f32), ((256, D), f32), ((16, 128), f32), ((16, 128), f32)],
        list(rows) + list(columns) + list(tails),
        [ANY] * 12,
        scratch=[
            pltpu.VMEM((4, 96, 1024), bf16),
            pltpu.VMEM((4, 16, QP), bf16),
            pltpu.VMEM((4, 16, 2048), bf16),
            pltpu.SemaphoreType.DMA((3, 4)),
        ],
        moved=10 * 2**20,
        name="results",
    )


def gather(w_qkv, w_proj, w_fc1, w_fc2, vectors, fc1_bias):
    unit, piece = pack(w_qkv, w_proj, w_fc1, w_fc2, vectors, fc1_bias)
    pieces = [
        piece if (dx, dz) == (0, 0) else from_shard(piece, dx=dx, dz=dz) for dx in range(XS) for dz in range(ZS)
    ]
    other = from_shard(unit, dz=1)
    plus = [from_shard(unit, dx=1), from_shard(other, dx=1)]
    minus = [from_shard(unit, dx=3), from_shard(other, dx=3)]
    far = [from_shard(plus[0], dx=1), from_shard(minus[1], dx=3)]
    mine = [[unit, other], plus, far, minus]
    columns = [mine, [[from_shard(v, dc=1) for v in pair] for pair in mine]]
    here = halves(pieces)
    up = [from_replica(v, 1) for v in here]
    down = [from_replica(v, 3) for v in here]
    opposite = [from_replica(up[0], 1), from_replica(down[1], 3)]
    mine = [here, up, opposite, down]
    rows = [mine, [[from_shard(v, dc=1) for v in pair] for pair in mine]]
    return columns, rows


def shards(edge_inputs, image_counts, w_qkv, w_proj, w_fc1, w_fc2, vectors, fc1_bias):
    section = lax.axis_index("section")
    _, _, _, y = place()
    source = edge_inputs[0, :, 0]
    present = (lax.axis_index("shard") * YS + y < image_counts).astype(f32)
    columns, rows = gather(w_qkv[0], w_proj[0], w_fc1[0], w_fc2[0], vectors[0], fc1_bias[0])
    vec, bias = gathered_vectors(columns)

    own = source.reshape(T, D)
    x1, c = attention_forward(False, own, vec, columns)
    (first_out,) = feed_forward(False, x1, c, vec, bias, columns, rows)
    received = passed_along(first_out, 1)
    inputs = jnp.where(section == 0, own, received)
    a, p, soft, m, o, x1, c = attention_forward(True, inputs, vec, columns)
    u, gp, f, output = feed_forward(True, x1, c, vec, bias, columns, rows)

    cotangent = (source.astype(f32) * present[:, None, None]).reshape(T, D)
    _, _, dx1, do, _, _ = feed_backward(cotangent, f, gp, x1, o, vec, columns, rows)
    _, dx, _ = attention_backward(do, dx1, inputs, p, soft, vec, columns)
    received_grad = passed_along(dx.astype(bf16), -1)
    mine, theirs = picked(a, m, c, u)
    theirs = from_shard(theirs, dc=1)
    upstream = jnp.where(section == 1, cotangent, received_grad.astype(f32))
    df, dh, dx1, do, small_a, gbias = feed_backward(upstream, f, gp, x1, o, vec, columns, rows)
    dp, dx, small_b = attention_backward(do, dx1, inputs, p, soft, vec, columns)
    twin = lambda v: from_shard(v, dc=1)
    row_parts, tail_parts = feed_grads(mine, theirs, dh, twin(dh), df, twin(df))
    tail = own_quarter(scatter_columns(tail_parts), y)
    row = scatter_rows(row_parts)
    column_parts = attention_grads(
        mine, theirs, dp, twin(dp), do, twin(do), [small_a, twin(small_a), small_b, twin(small_b)], [gbias, twin(gbias)]
    )
    column = own_quarter(scatter_columns(column_parts), y)
    around = lambda v: [v] + [from_replica(v, dy) for dy in range(1, YS)]
    g_qkv, g_proj, g_fc1, g_fc2, g_vec, g_bias = results(around(row), around(column), around(tail))
    edge_values = jnp.where(section == 0, dx, output).reshape(1, 2, 1, 128, D)
    return (
        edge_values,
        g_qkv[None],
        g_proj[None],
        g_fc1[None],
        g_fc2[None],
        g_vec[None, :10, :64],
        g_bias[:2].reshape(1, 256),
    )


def solution(mesh):
    placed = (
        P("section", None, ("shard", "replica"), None, None),
        P(),
        P("section", "shard", None),
        P("section", "shard", None),
        P("section", "shard", None),
        P("section", "shard", None),
        P("section", None, "shard"),
        P("section", "shard"),
    )
    return jax.shard_map(
        shards,
        mesh=mesh,
        in_specs=placed,
        out_specs=(placed[0],) + placed[2:],
        check_vma=False,
    )
```

time: 661 us -> 532 us (0.80)
  Pallas kernels: 0 us -> 225 us
  local copies, waits for them, and re-layouts: 168 us -> 14.3 us
  matrix products: 125 us -> 0 us
  other arithmetic: 129 us -> 6.89 us
  starting transfers between devices: 66.5 us -> 97.7 us
  waiting for transfers between devices: 159 us -> 176 us
    pallas_call x0 -> x30, Pallas kernels: none -> 225 us  [call(): pl.pallas_call(kernel, out_shape=[jax.ShapeDtypeStruct(s, d) for s, d in...]
    dot_general x36 -> x0, matrix products: 118 us -> none  [the longest x2 22.4 us: forward_layer(): out_branch = jnp.dot(activated, fc2, preferred_element_type=f32) + vec[8]]
    concatenate x25 -> x0, other arithmetic: 76.4 us -> none  [the longest x15 66.4 us: rolled(): twice = jnp.concatenate([array, array], axis=axis)]
    reshape x12 -> x0, local copies, waits for them, and re-layouts: 43.2 us -> none  [the longest x4 28.7 us: forward_layer(): projected.reshape(images, 128, 3, heads, HEAD_DIM).transpose(2, 0, 3, 1, 4)]
    unnamed x120 -> x171, local copies, waits for them, and re-layouts: 38.2 us -> 9.87 us
    transpose x10 -> x0, local copies, waits for them, and re-layouts: 24.1 us -> none  [the longest x2 19.6 us: gather_all(): fc1 = rows[..., :64, :].transpose(2, 3, 0, 4, 1, 5).reshape(1024, 4096)]
    dynamic_slice x6 -> x0, local copies, waits for them, and re-layouts: 22.3 us -> none  [the longest x3 20.2 us: pick(): return lax.dynamic_index_in_dim(array, index, axis, keepdims=keep)]
    ppermute x17 -> x27, starting transfers between devices: 19.5 us -> 37.9 us  [from_replica(): lax.ppermute(value, 'replica', [((y + dy) % YS, y) for y in range(YS)])]
  transfers between devices with their start and end apart: 62 -> 88, of which waited for: 21 -> 30; matrix products, arithmetic and copies ran while one was open for 34% -> 1% of each run, Pallas kernels for 0% -> 28%
where the time goes in v2:
time: 532 us; the launch traced here: 522 us
  Pallas kernels  225 us (42%)
  waiting for transfers between devices  176 us (33%)
  starting transfers between devices  97.7 us (18%)
  local copies, waits for them, and re-layouts  14.3 us (3%)
  other arithmetic  6.89 us (1%)
    pallas_call x30, Pallas kernels, call(): pl.pallas_call(kernel, out_shape=[jax.ShapeDtypeStruct(s, d) for s, d in...  225 us
    ppermute x27, waiting for transfers between devices, from_replica(): lax.ppermute(value, 'replica', [((y + dy) % YS, y) for y in range(YS)])  84.4 us
    ppermute x59, waiting for transfers between devices, from_shard(): return lax.ppermute(value, 'shard', pairs)  71.7 us
    ppermute x59, starting transfers between devices, from_shard(): return lax.ppermute(value, 'shard', pairs)  52.9 us
    ppermute x27, starting transfers between devices, from_replica(): lax.ppermute(value, 'replica', [((y + dy) % YS, y) for y in range(YS)])  37.9 us
    ppermute x2, waiting for transfers between devices, passed_along(): return lax.ppermute(value, 'section', [(0, 1)] if steps == 1 else [(1, 0)])  20.2 us
  transfers between devices with their start and end apart: 88, of which 30 were waited for; matrix products, arithmetic and copies ran while one was open for 1% of the time, Pallas kernels for 28%

profile of v2, /device:TPU:0, one launch (start us, length us, event | category | flops | bytes accessed | tf_op | source)
XLA Modules:
  0.0 522.5 jit_solution(17353067548658822129)
XLA Ops:
  16.4 7.2 %collective-permute-done.17.refs_3_ = bf16[96,1024]{1,0:T(8,128)(2,1)S(1)} collective-permute-done((bf16[96,1024]{1,0:T(8,128)(2,1)}, bf16[96,1024]{1,0:T(8,128)(2,1)S(1)}, u32[]{:S(2)}, u32[]{:S(2)}) %collective-permute-start.17) | collective-permute-done | bytes 196640 | tf_op jit(solution)/shard_map/ppermute | solution.py:32
  23.6 16.8 %collective-permute-done.19.refs_5_ = bf16[96,1024]{1,0:T(8,128)(2,1)S(1)} collective-permute-done((bf16[96,1024]{1,0:T(8,128)(2,1)}, bf16[96,1024]{1,0:T(8,128)(2,1)S(1)}, u32[]{:S(2)}, u32[]{:S(2)}) %collective-permute-start.19) | collective-permute-done | bytes 196640 | tf_op jit(solution)/shard_map/ppermute | solution.py:32
  52.5 5.6 %collective-permute-done.21.refs_7_ = bf16[96,1024]{1,0:T(8,128)(2,1)S(1)} collective-permute-done((bf16[96,1024]{1,0:T(8,128)(2,1)}, bf16[96,1024]{1,0:T(8,128)(2,1)S(1)}, u32[]{:S(2)}, u32[]{:S(2)}) %collective-permute-start.21) | collective-permute-done | bytes 196640 | tf_op jit(solution)/shard_map/ppermute | solution.py:32
  58.8 48.8 %place_pieces.1 = (bf16[4,96,1024]{2,1,0:T(8,128)(2,1)}, bf16[4,96,1024]{2,1,0:T(8,128)(2,1)}) custom-call(bf16[96,1024]{1,0:T(8,128)(2,1)} %get-tuple-element.83.refs_0_, bf16[96,1024]{1,0:T(8,128)(2,1)} %copy-done.48, bf16[96,1024]{1,0:T(8,128)(2,1)} %copy-done.49, bf16[96,1024]{1,0:T(8,128)(2,1)} %copy-done.51, bf16[96,1024]{1,0:T(8,128)(2,1)} %copy-done.52, ...), custom_call_target="tpu_custom_call" | custom-call | bytes 4194304 | tf_op jit(solution)/shard_map/place_pieces/pallas_call | solution.py:56
  114.1 14.9 %collective-permute-done.22.refs_22_.refs_18_ = bf16[4,96,1024]{2,1,0:T(8,128)(2,1)S(1)} collective-permute-done((bf16[4,96,1024]{2,1,0:T(8,128)(2,1)}, bf16[4,96,1024]{2,1,0:T(8,128)(2,1)S(1)}, u32[]{:S(2)}, u32[]{:S(2)}) %collective-permute-start.22) | collective-permute-done | bytes 786464 | tf_op jit(solution)/shard_map/ppermute | solution.py:36
  133.3 8.7 %collective-permute-done.23.refs_23_.refs_19_ = bf16[4,96,1024]{2,1,0:T(8,128)(2,1)} collective-permute-done((bf16[4,96,1024]{2,1,0:T(8,128)(2,1)}, bf16[4,96,1024]{2,1,0:T(8,128)(2,1)}, u32[]{:S(2)}, u32[]{:S(2)}) %collective-permute-start.23) | collective-permute-done | bytes 786464 | tf_op jit(solution)/shard_map/ppermute | solution.py:36
  148.1 14.2 %collective-permute-done.3.refs_4_.refs_6_.refs_8_ = bf16[64,6272]{1,0:T(8,128)(2,1)S(1)} collective-permute-done((bf16[64,6272]{1,0:T(8,128)(2,1)S(1)}, bf16[64,6272]{1,0:T(8,128)(2,1)S(1)}, u32[]{:S(2)}, u32[]{:S(2)}) %collective-permute-start.3) | collective-permute-done | bytes 802848 | tf_op jit(solution)/shard_map/ppermute | solution.py:32
  166.7 16.0 %collective-permute-done.24.refs_24_.refs_20_ = bf16[4,96,1024]{2,1,0:T(8,128)(2,1)} collective-permute-done((bf16[4,96,1024]{2,1,0:T(8,128)(2,1)S(1)}, bf16[4,96,1024]{2,1,0:T(8,128)(2,1)}, u32[]{:S(2)}, u32[]{:S(2)}) %collective-permute-start.24) | collective-permute-done | bytes 786464 | tf_op jit(solution)/shard_map/ppermute | solution.py:36
  192.7 11.3 %attention_forward.2 = (f32[256,1024]{1,0:T(8,128)}, bf16[256,1024]{1,0:T(8,128)(2,1)}) custom-call(bf16[256,1024]{1,0:T(8,128)(2,1)} %bitcast.41, f32[16,1024]{1,0:T(8,128)} %get-tuple-element.79.refs_1_.refs_2_.vec, bf16[64,6272]{1,0:T(8,128)(2,1)} %get-tuple-element.78.refs_0_.refs_2_.refs_4_, bf16[64,6272]{1,0:T(8,128)(2,1)} %copy-done, ...), custom_call_target="tpu_custom_call" | custom-call | flops 2147483648 | bytes 14680064 | tf_op jit(solution)/shard_map/attention_forward/pallas_call | solution.py:56
  204.1 13.6 %feed_forward.2 = bf16[256,1024]{1,0:T(8,128)(2,1)} custom-call(f32[256,1024]{1,0:T(8,128)} %get-tuple-element.80.refs_0_, bf16[256,1024]{1,0:T(8,128)(2,1)} %get-tuple-element.81.refs_1_, f32[16,1024]{1,0:T(8,128)} %get-tuple-element.79.refs_1_.refs_2_.vec, f32[1,4096]{1,0:T(1,128)} %get-tuple-element.82.refs_3_, ...), custom_call_target="tpu_custom_call" | custom-call | flops 4294967296 | bytes 25165824 | tf_op jit(solution)/shard_map/feed_forward/pallas_call | solution.py:56
  217.7 5.6 %collective-permute-start.36 = (bf16[256,1024]{1,0:T(8,128)(2,1)}, bf16[256,1024]{1,0:T(8,128)(2,1)S(1)}, u32[]{:S(2)}, u32[]{:S(2)}) collective-permute-start(bf16[256,1024]{1,0:T(8,128)(2,1)} %feed_forward.2), channel_id=1, source_target_pairs={{0,64},{1,65},{2,66},{3,67},{4,68},{5,69},{6,70},{7,71},{8,72},{9,... | collective-permute-start | bytes 1572872 | tf_op jit(solution)/shard_map/ppermute | solution.py:40
  224.5 10.6 %collective-permute-done.36 = bf16[256,1024]{1,0:T(8,128)(2,1)S(1)} collective-permute-done((bf16[256,1024]{1,0:T(8,128)(2,1)}, bf16[256,1024]{1,0:T(8,128)(2,1)S(1)}, u32[]{:S(2)}, u32[]{:S(2)}) %collective-permute-start.36) | collective-permute-done | bytes 524320 | tf_op jit(solution)/shard_map/ppermute | solution.py:40
  236.1 12.7 %attention_forward.3 = (bf16[256,1024]{1,0:T(8,128)(2,1)}, bf16[256,3072]{1,0:T(8,128)(2,1)}, f32[16,256,128]{2,1,0:T(8,128)}, bf16[256,1024]{1,0:T(8,128)(2,1)}...) custom-call(bf16[256,1024]{1,0:T(8,128)(2,1)} %broadcast_select_fusion.1.refs_0_.x_ref, ...), custom_call_target="tpu_custom_call" | custom-call | flops 2147483648 | bytes 14680064 | tf_op jit(solution)/shard_map/attention_forward/pallas_call | solution.py:56
  248.8 16.0 %feed_forward.3 = (bf16[256,4096]{1,0:T(8,128)(2,1)}, bf16[256,4096]{1,0:T(8,128)(2,1)}, f32[256,1024]{1,0:T(8,128)}, f32[256,1024]{1,0:T(8,128)}) custom-call(f32[256,1024]{1,0:T(8,128)} %get-tuple-element.86.refs_0_.x1_ref, bf16[256,1024]{1,0:T(8,128)(2,1)} %get-tuple-element.87.refs_1_.c_ref, f32[16,1024]{1,0:T(8,128)} %get-tuple-element.79.refs_1_.refs_2_.vec, ...), custom_call_target="tpu_custom_call" | custom-call | flops 4294967296 | bytes 25165824 | tf_op jit(solution)/shard_map/feed_forward/pallas_call | solution.py:56
  264.8 15.9 %feed_backward.2 = (bf16[256,1024]{1,0:T(8,128)(2,1)}, bf16[256,4096]{1,0:T(8,128)(2,1)}, f32[256,1024]{1,0:T(8,128)}, bf16[256,1024]{1,0:T(8,128)(2,1)}, f32[16,1024]{1,0:T(8,128)}, /*index=5*/f32[1,4096]{1,0:T(1,128)}) custom-call(f32[256,1024]{1,0:T(8,128)} %convert_multiply_fusion.g_ref, f32[256,1024]{1,0:T(8,128)} %get-tuple-element.88.f_ref, ...), custom_call_target="tpu_custom_call" | custom-call | flops 4294967296 | bytes 27262976 | tf_op jit(solution)/shard_map/feed_backward/pallas_call | solution.py:56
  280.7 14.8 %attention_backward.2 = (bf16[256,3072]{1,0:T(8,128)(2,1)}, f32[256,1024]{1,0:T(8,128)}, f32[16,1024]{1,0:T(8,128)}) custom-call(bf16[256,1024]{1,0:T(8,128)(2,1)} %get-tuple-element.91.do_ref, f32[256,1024]{1,0:T(8,128)} %get-tuple-element.92.dx1_ref, bf16[256,1024]{1,0:T(8,128)(2,1)} %broadcast_select_fusion.1.refs_0_.x_ref, ...), custom_call_target="tpu_custom_call" | custom-call | flops 2147483648 | bytes 18874368 | tf_op jit(solution)/shard_map/attention_backward/pallas_call | solution.py:56
  298.1 5.8 %transposed_acts.1 = (bf16[3584,256]{1,0:T(8,128)(2,1)}, bf16[3584,256]{1,0:T(8,128)(2,1)}) custom-call(bf16[256,1024]{1,0:T(8,128)(2,1)} %get-tuple-element.100.a_ref, bf16[256,1024]{1,0:T(8,128)(2,1)} %get-tuple-element.101.m_ref, bf16[256,1024]{1,0:T(8,128)(2,1)} %get-tuple-element.87.refs_1_.c_ref, bf16[256,4096]{1,0:T(8,128)(2,1)} %get-tuple-element.102.u_ref), custom_call_target="tpu_custom_call" | custom-call | flops 2000000000 | bytes 8388608 | tf_op jit(solution)/shard_map/transposed_acts/pallas_call | solution.py:56
  304.0 9.5 %collective-permute-done.37 = bf16[256,1024]{1,0:T(8,128)(2,1)S(1)} collective-permute-done((bf16[256,1024]{1,0:T(8,128)(2,1)S(1)}, bf16[256,1024]{1,0:T(8,128)(2,1)S(1)}, u32[]{:S(2)}, u32[]{:S(2)}) %collective-permute-start.37) | collective-permute-done | bytes 524320 | tf_op jit(solution)/shard_map/ppermute | solution.py:40
  314.7 15.9 %feed_backward.3 = (bf16[256,1024]{1,0:T(8,128)(2,1)}, bf16[256,4096]{1,0:T(8,128)(2,1)}, f32[256,1024]{1,0:T(8,128)}, bf16[256,1024]{1,0:T(8,128)(2,1)}, f32[16,1024]{1,0:T(8,128)}, /*index=5*/f32[1,4096]{1,0:T(1,128)}) custom-call(f32[256,1024]{1,0:T(8,128)} %convert_select_fusion.g_ref, f32[256,1024]{1,0:T(8,128)} %get-tuple-element.88.f_ref, ...), custom_call_target="tpu_custom_call" | custom-call | flops 4294967296 | bytes 27262976 | tf_op jit(solution)/shard_map/feed_backward/pallas_call | solution.py:56
  330.9 14.4 %attention_backward.3 = (bf16[256,3072]{1,0:T(8,128)(2,1)}, f32[256,1024]{1,0:T(8,128)}, f32[16,1024]{1,0:T(8,128)}) custom-call(bf16[256,1024]{1,0:T(8,128)(2,1)} %get-tuple-element.96.do_ref.do, f32[256,1024]{1,0:T(8,128)} %get-tuple-element.97.dx1_ref, bf16[256,1024]{1,0:T(8,128)(2,1)} %broadcast_select_fusion.1.refs_0_.x_ref, ...), custom_call_target="tpu_custom_call" | custom-call | flops 2147483648 | bytes 18874368 | tf_op jit(solution)/shard_map/attention_backward/pallas_call | solution.py:56
  354.5 7.5 %attention_grads.1 = (bf16[64,4224]{1,0:T(8,128)(2,1)}, bf16[64,4224]{1,0:T(8,128)(2,1)}, bf16[64,4224]{1,0:T(8,128)(2,1)}, bf16[64,4224]{1,0:T(8,128)(2,1)}, bf...) custom-call(bf16[3584,256]{1,0:T(8,128)(2,1)} %get-tuple-element.103.min, ...), custom_call_target="tpu_custom_call" | custom-call | flops 4294967296 | bytes 16777216 | tf_op jit(solution)/shard_map/attention_grads/pallas_call | solution.py:56
  366.5 7.8 %feed_grads.1 = (bf16[4,96,1024]{2,1,0:T(8,128)(2,1)}, bf16[4,96,1024]{2,1,0:T(8,128)(2,1)}, bf16[4,96,1024]{2,1,0:T(8,128)(2,1)}, bf16[4,96,1024]{2,1,0:T(8,128...) custom-call(bf16[3584,256]{1,0:T(8,128)(2,1)} %get-tuple-element.103, ...), custom_call_target="tpu_custom_call" | custom-call | flops 8589934592 | bytes 25165824 | tf_op jit(solution)/shard_map/feed_grads/pallas_call | solution.py:56
  387.6 9.7 %collective-permute-done.75.refs_1_ = bf16[64,2048]{1,0:T(8,128)(2,1)S(1)} collective-permute-done((bf16[64,2048]{1,0:T(8,128)(2,1)}, bf16[64,2048]{1,0:T(8,128)(2,1)S(1)}, u32[]{:S(2)}, u32[]{:S(2)}) %collective-permute-start.75) | collective-permute-done | bytes 262176 | tf_op jit(solution)/shard_map/ppermute | solution.py:32
  452.7 11.6 %collective-permute-done.49.refs_2_ = bf16[4,96,1024]{2,1,0:T(8,128)(2,1)S(1)} collective-permute-done((bf16[4,96,1024]{2,1,0:T(8,128)(2,1)S(1)}, bf16[4,96,1024]{2,1,0:T(8,128)(2,1)S(1)}, u32[]{:S(2)}, u32[]{:S(2)}) %collective-permute-start.49) | collective-permute-done | bytes 786464 | tf_op jit(solution)/shard_map/ppermute | solution.py:36
  (365 shorter events, 205.5 us)
Async XLA Ops:
  10.0 100.8 %collective-permute-start = (bf16[64,6272]{1,0:T(8,128)(2,1)}, bf16[64,6272]{1,0:T(8,128)(2,1)S(1)}, u32[]{:S(2)}, u32[]{:S(2)}) collective-permute-start(bf16[64,6272]{1,0:T(8,128)(2,1)} %get-tuple-element.78.refs_0_.refs_2_.refs_4_), channel_id=1, source_target_pairs={{8,0},{12,4},{0,8},{4,12},{24,16},{28,20},{16,24},{20,28},{40,32},... | collective-permute-start | bytes 2408456 | tf_op jit(solution)/shard_map/ppermute | solution.py:32
  12.4 98.4 %collective-permute-start.1 = (bf16[64,6272]{1,0:T(8,128)(2,1)}, bf16[64,6272]{1,0:T(8,128)(2,1)S(1)}, u32[]{:S(2)}, u32[]{:S(2)}) collective-permute-start(bf16[64,6272]{1,0:T(8,128)(2,1)} %get-tuple-element.78.refs_0_.refs_2_.refs_4_), channel_id=1, source_target_pairs={{16,0},{20,4},{24,8},{28,12},{32,16},{36,20},{40,24},{44,28},{48,3... | collective-permute-start | bytes 2408456 | tf_op jit(solution)/shard_map/ppermute | solution.py:32
  15.8 98.2 %collective-permute-start.6 = (bf16[64,6272]{1,0:T(8,128)(2,1)}, bf16[64,6272]{1,0:T(8,128)(2,1)S(1)}, u32[]{:S(2)}, u32[]{:S(2)}) collective-permute-start(bf16[64,6272]{1,0:T(8,128)(2,1)} %get-tuple-element.78.refs_0_.refs_2_.refs_4_), channel_id=1, source_target_pairs={{48,0},{52,4},{56,8},{60,12},{0,16},{4,20},{8,24},{12,28},{16,32},... | collective-permute-start | bytes 2408456 | tf_op jit(solution)/shard_map/ppermute | solution.py:32
  23.5 90.5 %collective-permute-start.7 = (bf16[64,6272]{1,0:T(8,128)(2,1)}, bf16[64,6272]{1,0:T(8,128)(2,1)S(1)}, u32[]{:S(2)}, u32[]{:S(2)}) collective-permute-start(bf16[64,6272]{1,0:T(8,128)(2,1)} %get-tuple-element.78.refs_0_.refs_2_.refs_4_), channel_id=1, source_target_pairs={{4,0},{0,4},{12,8},{8,12},{20,16},{16,20},{28,24},{24,28},{36,32},... | collective-permute-start | bytes 2408456 | tf_op jit(solution)/shard_map/ppermute | solution.py:32
  107.7 21.4 %collective-permute-start.22 = (bf16[4,96,1024]{2,1,0:T(8,128)(2,1)}, bf16[4,96,1024]{2,1,0:T(8,128)(2,1)S(1)}, u32[]{:S(2)}, u32[]{:S(2)}) collective-permute-start(bf16[4,96,1024]{2,1,0:T(8,128)(2,1)} %get-tuple-element.84.refs_20_.refs_16_), channel_id=1, source_target_pairs={{1,0},{2,1},{3,2},{0,3},{5,4},{6,5},{7,6},{4,7},{9,8},{10,9},{11,1... | collective-permute-start | bytes 2359304 | tf_op jit(solution)/shard_map/ppermute | solution.py:36
  110.8 22.0 %collective-permute-start.25 = (bf16[4,96,1024]{2,1,0:T(8,128)(2,1)}, bf16[4,96,1024]{2,1,0:T(8,128)(2,1)}, u32[]{:S(2)}, u32[]{:S(2)}) collective-permute-start(bf16[4,96,1024]{2,1,0:T(8,128)(2,1)} %get-tuple-element.85.refs_21_.refs_17_), channel_id=1, source_target_pairs={{3,0},{0,1},{1,2},{2,3},{7,4},{4,5},{5,6},{6,7},{11,8},{8,9},{9,10... | collective-permute-start | bytes 2359304 | tf_op jit(solution)/shard_map/ppermute | solution.py:36
  110.8 31.2 %collective-permute-start.23 = (bf16[4,96,1024]{2,1,0:T(8,128)(2,1)}, bf16[4,96,1024]{2,1,0:T(8,128)(2,1)}, u32[]{:S(2)}, u32[]{:S(2)}) collective-permute-start(bf16[4,96,1024]{2,1,0:T(8,128)(2,1)} %get-tuple-element.85.refs_21_.refs_17_), channel_id=1, source_target_pairs={{1,0},{2,1},{3,2},{0,3},{5,4},{6,5},{7,6},{4,7},{9,8},{10,9},{11,1... | collective-permute-start | bytes 2359304 | tf_op jit(solution)/shard_map/ppermute | solution.py:36
  114.0 31.4 %collective-permute-start.27 = (bf16[4,96,1024]{2,1,0:T(8,128)(2,1)}, bf16[4,96,1024]{2,1,0:T(8,128)(2,1)}, u32[]{:S(2)}, u32[]{:S(2)}) collective-permute-start(bf16[4,96,1024]{2,1,0:T(8,128)(2,1)} %get-tuple-element.84.refs_20_.refs_16_), channel_id=1, source_target_pairs={{3,0},{0,1},{1,2},{2,3},{7,4},{4,5},{5,6},{6,7},{11,8},{8,9},{9,10... | collective-permute-start | bytes 2359304 | tf_op jit(solution)/shard_map/ppermute | solution.py:36
  114.0 31.4 %collective-permute-start.28 = (bf16[4,96,1024]{2,1,0:T(8,128)(2,1)}, bf16[4,96,1024]{2,1,0:T(8,128)(2,1)}, u32[]{:S(2)}, u32[]{:S(2)}) collective-permute-start(bf16[4,96,1024]{2,1,0:T(8,128)(2,1)} %get-tuple-element.84.refs_20_.refs_16_), channel_id=1, source_target_pairs={{4,0},{0,4},{12,8},{8,12},{20,16},{16,20},{28,24},{24,28},{36,32},... | collective-permute-start | bytes 2359304 | tf_op jit(solution)/shard_map/ppermute | solution.py:32
  146.1 36.7 %collective-permute-start.5 = (bf16[64,6272]{1,0:T(8,128)(2,1)S(1)}, bf16[64,6272]{1,0:T(8,128)(2,1)S(1)}, u32[]{:S(2)}, u32[]{:S(2)}) collective-permute-start(bf16[64,6272]{1,0:T(8,128)(2,1)S(1)} %collective-permute-done.4.refs_7_.refs_9_.refs_11_), channel_id=1, source_target_pairs={{48,0},{52,4},{56,8},{60,12},{0,16},{4,20},{8,24},{12,28},{16,32},... | collective-permute-start | bytes 2408456 | tf_op jit(solution)/shard_map/ppermute | solution.py:32
  166.1 22.8 %collective-permute-start.14 = (bf16[64,6272]{1,0:T(8,128)(2,1)S(1)}, bf16[64,6272]{1,0:T(8,128)(2,1)S(1)}, u32[]{:S(2)}, u32[]{:S(2)}) collective-permute-start(bf16[64,6272]{1,0:T(8,128)(2,1)S(1)} %collective-permute-done.4.refs_7_.refs_9_.refs_11_), channel_id=1, source_target_pairs={{4,0},{0,4},{12,8},{8,12},{20,16},{16,20},{28,24},{24,28},{36,32},... | collective-permute-start | bytes 2408456 | tf_op jit(solution)/shard_map/ppermute | solution.py:32
  166.2 23.2 %collective-permute-start.10 = (bf16[64,6272]{1,0:T(8,128)(2,1)S(1)}, bf16[64,6272]{1,0:T(8,128)(2,1)S(1)}, u32[]{:S(2)}, u32[]{:S(2)}) collective-permute-start(bf16[64,6272]{1,0:T(8,128)(2,1)S(1)} %collective-permute-done.2.refs_3_.refs_5_.refs_7_), channel_id=1, source_target_pairs={{4,0},{0,4},{12,8},{8,12},{20,16},{16,20},{28,24},{24,28},{36,32},... | collective-permute-start | bytes 2408456 | tf_op jit(solution)/shard_map/ppermute | solution.py:32
  304.0 48.5 %collective-permute-start.38 = (bf16[3584,256]{1,0:T(8,128)(2,1)}, bf16[3584,256]{1,0:T(8,128)(2,1)S(1)}, u32[]{:S(2)}, u32[]{:S(2)}) collective-permute-start(bf16[3584,256]{1,0:T(8,128)(2,1)} %get-tuple-element.104), channel_id=1, source_target_pairs={{4,0},{0,4},{12,8},{8,12},{20,16},{16,20},{28,24},{24,28},{36,32},... | collective-permute-start | bytes 5505032 | tf_op jit(solution)/shard_map/ppermute | solution.py:32
  330.6 33.8 %collective-permute-start.39 = (bf16[256,4096]{1,0:T(8,128)(2,1)}, bf16[256,4096]{1,0:T(8,128)(2,1)S(1)}, u32[]{:S(2)}, u32[]{:S(2)}) collective-permute-start(bf16[256,4096]{1,0:T(8,128)(2,1)} %get-tuple-element.105.dh), channel_id=1, source_target_pairs={{4,0},{0,4},{12,8},{8,12},{20,16},{16,20},{28,24},{24,28},{36,32},... | collective-permute-start | bytes 6291464 | tf_op jit(solution)/shard_map/ppermute | solution.py:32
  363.6 43.3 %collective-permute-start.65 = (bf16[64,4224]{1,0:T(8,128)(2,1)}, bf16[64,4224]{1,0:T(8,128)(2,1)S(1)}, u32[]{:S(2)}, u32[]{:S(2)}) collective-permute-start(bf16[64,4224]{1,0:T(8,128)(2,1)} %get-tuple-element.132), channel_id=1, source_target_pairs={{48,0},{52,4},{56,8},{60,12},{0,16},{4,20},{8,24},{12,28},{16,32},... | collective-permute-start | bytes 1622024 | tf_op jit(solution)/shard_map/ppermute | solution.py:32
  364.1 43.0 %collective-permute-start.62 = (bf16[64,4224]{1,0:T(8,128)(2,1)}, bf16[64,4224]{1,0:T(8,128)(2,1)S(1)}, u32[]{:S(2)}, u32[]{:S(2)}) collective-permute-start(bf16[64,4224]{1,0:T(8,128)(2,1)} %get-tuple-element.129), channel_id=1, source_target_pairs={{48,0},{52,4},{56,8},{60,12},{0,16},{4,20},{8,24},{12,28},{16,32},... | collective-permute-start | bytes 1622024 | tf_op jit(solution)/shard_map/ppermute | solution.py:32
  380.5 29.0 %collective-permute-start.67 = (bf16[64,4224]{1,0:T(8,128)(2,1)}, bf16[64,4224]{1,0:T(8,128)(2,1)S(1)}, u32[]{:S(2)}, u32[]{:S(2)}) collective-permute-start(bf16[64,4224]{1,0:T(8,128)(2,1)} %summed.21), channel_id=1, source_target_pairs={{16,0},{20,4},{24,8},{28,12},{32,16},{36,20},{40,24},{44,28},{48,3... | collective-permute-start | bytes 1622024 | tf_op jit(solution)/shard_map/ppermute | solution.py:32
  424.5 22.2 %collective-permute-start.47 = (bf16[4,96,1024]{2,1,0:T(8,128)(2,1)}, bf16[4,96,1024]{2,1,0:T(8,128)(2,1)S(1)}, u32[]{:S(2)}, u32[]{:S(2)}) collective-permute-start(bf16[4,96,1024]{2,1,0:T(8,128)(2,1)} %get-tuple-element.116), channel_id=1, source_target_pairs={{3,0},{0,1},{1,2},{2,3},{7,4},{4,5},{5,6},{6,7},{11,8},{8,9},{9,10... | collective-permute-start | bytes 2359304 | tf_op jit(solution)/shard_map/ppermute | solution.py:36
  429.6 20.7 %collective-permute-start.43 = (bf16[4,96,1024]{2,1,0:T(8,128)(2,1)}, bf16[4,96,1024]{2,1,0:T(8,128)(2,1)S(1)}, u32[]{:S(2)}, u32[]{:S(2)}) collective-permute-start(bf16[4,96,1024]{2,1,0:T(8,128)(2,1)} %get-tuple-element.110), channel_id=1, source_target_pairs={{1,0},{2,1},{3,2},{0,3},{5,4},{6,5},{7,6},{4,7},{9,8},{10,9},{11,1... | collective-permute-start | bytes 2359304 | tf_op jit(solution)/shard_map/ppermute | solution.py:36
  434.0 30.4 %collective-permute-start.49 = (bf16[4,96,1024]{2,1,0:T(8,128)(2,1)S(1)}, bf16[4,96,1024]{2,1,0:T(8,128)(2,1)S(1)}, u32[]{:S(2)}, u32[]{:S(2)}) collective-permute-start(bf16[4,96,1024]{2,1,0:T(8,128)(2,1)S(1)} %copy-done.26), channel_id=1, source_target_pairs={{1,0},{2,1},{3,2},{0,3},{5,4},{6,5},{7,6},{4,7},{9,8},{10,9},{11,1... | collective-permute-start | bytes 2359304 | tf_op jit(solution)/shard_map/ppermute | solution.py:36
  435.2 42.0 %collective-permute-start.42 = (bf16[4,96,1024]{2,1,0:T(8,128)(2,1)}, bf16[4,96,1024]{2,1,0:T(8,128)(2,1)S(1)}, u32[]{:S(2)}, u32[]{:S(2)}) collective-permute-start(bf16[4,96,1024]{2,1,0:T(8,128)(2,1)} %summed.15), channel_id=1, source_target_pairs={{3,0},{0,1},{1,2},{2,3},{7,4},{4,5},{5,6},{6,7},{11,8},{8,9},{9,10... | collective-permute-start | bytes 2359304 | tf_op jit(solution)/shard_map/ppermute | solution.py:36
  440.5 33.7 %collective-permute-start.69 = (bf16[16,4224]{1,0:T(8,128)(2,1)S(1)}, bf16[16,4224]{1,0:T(8,128)(2,1)S(1)}, u32[]{:S(2)}, u32[]{:S(2)}) collective-permute-start(bf16[16,4224]{1,0:T(8,128)(2,1)S(1)} %get-tuple-element.158), channel_id=1, source_target_pairs={{3,0},{0,1},{1,2},{2,3},{7,4},{4,5},{5,6},{6,7},{11,8},{8,9},{9,10... | collective-permute-start | bytes 405512 | tf_op jit(solution)/shard_map/ppermute | solution.py:36
  446.7 23.9 %collective-permute-start.82 = (bf16[16,2048]{1,0:T(8,128)(2,1)S(1)}, bf16[16,2048]{1,0:T(8,128)(2,1)S(1)}, u32[]{:S(2)}, u32[]{:S(2)}) collective-permute-start(bf16[16,2048]{1,0:T(8,128)(2,1)S(1)} %get-tuple-element.162), channel_id=1, source_target_pairs={{3,0},{0,1},{1,2},{2,3},{7,4},{4,5},{5,6},{6,7},{11,8},{8,9},{9,10... | collective-permute-start | bytes 196616 | tf_op jit(solution)/shard_map/ppermute | solution.py:36
  450.3 21.6 %collective-permute-start.83 = (bf16[16,2048]{1,0:T(8,128)(2,1)S(1)}, bf16[16,2048]{1,0:T(8,128)(2,1)S(1)}, u32[]{:S(2)}, u32[]{:S(2)}) collective-permute-start(bf16[16,2048]{1,0:T(8,128)(2,1)S(1)} %get-tuple-element.161), channel_id=1, source_target_pairs={{2,0},{3,1},{0,2},{1,3},{6,4},{7,5},{4,6},{5,7},{10,8},{11,9},{8,1... | collective-permute-start | bytes 196616 | tf_op jit(solution)/shard_map/ppermute | solution.py:36
  (149 other events, 2032.7 us)

commit v3 on v2

--- a/solution.py
+++ b/solution.py
@@ -8,7 +8,9 @@
 XS, ZS, CS, YS = 4, 2, 2, 4
 T = 256
 D, FF = 1024, 4096
-UNIT = 6272
+GROWS = 48
+TAILS = 4 - GROWS // 16
+UNIT = 4096 + 1024 * TAILS + 128
 QP = 4224
 epsilon = 1e-06
 bf16, f32 = jnp.bfloat16, jnp.float32
@@ -34,6 +36,18 @@
 
 def from_replica(value, dy):
     return lax.ppermute(value, "replica", [((y + dy) % YS, y) for y in range(YS)])
+
+
+def onward(value, axis):
+    pairs = []
+    for x in range(XS):
+        for z in range(ZS):
+            for c in range(CS):
+                for y in range(YS):
+                    step = 1 - 2 * c
+                    tx, ty = (x + step, y) if axis == "x" else (x, y + step)
+                    pairs.append((shard_of(x, z, c) * YS + y, shard_of(tx, z, c) * YS + ty % YS))
+    return lax.ppermute(value, ("shard", "replica"), pairs)
 
 
 def passed_along(value, steps):
@@ -90,65 +104,55 @@
     small[...] = jnp.zeros_like(small)
     small[0:10, 0:64] = vectors[...].astype(f32)
     small[16:18, :] = bias[...].astype(f32)
-    low = small[...].astype(bf16)
     copies = [
         pltpu.make_async_copy(fc1.at[:, pl.ds(pl.multiple_of(y * 1024, 1024), 1024)], piece.at[0:64], sems.at[0]),
-        pltpu.make_async_copy(fc2.at[pl.ds(pl.multiple_of(y * 32, 32), 32)], piece.at[64:96], sems.at[1]),
+        pltpu.make_async_copy(fc2.at[pl.ds(pl.multiple_of(y * GROWS, 16), GROWS)], piece.at[64 : 64 + GROWS], sems.at[1]),
         pltpu.make_async_copy(qkv, unit.at[:, 0:3072], sems.at[2]),
         pltpu.make_async_copy(proj, unit.at[:, 3072:4096], sems.at[3]),
-        pltpu.make_async_copy(fc2.at[128:192], unit.at[:, 4096:5120], sems.at[4]),
-        pltpu.make_async_copy(fc2.at[192:256], unit.at[:, 5120:6144], sems.at[5]),
     ]
-    for copy in copies:
-        copy.start()
-    for copy in copies:
-        copy.wait()
-    unit[:, 6144:6272] = low
+    for n in range(TAILS):
+        row, col = 4 * GROWS + 64 * n, 4096 + 1024 * n
+        copies.append(
+            pltpu.make_async_copy(fc2.at[row : row + 64], unit.at[:, col : col + 1024], sems.at[4 + n])
+        )
+    start(copies)
+    wait(copies)
+    unit[:, UNIT - 128 : UNIT] = small[...].astype(bf16)
 
 
 def pack(w_qkv, w_proj, w_fc1, w_fc2, vectors, fc1_bias):
     return call(
         pack_kernel,
-        [((64, UNIT), bf16), ((96, 1024), bf16)],
+        [((64, UNIT), bf16), ((64 + GROWS, 1024), bf16)],
         (w_qkv, w_proj, w_fc1, w_fc2, vectors, fc1_bias.reshape(2, 128)),
         [ANY] * 4 + [VM] * 2,
-        scratch=[pltpu.VMEM((64, 128), f32), pltpu.SemaphoreType.DMA((6,))],
+        scratch=[pltpu.VMEM((64, 128), f32), pltpu.SemaphoreType.DMA((4 + TAILS,))],
         moved=4 * 2**20,
         name="pack_parts",
     )
 
 
-def halves_kernel(*refs):
-    pieces, low, high, sems = refs[:8], refs[8], refs[9], refs[10]
+def placed_kernel(*refs):
+    pieces, out, sems = refs[:8], refs[8], refs[9]
     x, z, _, _ = place()
-    waits = []
-    for n, piece in enumerate(pieces):
-        index = near(x, n // 2, XS) * 2 + near(z, n % 2, ZS)
-
-        @pl.when(index < 4)
-        def _(piece=piece, index=index, n=n):
-            pltpu.make_async_copy(piece, low.at[index], sems.at[n]).start()
-
-        @pl.when(index >= 4)
-        def _(piece=piece, index=index, n=n):
-            pltpu.make_async_copy(piece, high.at[index - 4], sems.at[n]).start()
-
-        waits.append(pltpu.make_async_copy(piece, low.at[0], sems.at[n]))
-    for copy in waits:
-        copy.wait()
-
-
-def halves(pieces):
-    return call(
-        halves_kernel,
-        [((4, 96, 1024), bf16)] * 2,
+    copies = [
+        pltpu.make_async_copy(piece, out.at[near(x, n // 2, XS) * 2 + near(z, n % 2, ZS)], sems.at[n])
+        for n, piece in enumerate(pieces)
+    ]
+    start(copies)
+    wait(copies)
+
+
+def placed_pieces(pieces):
+    return call(
+        placed_kernel,
+        [((8, 64 + GROWS, 1024), bf16)],
         pieces,
         [ANY] * 8,
         scratch=[pltpu.SemaphoreType.DMA((8,))],
-        out_kinds=[ANY] * 2,
         moved=4 * 2**20,
-        name="place_pieces",
-    )
+        name="placed_pieces",
+    )[0]
 
 
 def vectors_kernel(*refs):
@@ -158,7 +162,7 @@
     for n, piece in enumerate(pieces):
         k, dx, dz = n // 8, (n // 2) % 4, n % 2
         index = near(x, dx, XS) * 4 + near(z, dz, ZS) * 2 + near(c, k, CS)
-        copies.append(pltpu.make_async_copy(piece.at[0:32, 6144:6272], held.at[index], sems.at[n]))
+        copies.append(pltpu.make_async_copy(piece.at[0:32, UNIT - 128 : UNIT], held.at[index], sems.at[n]))
         copies[-1].start()
     for copy in copies:
         copy.wait()
@@ -211,27 +215,32 @@
 
 def feed_weights(columns, rows, w1, w2, sems):
     x, z, c, y = place()
+    step = 1 - 2 * c
     first, second = [], []
     for n, piece in enumerate(rows):
-        k, dy, half = n // 8, (n // 2) % 4, n % 2
-        ck, yk = near(c, k, CS), near(y, dy, YS)
-        first.append(pltpu.make_async_copy(piece.at[:, 0:64], w1.at[yk, 4 * half : 4 * half + 4, ck], sems.at[0, n]))
+        k, kind = n // 4, n % 4
+        ck = near(c, k, CS)
+        yk = near(y + 4, (0, -step, step, 2)[kind], YS)
+        first.append(pltpu.make_async_copy(piece.at[:, 0:64], w1.at[yk, :, ck], sems.at[0, n]))
         second.append(
             pltpu.make_async_copy(
-                piece.at[:, 64:96],
-                w2.at[4 * half : 4 * half + 4, ck, pl.ds(pl.multiple_of(yk * 32, 32), 32)],
+                piece.at[:, 64 : 64 + GROWS],
+                w2.at[:, ck, pl.ds(pl.multiple_of(yk * GROWS, 16), GROWS)],
                 sems.at[1, n],
             )
         )
-    second += column_copies(columns, lambda xz, c: w2.at[xz, c, 128:192], 4096, 5120, sems.at[2])
-    second += column_copies(columns, lambda xz, c: w2.at[xz, c, 192:256], 5120, 6144, sems.at[3])
+    for n in range(TAILS):
+        row, col = 4 * GROWS + 64 * n, 4096 + 1024 * n
+        second += column_copies(
+            columns, lambda xz, c, row=row: w2.at[xz, c, row : row + 64], col, col + 1024, sems.at[2 + n]
+        )
     return first, second
 
 
 FEED_SCRATCH = [
     pltpu.VMEM((4, 8, 2, 64, 1024), bf16),
     pltpu.VMEM((8, 2, 256, 1024), bf16),
-    pltpu.SemaphoreType.DMA((4, 16)),
+    pltpu.SemaphoreType.DMA((2 + TAILS, 16)),
 ]
 
 
@@ -319,7 +328,7 @@
 
 
 def feed_forward_kernel(keep, x1_ref, c_ref, vec, bias, *refs):
-    columns, rows, refs = refs[:16], refs[16:32], refs[32:]
+    columns, rows, refs = refs[:16], refs[16:24], refs[24:]
     if keep:
         u_out, gp_out, f_out, y_out, w1, w2, sems = refs
     else:
@@ -351,7 +360,7 @@
 
 def feed_forward(keep, x1, c, vec, bias, columns, rows):
     flat = [columns[k][dx][dz] for k in range(CS) for dx in range(XS) for dz in range(ZS)]
-    flat += [rows[k][dy][half] for k in range(CS) for dy in range(YS) for half in range(2)]
+    flat += [rows[k][n] for k in range(CS) for n in range(YS)]
     outs = [((T, D), f32 if keep else bf16)]
     if keep:
         outs = [((T, FF), bf16), ((T, FF), bf16), ((T, D), f32)] + outs
@@ -359,7 +368,7 @@
         lambda *refs: feed_forward_kernel(keep, *refs),
         outs,
         [x1, c, vec, bias] + flat,
-        [VM] * 4 + [ANY] * 32,
+        [VM] * 4 + [ANY] * 24,
         scratch=FEED_SCRATCH,
         flops=4 * T * D * FF,
         moved=24 * 2**20,
@@ -368,7 +377,7 @@
 
 
 def feed_backward_kernel(g_ref, f_ref, gp_ref, x1_ref, o_ref, vec, *refs):
-    columns, rows, refs = refs[:16], refs[16:32], refs[32:]
+    columns, rows, refs = refs[:16], refs[16:24], refs[24:]
     df_out, dh_out, dx1_out, do_out, small, gbias, w1, w2, sems = refs
     first, second = feed_weights(columns, rows, w1, w2, sems)
     start(second)
@@ -405,12 +414,12 @@
 
 def feed_backward(g, f, gp, x1, o, vec, columns, rows):
     flat = [columns[k][dx][dz] for k in range(CS) for dx in range(XS) for dz in range(ZS)]
-    flat += [rows[k][dy][half] for k in range(CS) for dy in range(YS) for half in range(2)]
+    flat += [rows[k][n] for k in range(CS) for n in range(YS)]
     return call(
         feed_backward_kernel,
         [((T, D), bf16), ((T, FF), bf16), ((T, D), f32), ((T, D), bf16), ((16, D), f32), ((1, FF), f32)],
         [g, f, gp, x1, o, vec] + flat,
-        [VM] * 6 + [ANY] * 32,
+        [VM] * 6 + [ANY] * 24,
         scratch=FEED_SCRATCH,
         flops=4 * T * D * FF,
         moved=26 * 2**20,
@@ -504,8 +513,9 @@
 
 
 def feed_grads_kernel(mine, theirs, dh, dh2, df, df2, *refs):
-    outs, acts, dh_all, df_all, rows, tail, sems, out_sems = refs[:16], *refs[16:]
-    _, _, _, y = place()
+    outs, acts, dh_all, df_all, rows, sems, out_sems = refs[:4], *refs[4:]
+    _, _, c, y = place()
+    step = 1 - 2 * c
     copies = [
         pltpu.make_async_copy(mine.at[1024:3584], acts.at[:, 0:256], sems.at[0]),
         pltpu.make_async_copy(theirs.at[1024:3584], acts.at[:, 256:512], sems.at[1]),
@@ -516,52 +526,45 @@
     ]
     start(copies)
     wait(copies[:4])
-    sends = []
+    kinds = [near(y + 4, dy, YS) for dy in (2, -step, step, 0)]
     for j in range(8):
         grad = dot(acts[512 + j * 256 : 768 + j * 256, :], df_all[...]).astype(bf16)
-        tail[j, :, 0:1024] = grad[128:192]
-        tail[j, :, 1024:2048] = grad[192:256]
-        sends.append(pltpu.make_async_copy(tail.at[j], outs[8 + j], out_sems.at[8 + j]))
+        rows[:, j, 64:128] = grad.reshape(YS, 64, 1024)
+    wait(copies[4:])
+    sends = []
+    for n, yk in enumerate(kinds):
+        cols = pl.ds(pl.multiple_of(yk * 1024, 1024), 1024)
+        for half in range(2):
+            grad = dot(acts[half * 256 : half * 256 + 256, :], dh_all[:, cols]).astype(bf16)
+            rows[yk, 4 * half : 4 * half + 4, 0:64] = grad.reshape(4, 64, 1024)
+        sends.append(pltpu.make_async_copy(rows.at[yk], outs[n], out_sems.at[n]))
         sends[-1].start()
-        for yk in range(YS):
-            dy = near(jnp.int32(yk + YS) - y, 0, YS)
-            rows[dy, j // 4, j % 4, 64:96] = grad[yk * 32 : yk * 32 + 32]
-    wait(copies[4:])
-    for dy in (2, 1, 3, 0):
-        start_col = pl.multiple_of(near(y, dy, YS) * 1024, 1024)
-        for half in range(2):
-            grad = dot(acts[half * 256 : half * 256 + 256, :], dh_all[:, pl.ds(start_col, 1024)]).astype(bf16)
-            rows[dy, half, :, 0:64] = grad.reshape(4, 64, 1024)
-            sends.append(pltpu.make_async_copy(rows.at[dy, half], outs[dy * 2 + half], out_sems.at[dy * 2 + half]))
-            sends[-1].start()
     wait(sends)
 
 
 def feed_grads(mine, theirs, dh, dh2, df, df2):
-    out = call(
+    return call(
         feed_grads_kernel,
-        [((4, 96, 1024), bf16)] * 8 + [((64, 2048), bf16)] * 8,
+        [((8, 128, 1024), bf16)] * 4,
         [mine, theirs, dh, dh2, df, df2],
         [ANY] * 6,
         scratch=[
             pltpu.VMEM((2560, 512), bf16),
             pltpu.VMEM((512, FF), bf16),
             pltpu.VMEM((512, D), bf16),
-            pltpu.VMEM((4, 2, 4, 96, 1024), bf16),
-            pltpu.VMEM((8, 64, 2048), bf16),
+            pltpu.VMEM((4, 8, 128, 1024), bf16),
             pltpu.SemaphoreType.DMA((6,)),
-            pltpu.SemaphoreType.DMA((16,)),
+            pltpu.SemaphoreType.DMA((4,)),
         ],
-        out_kinds=[ANY] * 16,
+        out_kinds=[ANY] * 4,
         flops=8 * T * D * FF,
         moved=24 * 2**20,
         name="feed_grads",
     )
-    return [[out[dy * 2], out[dy * 2 + 1]] for dy in range(YS)], out[8:]
 
 
 def attention_grads_kernel(mine, theirs, dp, dp2, do, do2, s1, s2, s3, s4, b1, b2, *refs):
-    outs, acts, dp_all, do_all, held, sems, out_sems = refs[:8], *refs[8:]
+    outs, acts, dp_all, do_all, held, sems, out_sems = refs[:4], *refs[4:]
     x, z, c, _ = place()
     copies = [
         pltpu.make_async_copy(mine.at[0:1024], acts.at[:, 0:256], sems.at[0]),
@@ -592,7 +595,9 @@
     for n in range(6):
         grad = dot(acts[0:512, :], dp_all[:, n * 512 : n * 512 + 512]).astype(bf16)
         held[:, :, n * 512 : n * 512 + 512] = grad.reshape(8, 64, 512)
-    sends = [pltpu.make_async_copy(held.at[j], outs[j], out_sems.at[j]) for j in range(8)]
+    step = 1 - 2 * c
+    kinds = [near(jnp.int32(4), dx, XS) for dx in (2, -step, step, 0)]
+    sends = [pltpu.make_async_copy(held.at[pl.ds(2 * dx, 2)], outs[n], out_sems.at[n]) for n, dx in enumerate(kinds)]
     start(sends)
     wait(sends)
 
@@ -600,7 +605,7 @@
 def attention_grads(mine, theirs, dp, dp2, do, do2, smalls, biases):
     return call(
         attention_grads_kernel,
-        [((64, QP), bf16)] * 8,
+        [((2, 64, QP), bf16)] * 4,
         [mine, theirs, dp, dp2, do, do2] + smalls + biases,
         [ANY] * 6 + [VM] * 6,
         scratch=[
@@ -609,9 +614,9 @@
             pltpu.VMEM((512, D), bf16),
             pltpu.VMEM((8, 64, QP), bf16),
             pltpu.SemaphoreType.DMA((6,)),
-            pltpu.SemaphoreType.DMA((8,)),
+            pltpu.SemaphoreType.DMA((4,)),
         ],
-        out_kinds=[ANY] * 8,
+        out_kinds=[ANY] * 4,
         flops=8 * T * D * 2 * D,
         moved=16 * 2**20,
         name="attention_grads",
@@ -648,28 +653,21 @@
     return out if split else out[0]
 
 
+def scattered(parts, axis):
+    opposite, behind, ahead, here = parts
+    far = onward(opposite, axis)
+    given = onward(from_shard(behind, dc=1), axis)
+    own = onward(summed([ahead, far]), axis)
+    return [here, own, from_shard(given, dc=1)]
+
+
 def scatter_columns(parts):
-    far_a = from_shard(parts[4], dx=3)
-    far_b = from_shard(parts[5], dx=1)
-    plus_b = from_shard(parts[3], dx=3)
-    minus_a = from_shard(parts[6], dx=1)
-    plus_a = from_shard(summed([parts[2], far_a]), dx=3)
-    minus_b = from_shard(summed([parts[7], far_b]), dx=1)
-    other = summed([parts[1], plus_b, minus_b])
-    got = from_shard(other, dz=1)
-    return summed([parts[0], plus_a, minus_a, got])
+    same, other = summed(scattered(parts, "x"), split=True)
+    return summed([same, from_shard(other, dz=1)])
 
 
 def scatter_rows(parts):
-    far_a = from_replica(parts[2][0], 3)
-    far_b = from_replica(parts[2][1], 1)
-    plus_b = from_replica(parts[1][1], 3)
-    minus_a = from_replica(parts[3][0], 1)
-    plus_a = from_replica(summed([parts[1][0], far_a]), 3)
-    minus_b = from_replica(summed([parts[3][1], far_b]), 1)
-    high = summed([parts[0][1], plus_b, minus_b], split=True)
-    low = summed([parts[0][0], plus_a, minus_a], split=True)
-    places = low + high
+    places = summed(scattered(parts, "y"), split=True)
     got = [
         from_shard(places[2 * dx + dz], dx=XS - dx, dz=dz)
         for dx in range(XS)
@@ -686,40 +684,36 @@
 
 
 def results_kernel(*refs):
-    rows, columns, tails = refs[0:4], refs[4:8], refs[8:12]
-    g_qkv, g_proj, g_fc1, g_fc2, g_vec, g_bias, rows_all, cols_all, tail_all, sems = refs[12:]
+    rows, columns = refs[0:4], refs[4:8]
+    g_qkv, g_proj, g_fc1, g_fc2, g_vec, g_bias, rows_all, cols_all, sems = refs[8:]
     _, _, _, y = place()
     copies = []
     for dy in range(YS):
         yk = near(y, dy, YS)
         copies.append(pltpu.make_async_copy(rows[dy], rows_all.at[yk], sems.at[0, dy]))
         copies.append(pltpu.make_async_copy(columns[dy], cols_all.at[yk], sems.at[1, dy]))
-        copies.append(pltpu.make_async_copy(tails[dy], tail_all.at[yk], sems.at[2, dy]))
     start(copies)
     wait(copies)
     for k in range(YS):
         g_fc1[:, k * 1024 : k * 1024 + 1024] = rows_all[k, 0:64].astype(f32)
-        g_fc2[k * 32 : k * 32 + 32, :] = rows_all[k, 64:96].astype(f32)
+        g_fc2[k * 64 : k * 64 + 64, :] = rows_all[k, 64:128].astype(f32)
         line = slice(k * 16, k * 16 + 16)
         g_qkv[line, :] = cols_all[k, :, 0:3072].astype(f32)
         g_proj[line, :] = cols_all[k, :, 3072:4096].astype(f32)
-        g_fc2[128 + k * 16 : 144 + k * 16, :] = tail_all[k, :, 0:1024].astype(f32)
-        g_fc2[192 + k * 16 : 208 + k * 16, :] = tail_all[k, :, 1024:2048].astype(f32)
     g_vec[...] = cols_all[0, :, 4096:4224].astype(f32)
     g_bias[...] = cols_all[1, :, 4096:4224].astype(f32)
 
 
-def results(rows, columns, tails):
+def results(rows, columns):
     return call(
         results_kernel,
         [((64, 3072), f32), ((64, 1024), f32), ((64, FF), f32), ((256, D), f32), ((16, 128), f32), ((16, 128), f32)],
-        list(rows) + list(columns) + list(tails),
-        [ANY] * 12,
+        list(rows) + list(columns),
+        [ANY] * 8,
         scratch=[
-            pltpu.VMEM((4, 96, 1024), bf16),
+            pltpu.VMEM((4, 128, 1024), bf16),
             pltpu.VMEM((4, 16, QP), bf16),
-            pltpu.VMEM((4, 16, 2048), bf16),
-            pltpu.SemaphoreType.DMA((3, 4)),
+            pltpu.SemaphoreType.DMA((2, 4)),
         ],
         moved=10 * 2**20,
         name="results",
@@ -727,22 +721,27 @@
 
 
 def gather(w_qkv, w_proj, w_fc1, w_fc2, vectors, fc1_bias):
+    twin = lambda v: from_shard(v, dc=1)
     unit, piece = pack(w_qkv, w_proj, w_fc1, w_fc2, vectors, fc1_bias)
     pieces = [
         piece if (dx, dz) == (0, 0) else from_shard(piece, dx=dx, dz=dz) for dx in range(XS) for dz in range(ZS)
+    ]
+    here = placed_pieces(pieces)
+    unit, here = lax.optimization_barrier((unit, here))
+    twin_here = twin(here)
+    behind = onward(here, "y")
+    twin_behind = onward(twin_here, "y")
+    opposite = onward(behind, "y")
+    rows = [
+        [here, behind, twin(twin_behind), opposite],
+        [twin_here, twin_behind, twin(behind), twin(opposite)],
     ]
     other = from_shard(unit, dz=1)
     plus = [from_shard(unit, dx=1), from_shard(other, dx=1)]
     minus = [from_shard(unit, dx=3), from_shard(other, dx=3)]
     far = [from_shard(plus[0], dx=1), from_shard(minus[1], dx=3)]
     mine = [[unit, other], plus, far, minus]
-    columns = [mine, [[from_shard(v, dc=1) for v in pair] for pair in mine]]
-    here = halves(pieces)
-    up = [from_replica(v, 1) for v in here]
-    down = [from_replica(v, 3) for v in here]
-    opposite = [from_replica(up[0], 1), from_replica(down[1], 3)]
-    mine = [here, up, opposite, down]
-    rows = [mine, [[from_shard(v, dc=1) for v in pair] for pair in mine]]
+    columns = [mine, [[twin(v) for v in pair] for pair in mine]]
     return columns, rows
 
 
@@ -772,15 +771,13 @@
     df, dh, dx1, do, small_a, gbias = feed_backward(upstream, f, gp, x1, o, vec, columns, rows)
     dp, dx, small_b = attention_backward(do, dx1, inputs, p, soft, vec, columns)
     twin = lambda v: from_shard(v, dc=1)
-    row_parts, tail_parts = feed_grads(mine, theirs, dh, twin(dh), df, twin(df))
-    tail = own_quarter(scatter_columns(tail_parts), y)
-    row = scatter_rows(row_parts)
+    row = scatter_rows(feed_grads(mine, theirs, dh, twin(dh), df, twin(df)))
     column_parts = attention_grads(
         mine, theirs, dp, twin(dp), do, twin(do), [small_a, twin(small_a), small_b, twin(small_b)], [gbias, twin(gbias)]
     )
     column = own_quarter(scatter_columns(column_parts), y)
     around = lambda v: [v] + [from_replica(v, dy) for dy in range(1, YS)]
-    g_qkv, g_proj, g_fc1, g_fc2, g_vec, g_bias = results(around(row), around(column), around(tail))
+    g_qkv, g_proj, g_fc1, g_fc2, g_vec, g_bias = results(around(row), around(column))
     edge_values = jnp.where(section == 0, dx, output).reshape(1, 2, 1, 128, D)
     return (
         edge_values,

time: 532 us -> 458 us (0.86)
  Pallas kernels: 225 us -> 167 us
  starting transfers between devices: 97.7 us -> 70.7 us
  waiting for transfers between devices: 176 us -> 186 us
    ppermute x27 -> x9, waiting for transfers between devices: 84.4 us -> 12.2 us  [from_replica(): lax.ppermute(value, 'replica', [((y + dy) % YS, y) for y in range(YS)])]
    ppermute x0 -> x9, waiting for transfers between devices: none -> 61.8 us  [onward(): return lax.ppermute(value, ('shard', 'replica'), pairs)]
    pallas_call x30 -> x22, Pallas kernels: 225 us -> 167 us  [call(): pl.pallas_call(kernel, out_shape=[jax.ShapeDtypeStruct(s, d) for s, d in...]
    ppermute x27 -> x9, starting transfers between devices: 37.9 us -> 14.7 us  [from_replica(): lax.ppermute(value, 'replica', [((y + dy) % YS, y) for y in range(YS)])]
    ppermute x59 -> x46, waiting for transfers between devices: 71.7 us -> 86.5 us  [from_shard(): return lax.ppermute(value, 'shard', pairs)]
    ppermute x59 -> x46, starting transfers between devices: 52.9 us -> 40.6 us  [from_shard(): return lax.ppermute(value, 'shard', pairs)]
    ppermute x0 -> x9, starting transfers between devices: none -> 8.51 us  [onward(): return lax.ppermute(value, ('shard', 'replica'), pairs)]
    ppermute x2, waiting for transfers between devices: 20.2 us -> 25.8 us  [passed_along(): return lax.ppermute(value, 'section', [(0, 1)] if steps == 1 else [(1, 0)])]
  transfers between devices with their start and end apart: 88 -> 66, of which waited for: 30 -> 29; matrix products, arithmetic and copies ran while one was open for 1% -> 1% of each run, Pallas kernels for 28% -> 16%
where the time goes in v3:
time: 458 us; the launch traced here: 449 us
  waiting for transfers between devices  186 us (41%)
  Pallas kernels  167 us (36%)
  starting transfers between devices  70.7 us (15%)
  local copies, waits for them, and re-layouts  17.1 us (4%)
  other arithmetic  6.92 us (2%)
    pallas_call x22, Pallas kernels, call(): pl.pallas_call(kernel, out_shape=[jax.ShapeDtypeStruct(s, d) for s, d in...  167 us
    ppermute x46, waiting for transfers between devices, from_shard(): return lax.ppermute(value, 'shard', pairs)  86.5 us
    ppermute x9, waiting for transfers between devices, onward(): return lax.ppermute(value, ('shard', 'replica'), pairs)  61.8 us
    ppermute x46, starting transfers between devices, from_shard(): return lax.ppermute(value, 'shard', pairs)  40.6 us
    ppermute x2, waiting for transfers between devices, passed_along(): return lax.ppermute(value, 'section', [(0, 1)] if steps == 1 else [(1, 0)])  25.8 us
    ppermute x9, starting transfers between devices, from_replica(): lax.ppermute(value, 'replica', [((y + dy) % YS, y) for y in range(YS)])  14.7 us
    unnamed x123, local copies, waits for them, and re-layouts  13.3 us
    ppermute x9, waiting for transfers between devices, from_replica(): lax.ppermute(value, 'replica', [((y + dy) % YS, y) for y in range(YS)])  12.2 us
  transfers between devices with their start and end apart: 66, of which 29 were waited for; matrix products, arithmetic and copies ran while one was open for 1% of the time, Pallas kernels for 16%

profile of v3, /device:TPU:0, one launch (start us, length us, event | category | flops | bytes accessed | tf_op | source)
XLA Modules:
  0.0 449.5 jit_solution(17001418274326769488)
XLA Ops:
  17.0 13.3 %collective-permute-done.2.refs_3_ = bf16[112,1024]{1,0:T(8,128)(2,1)S(1)} collective-permute-done((bf16[112,1024]{1,0:T(8,128)(2,1)}, bf16[112,1024]{1,0:T(8,128)(2,1)S(1)}, u32[]{:S(2)}, u32[]{:S(2)}) %collective-permute-start.2) | collective-permute-done | bytes 229408 | tf_op jit(solution)/shard_map/ppermute | solution.py:34
  43.8 18.8 %collective-permute-done.22.refs_21_.refs_17_ = bf16[8,112,1024]{2,1,0:T(8,128)(2,1)} collective-permute-done((bf16[8,112,1024]{2,1,0:T(8,128)(2,1)}, bf16[8,112,1024]{2,1,0:T(8,128)(2,1)}, u32[]{:S(2)}, u32[]{:S(2)}) %collective-permute-start.22) | collective-permute-done | bytes 1835040 | tf_op jit(solution)/shard_map/ppermute | solution.py:50
  70.0 13.6 %collective-permute-done.11.refs_7_.refs_9_.refs_11_ = bf16[64,5248]{1,0:T(8,128)(2,1)S(1)} collective-permute-done((bf16[64,5248]{1,0:T(8,128)(2,1)S(1)}, bf16[64,5248]{1,0:T(8,128)(2,1)S(1)}, u32[]{:S(2)}, u32[]{:S(2)}) %collective-permute-start.11) | collective-permute-done | bytes 671776 | tf_op jit(solution)/shard_map/ppermute | solution.py:34
  84.3 13.6 %collective-permute-done.10.refs_4_.refs_6_.refs_8_ = bf16[64,5248]{1,0:T(8,128)(2,1)S(1)} collective-permute-done((bf16[64,5248]{1,0:T(8,128)(2,1)S(1)}, bf16[64,5248]{1,0:T(8,128)(2,1)S(1)}, u32[]{:S(2)}, u32[]{:S(2)}) %collective-permute-start.10) | collective-permute-done | bytes 671776 | tf_op jit(solution)/shard_map/ppermute | solution.py:34
  99.8 7.3 %collective-permute-done.24.refs_25_.refs_21_ = bf16[8,112,1024]{2,1,0:T(8,128)(2,1)} collective-permute-done((bf16[8,112,1024]{2,1,0:T(8,128)(2,1)S(1)}, bf16[8,112,1024]{2,1,0:T(8,128)(2,1)}, u32[]{:S(2)}, u32[]{:S(2)}) %collective-permute-start.24) | collective-permute-done | bytes 1835040 | tf_op jit(solution)/shard_map/ppermute | solution.py:50
  107.7 9.3 %collective-permute-done.12.refs_5_.refs_7_.refs_9_ = bf16[64,5248]{1,0:T(8,128)(2,1)} collective-permute-done((bf16[64,5248]{1,0:T(8,128)(2,1)S(1)}, bf16[64,5248]{1,0:T(8,128)(2,1)}, u32[]{:S(2)}, u32[]{:S(2)}) %collective-permute-start.12) | collective-permute-done | bytes 671776 | tf_op jit(solution)/shard_map/ppermute | solution.py:34
  123.5 11.3 %attention_forward.2 = (f32[256,1024]{1,0:T(8,128)}, bf16[256,1024]{1,0:T(8,128)(2,1)}) custom-call(bf16[256,1024]{1,0:T(8,128)(2,1)} %bitcast.32, f32[16,1024]{1,0:T(8,128)} %get-tuple-element.67.refs_1_.refs_2_.vec, bf16[64,5248]{1,0:T(8,128)(2,1)} %get-tuple-element.66.refs_0_.refs_2_.refs_4_, bf16[64,5248]{1,0:T(8,128)(2,1)} %copy-done.1, ...), custom_call_target="tpu_custom_call" | custom-call | flops 2147483648 | bytes 14680064 | tf_op jit(solution)/shard_map/attention_forward/pallas_call | solution.py:70
  134.9 13.4 %feed_forward.2 = bf16[256,1024]{1,0:T(8,128)(2,1)} custom-call(f32[256,1024]{1,0:T(8,128)} %get-tuple-element.68.refs_0_, bf16[256,1024]{1,0:T(8,128)(2,1)} %get-tuple-element.69.refs_1_, f32[16,1024]{1,0:T(8,128)} %get-tuple-element.67.refs_1_.refs_2_.vec, f32[1,4096]{1,0:T(1,128)} %get-tuple-element.70.refs_3_, ...), custom_call_target="tpu_custom_call" | custom-call | flops 4294967296 | bytes 25165824 | tf_op jit(solution)/shard_map/feed_forward/pallas_call | solution.py:70
  155.1 10.5 %collective-permute-done.29 = bf16[256,1024]{1,0:T(8,128)(2,1)S(1)} collective-permute-done((bf16[256,1024]{1,0:T(8,128)(2,1)}, bf16[256,1024]{1,0:T(8,128)(2,1)S(1)}, u32[]{:S(2)}, u32[]{:S(2)}) %collective-permute-start.29) | collective-permute-done | bytes 524320 | tf_op jit(solution)/shard_map/ppermute | solution.py:54
  166.5 12.9 %attention_forward.3 = (bf16[256,1024]{1,0:T(8,128)(2,1)}, bf16[256,3072]{1,0:T(8,128)(2,1)}, f32[16,256,128]{2,1,0:T(8,128)}, bf16[256,1024]{1,0:T(8,128)(2,1)}...) custom-call(bf16[256,1024]{1,0:T(8,128)(2,1)} %broadcast_select_fusion.1.refs_0_.x_ref, ...), custom_call_target="tpu_custom_call" | custom-call | flops 2147483648 | bytes 14680064 | tf_op jit(solution)/shard_map/attention_forward/pallas_call | solution.py:70
  179.4 15.7 %feed_forward.3 = (bf16[256,4096]{1,0:T(8,128)(2,1)}, bf16[256,4096]{1,0:T(8,128)(2,1)}, f32[256,1024]{1,0:T(8,128)}, f32[256,1024]{1,0:T(8,128)}) custom-call(f32[256,1024]{1,0:T(8,128)} %get-tuple-element.72.refs_0_.x1_ref, bf16[256,1024]{1,0:T(8,128)(2,1)} %get-tuple-element.73.refs_1_.c_ref, f32[16,1024]{1,0:T(8,128)} %get-tuple-element.67.refs_1_.refs_2_.vec, ...), custom_call_target="tpu_custom_call" | custom-call | flops 4294967296 | bytes 25165824 | tf_op jit(solution)/shard_map/feed_forward/pallas_call | solution.py:70
  195.1 15.8 %feed_backward.2 = (bf16[256,1024]{1,0:T(8,128)(2,1)}, bf16[256,4096]{1,0:T(8,128)(2,1)}, f32[256,1024]{1,0:T(8,128)}, bf16[256,1024]{1,0:T(8,128)(2,1)}, f32[16,1024]{1,0:T(8,128)}, /*index=5*/f32[1,4096]{1,0:T(1,128)}) custom-call(f32[256,1024]{1,0:T(8,128)} %convert_multiply_fusion.g_ref, f32[256,1024]{1,0:T(8,128)} %get-tuple-element.74.f_ref, ...), custom_call_target="tpu_custom_call" | custom-call | flops 4294967296 | bytes 27262976 | tf_op jit(solution)/shard_map/feed_backward/pallas_call | solution.py:70
  210.9 14.5 %attention_backward.2 = (bf16[256,3072]{1,0:T(8,128)(2,1)}, f32[256,1024]{1,0:T(8,128)}, f32[16,1024]{1,0:T(8,128)}) custom-call(bf16[256,1024]{1,0:T(8,128)(2,1)} %get-tuple-element.77.do_ref, f32[256,1024]{1,0:T(8,128)} %get-tuple-element.78.dx1_ref, bf16[256,1024]{1,0:T(8,128)(2,1)} %broadcast_select_fusion.1.refs_0_.x_ref, ...), custom_call_target="tpu_custom_call" | custom-call | flops 2147483648 | bytes 18874368 | tf_op jit(solution)/shard_map/attention_backward/pallas_call | solution.py:70
  228.1 15.2 %collective-permute-done.30 = bf16[256,1024]{1,0:T(8,128)(2,1)S(1)} collective-permute-done((bf16[256,1024]{1,0:T(8,128)(2,1)S(1)}, bf16[256,1024]{1,0:T(8,128)(2,1)S(1)}, u32[]{:S(2)}, u32[]{:S(2)}) %collective-permute-start.30) | collective-permute-done | bytes 524320 | tf_op jit(solution)/shard_map/ppermute | solution.py:54
  244.5 15.7 %feed_backward.3 = (bf16[256,1024]{1,0:T(8,128)(2,1)}, bf16[256,4096]{1,0:T(8,128)(2,1)}, f32[256,1024]{1,0:T(8,128)}, bf16[256,1024]{1,0:T(8,128)(2,1)}, f32[16,1024]{1,0:T(8,128)}, /*index=5*/f32[1,4096]{1,0:T(1,128)}) custom-call(f32[256,1024]{1,0:T(8,128)} %convert_select_fusion.g_ref, f32[256,1024]{1,0:T(8,128)} %get-tuple-element.74.f_ref, ...), custom_call_target="tpu_custom_call" | custom-call | flops 4294967296 | bytes 27262976 | tf_op jit(solution)/shard_map/feed_backward/pallas_call | solution.py:70
  260.4 6.0 %transposed_acts.1 = (bf16[3584,256]{1,0:T(8,128)(2,1)}, bf16[3584,256]{1,0:T(8,128)(2,1)}) custom-call(bf16[256,1024]{1,0:T(8,128)(2,1)} %get-tuple-element.86.a_ref, bf16[256,1024]{1,0:T(8,128)(2,1)} %get-tuple-element.87.m_ref, bf16[256,1024]{1,0:T(8,128)(2,1)} %get-tuple-element.73.refs_1_.c_ref, bf16[256,4096]{1,0:T(8,128)(2,1)} %get-tuple-element.88.u_ref), custom_call_target="tpu_custom_call" | custom-call | flops 2000000000 | bytes 8388608 | tf_op jit(solution)/shard_map/transposed_acts/pallas_call | solution.py:70
  267.1 14.3 %attention_backward.3 = (bf16[256,3072]{1,0:T(8,128)(2,1)}, f32[256,1024]{1,0:T(8,128)}, f32[16,1024]{1,0:T(8,128)}) custom-call(bf16[256,1024]{1,0:T(8,128)(2,1)} %get-tuple-element.82.do_ref.do, f32[256,1024]{1,0:T(8,128)} %get-tuple-element.83.dx1_ref, bf16[256,1024]{1,0:T(8,128)(2,1)} %broadcast_select_fusion.1.refs_0_.x_ref, ...), custom_call_target="tpu_custom_call" | custom-call | flops 2147483648 | bytes 18874368 | tf_op jit(solution)/shard_map/attention_backward/pallas_call | solution.py:70
  284.0 8.4 %feed_grads.1 = (bf16[8,128,1024]{2,1,0:T(8,128)(2,1)}, bf16[8,128,1024]{2,1,0:T(8,128)(2,1)}, bf16[8,128,1024]{2,1,0:T(8,128)(2,1)}, bf16[8,128,1024]{2,1,0:T(8,128)(2,1)}) custom-call(bf16[3584,256]{1,0:T(8,128)(2,1)} %get-tuple-element.89.mine, bf16[3584,256]{1,0:T(8,128)(2,1)} %copy-done.49, bf16[256,4096]{1,0:T(8,128)(2,1)} %get-tuple-element.91.dh, ...), custom_call_target="tpu_custom_call" | custom-call | flops 8589934592 | bytes 25165824 | tf_op jit(solution)/shard_map/feed_grads/pallas_call | solution.py:70
  300.5 7.5 %attention_grads.1 = (bf16[2,64,4224]{2,1,0:T(8,128)(2,1)}, bf16[2,64,4224]{2,1,0:T(8,128)(2,1)}, bf16[2,64,4224]{2,1,0:T(8,128)(2,1)}, bf16[2,64,4224]{2,1,0:T(8,128)(2,1)}) custom-call(bf16[3584,256]{1,0:T(8,128)(2,1)} %get-tuple-element.89.mine, bf16[3584,256]{1,0:T(8,128)(2,1)} %copy-done.49, bf16[256,3072]{1,0:T(8,128)(2,1)} %get-tuple-element.105.dp, ...), custom_call_target="tpu_custom_call" | custom-call | flops 4294967296 | bytes 16777216 | tf_op jit(solution)/shard_map/attention_grads/pallas_call | solution.py:70
  313.1 15.0 %collective-permute-done.54.refs_1_ = bf16[2,64,4224]{2,1,0:T(8,128)(2,1)S(1)} collective-permute-done((bf16[2,64,4224]{2,1,0:T(8,128)(2,1)}, bf16[2,64,4224]{2,1,0:T(8,128)(2,1)S(1)}, u32[]{:S(2)}, u32[]{:S(2)}) %collective-permute-start.54) | collective-permute-done | bytes 1081376 | tf_op jit(solution)/shard_map/ppermute | solution.py:50
  331.8 7.8 %collective-permute-done.57 = bf16[2,64,4224]{2,1,0:T(8,128)(2,1)S(1)} collective-permute-done((bf16[2,64,4224]{2,1,0:T(8,128)(2,1)S(1)}, bf16[2,64,4224]{2,1,0:T(8,128)(2,1)S(1)}, u32[]{:S(2)}, u32[]{:S(2)}) %collective-permute-start.57) | collective-permute-done | bytes 1081376 | tf_op jit(solution)/shard_map/ppermute | solution.py:50
  345.3 13.0 %collective-permute-done.37 = bf16[8,128,1024]{2,1,0:T(8,128)(2,1)} collective-permute-done((bf16[8,128,1024]{2,1,0:T(8,128)(2,1)}, bf16[8,128,1024]{2,1,0:T(8,128)(2,1)}, u32[]{:S(2)}, u32[]{:S(2)}) %collective-permute-start.37) | collective-permute-done | bytes 2097184 | tf_op jit(solution)/shard_map/ppermute | solution.py:50
  363.8 13.9 %collective-permute-done.59.refs_1_ = bf16[64,4224]{1,0:T(8,128)(2,1)S(1)} collective-permute-done((bf16[64,4224]{1,0:T(8,128)(2,1)}, bf16[64,4224]{1,0:T(8,128)(2,1)S(1)}, u32[]{:S(2)}, u32[]{:S(2)}) %collective-permute-start.59) | collective-permute-done | bytes 540704 | tf_op jit(solution)/shard_map/ppermute | solution.py:34
  430.9 8.2 %collective-permute-done.46.refs_1_ = bf16[128,1024]{1,0:T(8,128)(2,1)S(1)} collective-permute-done((bf16[128,1024]{1,0:T(8,128)(2,1)}, bf16[128,1024]{1,0:T(8,128)(2,1)S(1)}, u32[]{:S(2)}, u32[]{:S(2)}) %collective-permute-start.46) | collective-permute-done | bytes 262176 | tf_op jit(solution)/shard_map/ppermute | solution.py:38
  (264 shorter events, 152.7 us)
Async XLA Ops:
  9.5 20.8 %collective-permute-start.2 = (bf16[112,1024]{1,0:T(8,128)(2,1)}, bf16[112,1024]{1,0:T(8,128)(2,1)S(1)}, u32[]{:S(2)}, u32[]{:S(2)}) collective-permute-start(bf16[112,1024]{1,0:T(8,128)(2,1)} %get-tuple-element.65.refs_0_), channel_id=1, source_target_pairs={{24,0},{28,4},{16,8},{20,12},{40,16},{44,20},{32,24},{36,28},{56,3... | collective-permute-start | bytes 688136 | tf_op jit(solution)/shard_map/ppermute | solution.py:34
  9.9 20.5 %collective-permute-start.3 = (bf16[112,1024]{1,0:T(8,128)(2,1)}, bf16[112,1024]{1,0:T(8,128)(2,1)S(1)}, u32[]{:S(2)}, u32[]{:S(2)}) collective-permute-start(bf16[112,1024]{1,0:T(8,128)(2,1)} %get-tuple-element.65.refs_0_), channel_id=1, source_target_pairs={{32,0},{36,4},{40,8},{44,12},{48,16},{52,20},{56,24},{60,28},{0,32... | collective-permute-start | bytes 688136 | tf_op jit(solution)/shard_map/ppermute | solution.py:34
  10.4 20.0 %collective-permute-start.4 = (bf16[112,1024]{1,0:T(8,128)(2,1)}, bf16[112,1024]{1,0:T(8,128)(2,1)S(1)}, u32[]{:S(2)}, u32[]{:S(2)}) collective-permute-start(bf16[112,1024]{1,0:T(8,128)(2,1)} %get-tuple-element.65.refs_0_), channel_id=1, source_target_pairs={{40,0},{44,4},{32,8},{36,12},{56,16},{60,20},{48,24},{52,28},{8,32... | collective-permute-start | bytes 688136 | tf_op jit(solution)/shard_map/ppermute | solution.py:34
  37.8 24.8 %collective-permute-start.22 = (bf16[8,112,1024]{2,1,0:T(8,128)(2,1)}, bf16[8,112,1024]{2,1,0:T(8,128)(2,1)}, u32[]{:S(2)}, u32[]{:S(2)}) collective-permute-start(bf16[8,112,1024]{2,1,0:T(8,128)(2,1)} %placed_pieces.1.refs_20_.refs_16_), channel_id=1, source_target_pairs={{0,1},{1,2},{2,3},{3,0},{4,7},{5,4},{6,5},{7,6},{8,9},{9,10},{10,1... | collective-permute-start | bytes 5505032 | tf_op jit(solution)/shard_map/ppermute | solution.py:50
  39.5 23.5 %collective-permute-start.23 = (bf16[8,112,1024]{2,1,0:T(8,128)(2,1)}, bf16[8,112,1024]{2,1,0:T(8,128)(2,1)S(1)}, u32[]{:S(2)}, u32[]{:S(2)}) collective-permute-start(bf16[8,112,1024]{2,1,0:T(8,128)(2,1)} %placed_pieces.1.refs_20_.refs_16_), channel_id=1, source_target_pairs={{4,0},{0,4},{12,8},{8,12},{20,16},{16,20},{28,24},{24,28},{36,32},... | collective-permute-start | bytes 5505032 | tf_op jit(solution)/shard_map/ppermute | solution.py:34
  40.6 23.9 %collective-permute-start.7 = (bf16[64,5248]{1,0:T(8,128)(2,1)S(1)}, bf16[64,5248]{1,0:T(8,128)(2,1)S(1)}, u32[]{:S(2)}, u32[]{:S(2)}) collective-permute-start(bf16[64,5248]{1,0:T(8,128)(2,1)S(1)} %copy-done), channel_id=1, source_target_pairs={{8,0},{12,4},{0,8},{4,12},{24,16},{28,20},{16,24},{20,28},{40,32},... | collective-permute-start | bytes 2015240 | tf_op jit(solution)/shard_map/ppermute | solution.py:34
  41.0 23.6 %collective-permute-start.8 = (bf16[64,5248]{1,0:T(8,128)(2,1)S(1)}, bf16[64,5248]{1,0:T(8,128)(2,1)S(1)}, u32[]{:S(2)}, u32[]{:S(2)}) collective-permute-start(bf16[64,5248]{1,0:T(8,128)(2,1)S(1)} %copy-done), channel_id=1, source_target_pairs={{16,0},{20,4},{24,8},{28,12},{32,16},{36,20},{40,24},{44,28},{48,3... | collective-permute-start | bytes 2015240 | tf_op jit(solution)/shard_map/ppermute | solution.py:34
  43.8 22.5 %collective-permute-start.13 = (bf16[64,5248]{1,0:T(8,128)(2,1)S(1)}, bf16[64,5248]{1,0:T(8,128)(2,1)S(1)}, u32[]{:S(2)}, u32[]{:S(2)}) collective-permute-start(bf16[64,5248]{1,0:T(8,128)(2,1)S(1)} %copy-done), channel_id=1, source_target_pairs={{48,0},{52,4},{56,8},{60,12},{0,16},{4,20},{8,24},{12,28},{16,32},... | collective-permute-start | bytes 2015240 | tf_op jit(solution)/shard_map/ppermute | solution.py:34
  62.6 36.8 %collective-permute-start.26 = (bf16[8,112,1024]{2,1,0:T(8,128)(2,1)}, bf16[8,112,1024]{2,1,0:T(8,128)(2,1)}, u32[]{:S(2)}, u32[]{:S(2)}) collective-permute-start(bf16[8,112,1024]{2,1,0:T(8,128)(2,1)} %collective-permute-done.22.refs_21_.refs_17_), channel_id=1, source_target_pairs={{0,1},{1,2},{2,3},{3,0},{4,7},{5,4},{6,5},{7,6},{8,9},{9,10},{10,1... | collective-permute-start | bytes 5505032 | tf_op jit(solution)/shard_map/ppermute | solution.py:50
  63.0 44.0 %collective-permute-start.24 = (bf16[8,112,1024]{2,1,0:T(8,128)(2,1)S(1)}, bf16[8,112,1024]{2,1,0:T(8,128)(2,1)}, u32[]{:S(2)}, u32[]{:S(2)}) collective-permute-start(bf16[8,112,1024]{2,1,0:T(8,128)(2,1)S(1)} %collective-permute-done.23.refs_24_.refs_20_), channel_id=1, source_target_pairs={{0,1},{1,2},{2,3},{3,0},{4,7},{5,4},{6,5},{7,6},{8,9},{9,10},{10,1... | collective-permute-start | bytes 5505032 | tf_op jit(solution)/shard_map/ppermute | solution.py:50
  68.0 29.8 %collective-permute-start.10 = (bf16[64,5248]{1,0:T(8,128)(2,1)S(1)}, bf16[64,5248]{1,0:T(8,128)(2,1)S(1)}, u32[]{:S(2)}, u32[]{:S(2)}) collective-permute-start(bf16[64,5248]{1,0:T(8,128)(2,1)S(1)} %collective-permute-done.8.refs_2_.refs_4_.refs_6_), channel_id=1, source_target_pairs={{16,0},{20,4},{24,8},{28,12},{32,16},{36,20},{40,24},{44,28},{48,3... | collective-permute-start | bytes 2015240 | tf_op jit(solution)/shard_map/ppermute | solution.py:34
  97.9 19.0 %collective-permute-start.12 = (bf16[64,5248]{1,0:T(8,128)(2,1)S(1)}, bf16[64,5248]{1,0:T(8,128)(2,1)}, u32[]{:S(2)}, u32[]{:S(2)}) collective-permute-start(bf16[64,5248]{1,0:T(8,128)(2,1)S(1)} %collective-permute-done.11.refs_7_.refs_9_.refs_11_), channel_id=1, source_target_pairs={{48,0},{52,4},{56,8},{60,12},{0,16},{4,20},{8,24},{12,28},{16,32},... | collective-permute-start | bytes 2015240 | tf_op jit(solution)/shard_map/ppermute | solution.py:34
  99.3 35.6 %collective-permute-start.27 = (bf16[8,112,1024]{2,1,0:T(8,128)(2,1)}, bf16[8,112,1024]{2,1,0:T(8,128)(2,1)}, u32[]{:S(2)}, u32[]{:S(2)}) collective-permute-start(bf16[8,112,1024]{2,1,0:T(8,128)(2,1)} %collective-permute-done.22.refs_21_.refs_17_), channel_id=1, source_target_pairs={{4,0},{0,4},{12,8},{8,12},{20,16},{16,20},{28,24},{24,28},{36,32},... | collective-permute-start | bytes 5505032 | tf_op jit(solution)/shard_map/ppermute | solution.py:34
  99.4 35.5 %collective-permute-start.28 = (bf16[8,112,1024]{2,1,0:T(8,128)(2,1)}, bf16[8,112,1024]{2,1,0:T(8,128)(2,1)}, u32[]{:S(2)}, u32[]{:S(2)}) collective-permute-start(bf16[8,112,1024]{2,1,0:T(8,128)(2,1)} %collective-permute-done.26.refs_23_.refs_19_), channel_id=1, source_target_pairs={{4,0},{0,4},{12,8},{8,12},{20,16},{16,20},{28,24},{24,28},{36,32},... | collective-permute-start | bytes 5505032 | tf_op jit(solution)/shard_map/ppermute | solution.py:34
  107.0 27.8 %collective-permute-start.25 = (bf16[8,112,1024]{2,1,0:T(8,128)(2,1)}, bf16[8,112,1024]{2,1,0:T(8,128)(2,1)}, u32[]{:S(2)}, u32[]{:S(2)}) collective-permute-start(bf16[8,112,1024]{2,1,0:T(8,128)(2,1)} %collective-permute-done.24.refs_25_.refs_21_), channel_id=1, source_target_pairs={{4,0},{0,4},{12,8},{8,12},{20,16},{16,20},{28,24},{24,28},{36,32},... | collective-permute-start | bytes 5505032 | tf_op jit(solution)/shard_map/ppermute | solution.py:34
  260.3 21.7 %collective-permute-start.32 = (bf16[256,4096]{1,0:T(8,128)(2,1)}, bf16[256,4096]{1,0:T(8,128)(2,1)S(1)}, u32[]{:S(2)}, u32[]{:S(2)}) collective-permute-start(bf16[256,4096]{1,0:T(8,128)(2,1)} %get-tuple-element.91.dh), channel_id=1, source_target_pairs={{4,0},{0,4},{12,8},{8,12},{20,16},{16,20},{28,24},{24,28},{36,32},... | collective-permute-start | bytes 6291464 | tf_op jit(solution)/shard_map/ppermute | solution.py:34
  308.5 31.1 %collective-permute-start.34 = (bf16[8,128,1024]{2,1,0:T(8,128)(2,1)S(1)}, bf16[8,128,1024]{2,1,0:T(8,128)(2,1)S(1)}, u32[]{:S(2)}, u32[]{:S(2)}) collective-permute-start(bf16[8,128,1024]{2,1,0:T(8,128)(2,1)S(1)} %copy-done.47), channel_id=1, source_target_pairs={{0,1},{1,2},{2,3},{3,0},{4,7},{5,4},{6,5},{7,6},{8,9},{9,10},{10,1... | collective-permute-start | bytes 6291464 | tf_op jit(solution)/shard_map/ppermute | solution.py:50
  309.8 48.5 %collective-permute-start.37 = (bf16[8,128,1024]{2,1,0:T(8,128)(2,1)}, bf16[8,128,1024]{2,1,0:T(8,128)(2,1)}, u32[]{:S(2)}, u32[]{:S(2)}) collective-permute-start(bf16[8,128,1024]{2,1,0:T(8,128)(2,1)} %collective-permute-done.36), channel_id=1, source_target_pairs={{0,1},{1,2},{2,3},{3,0},{4,7},{5,4},{6,5},{7,6},{8,9},{9,10},{10,1... | collective-permute-start | bytes 6291464 | tf_op jit(solution)/shard_map/ppermute | solution.py:50
  311.5 28.2 %collective-permute-start.57 = (bf16[2,64,4224]{2,1,0:T(8,128)(2,1)S(1)}, bf16[2,64,4224]{2,1,0:T(8,128)(2,1)S(1)}, u32[]{:S(2)}, u32[]{:S(2)}) collective-permute-start(bf16[2,64,4224]{2,1,0:T(8,128)(2,1)S(1)} %collective-permute-done.56), channel_id=1, source_target_pairs={{0,16},{1,17},{2,18},{3,19},{4,52},{5,53},{6,54},{7,55},{8,24},{9,... | collective-permute-start | bytes 3244040 | tf_op jit(solution)/shard_map/ppermute | solution.py:50
  331.8 26.5 %collective-permute-start.55 = (bf16[2,64,4224]{2,1,0:T(8,128)(2,1)}, bf16[2,64,4224]{2,1,0:T(8,128)(2,1)S(1)}, u32[]{:S(2)}, u32[]{:S(2)}) collective-permute-start(bf16[2,64,4224]{2,1,0:T(8,128)(2,1)} %summed.10), channel_id=1, source_target_pairs={{0,16},{1,17},{2,18},{3,19},{4,52},{5,53},{6,54},{7,55},{8,24},{9,... | collective-permute-start | bytes 3244040 | tf_op jit(solution)/shard_map/ppermute | solution.py:50
  345.0 37.5 %collective-permute-start.35 = (bf16[8,128,1024]{2,1,0:T(8,128)(2,1)}, bf16[8,128,1024]{2,1,0:T(8,128)(2,1)S(1)}, u32[]{:S(2)}, u32[]{:S(2)}) collective-permute-start(bf16[8,128,1024]{2,1,0:T(8,128)(2,1)} %summed.7), channel_id=1, source_target_pairs={{0,1},{1,2},{2,3},{3,0},{4,7},{5,4},{6,5},{7,6},{8,9},{9,10},{10,1... | collective-permute-start | bytes 6291464 | tf_op jit(solution)/shard_map/ppermute | solution.py:50
  358.3 24.2 %collective-permute-start.38 = (bf16[8,128,1024]{2,1,0:T(8,128)(2,1)}, bf16[8,128,1024]{2,1,0:T(8,128)(2,1)}, u32[]{:S(2)}, u32[]{:S(2)}) collective-permute-start(bf16[8,128,1024]{2,1,0:T(8,128)(2,1)} %collective-permute-done.37), channel_id=1, source_target_pairs={{4,0},{0,4},{12,8},{8,12},{20,16},{16,20},{28,24},{24,28},{36,32},... | collective-permute-start | bytes 6291464 | tf_op jit(solution)/shard_map/ppermute | solution.py:34
  406.4 22.6 %collective-permute-start.63 = (bf16[16,4224]{1,0:T(8,128)(2,1)}, bf16[16,4224]{1,0:T(8,128)(2,1)S(1)}, u32[]{:S(2)}, u32[]{:S(2)}) collective-permute-start(bf16[16,4224]{1,0:T(8,128)(2,1)} %summed.13.refs_4_), channel_id=1, source_target_pairs={{1,0},{2,1},{3,2},{0,3},{5,4},{6,5},{7,6},{4,7},{9,8},{10,9},{11,1... | collective-permute-start | bytes 405512 | tf_op jit(solution)/shard_map/ppermute | solution.py:38
  411.7 19.2 %collective-permute-start.64 = (bf16[16,4224]{1,0:T(8,128)(2,1)}, bf16[16,4224]{1,0:T(8,128)(2,1)S(1)}, u32[]{:S(2)}, u32[]{:S(2)}) collective-permute-start(bf16[16,4224]{1,0:T(8,128)(2,1)} %summed.13.refs_4_), channel_id=1, source_target_pairs={{2,0},{3,1},{0,2},{1,3},{6,4},{7,5},{4,6},{5,7},{10,8},{11,9},{8,1... | collective-permute-start | bytes 405512 | tf_op jit(solution)/shard_map/ppermute | solution.py:38
  (103 other events, 1335.0 us)

commit v4 on v3

--- a/solution.py
+++ b/solution.py
@@ -376,19 +376,18 @@
     )
 
 
-def feed_backward_kernel(g_ref, f_ref, gp_ref, x1_ref, o_ref, vec, *refs):
+def feed_backward_kernel(g_ref, df_ref, f_ref, gp_ref, x1_ref, o_ref, vec, *refs):
     columns, rows, refs = refs[:16], refs[16:24], refs[24:]
-    df_out, dh_out, dx1_out, do_out, small, gbias, w1, w2, sems = refs
+    dh_out, dx1_out, do_out, small, w1, w2, sems = refs
     first, second = feed_weights(columns, rows, w1, w2, sems)
     start(second)
     start(first)
     g = g_ref[...]
-    df = (vec[9:10, :] * g).astype(bf16)
-    df_out[...] = df
+    df = df_ref[...]
     small[8:9, :] = jnp.sum(df.astype(f32), axis=0, keepdims=True)
     small[9:10, :] = jnp.sum(g * f_ref[...], axis=0, keepdims=True)
     small[0:4, :] = jnp.zeros((4, D), f32)
-    small[10:16, :] = jnp.zeros((6, D), f32)
+    small[14:16, :] = jnp.zeros((2, D), f32)
     wait(second)
     total = None
     for t in range(8):
@@ -397,7 +396,7 @@
         du = dot(df, w2[t].reshape(512, D), NT)
         dh = (gp_ref[:, cols].astype(f32) * du).astype(bf16)
         dh_out[:, cols] = dh
-        gbias[0:1, cols] = jnp.sum(dh.astype(f32), axis=0, keepdims=True)
+        small[10 + y : 11 + y, off : off + 512] = jnp.sum(dh.astype(f32), axis=0, keepdims=True)
         if t == 0:
             wait(first)
         part = dot(dh, w1[y, :, :, :, off : off + 512].reshape(D, 512), NT)
@@ -412,14 +411,14 @@
     small[4:5, :] = jnp.sum(do.astype(f32), axis=0, keepdims=True)
 
 
-def feed_backward(g, f, gp, x1, o, vec, columns, rows):
+def feed_backward(g, df, f, gp, x1, o, vec, columns, rows):
     flat = [columns[k][dx][dz] for k in range(CS) for dx in range(XS) for dz in range(ZS)]
     flat += [rows[k][n] for k in range(CS) for n in range(YS)]
     return call(
         feed_backward_kernel,
-        [((T, D), bf16), ((T, FF), bf16), ((T, D), f32), ((T, D), bf16), ((16, D), f32), ((1, FF), f32)],
-        [g, f, gp, x1, o, vec] + flat,
-        [VM] * 6 + [ANY] * 24,
+        [((T, FF), bf16), ((T, D), f32), ((T, D), bf16), ((16, D), f32)],
+        [g, df, f, gp, x1, o, vec] + flat,
+        [VM] * 7 + [ANY] * 24,
         scratch=FEED_SCRATCH,
         flops=4 * T * D * FF,
         moved=26 * 2**20,
@@ -427,7 +426,7 @@
     )
 
 
-def attention_backward_kernel(do_ref, dx1_ref, x_ref, p_ref, soft_ref, vec, *refs):
+def attention_backward_kernel(do_ref, dx1_ref, x_ref, p_ref, soft_ref, small_ref, vec, *refs):
     pieces, refs = refs[:16], refs[16:]
     dp_out, dx_out, small, w_qkv, w_proj, sems, dm_ref = refs
     first, second = attention_weights(pieces, w_qkv, w_proj, sems)
@@ -455,7 +454,8 @@
     lax.fori_loop(0, 16, unit, 0, unroll=4)
     small[2:3, :] = jnp.sum(dp_out[:, 0:1024].astype(f32), axis=0, keepdims=True)
     small[3:4, :] = jnp.sum(dp_out[:, 2048:3072].astype(f32), axis=0, keepdims=True)
-    small[4:16, :] = jnp.zeros((12, D), f32)
+    small[4:16, :] = small_ref[4:16, :]
+    dp_out[:, 3072:4096] = do_ref[...]
     wait(first)
     total = None
     for j in range(6):
@@ -464,16 +464,16 @@
         total = part if total is None else total + part
     hat, scale = stats(x_ref[...].astype(f32))
     d_norm, small[0:1, :], small[1:2, :] = norm_back(total, vec[0:1, :], hat, scale)
-    dx_out[...] = dx1_ref[...] + d_norm
-
-
-def attention_backward(do, dx1, x, p, soft, vec, columns):
+    dx_out[...] = (dx1_ref[...] + d_norm).astype(dx_out.dtype)
+
+
+def attention_backward(do, dx1, x, p, soft, small, vec, columns, kind):
     flat = [columns[k][dx][dz] for k in range(CS) for dx in range(XS) for dz in range(ZS)]
     return call(
         attention_backward_kernel,
-        [((T, 3072), bf16), ((T, D), f32), ((16, D), f32)],
-        [do, dx1, x, p, soft, vec] + flat,
-        [VM] * 6 + [ANY] * 16,
+        [((T, 4096), bf16), ((T, D), kind), ((16, D), f32)],
+        [do, dx1, x, p, soft, small, vec] + flat,
+        [VM] * 7 + [ANY] * 16,
         scratch=list(ATTENTION_SCRATCH) + [pltpu.VMEM((T, D), bf16)],
         flops=2 * T * D * 4 * D,
         moved=18 * 2**20,
@@ -489,13 +489,16 @@
     eye = jnp.where(eye_r == lax.broadcasted_iota(jnp.int32, (256, 256), 1), 1.0, 0.0).astype(bf16)
     dx, dz, inner = row >> 7, (row >> 6) & 1, row & 63
     base = (((x + dx) & 3) << 8) + (((z + dz) & 1) << 7) + inner
+    place_base = (dx << 8) + (dz << 7) + inner
     for k, out in enumerate((mine, theirs)):
         ck = near(c, k, CS)
         chosen = jnp.where(col == base + ck * 64, 1.0, 0.0).astype(bf16)
-        for n, ref in enumerate((a_ref, m_ref, c_ref)):
+        for n, ref in enumerate((a_ref, m_ref)):
             out[n * 512 : n * 512 + 512, :] = dot(chosen, ref[...], NT).astype(bf16)
+        chosen = jnp.where(col == place_base + ck * 64, 1.0, 0.0).astype(bf16)
+        out[1024:1536, :] = dot(chosen, c_ref[...], NT).astype(bf16)
         for j in range(8):
-            s = near(x, j // 2, XS) * 4 + near(z, j % 2, ZS) * 2 + ck
+            s = 2 * j + ck
             block = u_ref[:, pl.ds(pl.multiple_of(s * 256, 256), 256)]
             out[1536 + j * 256 : 1792 + j * 256, :] = dot(eye, block, NT).astype(bf16)
 
@@ -512,108 +515,141 @@
     )
 
 
-def feed_grads_kernel(mine, theirs, dh, dh2, df, df2, *refs):
-    outs, acts, dh_all, df_all, rows, sems, out_sems = refs[:4], *refs[4:]
+def kinds(base, c, size):
+    step = 1 - 2 * c
+    return [near(base + 4, d, size) for d in (2, -step, step, 0)]
+
+
+def fc2_grads_kernel(mine, theirs, df, df2, *refs):
+    outs, acts, df_all, rows, sems, out_sems = refs[:4], *refs[4:]
     _, _, c, y = place()
-    step = 1 - 2 * c
     copies = [
-        pltpu.make_async_copy(mine.at[1024:3584], acts.at[:, 0:256], sems.at[0]),
-        pltpu.make_async_copy(theirs.at[1024:3584], acts.at[:, 256:512], sems.at[1]),
+        pltpu.make_async_copy(mine.at[1536:3584], acts.at[:, 0:256], sems.at[0]),
+        pltpu.make_async_copy(theirs.at[1536:3584], acts.at[:, 256:512], sems.at[1]),
         pltpu.make_async_copy(df, df_all.at[0:256], sems.at[2]),
         pltpu.make_async_copy(df2, df_all.at[256:512], sems.at[3]),
-        pltpu.make_async_copy(dh, dh_all.at[0:256], sems.at[4]),
-        pltpu.make_async_copy(dh2, dh_all.at[256:512], sems.at[5]),
     ]
     start(copies)
-    wait(copies[:4])
-    kinds = [near(y + 4, dy, YS) for dy in (2, -step, step, 0)]
+    wait(copies)
     for j in range(8):
-        grad = dot(acts[512 + j * 256 : 768 + j * 256, :], df_all[...]).astype(bf16)
-        rows[:, j, 64:128] = grad.reshape(YS, 64, 1024)
-    wait(copies[4:])
+        grad = dot(acts[j * 256 : j * 256 + 256, :], df_all[...]).astype(bf16)
+        rows[:, j] = grad.reshape(YS, 64, 1024)
+    sends = [pltpu.make_async_copy(rows.at[yk], outs[n], out_sems.at[n]) for n, yk in enumerate(kinds(y, c, YS))]
+    start(sends)
+    wait(sends)
+
+
+def fc2_grads(mine, theirs, df, df2):
+    return call(
+        fc2_grads_kernel,
+        [((8, 64, 1024), bf16)] * 4,
+        [mine, theirs, df, df2],
+        [ANY] * 4,
+        scratch=[
+            pltpu.VMEM((2048, 512), bf16),
+            pltpu.VMEM((512, D), bf16),
+            pltpu.VMEM((4, 8, 64, 1024), bf16),
+            pltpu.SemaphoreType.DMA((4,)),
+            pltpu.SemaphoreType.DMA((4,)),
+        ],
+        out_kinds=[ANY] * 4,
+        flops=4 * T * D * FF,
+        moved=12 * 2**20,
+        name="fc2_grads",
+    )
+
+
+def fc1_grads_kernel(mine, theirs, dh, dh2, *refs):
+    outs, acts, dh_all, rows, sems, out_sems = refs[:4], *refs[4:]
+    _, _, c, y = place()
+    copies = [
+        pltpu.make_async_copy(mine.at[1024:1536], acts.at[:, 0:256], sems.at[0]),
+        pltpu.make_async_copy(theirs.at[1024:1536], acts.at[:, 256:512], sems.at[1]),
+        pltpu.make_async_copy(dh, dh_all.at[0:256], sems.at[2]),
+        pltpu.make_async_copy(dh2, dh_all.at[256:512], sems.at[3]),
+    ]
+    start(copies)
+    wait(copies)
     sends = []
-    for n, yk in enumerate(kinds):
+    for n, yk in enumerate(kinds(y, c, YS)):
         cols = pl.ds(pl.multiple_of(yk * 1024, 1024), 1024)
         for half in range(2):
             grad = dot(acts[half * 256 : half * 256 + 256, :], dh_all[:, cols]).astype(bf16)
-            rows[yk, 4 * half : 4 * half + 4, 0:64] = grad.reshape(4, 64, 1024)
-        sends.append(pltpu.make_async_copy(rows.at[yk], outs[n], out_sems.at[n]))
+            rows[n, 4 * half : 4 * half + 4] = grad.reshape(4, 64, 1024)
+        sends.append(pltpu.make_async_copy(rows.at[n], outs[n], out_sems.at[n]))
         sends[-1].start()
     wait(sends)
 
 
-def feed_grads(mine, theirs, dh, dh2, df, df2):
-    return call(
-        feed_grads_kernel,
-        [((8, 128, 1024), bf16)] * 4,
-        [mine, theirs, dh, dh2, df, df2],
-        [ANY] * 6,
+def fc1_grads(mine, theirs, dh, dh2):
+    return call(
+        fc1_grads_kernel,
+        [((8, 64, 1024), bf16)] * 4,
+        [mine, theirs, dh, dh2],
+        [ANY] * 4,
         scratch=[
-            pltpu.VMEM((2560, 512), bf16),
+            pltpu.VMEM((512, 512), bf16),
             pltpu.VMEM((512, FF), bf16),
-            pltpu.VMEM((512, D), bf16),
-            pltpu.VMEM((4, 8, 128, 1024), bf16),
-            pltpu.SemaphoreType.DMA((6,)),
+            pltpu.VMEM((4, 8, 64, 1024), bf16),
+            pltpu.SemaphoreType.DMA((4,)),
             pltpu.SemaphoreType.DMA((4,)),
         ],
         out_kinds=[ANY] * 4,
-        flops=8 * T * D * FF,
-        moved=24 * 2**20,
-        name="feed_grads",
-    )
-
-
-def attention_grads_kernel(mine, theirs, dp, dp2, do, do2, s1, s2, s3, s4, b1, b2, *refs):
-    outs, acts, dp_all, do_all, held, sems, out_sems = refs[:4], *refs[4:]
+        flops=4 * T * D * FF,
+        moved=14 * 2**20,
+        name="fc1_grads",
+    )
+
+
+def attention_grads_kernel(mine, theirs, dp, dp2, small, small2, *refs):
+    outs, acts, dp_all, total, held, sems, out_sems = refs[:4], *refs[4:]
     x, z, c, _ = place()
     copies = [
         pltpu.make_async_copy(mine.at[0:1024], acts.at[:, 0:256], sems.at[0]),
         pltpu.make_async_copy(theirs.at[0:1024], acts.at[:, 256:512], sems.at[1]),
-        pltpu.make_async_copy(do, do_all.at[0:256], sems.at[2]),
-        pltpu.make_async_copy(do2, do_all.at[256:512], sems.at[3]),
-        pltpu.make_async_copy(dp, dp_all.at[0:256], sems.at[4]),
-        pltpu.make_async_copy(dp2, dp_all.at[256:512], sems.at[5]),
+        pltpu.make_async_copy(dp, dp_all.at[0:256], sems.at[2]),
+        pltpu.make_async_copy(dp2, dp_all.at[256:512], sems.at[3]),
     ]
     start(copies)
-    vec = (s1[...] + s2[...] + s3[...] + s4[...]).astype(bf16)
+    total[...] = small[...] + small2[...]
+    vec = total[...].astype(bf16)
     row = lax.broadcasted_iota(jnp.int32, (D, 128), 0)
     col = lax.broadcasted_iota(jnp.int32, (D, 128), 1)
+    line = lax.broadcasted_iota(jnp.int32, (16, 128), 0)
     for j in range(8):
-        s = near(x, j // 2, XS) * 4 + near(z, j % 2, ZS) * 2 + c
-        chosen = jnp.where((row == col + s * 64) & (col < 64), 1.0, 0.0).astype(bf16)
+        x_there = near(x, j // 2, XS)
+        inner = near(z, j % 2, ZS) * 2 + c
+        chosen = jnp.where((row == col + x_there * 256 + inner * 64) & (col < 64), 1.0, 0.0).astype(bf16)
         held[j, :, 4096:4224] = jnp.zeros((64, 128), bf16)
         held[j, 0:16, 4096:4224] = dot(vec, chosen).astype(bf16)
-        a = b1[0:1, pl.ds(pl.multiple_of(s * 256, 256), 128)] + b2[0:1, pl.ds(pl.multiple_of(s * 256, 256), 128)]
-        b = b1[0:1, pl.ds(pl.multiple_of(s * 256 + 128, 128), 128)] + b2[0:1, pl.ds(pl.multiple_of(s * 256 + 128, 128), 128)]
-        line = lax.broadcasted_iota(jnp.int32, (16, 128), 0)
+        there = total[pl.ds(10 + x_there, 1), pl.ds(pl.multiple_of(inner * 256, 256), 256)]
+        a, b = there[:, 0:128], there[:, 128:256]
         held[j, 16:32, 4096:4224] = jnp.where(line == 0, a, jnp.where(line == 1, b, 0.0)).astype(bf16)
-    wait(copies[:4])
-    for n in range(2):
-        grad = dot(acts[512:1024, :], do_all[:, n * 512 : n * 512 + 512]).astype(bf16)
-        held[:, :, 3072 + n * 512 : 3584 + n * 512] = grad.reshape(8, 64, 512)
-    wait(copies[4:])
-    for n in range(6):
-        grad = dot(acts[0:512, :], dp_all[:, n * 512 : n * 512 + 512]).astype(bf16)
+    wait(copies)
+    for n in range(8):
+        source = acts[0:512, :] if n < 6 else acts[512:1024, :]
+        grad = dot(source, dp_all[:, n * 512 : n * 512 + 512]).astype(bf16)
         held[:, :, n * 512 : n * 512 + 512] = grad.reshape(8, 64, 512)
-    step = 1 - 2 * c
-    kinds = [near(jnp.int32(4), dx, XS) for dx in (2, -step, step, 0)]
-    sends = [pltpu.make_async_copy(held.at[pl.ds(2 * dx, 2)], outs[n], out_sems.at[n]) for n, dx in enumerate(kinds)]
+    sends = [
+        pltpu.make_async_copy(held.at[pl.ds(2 * dx, 2)], outs[n], out_sems.at[n])
+        for n, dx in enumerate(kinds(jnp.int32(0), c, XS))
+    ]
     start(sends)
     wait(sends)
 
 
-def attention_grads(mine, theirs, dp, dp2, do, do2, smalls, biases):
+def attention_grads(mine, theirs, dp, dp2, small, small2):
     return call(
         attention_grads_kernel,
         [((2, 64, QP), bf16)] * 4,
-        [mine, theirs, dp, dp2, do, do2] + smalls + biases,
-        [ANY] * 6 + [VM] * 6,
+        [mine, theirs, dp, dp2, small, small2],
+        [ANY] * 4 + [VM] * 2,
         scratch=[
             pltpu.VMEM((1024, 512), bf16),
-            pltpu.VMEM((512, 3072), bf16),
-            pltpu.VMEM((512, D), bf16),
+            pltpu.VMEM((512, 4096), bf16),
+            pltpu.VMEM((16, D), f32),
             pltpu.VMEM((8, 64, QP), bf16),
-            pltpu.SemaphoreType.DMA((6,)),
+            pltpu.SemaphoreType.DMA((4,)),
             pltpu.SemaphoreType.DMA((4,)),
         ],
         out_kinds=[ANY] * 4,
@@ -623,26 +659,28 @@
     )
 
 
-def sum_kernel(count, *refs):
+def sum_kernel(count, axis, *refs):
     total = refs[0][...].astype(f32)
     for ref in refs[1:count]:
         total = total + ref[...].astype(f32)
     outs = refs[count:]
-    if len(outs) == 1:
-        outs[0][...] = total.astype(bf16)
-    else:
+    if axis == "add":
+        outs[0][...] = jnp.sum(total, axis=0).astype(bf16)
+    elif axis == "split":
         for n, out in enumerate(outs):
             out[...] = total[n].astype(bf16)
-
-
-def summed(parts, split=False):
+    else:
+        outs[0][...] = total.astype(bf16)
+
+
+def summed(parts, axis=None):
     shape = parts[0].shape
-    outs = [(shape[1:], bf16)] * shape[0] if split else [(shape, bf16)]
+    outs = [(shape[1:], bf16)] * shape[0] if axis == "split" else [(shape[1:] if axis else shape, bf16)]
     size = 1
     for n in shape:
         size *= n
     out = call(
-        lambda *refs: sum_kernel(len(parts), *refs),
+        lambda *refs: sum_kernel(len(parts), axis, *refs),
         outs,
         parts,
         [VM] * len(parts),
@@ -650,7 +688,7 @@
         moved=2 * size * (len(parts) + 1),
         name="summed",
     )
-    return out if split else out[0]
+    return out if axis == "split" else out[0]
 
 
 def scattered(parts, axis):
@@ -662,58 +700,50 @@
 
 
 def scatter_columns(parts):
-    same, other = summed(scattered(parts, "x"), split=True)
+    same, other = summed(scattered(parts, "x"), "split")
     return summed([same, from_shard(other, dz=1)])
 
 
 def scatter_rows(parts):
-    places = summed(scattered(parts, "y"), split=True)
-    got = [
-        from_shard(places[2 * dx + dz], dx=XS - dx, dz=dz)
-        for dx in range(XS)
-        for dz in range(ZS)
-        if (dx, dz) != (0, 0)
-    ]
-    return summed([places[0]] + got)
-
-
-def own_quarter(part, y):
-    quarters = part.reshape(YS, 16, -1)
-    at = lambda dy: lax.dynamic_index_in_dim(quarters, lax.rem(y + dy, YS), 0, keepdims=False)
-    return summed([at(0)] + [from_replica(at(dy), YS - dy) for dy in range(1, YS)])
+    groups = [[shard_of(x, z, c) for x in range(XS) for z in range(ZS)] for c in range(CS)]
+    places = summed(scattered(parts, "y"))
+    got = lax.all_to_all(places, "shard", split_axis=0, concat_axis=0, axis_index_groups=groups, tiled=True)
+    return summed([got], "add")
 
 
 def results_kernel(*refs):
-    rows, columns = refs[0:4], refs[4:8]
-    g_qkv, g_proj, g_fc1, g_fc2, g_vec, g_bias, rows_all, cols_all, sems = refs[8:]
+    fc1, fc2, columns = refs[0:4], refs[4:8], refs[8:12]
+    g_qkv, g_proj, g_fc1, g_fc2, g_vec, g_bias, fc1_all, fc2_all, cols_all, sems = refs[12:]
     _, _, _, y = place()
     copies = []
     for dy in range(YS):
         yk = near(y, dy, YS)
-        copies.append(pltpu.make_async_copy(rows[dy], rows_all.at[yk], sems.at[0, dy]))
-        copies.append(pltpu.make_async_copy(columns[dy], cols_all.at[yk], sems.at[1, dy]))
+        copies.append(pltpu.make_async_copy(fc1[dy], fc1_all.at[yk], sems.at[0, dy]))
+        copies.append(pltpu.make_async_copy(fc2[dy], fc2_all.at[yk], sems.at[1, dy]))
+        copies.append(pltpu.make_async_copy(columns[dy], cols_all.at[yk], sems.at[2, dy]))
     start(copies)
     wait(copies)
     for k in range(YS):
-        g_fc1[:, k * 1024 : k * 1024 + 1024] = rows_all[k, 0:64].astype(f32)
-        g_fc2[k * 64 : k * 64 + 64, :] = rows_all[k, 64:128].astype(f32)
-        line = slice(k * 16, k * 16 + 16)
-        g_qkv[line, :] = cols_all[k, :, 0:3072].astype(f32)
-        g_proj[line, :] = cols_all[k, :, 3072:4096].astype(f32)
-    g_vec[...] = cols_all[0, :, 4096:4224].astype(f32)
-    g_bias[...] = cols_all[1, :, 4096:4224].astype(f32)
-
-
-def results(rows, columns):
+        g_fc1[:, k * 1024 : k * 1024 + 1024] = fc1_all[k].astype(f32)
+        g_fc2[k * 64 : k * 64 + 64, :] = fc2_all[k].astype(f32)
+    total = lambda rows, low, high: sum(cols_all[k, rows, low:high].astype(f32) for k in range(YS))
+    g_qkv[...] = total(slice(0, 64), 0, 3072)
+    g_proj[...] = total(slice(0, 64), 3072, 4096)
+    g_vec[...] = total(slice(0, 16), 4096, 4224)
+    g_bias[...] = total(slice(16, 32), 4096, 4224)
+
+
+def results(fc1, fc2, columns):
     return call(
         results_kernel,
         [((64, 3072), f32), ((64, 1024), f32), ((64, FF), f32), ((256, D), f32), ((16, 128), f32), ((16, 128), f32)],
-        list(rows) + list(columns),
-        [ANY] * 8,
+        list(fc1) + list(fc2) + list(columns),
+        [ANY] * 12,
         scratch=[
-            pltpu.VMEM((4, 128, 1024), bf16),
-            pltpu.VMEM((4, 16, QP), bf16),
-            pltpu.SemaphoreType.DMA((2, 4)),
+            pltpu.VMEM((4, 64, 1024), bf16),
+            pltpu.VMEM((4, 64, 1024), bf16),
+            pltpu.VMEM((4, 64, QP), bf16),
+            pltpu.SemaphoreType.DMA((3, 4)),
         ],
         moved=10 * 2**20,
         name="results",
@@ -761,23 +791,30 @@
     a, p, soft, m, o, x1, c = attention_forward(True, inputs, vec, columns)
     u, gp, f, output = feed_forward(True, x1, c, vec, bias, columns, rows)
 
+    twin = lambda v: from_shard(v, dc=1)
+    around = lambda v: [v] + [from_replica(v, dy) for dy in range(1, YS)]
+    second_scale = vec[9:10, :]
     cotangent = (source.astype(f32) * present[:, None, None]).reshape(T, D)
-    _, _, dx1, do, _, _ = feed_backward(cotangent, f, gp, x1, o, vec, columns, rows)
-    _, dx, _ = attention_backward(do, dx1, inputs, p, soft, vec, columns)
-    received_grad = passed_along(dx.astype(bf16), -1)
+    df = (second_scale * cotangent).astype(bf16)
+    _, dx1, do, small = feed_backward(cotangent, df, f, gp, x1, o, vec, columns, rows)
+    _, dx, _ = attention_backward(do, dx1, inputs, p, soft, small, vec, columns, bf16)
+    received_grad = passed_along(dx, -1)
     mine, theirs = picked(a, m, c, u)
-    theirs = from_shard(theirs, dc=1)
+    received_grad, mine, theirs = lax.optimization_barrier((received_grad, mine, twin(theirs)))
+
     upstream = jnp.where(section == 1, cotangent, received_grad.astype(f32))
-    df, dh, dx1, do, small_a, gbias = feed_backward(upstream, f, gp, x1, o, vec, columns, rows)
-    dp, dx, small_b = attention_backward(do, dx1, inputs, p, soft, vec, columns)
-    twin = lambda v: from_shard(v, dc=1)
-    row = scatter_rows(feed_grads(mine, theirs, dh, twin(dh), df, twin(df)))
-    column_parts = attention_grads(
-        mine, theirs, dp, twin(dp), do, twin(do), [small_a, twin(small_a), small_b, twin(small_b)], [gbias, twin(gbias)]
-    )
-    column = own_quarter(scatter_columns(column_parts), y)
-    around = lambda v: [v] + [from_replica(v, dy) for dy in range(1, YS)]
-    g_qkv, g_proj, g_fc1, g_fc2, g_vec, g_bias = results(around(row), around(column))
+    df = (second_scale * upstream).astype(bf16)
+    fc2_parts = fc2_grads(mine, theirs, df, twin(df))
+    upstream, df, fc2_parts = lax.optimization_barrier((upstream, df, fc2_parts))
+    fc2 = scatter_rows(fc2_parts)
+    dh, dx1, do, small = feed_backward(upstream, df, f, gp, x1, o, vec, columns, rows)
+    dp, dx, small = attention_backward(do, dx1, inputs, p, soft, small, vec, columns, f32)
+    dh, dh2, dp, small = lax.optimization_barrier((dh, twin(dh), dp, small))
+    fc1_parts = fc1_grads(mine, theirs, dh, dh2)
+    dp, dp2, small, small2, fc1_parts = lax.optimization_barrier((dp, twin(dp), small, twin(small), fc1_parts))
+    fc1 = scatter_rows(fc1_parts)
+    column = scatter_columns(attention_grads(mine, theirs, dp, dp2, small, small2))
+    g_qkv, g_proj, g_fc1, g_fc2, g_vec, g_bias = results(around(fc1), around(fc2), around(column))
     edge_values = jnp.where(section == 0, dx, output).reshape(1, 2, 1, 128, D)
     return (
         edge_values,

time: 458 us -> 486 us (1.061)
  waiting for transfers between devices: 186 us -> 212 us
  Pallas kernels: 167 us -> 175 us
    ppermute x9, waiting for transfers between devices: 12.2 us -> 27 us  [from_replica(): lax.ppermute(value, 'replica', [((y + dy) % YS, y) for y in range(YS)])]
    all_to_all x0 -> x2, waiting for transfers between devices: none -> 8.03 us  [scatter_rows(): lax.all_to_all(places, 'shard', split_axis=0, concat_axis=0, axis_index_g...]
    pallas_call x22 -> x25, Pallas kernels: 167 us -> 175 us  [call(): pl.pallas_call(kernel, out_shape=[jax.ShapeDtypeStruct(s, d) for s, d in...]
    all_to_all x0 -> x2, starting transfers between devices: none -> 7.12 us  [scatter_rows(): lax.all_to_all(places, 'shard', split_axis=0, concat_axis=0, axis_index_g...]
    ppermute x46 -> x38, waiting for transfers between devices: 86.5 us -> 93 us  [from_shard(): return lax.ppermute(value, 'shard', pairs)]
    ppermute x9 -> x12, waiting for transfers between devices: 61.8 us -> 56.1 us  [onward(): return lax.ppermute(value, ('shard', 'replica'), pairs)]
    ppermute x46 -> x38, starting transfers between devices: 40.6 us -> 35.1 us  [from_shard(): return lax.ppermute(value, 'shard', pairs)]
    unnamed x123 -> x105, local copies, waits for them, and re-layouts: 13.3 us -> 11.5 us
  transfers between devices with their start and end apart: 66 -> 63, of which waited for: 29 -> 27; matrix products, arithmetic and copies ran while one was open for 1% -> 1% of each run, Pallas kernels for 16% -> 20%
where the time goes in v4:
time: 486 us; the launch traced here: 478 us
  waiting for transfers between devices  212 us (44%)
  Pallas kernels  175 us (36%)
  starting transfers between devices  69.6 us (14%)
  local copies, waits for them, and re-layouts  14.2 us (3%)
  other arithmetic  5.96 us (1%)
    pallas_call x25, Pallas kernels, call(): pl.pallas_call(kernel, out_shape=[jax.ShapeDtypeStruct(s, d) for s, d in...  175 us
    ppermute x38, waiting for transfers between devices, from_shard(): return lax.ppermute(value, 'shard', pairs)  93 us
    ppermute x12, waiting for transfers between devices, onward(): return lax.ppermute(value, ('shard', 'replica'), pairs)  56.1 us
    ppermute x38, starting transfers between devices, from_shard(): return lax.ppermute(value, 'shard', pairs)  35.1 us
    ppermute x2, waiting for transfers between devices, passed_along(): return lax.ppermute(value, 'section', [(0, 1)] if steps == 1 else [(1, 0)])  27.8 us
    ppermute x9, waiting for transfers between devices, from_replica(): lax.ppermute(value, 'replica', [((y + dy) % YS, y) for y in range(YS)])  27 us
    unnamed x105, local copies, waits for them, and re-layouts  11.5 us
    ppermute x9, starting transfers between devices, from_replica(): lax.ppermute(value, 'replica', [((y + dy) % YS, y) for y in range(YS)])  10.6 us
  transfers between devices with their start and end apart: 63, of which 27 were waited for; matrix products, arithmetic and copies ran while one was open for 1% of the time, Pallas kernels for 20%

profile of v4, /device:TPU:0, one launch (start us, length us, event | category | flops | bytes accessed | tf_op | source)
XLA Modules:
  0.0 478.0 jit_solution(8521531615091472611)
XLA Ops:
  21.3 6.5 %collective-permute-done.4.refs_5_ = bf16[112,1024]{1,0:T(8,128)(2,1)S(1)} collective-permute-done((bf16[112,1024]{1,0:T(8,128)(2,1)}, bf16[112,1024]{1,0:T(8,128)(2,1)S(1)}, u32[]{:S(2)}, u32[]{:S(2)}) %collective-permute-start.4) | collective-permute-done | bytes 229408 | tf_op jit(solution)/shard_map/ppermute | solution.py:34
  45.2 18.3 %collective-permute-done.22.refs_21_.refs_17_ = bf16[8,112,1024]{2,1,0:T(8,128)(2,1)} collective-permute-done((bf16[8,112,1024]{2,1,0:T(8,128)(2,1)}, bf16[8,112,1024]{2,1,0:T(8,128)(2,1)}, u32[]{:S(2)}, u32[]{:S(2)}) %collective-permute-start.22) | collective-permute-done | bytes 1835040 | tf_op jit(solution)/shard_map/ppermute | solution.py:50
  67.0 14.2 %collective-permute-done.7.refs_1_.refs_3_.refs_5_ = bf16[64,5248]{1,0:T(8,128)(2,1)S(1)} collective-permute-done((bf16[64,5248]{1,0:T(8,128)(2,1)S(1)}, bf16[64,5248]{1,0:T(8,128)(2,1)S(1)}, u32[]{:S(2)}, u32[]{:S(2)}) %collective-permute-start.7) | collective-permute-done | bytes 671776 | tf_op jit(solution)/shard_map/ppermute | solution.py:34
  83.9 15.2 %collective-permute-done.10.refs_4_.refs_6_.refs_8_ = bf16[64,5248]{1,0:T(8,128)(2,1)S(1)} collective-permute-done((bf16[64,5248]{1,0:T(8,128)(2,1)S(1)}, bf16[64,5248]{1,0:T(8,128)(2,1)S(1)}, u32[]{:S(2)}, u32[]{:S(2)}) %collective-permute-start.10) | collective-permute-done | bytes 671776 | tf_op jit(solution)/shard_map/ppermute | solution.py:34
  102.9 13.3 %collective-permute-done.9.refs_3_.refs_5_.refs_7_ = bf16[64,5248]{1,0:T(8,128)(2,1)S(1)} collective-permute-done((bf16[64,5248]{1,0:T(8,128)(2,1)S(1)}, bf16[64,5248]{1,0:T(8,128)(2,1)S(1)}, u32[]{:S(2)}, u32[]{:S(2)}) %collective-permute-start.9) | collective-permute-done | bytes 671776 | tf_op jit(solution)/shard_map/ppermute | solution.py:34
  118.4 16.5 %collective-permute-done.12.refs_5_.refs_7_.refs_9_ = bf16[64,5248]{1,0:T(8,128)(2,1)S(1)} collective-permute-done((bf16[64,5248]{1,0:T(8,128)(2,1)S(1)}, bf16[64,5248]{1,0:T(8,128)(2,1)S(1)}, u32[]{:S(2)}, u32[]{:S(2)}) %collective-permute-start.12) | collective-permute-done | bytes 671776 | tf_op jit(solution)/shard_map/ppermute | solution.py:34
  139.4 11.3 %attention_forward.2 = (f32[256,1024]{1,0:T(8,128)}, bf16[256,1024]{1,0:T(8,128)(2,1)}) custom-call(bf16[256,1024]{1,0:T(8,128)(2,1)} %bitcast.27, f32[16,1024]{1,0:T(8,128)} %get-tuple-element.83.refs_1_.refs_2_.vec, bf16[64,5248]{1,0:T(8,128)(2,1)} %get-tuple-element.82.refs_0_.refs_2_.refs_4_, bf16[64,5248]{1,0:T(8,128)(2,1)} %copy-done.4, ...), custom_call_target="tpu_custom_call" | custom-call | flops 2147483648 | bytes 14680064 | tf_op jit(solution)/shard_map/attention_forward/pallas_call | solution.py:70
  150.8 13.4 %feed_forward.2 = bf16[256,1024]{1,0:T(8,128)(2,1)} custom-call(f32[256,1024]{1,0:T(8,128)} %get-tuple-element.84.refs_0_, bf16[256,1024]{1,0:T(8,128)(2,1)} %get-tuple-element.85.refs_1_, f32[16,1024]{1,0:T(8,128)} %get-tuple-element.83.refs_1_.refs_2_.vec, f32[1,4096]{1,0:T(1,128)} %get-tuple-element.86.refs_3_, ...), custom_call_target="tpu_custom_call" | custom-call | flops 4294967296 | bytes 25165824 | tf_op jit(solution)/shard_map/feed_forward/pallas_call | solution.py:70
  170.4 11.2 %collective-permute-done.29 = bf16[256,1024]{1,0:T(8,128)(2,1)S(1)} collective-permute-done((bf16[256,1024]{1,0:T(8,128)(2,1)}, bf16[256,1024]{1,0:T(8,128)(2,1)S(1)}, u32[]{:S(2)}, u32[]{:S(2)}) %collective-permute-start.29) | collective-permute-done | bytes 524320 | tf_op jit(solution)/shard_map/ppermute | solution.py:54
  182.4 12.4 %attention_forward.3 = (bf16[256,1024]{1,0:T(8,128)(2,1)}, bf16[256,3072]{1,0:T(8,128)(2,1)}, f32[16,256,128]{2,1,0:T(8,128)}, bf16[256,1024]{1,0:T(8,128)(2,1)}...) custom-call(bf16[256,1024]{1,0:T(8,128)(2,1)} %broadcast_select_fusion.1.refs_0_.x_ref, ...), custom_call_target="tpu_custom_call" | custom-call | flops 2147483648 | bytes 14680064 | tf_op jit(solution)/shard_map/attention_forward/pallas_call | solution.py:70
  194.9 15.6 %feed_forward.3 = (bf16[256,4096]{1,0:T(8,128)(2,1)}, bf16[256,4096]{1,0:T(8,128)(2,1)}, f32[256,1024]{1,0:T(8,128)}, f32[256,1024]{1,0:T(8,128)}) custom-call(f32[256,1024]{1,0:T(8,128)} %get-tuple-element.88.refs_0_.x1_ref, bf16[256,1024]{1,0:T(8,128)(2,1)} %get-tuple-element.89.refs_1_.c_ref, f32[16,1024]{1,0:T(8,128)} %get-tuple-element.83.refs_1_.refs_2_.vec, ...), custom_call_target="tpu_custom_call" | custom-call | flops 4294967296 | bytes 25165824 | tf_op jit(solution)/shard_map/feed_forward/pallas_call | solution.py:70
  218.6 16.1 %feed_backward.2 = (bf16[256,4096]{1,0:T(8,128)(2,1)}, f32[256,1024]{1,0:T(8,128)}, bf16[256,1024]{1,0:T(8,128)(2,1)}, f32[16,1024]{1,0:T(8,128)}) custom-call(f32[256,1024]{1,0:T(8,128)} %get-tuple-element.163.g_ref, bf16[256,1024]{1,0:T(8,128)(2,1)} %get-tuple-element.162.df_ref, f32[256,1024]{1,0:T(8,128)} %get-tuple-element.90.f_ref, ...), custom_call_target="tpu_custom_call" | custom-call | flops 4294967296 | bytes 27262976 | tf_op jit(solution)/shard_map/feed_backward/pallas_call | solution.py:70
  234.7 14.3 %attention_backward.2 = (bf16[256,4096]{1,0:T(8,128)(2,1)}, bf16[256,1024]{1,0:T(8,128)(2,1)}, f32[16,1024]{1,0:T(8,128)}) custom-call(bf16[256,1024]{1,0:T(8,128)(2,1)} %get-tuple-element.93.do_ref, f32[256,1024]{1,0:T(8,128)} %get-tuple-element.94.dx1_ref, bf16[256,1024]{1,0:T(8,128)(2,1)} %broadcast_select_fusion.1.refs_0_.x_ref, ...), custom_call_target="tpu_custom_call" | custom-call | flops 2147483648 | bytes 18874368 | tf_op jit(solution)/shard_map/attention_backward/pallas_call | solution.py:70
  250.3 16.6 %collective-permute-done.30 = bf16[256,1024]{1,0:T(8,128)(2,1)S(1)} collective-permute-done((bf16[256,1024]{1,0:T(8,128)(2,1)}, bf16[256,1024]{1,0:T(8,128)(2,1)S(1)}, u32[]{:S(2)}, u32[]{:S(2)}) %collective-permute-start.30) | collective-permute-done | bytes 524320 | tf_op jit(solution)/shard_map/ppermute | solution.py:54
  277.6 16.2 %feed_backward.3 = (bf16[256,4096]{1,0:T(8,128)(2,1)}, f32[256,1024]{1,0:T(8,128)}, bf16[256,1024]{1,0:T(8,128)(2,1)}, f32[16,1024]{1,0:T(8,128)}) custom-call(f32[256,1024]{1,0:T(8,128)} %get-tuple-element.111.g_ref, bf16[256,1024]{1,0:T(8,128)(2,1)} %copy-done.19, f32[256,1024]{1,0:T(8,128)} %get-tuple-element.90.f_ref, ...), custom_call_target="tpu_custom_call" | custom-call | flops 4294967296 | bytes 27262976 | tf_op jit(solution)/shard_map/feed_backward/pallas_call | solution.py:70
  294.0 14.5 %attention_backward.3 = (bf16[256,4096]{1,0:T(8,128)(2,1)}, f32[256,1024]{1,0:T(8,128)}, f32[16,1024]{1,0:T(8,128)}) custom-call(bf16[256,1024]{1,0:T(8,128)(2,1)} %get-tuple-element.113.do_ref, f32[256,1024]{1,0:T(8,128)} %get-tuple-element.114.dx1_ref, bf16[256,1024]{1,0:T(8,128)(2,1)} %broadcast_select_fusion.1.refs_0_.x_ref, ...), custom_call_target="tpu_custom_call" | custom-call | flops 2147483648 | bytes 18874368 | tf_op jit(solution)/shard_map/attention_backward/pallas_call | solution.py:70
  322.0 8.0 %attention_grads.1 = (bf16[2,64,4224]{2,1,0:T(8,128)(2,1)}, bf16[2,64,4224]{2,1,0:T(8,128)(2,1)}, bf16[2,64,4224]{2,1,0:T(8,128)(2,1)}, bf16[2,64,4224]{2,1,0:T(8,128)(2,1)}) custom-call(bf16[3584,256]{1,0:T(8,128)(2,1)} %get-tuple-element.105.mine, bf16[3584,256]{1,0:T(8,128)(2,1)} %copy-done.45, bf16[256,4096]{1,0:T(8,128)(2,1)} %get-tuple-element.137.dp, ...), custom_call_target="tpu_custom_call" | custom-call | flops 4294967296 | bytes 16777216 | tf_op jit(solution)/shard_map/attention_grads/pallas_call | solution.py:70
  338.7 9.3 %collective-permute-done.36.refs_1_ = bf16[8,64,1024]{2,1,0:T(8,128)(2,1)S(1)} collective-permute-done((bf16[8,64,1024]{2,1,0:T(8,128)(2,1)}, bf16[8,64,1024]{2,1,0:T(8,128)(2,1)S(1)}, u32[]{:S(2)}, u32[]{:S(2)}) %collective-permute-start.36) | collective-permute-done | bytes 1048608 | tf_op jit(solution)/shard_map/ppermute | solution.py:50
  351.7 7.5 %collective-permute-done.45.refs_1_ = bf16[8,64,1024]{2,1,0:T(8,128)(2,1)S(1)} collective-permute-done((bf16[8,64,1024]{2,1,0:T(8,128)(2,1)}, bf16[8,64,1024]{2,1,0:T(8,128)(2,1)S(1)}, u32[]{:S(2)}, u32[]{:S(2)}) %collective-permute-start.45) | collective-permute-done | bytes 1048608 | tf_op jit(solution)/shard_map/ppermute | solution.py:50
  359.2 11.3 %collective-permute-done.39 = bf16[8,64,1024]{2,1,0:T(8,128)(2,1)} collective-permute-done((bf16[8,64,1024]{2,1,0:T(8,128)(2,1)}, bf16[8,64,1024]{2,1,0:T(8,128)(2,1)}, u32[]{:S(2)}, u32[]{:S(2)}) %collective-permute-start.39) | collective-permute-done | bytes 1048608 | tf_op jit(solution)/shard_map/ppermute | solution.py:50
  388.5 8.0 %all-to-all-done.1.refs_0_ = bf16[8,64,1024]{2,1,0:T(8,128)(2,1)S(1)} async-done(((bf16[8,64,1024]{2,1,0:T(8,128)(2,1)}), bf16[8,64,1024]{2,1,0:T(8,128)(2,1)S(1)}, u32[]{:S(2)}, u32[]{:S(2)}) %all-to-all-start.1) | async-done | bytes 1048608 | tf_op jit(solution)/shard_map/all_to_all | solution.py:710
  400.1 7.9 %collective-permute-done.53.refs_1_ = bf16[2,64,4224]{2,1,0:T(8,128)(2,1)S(1)} collective-permute-done((bf16[2,64,4224]{2,1,0:T(8,128)(2,1)}, bf16[2,64,4224]{2,1,0:T(8,128)(2,1)S(1)}, u32[]{:S(2)}, u32[]{:S(2)}) %collective-permute-start.53) | collective-permute-done | bytes 1081376 | tf_op jit(solution)/shard_map/ppermute | solution.py:50
  420.1 8.4 %collective-permute-done.57.refs_1_ = bf16[64,4224]{1,0:T(8,128)(2,1)S(1)} collective-permute-done((bf16[64,4224]{1,0:T(8,128)(2,1)}, bf16[64,4224]{1,0:T(8,128)(2,1)S(1)}, u32[]{:S(2)}, u32[]{:S(2)}) %collective-permute-start.57) | collective-permute-done | bytes 540704 | tf_op jit(solution)/shard_map/ppermute | solution.py:34
  439.8 21.8 %collective-permute-done.49.refs_5_ = bf16[64,1024]{1,0:T(8,128)(2,1)S(1)} collective-permute-done((bf16[64,1024]{1,0:T(8,128)(2,1)S(1)}, bf16[64,1024]{1,0:T(8,128)(2,1)S(1)}, u32[]{:S(2)}, u32[]{:S(2)}) %collective-permute-start.49) | collective-permute-done | bytes 131104 | tf_op jit(solution)/shard_map/ppermute | solution.py:38
  (242 shorter events, 168.3 us)
Async XLA Ops:
  38.7 24.8 %collective-permute-start.22 = (bf16[8,112,1024]{2,1,0:T(8,128)(2,1)}, bf16[8,112,1024]{2,1,0:T(8,128)(2,1)}, u32[]{:S(2)}, u32[]{:S(2)}) collective-permute-start(bf16[8,112,1024]{2,1,0:T(8,128)(2,1)} %placed_pieces.1.refs_20_.refs_16_), channel_id=1, source_target_pairs={{0,1},{1,2},{2,3},{3,0},{4,7},{5,4},{6,5},{7,6},{8,9},{9,10},{10,1... | collective-permute-start | bytes 5505032 | tf_op jit(solution)/shard_map/ppermute | solution.py:50
  42.0 23.6 %collective-permute-start.13 = (bf16[64,5248]{1,0:T(8,128)(2,1)S(1)}, bf16[64,5248]{1,0:T(8,128)(2,1)S(1)}, u32[]{:S(2)}, u32[]{:S(2)}) collective-permute-start(bf16[64,5248]{1,0:T(8,128)(2,1)S(1)} %copy-done), channel_id=1, source_target_pairs={{48,0},{52,4},{56,8},{60,12},{0,16},{4,20},{8,24},{12,28},{16,32},... | collective-permute-start | bytes 2015240 | tf_op jit(solution)/shard_map/ppermute | solution.py:34
  42.0 25.0 %collective-permute-start.8 = (bf16[64,5248]{1,0:T(8,128)(2,1)S(1)}, bf16[64,5248]{1,0:T(8,128)(2,1)S(1)}, u32[]{:S(2)}, u32[]{:S(2)}) collective-permute-start(bf16[64,5248]{1,0:T(8,128)(2,1)S(1)} %copy-done), channel_id=1, source_target_pairs={{16,0},{20,4},{24,8},{28,12},{32,16},{36,20},{40,24},{44,28},{48,3... | collective-permute-start | bytes 2015240 | tf_op jit(solution)/shard_map/ppermute | solution.py:34
  45.2 55.9 %collective-permute-start.24 = (bf16[8,112,1024]{2,1,0:T(8,128)(2,1)S(1)}, bf16[8,112,1024]{2,1,0:T(8,128)(2,1)}, u32[]{:S(2)}, u32[]{:S(2)}) collective-permute-start(bf16[8,112,1024]{2,1,0:T(8,128)(2,1)S(1)} %collective-permute-done.23.refs_24_.refs_20_), channel_id=1, source_target_pairs={{0,1},{1,2},{2,3},{3,0},{4,7},{5,4},{6,5},{7,6},{8,9},{9,10},{10,1... | collective-permute-start | bytes 5505032 | tf_op jit(solution)/shard_map/ppermute | solution.py:50
  63.5 39.3 %collective-permute-start.26 = (bf16[8,112,1024]{2,1,0:T(8,128)(2,1)}, bf16[8,112,1024]{2,1,0:T(8,128)(2,1)}, u32[]{:S(2)}, u32[]{:S(2)}) collective-permute-start(bf16[8,112,1024]{2,1,0:T(8,128)(2,1)} %collective-permute-done.22.refs_21_.refs_17_), channel_id=1, source_target_pairs={{0,1},{1,2},{2,3},{3,0},{4,7},{5,4},{6,5},{7,6},{8,9},{9,10},{10,1... | collective-permute-start | bytes 5505032 | tf_op jit(solution)/shard_map/ppermute | solution.py:50
  100.6 50.1 %collective-permute-start.27 = (bf16[8,112,1024]{2,1,0:T(8,128)(2,1)}, bf16[8,112,1024]{2,1,0:T(8,128)(2,1)}, u32[]{:S(2)}, u32[]{:S(2)}) collective-permute-start(bf16[8,112,1024]{2,1,0:T(8,128)(2,1)} %collective-permute-done.22.refs_21_.refs_17_), channel_id=1, source_target_pairs={{4,0},{0,4},{12,8},{8,12},{20,16},{16,20},{28,24},{24,28},{36,32},... | collective-permute-start | bytes 5505032 | tf_op jit(solution)/shard_map/ppermute | solution.py:34
  101.1 49.6 %collective-permute-start.25 = (bf16[8,112,1024]{2,1,0:T(8,128)(2,1)}, bf16[8,112,1024]{2,1,0:T(8,128)(2,1)}, u32[]{:S(2)}, u32[]{:S(2)}) collective-permute-start(bf16[8,112,1024]{2,1,0:T(8,128)(2,1)} %collective-permute-done.24.refs_25_.refs_21_), channel_id=1, source_target_pairs={{4,0},{0,4},{12,8},{8,12},{20,16},{16,20},{28,24},{24,28},{36,32},... | collective-permute-start | bytes 5505032 | tf_op jit(solution)/shard_map/ppermute | solution.py:34
  102.9 47.9 %collective-permute-start.28 = (bf16[8,112,1024]{2,1,0:T(8,128)(2,1)}, bf16[8,112,1024]{2,1,0:T(8,128)(2,1)}, u32[]{:S(2)}, u32[]{:S(2)}) collective-permute-start(bf16[8,112,1024]{2,1,0:T(8,128)(2,1)} %collective-permute-done.26.refs_23_.refs_19_), channel_id=1, source_target_pairs={{4,0},{0,4},{12,8},{8,12},{20,16},{16,20},{28,24},{24,28},{36,32},... | collective-permute-start | bytes 5505032 | tf_op jit(solution)/shard_map/ppermute | solution.py:34
  216.3 50.7 %collective-permute-start.31 = (bf16[3584,256]{1,0:T(8,128)(2,1)}, bf16[3584,256]{1,0:T(8,128)(2,1)S(1)}, u32[]{:S(2)}, u32[]{:S(2)}) collective-permute-start(bf16[3584,256]{1,0:T(8,128)(2,1)} %get-tuple-element.103), channel_id=1, source_target_pairs={{4,0},{0,4},{12,8},{8,12},{20,16},{16,20},{28,24},{24,28},{36,32},... | collective-permute-start | bytes 5505032 | tf_op jit(solution)/shard_map/ppermute | solution.py:34
  314.4 24.2 %collective-permute-start.47 = (bf16[8,64,1024]{2,1,0:T(8,128)(2,1)}, bf16[8,64,1024]{2,1,0:T(8,128)(2,1)}, u32[]{:S(2)}, u32[]{:S(2)}) collective-permute-start(bf16[8,64,1024]{2,1,0:T(8,128)(2,1)} %collective-permute-done.46), channel_id=1, source_target_pairs={{0,1},{1,2},{2,3},{3,0},{4,7},{5,4},{6,5},{7,6},{8,9},{9,10},{10,1... | collective-permute-start | bytes 3145736 | tf_op jit(solution)/shard_map/ppermute | solution.py:50
  335.7 23.5 %collective-permute-start.45 = (bf16[8,64,1024]{2,1,0:T(8,128)(2,1)}, bf16[8,64,1024]{2,1,0:T(8,128)(2,1)S(1)}, u32[]{:S(2)}, u32[]{:S(2)}) collective-permute-start(bf16[8,64,1024]{2,1,0:T(8,128)(2,1)} %summed.12), channel_id=1, source_target_pairs={{0,1},{1,2},{2,3},{3,0},{4,7},{5,4},{6,5},{7,6},{8,9},{9,10},{10,1... | collective-permute-start | bytes 3145736 | tf_op jit(solution)/shard_map/ppermute | solution.py:50
  335.7 34.9 %collective-permute-start.39 = (bf16[8,64,1024]{2,1,0:T(8,128)(2,1)}, bf16[8,64,1024]{2,1,0:T(8,128)(2,1)}, u32[]{:S(2)}, u32[]{:S(2)}) collective-permute-start(bf16[8,64,1024]{2,1,0:T(8,128)(2,1)} %collective-permute-done.38), channel_id=1, source_target_pairs={{0,1},{1,2},{2,3},{3,0},{4,7},{5,4},{6,5},{7,6},{8,9},{9,10},{10,1... | collective-permute-start | bytes 3145736 | tf_op jit(solution)/shard_map/ppermute | solution.py:50
  338.7 31.9 %collective-permute-start.48 = (bf16[8,64,1024]{2,1,0:T(8,128)(2,1)}, bf16[8,64,1024]{2,1,0:T(8,128)(2,1)S(1)}, u32[]{:S(2)}, u32[]{:S(2)}) collective-permute-start(bf16[8,64,1024]{2,1,0:T(8,128)(2,1)} %collective-permute-done.47), channel_id=1, source_target_pairs={{4,0},{0,4},{12,8},{8,12},{20,16},{16,20},{28,24},{24,28},{36,32},... | collective-permute-start | bytes 3145736 | tf_op jit(solution)/shard_map/ppermute | solution.py:34
  348.0 30.4 %collective-permute-start.52 = (bf16[2,64,4224]{2,1,0:T(8,128)(2,1)S(1)}, bf16[2,64,4224]{2,1,0:T(8,128)(2,1)S(1)}, u32[]{:S(2)}, u32[]{:S(2)}) collective-permute-start(bf16[2,64,4224]{2,1,0:T(8,128)(2,1)S(1)} %copy-done.46), channel_id=1, source_target_pairs={{0,16},{1,17},{2,18},{3,19},{4,52},{5,53},{6,54},{7,55},{8,24},{9,... | collective-permute-start | bytes 3244040 | tf_op jit(solution)/shard_map/ppermute | solution.py:50
  348.0 36.1 %collective-permute-start.55 = (bf16[2,64,4224]{2,1,0:T(8,128)(2,1)}, bf16[2,64,4224]{2,1,0:T(8,128)(2,1)}, u32[]{:S(2)}, u32[]{:S(2)}) collective-permute-start(bf16[2,64,4224]{2,1,0:T(8,128)(2,1)} %collective-permute-done.54), channel_id=1, source_target_pairs={{0,16},{1,17},{2,18},{3,19},{4,52},{5,53},{6,54},{7,55},{8,24},{9,... | collective-permute-start | bytes 3244040 | tf_op jit(solution)/shard_map/ppermute | solution.py:50
  359.2 26.1 %collective-permute-start.37 = (bf16[8,64,1024]{2,1,0:T(8,128)(2,1)}, bf16[8,64,1024]{2,1,0:T(8,128)(2,1)}, u32[]{:S(2)}, u32[]{:S(2)}) collective-permute-start(bf16[8,64,1024]{2,1,0:T(8,128)(2,1)} %summed.9), channel_id=1, source_target_pairs={{0,1},{1,2},{2,3},{3,0},{4,7},{5,4},{6,5},{7,6},{8,9},{9,10},{10,1... | collective-permute-start | bytes 3145736 | tf_op jit(solution)/shard_map/ppermute | solution.py:50
  382.2 25.8 %collective-permute-start.53 = (bf16[2,64,4224]{2,1,0:T(8,128)(2,1)}, bf16[2,64,4224]{2,1,0:T(8,128)(2,1)S(1)}, u32[]{:S(2)}, u32[]{:S(2)}) collective-permute-start(bf16[2,64,4224]{2,1,0:T(8,128)(2,1)} %summed.15), channel_id=1, source_target_pairs={{0,16},{1,17},{2,18},{3,19},{4,52},{5,53},{6,54},{7,55},{8,24},{9,... | collective-permute-start | bytes 3244040 | tf_op jit(solution)/shard_map/ppermute | solution.py:50
  384.1 23.9 %collective-permute-start.56 = (bf16[2,64,4224]{2,1,0:T(8,128)(2,1)}, bf16[2,64,4224]{2,1,0:T(8,128)(2,1)}, u32[]{:S(2)}, u32[]{:S(2)}) collective-permute-start(bf16[2,64,4224]{2,1,0:T(8,128)(2,1)} %collective-permute-done.55), channel_id=1, source_target_pairs={{4,0},{0,4},{12,8},{8,12},{20,16},{16,20},{28,24},{24,28},{36,32},... | collective-permute-start | bytes 3244040 | tf_op jit(solution)/shard_map/ppermute | solution.py:34
  396.6 38.1 %all-to-all-start = ((bf16[8,64,1024]{2,1,0:T(8,128)(2,1)}), bf16[8,64,1024]{2,1,0:T(8,128)(2,1)S(1)}, u32[]{:S(2)}, u32[]{:S(2)}) async-start(bf16[8,64,1024]{2,1,0:T(8,128)(2,1)} %summed.10), calls=%async_computation | async-start | bytes 2097152 | tf_op jit(solution)/shard_map/all_to_all | solution.py:710
  431.5 39.4 %collective-permute-start.60 = (bf16[64,4224]{1,0:T(8,128)(2,1)}, bf16[64,4224]{1,0:T(8,128)(2,1)}, u32[]{:S(2)}, u32[]{:S(2)}) collective-permute-start(bf16[64,4224]{1,0:T(8,128)(2,1)} %summed.17.refs_8_), channel_id=1, source_target_pairs={{3,0},{0,1},{1,2},{2,3},{7,4},{4,5},{5,6},{6,7},{11,8},{8,9},{9,10... | collective-permute-start | bytes 1622024 | tf_op jit(solution)/shard_map/ppermute | solution.py:38
  431.5 39.4 %collective-permute-start.59 = (bf16[64,4224]{1,0:T(8,128)(2,1)}, bf16[64,4224]{1,0:T(8,128)(2,1)}, u32[]{:S(2)}, u32[]{:S(2)}) collective-permute-start(bf16[64,4224]{1,0:T(8,128)(2,1)} %summed.17.refs_8_), channel_id=1, source_target_pairs={{2,0},{3,1},{0,2},{1,3},{6,4},{7,5},{4,6},{5,7},{10,8},{11,9},{8,1... | collective-permute-start | bytes 1622024 | tf_op jit(solution)/shard_map/ppermute | solution.py:38
  432.2 38.7 %collective-permute-start.58 = (bf16[64,4224]{1,0:T(8,128)(2,1)}, bf16[64,4224]{1,0:T(8,128)(2,1)}, u32[]{:S(2)}, u32[]{:S(2)}) collective-permute-start(bf16[64,4224]{1,0:T(8,128)(2,1)} %summed.17.refs_8_), channel_id=1, source_target_pairs={{1,0},{2,1},{3,2},{0,3},{5,4},{6,5},{7,6},{4,7},{9,8},{10,9},{11,1... | collective-permute-start | bytes 1622024 | tf_op jit(solution)/shard_map/ppermute | solution.py:38
  437.7 23.9 %collective-permute-start.49 = (bf16[64,1024]{1,0:T(8,128)(2,1)S(1)}, bf16[64,1024]{1,0:T(8,128)(2,1)S(1)}, u32[]{:S(2)}, u32[]{:S(2)}) collective-permute-start(bf16[64,1024]{1,0:T(8,128)(2,1)S(1)} %copy-done.29), channel_id=1, source_target_pairs={{1,0},{2,1},{3,2},{0,3},{5,4},{6,5},{7,6},{4,7},{9,8},{10,9},{11,1... | collective-permute-start | bytes 393224 | tf_op jit(solution)/shard_map/ppermute | solution.py:38
  438.6 23.9 %collective-permute-start.43 = (bf16[64,1024]{1,0:T(8,128)(2,1)}, bf16[64,1024]{1,0:T(8,128)(2,1)S(1)}, u32[]{:S(2)}, u32[]{:S(2)}) collective-permute-start(bf16[64,1024]{1,0:T(8,128)(2,1)} %summed.11.refs_0_), channel_id=1, source_target_pairs={{3,0},{0,1},{1,2},{2,3},{7,4},{4,5},{5,6},{6,7},{11,8},{8,9},{9,10... | collective-permute-start | bytes 393224 | tf_op jit(solution)/shard_map/ppermute | solution.py:38
  (91 other events, 1642.5 us)

commit v5 on v4

v5 whole, which is shorter than its diff:
```python
import jax
import jax.numpy as jnp
from jax import lax
from jax.experimental import pallas as pl
from jax.experimental.pallas import tpu as pltpu
from jax.sharding import PartitionSpec as P

XS, ZS, CS, YS = 4, 2, 2, 4
T = 256
D, FF = 1024, 4096
GROWS = 32
TAILS = 4 - GROWS // 16
UNIT = 4096 + 1024 * TAILS + 128
QP = 4224
LIMIT = 8
epsilon = 1e-06
bf16, f32 = jnp.bfloat16, jnp.float32
ANY = pl.BlockSpec(memory_space=pl.ANY)
HB = pl.BlockSpec(memory_space=pltpu.HBM)
VM = pl.BlockSpec(memory_space=pltpu.VMEM)
SM = pl.BlockSpec(memory_space=pltpu.SMEM)
NT = (((1,), (1,)), ((), ()))
TN = (((0,), (0,)), ((), ()))


def shard_of(x, z, c):
    return (x % XS) * 4 + (z % ZS) * 2 + (c % CS)


def from_shard(value, dx=0, dz=0, dc=0, name="from_shard"):
    pairs = [
        (shard_of(x + dx, z + dz, c + dc), shard_of(x, z, c))
        for x in range(XS)
        for z in range(ZS)
        for c in range(CS)
    ]
    with jax.named_scope(name):
        return lax.ppermute(value, "shard", pairs)


def from_replica(value, dy):
    return lax.ppermute(value, "replica", [((y + dy) % YS, y) for y in range(YS)])


def onward(value, axis, name="onward"):
    pairs = []
    for x in range(XS):
        for z in range(ZS):
            for c in range(CS):
                for y in range(YS):
                    step = 1 - 2 * c
                    tx, ty = (x + step, y) if axis == "x" else (x, y + step)
                    pairs.append((shard_of(x, z, c) * YS + y, shard_of(tx, z, c) * YS + ty % YS))
    with jax.named_scope(name):
        return lax.ppermute(value, ("shard", "replica"), pairs)


def passed_along(value, steps):
    return lax.ppermute(value, "section", [(0, 1)] if steps == 1 else [(1, 0)])


def place():
    shard = lax.axis_index("shard")
    x = lax.div(shard, jnp.int32(4))
    z = lax.rem(lax.div(shard, jnp.int32(2)), jnp.int32(2))
    c = lax.rem(shard, jnp.int32(2))
    return x, z, c, lax.axis_index("replica")


def near(base, step, size):
    return lax.rem(base + jnp.int32(step), jnp.int32(size))


def call(kernel, outs, args, kinds, scratch=(), flops=0, moved=0, out_kinds=None, name=None, aliases=None, limit=LIMIT):
    return pl.pallas_call(
        kernel,
        out_shape=[jax.ShapeDtypeStruct(s, d) for s, d in outs],
        in_specs=list(kinds),
        out_specs=list(out_kinds or [VM] * len(outs)),
        scratch_shapes=list(scratch),
        compiler_params=pltpu.CompilerParams(vmem_limit_bytes=limit * 2**20),
        cost_estimate=pl.CostEstimate(flops=1, bytes_accessed=1, transcendentals=0),
        name=name,
        input_output_aliases=aliases or {},
    )(*args)


def after(values, token):
    return lax.optimization_barrier((values, token))[0]


def dot(a, b, dims=(((1,), (0,)), ((), ()))):
    return lax.dot_general(a, b, dims, preferred_element_type=f32)


def stats(values):
    average = jnp.mean(values, axis=-1, keepdims=True)
    centered = values - average
    spread = jnp.mean(centered * centered, axis=-1, keepdims=True)
    scale = lax.rsqrt(spread + epsilon)
    return centered * scale, scale


def norm_back(grad, gain, hat, scale):
    d_hat = grad * gain
    d_in = scale * (
        d_hat - jnp.mean(d_hat, axis=-1, keepdims=True) - hat * jnp.mean(d_hat * hat, axis=-1, keepdims=True)
    )
    return d_in, jnp.sum(grad * hat, axis=0, keepdims=True), jnp.sum(grad, axis=0, keepdims=True)


def places(base, c, size):
    step = 1 - 2 * c
    return [near(base + 4, d, size) for d in (2, -step, step, 0)]


def pack_kernel(qkv, proj, fc1, fc2, vectors, bias, unit, pieces, small, sems):
    _, _, _, y = place()
    small[...] = jnp.zeros_like(small)
    small[0:10, 0:64] = vectors[...].astype(f32)
    small[16:17, :] = bias[:, 0:128].astype(f32)
    small[17:18, :] = bias[:, 128:256].astype(f32)
    copies = [pltpu.make_async_copy(qkv, unit.at[:, 0:3072], sems.at[0])]
    copies.append(pltpu.make_async_copy(proj, unit.at[:, 3072:4096], sems.at[1]))
    for n in range(TAILS):
        row, col = 4 * GROWS + 64 * n, 4096 + 1024 * n
        copies.append(
            pltpu.make_async_copy(fc2.at[row : row + 64], unit.at[:, col : col + 1024], sems.at[2 + n])
        )
    block = fc1.at[:, pl.ds(pl.multiple_of(y * 1024, 1024), 1024)]
    rows = fc2.at[pl.ds(pl.multiple_of(y * GROWS, 16), GROWS)]
    for n in range(8):
        at = 2 + TAILS + 2 * n
        copies.append(pltpu.make_async_copy(block, pieces.at[n, 0:64], sems.at[at]))
        copies.append(pltpu.make_async_copy(rows, pieces.at[n, 64 : 64 + GROWS], sems.at[at + 1]))
    start(copies)
    wait(copies)
    unit[:, UNIT - 128 : UNIT] = small[...].astype(bf16)


def pack(w_qkv, w_proj, w_fc1, w_fc2, vectors, fc1_bias):
    return call(
        pack_kernel,
        [((64, UNIT), bf16), ((8, 64 + GROWS, 1024), bf16)],
        (w_qkv, w_proj, w_fc1, w_fc2, vectors, fc1_bias),
        [HB] * 4 + [VM] * 2,
        scratch=[pltpu.VMEM((64, 128), f32), pltpu.SemaphoreType.DMA((18 + TAILS,))],
        moved=4 * 2**20,
        name="pack_parts",
        limit=56,
    )


def start(copies):
    for copy in copies:
        copy.start()


def wait(copies):
    for copy in copies:
        copy.wait()


def columns_kernel(keys, *refs):
    pieces, (qkv, proj, fc2, small), sems = refs, refs[-5:-1], refs[-1]
    x, z, c, _ = place()
    copies = []
    for n, (k, dx, dz, array, row) in enumerate(keys):
        piece = pieces[array] if row is None else pieces[array].at[row]
        xz, ck = near(x, dx, XS) * 2 + near(z, dz, ZS), near(c, k, CS)
        parts = [(0, 3072, qkv.at[xz, ck]), (3072, 4096, proj.at[xz, ck]), (UNIT - 128, UNIT, small.at[xz, ck])]
        for t in range(TAILS):
            first, col = 4 * GROWS + 64 * t, 4096 + 1024 * t
            parts.append((col, col + 1024, fc2.at[xz, ck, first : first + 64]))
        for t, (low, high, target) in enumerate(parts):
            copies.append(pltpu.make_async_copy(piece.at[:, low:high], target, sems.at[n, t]))
    start(copies)
    wait(copies)


def put_columns(weights, keys, arrays):
    held = list(weights or [])
    count = len(arrays)
    return list(
        call(
            lambda *refs: columns_kernel(keys, *refs),
            [((8, 2, 64, 3072), bf16), ((8, 2, 64, 1024), bf16), ((8, 2, 256, 1024), bf16), ((8, 2, 64, 128), bf16)],
            list(arrays) + held,
            [ANY] * count + [VM] * len(held),
            scratch=[pltpu.SemaphoreType.DMA((len(keys), 3 + TAILS))],
            moved=count * 2**20,
            name="put_columns",
            aliases={count + n: n for n in range(len(held))},
        )
    )


def stack_kernel(*refs):
    pieces, out, sems = refs[:-2], refs[-2], refs[-1]
    copies = [pltpu.make_async_copy(piece, out.at[n], sems.at[n]) for n, piece in enumerate(pieces)]
    start(copies)
    wait(copies)


def stacked(pieces):
    return call(
        stack_kernel,
        [((len(pieces),) + pieces[0].shape, bf16)],
        pieces,
        [ANY] * len(pieces),
        scratch=[pltpu.SemaphoreType.DMA((len(pieces),))],
        moved=4 * 2**20,
        name="stacked",
    )[0]


def rows_kernel(keys, *refs):
    count = len(keys)
    pieces, (fc1, fc2), sems = refs[:count], refs[-3:-1], refs[-1]
    _, _, c, y = place()
    copies = []
    for n, (k, kind) in enumerate(keys):
        ck, yk = near(c, k, CS), places(y, c, YS)[kind]
        copies.append(pltpu.make_async_copy(pieces[n].at[:, 0:64], fc1.at[yk, :, ck], sems.at[n, 0]))
        target = fc2.at[:, ck, pl.ds(pl.multiple_of(yk * GROWS, 16), GROWS)]
        copies.append(pltpu.make_async_copy(pieces[n].at[:, 64 : 64 + GROWS], target, sems.at[n, 1]))
    start(copies)
    wait(copies)


def put_rows(fc1, fc2, pieces):
    keys = list(pieces)
    held = [fc1, fc2] if fc1 is not None else [fc2]
    count = len(keys)
    return call(
        lambda *refs: rows_kernel(keys, *refs),
        [((4, 8, 2, 64, 1024), bf16), ((8, 2, 256, 1024), bf16)],
        [pieces[key] for key in keys] + held,
        [ANY] * count + [VM] * len(held),
        scratch=[pltpu.SemaphoreType.DMA((count, 2))],
        moved=2 * count * 2**20,
        name="put_rows",
        aliases={count + n: 2 - len(held) + n for n in range(len(held))},
    )


def vectors_kernel(small, vec, bias):
    lane = lax.broadcasted_iota(jnp.int32, (16, 128), 1)
    for t in range(8):
        a = small[t, 0, 0:16].astype(f32)
        b = small[t, 1, 0:16].astype(f32)
        vec[:, t * 128 : t * 128 + 128] = jnp.where(lane < 64, a, pltpu.roll(b, 64, 1))
    for s in range(16):
        tail = small[s // 2, s % 2, 16:32].astype(f32)
        bias[0:1, s * 256 : s * 256 + 128] = tail[0:1]
        bias[0:1, s * 256 + 128 : s * 256 + 256] = tail[1:2]


def gathered_vectors(small):
    return call(
        vectors_kernel, [((16, 1024), f32), ((1, FF), f32)], [small], [VM], moved=2**20, name="gathered_vectors"
    )


def stacked_heads(pair, lane):
    zero = jnp.zeros_like(pair)
    return jnp.concatenate([jnp.where(lane, pair, zero), jnp.where(lane, zero, pair)], axis=0)


def attention_forward_kernel(keep, x_ref, vec, w_qkv, w_proj, *refs):
    if keep:
        received, x_out, a_out, p_out, soft_out, m_out, o_out, x1_out, c_out = refs
        x_out[...] = jnp.where(lax.axis_index("section") == 0, x_ref[...].astype(f32), received[...].astype(f32)).astype(bf16)
        x = x_out[...].astype(f32)
    else:
        x1_out, c_out, p_out, m_out = refs
        x = x_ref[...].astype(f32)
    hat, _ = stats(x)
    a = (hat * vec[0:1, :] + vec[1:2, :]).astype(bf16)
    if keep:
        a_out[...] = a
    for j in range(6):
        part = dot(a, w_qkv[:, :, :, j * 512 : j * 512 + 512].reshape(D, 512))
        if j < 2:
            part = part + vec[2:3, j * 512 : j * 512 + 512]
        if j >= 4:
            part = part + vec[3:4, j * 512 - 2048 : j * 512 - 1536]
        p_out[:, j * 512 : j * 512 + 512] = part.astype(bf16)
    lane = lax.broadcasted_iota(jnp.int32, (128, 128), 1) < 64

    def unit(u, _):
        i, h = lax.div(u, jnp.int32(8)), lax.rem(u, jnp.int32(8))
        rows = pl.ds(pl.multiple_of(i * 128, 128), 128)
        q, k, v = [p_out[rows, pl.ds(pl.multiple_of(h * 128 + o, 128), 128)] for o in (0, 1024, 2048)]
        s = dot(stacked_heads(q, lane), k, NT) * 0.125
        e = jnp.exp(s - jnp.max(s, axis=-1, keepdims=True))
        soft = e / jnp.sum(e, axis=-1, keepdims=True)
        if keep:
            soft_out[u] = soft
        mixed = dot(soft.astype(bf16), v)
        m_out[rows, pl.ds(pl.multiple_of(h * 128, 128), 128)] = jnp.where(lane, mixed[:128], mixed[128:]).astype(bf16)
        return 0

    lax.fori_loop(0, 16, unit, 0, unroll=16)
    o = dot(m_out[...], w_proj[...].reshape(D, D)) + vec[4:5, :]
    x1 = x + vec[5:6, :] * o
    if keep:
        o_out[...] = o
    x1_out[...] = x1
    hat, _ = stats(x1)
    c_out[...] = (hat * vec[6:7, :] + vec[7:8, :]).astype(bf16)


def attention_forward(keep, x, vec, weights, received=None):
    outs = [((T, D), f32), ((T, D), bf16)]
    scratch = []
    if keep:
        outs = [((T, D), bf16)] * 2 + [((T, 3072), bf16), ((16, 256, 128), f32), ((T, D), bf16), ((T, D), f32)] + outs
    else:
        scratch = [pltpu.VMEM((T, 3072), bf16), pltpu.VMEM((T, D), bf16)]
    return call(
        lambda *refs: attention_forward_kernel(keep, *refs),
        outs,
        [x, vec, weights[0], weights[1]] + ([received] if keep else []),
        [VM] * (5 if keep else 4),
        scratch=scratch,
        flops=2 * T * D * 4 * D,
        moved=14 * 2**20,
        name="attention_forward",
    )


def fc1_tile(w1, t):
    return w1[t // 2, :, :, :, (t % 2) * 512 : (t % 2) * 512 + 512].reshape(D, 512)


def feed_forward_kernel(keep, x1_ref, c_ref, vec, bias, w1, w2, *refs):
    if keep:
        u_out, gp_out, f_out, y_out = refs
    else:
        (y_out,) = refs
    c = c_ref[...]
    total = None
    ahead = dot(c, fc1_tile(w1, 0))
    for t in range(8):
        cols = slice(t * 512, t * 512 + 512)
        h = ahead + bias[0:1, cols]
        if t < 7:
            ahead = dot(c, fc1_tile(w1, t + 1))
        cdf = 0.5 * (1.0 + lax.erf(h * 0.7071067811865476))
        u = (h * cdf).astype(bf16)
        if keep:
            gp = cdf + h * (jnp.exp(-0.5 * h * h) * 0.3989422804014327)
            u_out[:, cols] = u
            gp_out[:, cols] = gp.astype(bf16)
        part = dot(u, w2[t].reshape(512, D))
        total = part if total is None else total + part
    f = total + vec[8:9, :]
    if keep:
        f_out[...] = f
    y_out[...] = (x1_ref[...] + vec[9:10, :] * f).astype(y_out.dtype)


def feed_forward(keep, x1, c, vec, bias, weights):
    outs = [((T, D), f32 if keep else bf16)]
    if keep:
        outs = [((T, FF), bf16), ((T, FF), bf16), ((T, D), f32)] + outs
    return call(
        lambda *refs: feed_forward_kernel(keep, *refs),
        outs,
        [x1, c, vec, bias, weights[2], weights[3]],
        [VM] * 6,
        flops=4 * T * D * FF,
        moved=24 * 2**20,
        name="feed_forward",
    )


def upstream_kernel(first, counts, source, *refs):
    vec, g_out, df_out = refs[-3:]
    image = lax.axis_index("shard") * YS + lax.axis_index("replica")
    for m in range(2):
        rows = slice(m * 128, m * 128 + 128)
        g = source[rows, :].astype(f32) * jnp.where(image < counts[m], 1.0, 0.0)
        if not first:
            g = jnp.where(lax.axis_index("section") == 1, g, refs[0][rows, :].astype(f32))
        g_out[rows, :] = g
        df_out[rows, :] = (vec[9:10, :] * g).astype(bf16)


def upstream(counts, source, vec, received=None):
    extra = [] if received is None else [received]
    return call(
        lambda *refs: upstream_kernel(received is None, *refs),
        [((T, D), f32), ((T, D), bf16)],
        [counts, source] + extra + [vec],
        [SM] + [VM] * (2 + len(extra)),
        moved=2**20,
        name="upstream",
    )


def feed_backward_kernel(g_ref, df_ref, f_ref, gp_ref, x1_ref, o_ref, vec, w1, w2, dh_out, dx1_out, do_out, small):
    g = g_ref[...]
    df = df_ref[...]
    small[8:9, :] = jnp.sum(df.astype(f32), axis=0, keepdims=True)
    small[9:10, :] = jnp.sum(g * f_ref[...], axis=0, keepdims=True)
    small[0:4, :] = jnp.zeros((4, D), f32)
    small[14:16, :] = jnp.zeros((2, D), f32)
    total = None
    ahead = dot(df, w2[0].reshape(512, D), NT)
    for t in range(8):
        y, off = t // 2, (t % 2) * 512
        cols = slice(t * 512, t * 512 + 512)
        du = ahead
        if t < 7:
            ahead = dot(df, w2[t + 1].reshape(512, D), NT)
        dh = (gp_ref[:, cols].astype(f32) * du).astype(bf16)
        dh_out[:, cols] = dh
        small[10 + y : 11 + y, off : off + 512] = jnp.sum(dh.astype(f32), axis=0, keepdims=True)
        part = dot(dh, fc1_tile(w1, t), NT)
        total = part if total is None else total + part
    hat, scale = stats(x1_ref[...])
    d_norm, small[6:7, :], small[7:8, :] = norm_back(total, vec[6:7, :], hat, scale)
    dx1 = g + d_norm
    dx1_out[...] = dx1
    small[5:6, :] = jnp.sum(dx1 * o_ref[...], axis=0, keepdims=True)
    do = (vec[5:6, :] * dx1).astype(bf16)
    do_out[...] = do
    small[4:5, :] = jnp.sum(do.astype(f32), axis=0, keepdims=True)


def feed_backward(g, df, f, gp, x1, o, vec, weights):
    return call(
        feed_backward_kernel,
        [((T, FF), bf16), ((T, D), f32), ((T, D), bf16), ((16, D), f32)],
        [g, df, f, gp, x1, o, vec, weights[2], weights[3]],
        [VM] * 9,
        flops=4 * T * D * FF,
        moved=26 * 2**20,
        name="feed_backward",
    )


def attention_backward_kernel(
    do_ref, dx1_ref, x_ref, p_ref, soft_ref, small_ref, vec, w_qkv, w_proj, *refs
):
    dp_out, dx_out, small, dm_ref = refs[-4:]
    dm_ref[...] = dot(do_ref[...], w_proj[...].reshape(D, D), NT).astype(bf16)
    lane = lax.broadcasted_iota(jnp.int32, (128, 128), 1) < 64

    def unit(u, _):
        i, h = lax.div(u, jnp.int32(8)), lax.rem(u, jnp.int32(8))
        rows = pl.ds(pl.multiple_of(i * 128, 128), 128)
        at = lambda o: pl.ds(pl.multiple_of(h * 128 + o, 128), 128)
        q, k, v = [p_ref[rows, at(o)] for o in (0, 1024, 2048)]
        dm = stacked_heads(dm_ref[rows, at(0)], lane)
        soft = soft_ref[u]
        dp_out[rows, at(2048)] = dot(soft.astype(bf16), dm, TN).astype(bf16)
        dw = dot(dm, v, NT)
        ds = (soft * (dw - jnp.sum(soft * dw, axis=-1, keepdims=True))).astype(bf16)
        dq = dot(ds, k) * 0.125
        dp_out[rows, at(0)] = jnp.where(lane, dq[:128], dq[128:]).astype(bf16)
        dp_out[rows, at(1024)] = (dot(ds, stacked_heads(q, lane), TN) * 0.125).astype(bf16)
        return 0

    lax.fori_loop(0, 16, unit, 0, unroll=16)
    small[2:3, :] = jnp.sum(dp_out[:, 0:1024].astype(f32), axis=0, keepdims=True)
    small[3:4, :] = jnp.sum(dp_out[:, 2048:3072].astype(f32), axis=0, keepdims=True)
    small[4:16, :] = small_ref[4:16, :]
    dp_out[:, 3072:4096] = do_ref[...]
    total = None
    for j in range(6):
        cols = slice(j * 512, j * 512 + 512)
        part = dot(dp_out[:, cols], w_qkv[:, :, :, cols].reshape(D, 512), NT)
        total = part if total is None else total + part
    hat, scale = stats(x_ref[...].astype(f32))
    d_norm, small[0:1, :], small[1:2, :] = norm_back(total, vec[0:1, :], hat, scale)
    dx = dx1_ref[...] + d_norm
    if len(refs) > 4:
        dx = jnp.where(lax.axis_index("section") == 0, dx, refs[0][...])
    dx_out[...] = dx.astype(dx_out.dtype)


def attention_backward(do, dx1, x, p, soft, small, vec, weights, output=None):
    extra = [] if output is None else [output]
    return call(
        attention_backward_kernel,
        [((T, 4096), bf16), ((T, D), f32 if extra else bf16), ((16, D), f32)],
        [do, dx1, x, p, soft, small, vec, weights[0], weights[1]] + extra,
        [VM] * (9 + len(extra)),
        scratch=[pltpu.VMEM((T, D), bf16)],
        flops=2 * T * D * 4 * D,
        moved=18 * 2**20,
        name="attention_backward",
    )


def picked_kernel(a_ref, m_ref, c_ref, u_ref, mine, theirs):
    x, z, c, _ = place()
    row = lax.broadcasted_iota(jnp.int32, (512, D), 0)
    col = lax.broadcasted_iota(jnp.int32, (512, D), 1)
    eye_r = lax.broadcasted_iota(jnp.int32, (256, 256), 0)
    eye = jnp.where(eye_r == lax.broadcasted_iota(jnp.int32, (256, 256), 1), 1.0, 0.0).astype(bf16)
    kind, dz, inner = row >> 7, (row >> 6) & 1, row & 63
    for k, out in enumerate((mine, theirs)):
        ck = near(c, k, CS)
        step = 1 - 2 * ck
        there = jnp.where(kind == 0, 2, jnp.where(kind == 1, 4 - step, jnp.where(kind == 2, 4 + step, 0)))
        there = (((x + there) & 3) << 8) + (((z + dz) & 1) << 7) + inner + ck * 64
        chosen = jnp.where(col == there, 1.0, 0.0).astype(bf16)
        for n, ref in enumerate((a_ref, m_ref)):
            out[n * 512 : n * 512 + 512, :] = dot(chosen, ref[...], NT).astype(bf16)
        there = ((row >> 6) << 7) + inner + ck * 64
        chosen = jnp.where(col == there, 1.0, 0.0).astype(bf16)
        out[1024:1536, :] = dot(chosen, c_ref[...], NT).astype(bf16)
        for j in range(8):
            block = u_ref[:, pl.ds(pl.multiple_of((2 * j + ck) * 256, 256), 256)]
            turned = dot(eye, block, NT).astype(bf16)
            for k2 in range(YS):
                out[1536 + k2 * 512 + j * 64 : 1600 + k2 * 512 + j * 64, :] = turned[k2 * 64 : k2 * 64 + 64]


def picked(a, m, c, u):
    return call(
        picked_kernel,
        [((3584, T), bf16)] * 2,
        [a, m, c, u],
        [VM] * 4,
        flops=2 * 10**9,
        moved=8 * 2**20,
        name="transposed_acts",
    )


def fc2_grads_kernel(mine, theirs, df, df2, *outs):
    _, _, c, y = place()
    for n, yk in enumerate(places(y, c, YS)):
        rows = pl.ds(pl.multiple_of(1536 + yk * 512, 512), 512)
        grad = dot(mine[rows, :], df[...]) + dot(theirs[rows, :], df2[...])
        outs[n][...] = grad.astype(bf16).reshape(8, 64, 1024)


def fc1_grads_kernel(mine, theirs, dh, dh2, *outs):
    _, _, c, y = place()
    for n, yk in enumerate(places(y, c, YS)):
        cols = pl.ds(pl.multiple_of(yk * 1024, 1024), 1024)
        grad = dot(mine[1024:1536, :], dh[:, cols]) + dot(theirs[1024:1536, :], dh2[:, cols])
        outs[n][...] = grad.astype(bf16).reshape(8, 64, 1024)


def feed_grads(kernel, name, mine, theirs, given, given2):
    return call(
        kernel,
        [((8, 64, 1024), bf16)] * 4,
        [mine, theirs, given, given2],
        [VM] * 4,
        flops=4 * T * D * FF,
        moved=12 * 2**20,
        name=name,
    )


def attention_grads_kernel(mine, theirs, dp, dp2, small, small2, *refs):
    outs, total = refs[:4], refs[4]
    x, z, c, _ = place()
    total[...] = small[...] + small2[...]
    vec = total[...].astype(bf16)
    row = lax.broadcasted_iota(jnp.int32, (D, 128), 0)
    col = lax.broadcasted_iota(jnp.int32, (D, 128), 1)
    line = lax.broadcasted_iota(jnp.int32, (16, 128), 0)
    for n, x_there in enumerate(places(x, c, XS)):
        for dz in range(ZS):
            inner = near(z, dz, ZS) * 2 + c
            chosen = jnp.where((row == col + x_there * 256 + inner * 64) & (col < 64), 1.0, 0.0).astype(bf16)
            outs[n][dz, 32:64, 4096:4224] = jnp.zeros((32, 128), bf16)
            outs[n][dz, 0:16, 4096:4224] = dot(vec, chosen).astype(bf16)
            there = total[pl.ds(10 + x_there, 1), pl.ds(pl.multiple_of(inner * 256, 256), 256)]
            a, b = there[:, 0:128], there[:, 128:256]
            outs[n][dz, 16:32, 4096:4224] = jnp.where(line == 0, a, jnp.where(line == 1, b, 0.0)).astype(bf16)
    for t in range(8):
        low = 0 if t < 6 else 512
        cols = slice(t * 512, t * 512 + 512)
        grad = dot(mine[low : low + 512, :], dp[:, cols]) + dot(theirs[low : low + 512, :], dp2[:, cols])
        grad = grad.astype(bf16)
        for n in range(4):
            outs[n][:, :, cols] = grad[n * 128 : n * 128 + 128].reshape(2, 64, 512)


def attention_grads(mine, theirs, dp, dp2, small, small2):
    return call(
        attention_grads_kernel,
        [((2, 64, QP), bf16)] * 4,
        [mine, theirs, dp, dp2, small, small2],
        [VM] * 6,
        scratch=[pltpu.VMEM((16, D), f32)],
        flops=8 * T * D * 2 * D,
        moved=16 * 2**20,
        name="attention_grads",
    )


def sum_kernel(count, axis, *refs):
    total = refs[0][...].astype(f32)
    for ref in refs[1:count]:
        total = total + ref[...].astype(f32)
    outs = refs[count:]
    if axis == "add":
        outs[0][...] = jnp.sum(total, axis=0).astype(bf16)
    elif axis == "split":
        for n, out in enumerate(outs):
            out[...] = total[n].astype(bf16)
    elif axis == "quarters":
        outs, held = outs[:4], outs[4]
        held[...] = total
        _, _, _, y = place()
        for dy, out in enumerate(outs):
            out[...] = held[pl.ds(pl.multiple_of(near(y, dy, YS) * 16, 16), 16), :].astype(bf16)
    else:
        outs[0][...] = total.astype(bf16)


def summed(parts, axis=None):
    shape = parts[0].shape
    scratch = []
    if axis == "split":
        outs = [(shape[1:], bf16)] * shape[0]
    elif axis == "quarters":
        outs = [((16,) + shape[1:], bf16)] * 4
        scratch = [pltpu.VMEM(shape, f32)]
    else:
        outs = [(shape[1:] if axis else shape, bf16)]
    size = 1
    for n in shape:
        size *= n
    out = call(
        lambda *refs: sum_kernel(len(parts), axis, *refs),
        outs,
        parts,
        [VM] * len(parts),
        scratch=scratch,
        flops=size * len(parts),
        moved=2 * size * (len(parts) + 1),
        name="summed",
    )
    return out if len(outs) > 1 else out[0]


def results_kernel(*refs):
    fc1, fc2, columns = refs[0:4], refs[4:8], refs[8:12]
    g_qkv, g_proj, g_fc1, g_fc2, g_vec, g_bias, fc1_all, fc2_all, cols_all, sems = refs[12:]
    _, _, _, y = place()
    copies = []
    for dy in range(YS):
        yk = near(y, dy, YS)
        copies.append(pltpu.make_async_copy(fc1[dy], fc1_all.at[yk], sems.at[0, dy]))
        copies.append(pltpu.make_async_copy(fc2[dy], fc2_all.at[yk], sems.at[1, dy]))
        copies.append(pltpu.make_async_copy(columns[dy], cols_all.at[yk], sems.at[2, dy]))
    start(copies)
    wait(copies)
    for k in range(YS):
        g_fc1[:, k * 1024 : k * 1024 + 1024] = fc1_all[k].astype(f32)
        g_fc2[k * 64 : k * 64 + 64, :] = fc2_all[k].astype(f32)
        line = slice(k * 16, k * 16 + 16)
        g_qkv[line, :] = cols_all[k, :, 0:3072].astype(f32)
        g_proj[line, :] = cols_all[k, :, 3072:4096].astype(f32)
    g_vec[...] = cols_all[0, 0:10, 4096:4160].astype(f32)
    g_bias[...] = cols_all[1, 0:2, 4096:4224].astype(f32)


def results(fc1, fc2, columns):
    return call(
        results_kernel,
        [((64, 3072), f32), ((64, 1024), f32), ((64, FF), f32), ((256, D), f32), ((10, 64), f32), ((2, 128), f32)],
        list(fc1) + list(fc2) + list(columns),
        [ANY] * 12,
        scratch=[
            pltpu.VMEM((4, 64, 1024), bf16),
            pltpu.VMEM((4, 64, 1024), bf16),
            pltpu.VMEM((4, 16, QP), bf16),
            pltpu.SemaphoreType.DMA((3, 4)),
        ],
        moved=10 * 2**20,
        name="results",
    )


def twin(value, name="twin"):
    with jax.named_scope(name):
        return from_shard(value, dc=1)


def around(value, name):
    with jax.named_scope(name):
        return [value] + [from_replica(value, dy) for dy in range(1, YS)]


def swap(value, name):
    groups = [[shard_of(x, z, c) for x in range(XS) for z in range(ZS)] for c in range(CS)]
    with jax.named_scope(name):
        return lax.all_to_all(value, "shard", split_axis=0, concat_axis=0, axis_index_groups=groups, tiled=True)


def gather(w_qkv, w_proj, w_fc1, w_fc2, vectors, fc1_bias):
    hold = lax.optimization_barrier
    unit, pieces = pack(w_qkv, w_proj, w_fc1, w_fc2, vectors, fc1_bias)
    here, twin_unit = swap(pieces, "here"), twin(unit, "twin_unit")
    unit, here, twin_unit = hold((unit, here, twin_unit))
    behind, twin_here = onward(here, "y", "behind"), twin(here, "twin_here")
    other = from_shard(unit, dz=1, name="other")
    plus, minus = from_shard(unit, dx=1, name="plus"), from_shard(unit, dx=3, name="minus")
    behind, twin_here, other, plus, minus = hold((behind, twin_here, other, plus, minus))
    twin_behind = onward(twin_here, "y", "twin_behind")
    minus_other, plus_other = from_shard(other, dx=3, name="minus_other"), from_shard(plus, dz=1, name="plus_other")
    far = from_shard(plus, dx=1, name="far")
    first = stacked([other, plus, minus])
    twins = twin(first, "twin_first")
    weights = put_columns(None, [(0, 0, 0, 0, None), (1, 0, 0, 1, None)], [unit, twin_unit])
    fc1, weights[2] = put_rows(None, weights[2], {(0, 3): here, (1, 3): twin_here})
    held = hold((twin_behind, minus_other, plus_other, far, first, twins, fc1, weights))
    twin_behind, minus_other, plus_other, far, first, twins, fc1, weights = held
    opposite = onward(behind, "y", "opposite")
    far_other = from_shard(far, dz=1, name="far_other")
    ahead, twin_ahead = twin(twin_behind, "ahead"), twin(behind, "twin_ahead")
    second = stacked([minus_other, plus_other, far])
    second_twins = twin(second, "twin_second")
    order = [(0, 1), (1, 0), (3, 0)]
    weights = put_columns(weights, [(k, dx, dz, k, n) for k in range(2) for n, (dx, dz) in enumerate(order)], [first, twins])
    fc1, weights[2] = put_rows(fc1, weights[2], {(0, 1): behind, (1, 1): twin_behind})
    held = hold((opposite, far_other, ahead, twin_ahead, second, second_twins, fc1, weights))
    opposite, far_other, ahead, twin_ahead, second, second_twins, fc1, weights = held
    twin_opposite, twin_far_other = twin(opposite, "twin_opposite"), twin(far_other, "twin_far_other")
    order = [(3, 1), (1, 1), (2, 0)]
    keys = [(k, dx, dz, k, n) for k in range(2) for n, (dx, dz) in enumerate(order)]
    weights = put_columns(weights, keys, [second, second_twins])
    fc1, weights[2] = put_rows(fc1, weights[2], {(0, 2): ahead, (1, 2): twin_ahead})
    weights = put_columns(weights, [(0, 2, 1, 0, None), (1, 2, 1, 1, None)], [far_other, twin_far_other])
    fc1, weights[2] = put_rows(fc1, weights[2], {(0, 0): opposite, (1, 0): twin_opposite})
    vec, bias = gathered_vectors(weights[3])
    return (weights[0], weights[1], fc1, weights[2]), vec, bias


def shards(edge_inputs, image_counts, w_qkv, w_proj, w_fc1, w_fc2, vectors, fc1_bias):
    source = edge_inputs[0, :, 0].reshape(T, D)
    weights, vec, bias = gather(w_qkv[0], w_proj[0], w_fc1[0], w_fc2[0], vectors[0], fc1_bias)

    x1, c = attention_forward(False, source, vec, weights)
    (first_out,) = feed_forward(False, x1, c, vec, bias, weights)
    received = passed_along(first_out, 1)
    inputs, a, p, soft, m, o, x1, c = attention_forward(True, source, vec, weights, received)
    u, gp, f, output = feed_forward(True, x1, c, vec, bias, weights)

    g, df = upstream(image_counts, source, vec)
    _, dx1, do, small = feed_backward(g, df, f, gp, x1, o, vec, weights)
    _, dx, _ = attention_backward(do, dx1, inputs, p, soft, small, vec, weights)
    received_grad = passed_along(dx, -1)
    mine, theirs = picked(a, m, c, u)
    received_grad, mine, theirs = lax.optimization_barrier((received_grad, mine, twin(theirs)))

    hold = lax.optimization_barrier
    g, df = upstream(image_counts, source, vec, received_grad)
    opposite, behind, ahead_2, here_2 = feed_grads(fc2_grads_kernel, "fc2_grads", mine, theirs, df, twin(df, "twin_df"))
    far_2, given_2 = onward(opposite, "y", "far_2"), onward(twin(behind, "behind_2"), "y", "given_2")
    g = after(g, opposite)
    dh, dx1, do, small = feed_backward(g, df, f, gp, x1, o, vec, weights)
    dh2 = twin(dh, "twin_dh")
    dp, edge, small = attention_backward(do, dx1, inputs, p, soft, small, vec, weights, output)
    dh, dh2, dp, far_2 = hold((dh, dh2, dp, far_2))
    dp2, small2 = twin(dp, "twin_dp"), twin(small, "twin_small")
    ahead_2 = summed([ahead_2, far_2])
    own_2 = onward(ahead_2, "y", "own_2")
    parts_1 = feed_grads(fc1_grads_kernel, "fc1_grads", mine, theirs, after(dh, ahead_2), dh2)
    opposite, behind, ahead_1, here_1 = parts_1
    far_1, given_1 = onward(opposite, "y", "far_1"), onward(twin(behind, "behind_1"), "y", "given_1")
    parts_c = attention_grads(mine, theirs, after(dp, here_1), dp2, small, small2)
    opposite, behind, ahead_c, here_c = parts_c
    far_c, given_c = onward(opposite, "x", "far_c"), onward(twin(behind, "behind_c"), "x", "given_c")

    ahead_c = summed([ahead_c, far_c])
    own_c = onward(ahead_c, "x", "own_c")
    sum_2 = summed([after(here_2, ahead_c), own_2, twin(given_2, "twin_given_2")])
    got_2 = swap(sum_2, "swap_2")
    ahead_1 = summed([after(ahead_1, sum_2), far_1])
    own_1 = onward(ahead_1, "y", "own_1")
    fc2 = summed([after(got_2, ahead_1)], "add")
    same, other = summed([after(here_c, fc2), own_c, twin(given_c, "twin_given_c")], "split")
    fc2 = around(fc2, "around_fc2")
    with jax.named_scope("other_z"):
        other = from_shard(other, dz=1)
    quarters = summed([same, other], "quarters")
    with jax.named_scope("quarters"):
        quarters = [quarters[0]] + [from_replica(quarters[dy], YS - dy) for dy in range(1, YS)]
    sum_1 = summed([after(here_1, quarters[0]), own_1, twin(given_1, "twin_given_1")])
    got_1 = swap(sum_1, "swap_1")
    quarters[0] = after(quarters[0], sum_1)
    column = around(summed(quarters), "around_c")
    fc1 = around(summed([got_1], "add"), "around_fc1")
    g_qkv, g_proj, g_fc1, g_fc2, g_vec, g_bias = results(fc1, fc2, column)
    return (
        edge.reshape(1, 2, 1, 128, D),
        g_qkv[None],
        g_proj[None],
        g_fc1[None],
        g_fc2[None],
        g_vec[None],
        g_bias.reshape(1, 256),
    )


def solution(mesh):
    placed = (
        P("section", None, ("shard", "replica"), None, None),
        P(),
        P("section", "shard", None),
        P("section", "shard", None),
        P("section", "shard", None),
        P("section", "shard", None),
        P("section", None, "shard"),
        P("section", "shard"),
    )
    return jax.shard_map(
        shards,
        mesh=mesh,
        in_specs=placed,
        out_specs=(placed[0],) + placed[2:],
        check_vma=False,
    )
```

time: 486 us -> 339 us (0.70)
  Pallas kernels: 175 us -> 84 us
  waiting for transfers between devices: 212 us -> 186 us
  starting transfers between devices: 69.6 us -> 56.8 us
  local copies, waits for them, and re-layouts: 14.2 us -> 4.48 us
  other arithmetic: 5.96 us -> 0 us
    pallas_call x25 -> x37, Pallas kernels: 175 us -> 84 us  [call(): pl.pallas_call(kernel, out_shape=[jax.ShapeDtypeStruct(s, d) for s, d in...]
    ppermute x38 -> x27, waiting for transfers between devices: 93 us -> 62.4 us  [from_shard(): return lax.ppermute(value, 'shard', pairs)]
    ppermute x38 -> x27, starting transfers between devices: 35.1 us -> 11 us  [from_shard(): return lax.ppermute(value, 'shard', pairs)]
    all_to_all x2 -> x3, waiting for transfers between devices: 8.03 us -> 22.9 us  [swap(): lax.all_to_all(value, 'shard', split_axis=0, concat_axis=0, axis_index_gr...]
    ppermute x9 -> x12, waiting for transfers between devices: 27 us -> 12.7 us  [from_replica(): lax.ppermute(value, 'replica', [((y + dy) % YS, y) for y in range(YS)])]
    unnamed x105 -> x35, local copies, waits for them, and re-layouts: 11.5 us -> 4.48 us
    ppermute x9 -> x12, starting transfers between devices: 10.6 us -> 17.2 us  [from_replica(): lax.ppermute(value, 'replica', [((y + dy) % YS, y) for y in range(YS)])]
    all_to_all x2 -> x3, starting transfers between devices: 7.12 us -> 13.1 us  [swap(): lax.all_to_all(value, 'shard', split_axis=0, concat_axis=0, axis_index_gr...]
  transfers between devices with their start and end apart: 63 -> 56, of which waited for: 27 -> 31; matrix products, arithmetic and copies ran while one was open for 1% -> 0% of each run, Pallas kernels for 20% -> 14%
where the time goes in v5:
time: 339 us; the launch traced here: 333 us
  waiting for transfers between devices  186 us (55%)
  Pallas kernels  84 us (25%)
  starting transfers between devices  56.8 us (17%)
  local copies, waits for them, and re-layouts  4.48 us (1%)
    pallas_call x37, Pallas kernels, call(): pl.pallas_call(kernel, out_shape=[jax.ShapeDtypeStruct(s, d) for s, d in...  84 us
    ppermute x27, waiting for transfers between devices, from_shard(): return lax.ppermute(value, 'shard', pairs)  62.4 us
    ppermute x12, waiting for transfers between devices, onward(): return lax.ppermute(value, ('shard', 'replica'), pairs)  59.9 us
    ppermute x2, waiting for transfers between devices, passed_along(): return lax.ppermute(value, 'section', [(0, 1)] if steps == 1 else [(1, 0)])  27.8 us
    all_to_all x3, waiting for transfers between devices, swap(): lax.all_to_all(value, 'shard', split_axis=0, concat_axis=0, axis_index_gr...  22.9 us
    ppermute x12, starting transfers between devices, from_replica(): lax.ppermute(value, 'replica', [((y + dy) % YS, y) for y in range(YS)])  17.2 us
    all_to_all x3, starting transfers between devices, swap(): lax.all_to_all(value, 'shard', split_axis=0, concat_axis=0, axis_index_gr...  13.1 us
    ppermute x12, waiting for transfers between devices, from_replica(): lax.ppermute(value, 'replica', [((y + dy) % YS, y) for y in range(YS)])  12.7 us
  transfers between devices with their start and end apart: 56, of which 31 were waited for; matrix products, arithmetic and copies ran while one was open for 0% of the time, Pallas kernels for 14%

profile of v5, /device:TPU:0, one launch (start us, length us, event | category | flops | bytes accessed | tf_op | source)
XLA Modules:
  0.0 332.5 jit_solution(18175694389259472387)
XLA Ops:
  0.6 4.2 %pack_parts.1 = (bf16[64,6272]{1,0:T(8,128)(2,1)}, bf16[8,96,1024]{2,1,0:T(8,128)(2,1)}) custom-call(bf16[64,3072]{1,0:T(8,128)(2,1)} %bitcast.22, bf16[64,1024]{1,0:T(8,128)(2,1)} %bitcast.23, bf16[64,4096]{1,0:T(8,128)(2,1)} %bitcast.20, bf16[256,1024]{1,0:T(8,128)(2,1)} %bitcast.21, bf16[10,64]{1,0:T(8,128)(2,1)} %bitcast.24, bf16[1,256]{1,0:T(2,128)(2,1)} %bias.1), custom_call_target="tpu_custom_call" | custom-call | flops 1 | bytes 1 | tf_op jit(solution)/shard_map/pack_parts/pallas_call | solution.py:75
  4.8 5.9 %all-to-all-start = ((bf16[8,96,1024]{2,1,0:T(8,128)(2,1)}), bf16[8,96,1024]{2,1,0:T(8,128)(2,1)S(1)}, u32[]{:S(2)}, u32[]{:S(2)}) async-start(bf16[8,96,1024]{2,1,0:T(8,128)(2,1)} %get-tuple-element.137), calls=%async_computation | async-start | bytes 3145728 | tf_op jit(solution)/shard_map/here/all_to_all | solution.py:701
  13.1 21.3 %all-to-all-done.refs_0_ = bf16[8,96,1024]{2,1,0:T(8,128)(2,1)S(1)} async-done(((bf16[8,96,1024]{2,1,0:T(8,128)(2,1)}), bf16[8,96,1024]{2,1,0:T(8,128)(2,1)S(1)}, u32[]{:S(2)}, u32[]{:S(2)}) %all-to-all-start) | async-done | bytes 1572896 | tf_op jit(solution)/shard_map/here/all_to_all | solution.py:701
  38.2 18.2 %collective-permute-done.3.refs_0_ = bf16[64,6272]{1,0:T(8,128)(2,1)S(1)} collective-permute-done((bf16[64,6272]{1,0:T(8,128)(2,1)S(1)}, bf16[64,6272]{1,0:T(8,128)(2,1)S(1)}, u32[]{:S(2)}, u32[]{:S(2)}) %collective-permute-start.3) | collective-permute-done | bytes 802848 | tf_op jit(solution)/shard_map/other/ppermute | solution.py:38
  64.3 15.3 %collective-permute-done.10.refs_2_ = bf16[64,6272]{1,0:T(8,128)(2,1)S(1)} collective-permute-done((bf16[64,6272]{1,0:T(8,128)(2,1)S(1)}, bf16[64,6272]{1,0:T(8,128)(2,1)S(1)}, u32[]{:S(2)}, u32[]{:S(2)}) %collective-permute-start.10) | collective-permute-done | bytes 802848 | tf_op jit(solution)/shard_map/far/ppermute | solution.py:38
  89.5 15.3 %collective-permute-done.6.refs_0_ = bf16[8,96,1024]{2,1,0:T(8,128)(2,1)S(1)} collective-permute-done((bf16[8,96,1024]{2,1,0:T(8,128)(2,1)S(1)}, bf16[8,96,1024]{2,1,0:T(8,128)(2,1)S(1)}, u32[]{:S(2)}, u32[]{:S(2)}) %collective-permute-start.6) | collective-permute-done | bytes 1572896 | tf_op jit(solution)/shard_map/opposite/ppermute | solution.py:55
  110.4 4.3 %attention_forward.2 = (f32[256,1024]{1,0:T(8,128)S(1)}, bf16[256,1024]{1,0:T(8,128)(2,1)S(1)}) custom-call(bf16[256,1024]{1,0:T(8,128)(2,1)S(1)} %bitcast.15, f32[16,1024]{1,0:T(8,128)S(1)} %get-tuple-element.185.refs_2_.refs_1_.vec.refs_3_, bf16[8,2,64,3072]{3,2,1,0:T(8,128)(2,1)S(1)} %get-tuple-element.188.refs_2_.w_qkv, ...), custom_call_target="tpu_custom_call" | custom-call | flops 1 | bytes 1 | tf_op jit(solution)/shard_map/attention_forward/pallas_call | solution.py:75
  115.0 5.3 %feed_forward.2 = bf16[256,1024]{1,0:T(8,128)(2,1)S(1)} custom-call(f32[256,1024]{1,0:T(8,128)S(1)} %get-tuple-element.190.refs_0_, bf16[256,1024]{1,0:T(8,128)(2,1)S(1)} %get-tuple-element.191.refs_1_, f32[16,1024]{1,0:T(8,128)S(1)} %get-tuple-element.185.refs_2_.refs_1_.vec.refs_3_, f32[1,4096]{1,0:T(1,128)S(1)} %get-tuple-element.192.refs_3_, ...), custom_call_target="tpu_custom_call" | custom-call | flops 1 | bytes 1 | tf_op jit(solution)/shard_map/feed_forward/pallas_call | solution.py:75
  120.3 5.7 %collective-permute-start.18 = (bf16[256,1024]{1,0:T(8,128)(2,1)S(1)}, bf16[256,1024]{1,0:T(8,128)(2,1)S(1)}, u32[]{:S(2)}, u32[]{:S(2)}) collective-permute-start(bf16[256,1024]{1,0:T(8,128)(2,1)S(1)} %feed_forward.2), channel_id=1, source_target_pairs={{0,64},{1,65},{2,66},{3,67},{4,68},{5,69},{6,70},{7,71},{8,72},{9,... | collective-permute-start | bytes 1572872 | tf_op jit(solution)/shard_map/ppermute | solution.py:59
  126.1 11.2 %collective-permute-done.18.refs_4_ = bf16[256,1024]{1,0:T(8,128)(2,1)S(1)} collective-permute-done((bf16[256,1024]{1,0:T(8,128)(2,1)S(1)}, bf16[256,1024]{1,0:T(8,128)(2,1)S(1)}, u32[]{:S(2)}, u32[]{:S(2)}) %collective-permute-start.18) | collective-permute-done | bytes 524320 | tf_op jit(solution)/shard_map/ppermute | solution.py:59
  137.3 4.4 %attention_forward.3 = (bf16[256,1024]{1,0:T(8,128)(2,1)S(1)}, bf16[256,1024]{1,0:T(8,128)(2,1)S(1)}, bf16[256,3072]{1,0:T(8,128)(2,1)S(1)}, f32[16,256,128]{2,1...) custom-call(bf16[256,1024]{1,0:T(8,128)(2,1)S(1)} %bitcast.16, ...), custom_call_target="tpu_custom_call" | custom-call | flops 1 | bytes 1 | tf_op jit(solution)/shard_map/attention_forward/pallas_call | solution.py:75
  141.7 6.0 %feed_forward.3 = (bf16[256,4096]{1,0:T(8,128)(2,1)S(1)}, bf16[256,4096]{1,0:T(8,128)(2,1)S(1)}, f32[256,1024]{1,0:T(8,128)S(1)}, f32[256,1024]{1,0:T(8,128)S(1)}) custom-call(f32[256,1024]{1,0:T(8,128)S(1)} %get-tuple-element.198.refs_0_.x1_ref, bf16[256,1024]{1,0:T(8,128)(2,1)S(1)} %get-tuple-element.199.refs_1_.c_ref, ...), custom_call_target="tpu_custom_call" | custom-call | flops 1 | bytes 1 | tf_op jit(solution)/shard_map/feed_forward/pallas_call | solution.py:75
  152.5 5.9 %feed_backward.2 = (bf16[256,4096]{1,0:T(8,128)(2,1)}, f32[256,1024]{1,0:T(8,128)S(1)}, bf16[256,1024]{1,0:T(8,128)(2,1)S(1)}, f32[16,1024]{1,0:T(8,128)S(1)}) custom-call(f32[256,1024]{1,0:T(8,128)S(1)} %get-tuple-element.186.g_ref, bf16[256,1024]{1,0:T(8,128)(2,1)S(1)} %get-tuple-element.187.df_ref, f32[256,1024]{1,0:T(8,128)S(1)} %get-tuple-element.200.f_ref, ...), custom_call_target="tpu_custom_call" | custom-call | flops 1 | bytes 1 | tf_op jit(solution)/shard_map/feed_backward/pallas_call | solution.py:75
  158.3 9.1 %attention_backward.2 = (bf16[256,4096]{1,0:T(8,128)(2,1)}, bf16[256,1024]{1,0:T(8,128)(2,1)S(1)}, f32[16,1024]{1,0:T(8,128)}) custom-call(bf16[256,1024]{1,0:T(8,128)(2,1)S(1)} %get-tuple-element.203.do_ref, f32[256,1024]{1,0:T(8,128)S(1)} %get-tuple-element.204.dx1_ref, bf16[256,1024]{1,0:T(8,128)(2,1)S(1)} %get-tuple-element.205.x_ref, ...), custom_call_target="tpu_custom_call" | custom-call | flops 1 | bytes 1 | tf_op jit(solution)/shard_map/attention_backward/pallas_call | solution.py:75
  168.7 16.5 %collective-permute-done.19.refs_2_ = bf16[256,1024]{1,0:T(8,128)(2,1)S(1)} collective-permute-done((bf16[256,1024]{1,0:T(8,128)(2,1)S(1)}, bf16[256,1024]{1,0:T(8,128)(2,1)S(1)}, u32[]{:S(2)}, u32[]{:S(2)}) %collective-permute-start.19) | collective-permute-done | bytes 524320 | tf_op jit(solution)/shard_map/ppermute | solution.py:59
  190.6 5.5 %feed_backward.3 = (bf16[256,4096]{1,0:T(8,128)(2,1)S(1)}, f32[256,1024]{1,0:T(8,128)S(1)}, bf16[256,1024]{1,0:T(8,128)(2,1)S(1)}, f32[16,1024]{1,0:T(8,128)S(1)}) custom-call(f32[256,1024]{1,0:T(8,128)S(1)} %get-tuple-element.221.g_ref, bf16[256,1024]{1,0:T(8,128)(2,1)S(1)} %get-tuple-element.219.df.df_ref, f32[256,1024]{1,0:T(8,128)S(1)} %copy-done.8, ...), custom_call_target="tpu_custom_call" | custom-call | flops 1 | bytes 1 | tf_op jit(solution)/shard_map/feed_backward/pallas_call | solution.py:75
  197.4 8.8 %attention_backward.3 = (bf16[256,4096]{1,0:T(8,128)(2,1)S(1)}, f32[256,1024]{1,0:T(8,128)}, f32[16,1024]{1,0:T(8,128)S(1)}) custom-call(bf16[256,1024]{1,0:T(8,128)(2,1)S(1)} %get-tuple-element.222.do_ref, f32[256,1024]{1,0:T(8,128)S(1)} %get-tuple-element.223.dx1_ref, bf16[256,1024]{1,0:T(8,128)(2,1)S(1)} %get-tuple-element.205.x_ref, ...), custom_call_target="tpu_custom_call" | custom-call | flops 1 | bytes 1 | tf_op jit(solution)/shard_map/attention_backward/pallas_call | solution.py:75
  206.2 6.3 %collective-permute-done.23.refs_1_ = bf16[8,64,1024]{2,1,0:T(8,128)(2,1)S(1)} collective-permute-done((bf16[8,64,1024]{2,1,0:T(8,128)(2,1)S(1)}, bf16[8,64,1024]{2,1,0:T(8,128)(2,1)S(1)}, u32[]{:S(2)}, u32[]{:S(2)}) %collective-permute-start.23) | collective-permute-done | bytes 1048608 | tf_op jit(solution)/shard_map/far_2/ppermute | solution.py:55
  225.2 11.9 %collective-permute-done.29 = bf16[8,64,1024]{2,1,0:T(8,128)(2,1)S(1)} collective-permute-done((bf16[8,64,1024]{2,1,0:T(8,128)(2,1)S(1)}, bf16[8,64,1024]{2,1,0:T(8,128)(2,1)S(1)}, u32[]{:S(2)}, u32[]{:S(2)}) %collective-permute-start.29) | collective-permute-done | bytes 1048608 | tf_op jit(solution)/shard_map/given_2/ppermute | solution.py:55
  239.5 8.8 %collective-permute-done.27.refs_1_ = bf16[8,64,1024]{2,1,0:T(8,128)(2,1)S(1)} collective-permute-done((bf16[8,64,1024]{2,1,0:T(8,128)(2,1)S(1)}, bf16[8,64,1024]{2,1,0:T(8,128)(2,1)S(1)}, u32[]{:S(2)}, u32[]{:S(2)}) %collective-permute-start.27) | collective-permute-done | bytes 1048608 | tf_op jit(solution)/shard_map/own_2/ppermute | solution.py:55
  254.2 5.5 %collective-permute-done.39 = bf16[8,64,1024]{2,1,0:T(8,128)(2,1)} collective-permute-done((bf16[8,64,1024]{2,1,0:T(8,128)(2,1)}, bf16[8,64,1024]{2,1,0:T(8,128)(2,1)}, u32[]{:S(2)}, u32[]{:S(2)}) %collective-permute-start.39) | collective-permute-done | bytes 1048608 | tf_op jit(solution)/shard_map/given_1/ppermute | solution.py:55
  259.7 11.2 %collective-permute-done.31.refs_1_ = bf16[8,64,1024]{2,1,0:T(8,128)(2,1)} collective-permute-done((bf16[8,64,1024]{2,1,0:T(8,128)(2,1)}, bf16[8,64,1024]{2,1,0:T(8,128)(2,1)}, u32[]{:S(2)}, u32[]{:S(2)}) %collective-permute-start.31) | collective-permute-done | bytes 1048608 | tf_op jit(solution)/shard_map/far_1/ppermute | solution.py:55
  278.2 12.4 %collective-permute-done.36.refs_1_ = bf16[64,4224]{1,0:T(8,128)(2,1)S(1)} collective-permute-done((bf16[64,4224]{1,0:T(8,128)(2,1)S(1)}, bf16[64,4224]{1,0:T(8,128)(2,1)S(1)}, u32[]{:S(2)}, u32[]{:S(2)}) %collective-permute-start.36) | collective-permute-done | bytes 540704 | tf_op jit(solution)/shard_map/other_z/from_shard/ppermute | solution.py:38
  327.5 4.0 %results.1 = (f32[64,3072]{1,0:T(8,128)}, f32[64,1024]{1,0:T(8,128)}, f32[64,4096]{1,0:T(8,128)}, f32[256,1024]{1,0:T(8,128)}, f32[10,64]{1,0:T(8,128)S(1)}, /*index=5*/f32[2,128]{1,0:T(2,128)}) custom-call(bf16[64,1024]{1,0:T(8,128)(2,1)S(1)} %summed.18.refs_0_, bf16[64,1024]{1,0:T(8,128)(2,1)S(1)} %collective-permute-done.41.refs_1_, ...), custom_call_target="tpu_custom_call" | custom-call | flops 1 | bytes 1 | tf_op jit(solution)/shard_map/results/pallas_call | solution.py:75
  (160 shorter events, 108.0 us)
Async XLA Ops:
  4.8 29.6 %all-to-all-start = ((bf16[8,96,1024]{2,1,0:T(8,128)(2,1)}), bf16[8,96,1024]{2,1,0:T(8,128)(2,1)S(1)}, u32[]{:S(2)}, u32[]{:S(2)}) async-start(bf16[8,96,1024]{2,1,0:T(8,128)(2,1)} %get-tuple-element.137), calls=%async_computation | async-start | bytes 3145728 | tf_op jit(solution)/shard_map/here/all_to_all | solution.py:701
  34.4 23.2 %collective-permute-start.1 = (bf16[8,96,1024]{2,1,0:T(8,128)(2,1)S(1)}, bf16[8,96,1024]{2,1,0:T(8,128)(2,1)S(1)}, u32[]{:S(2)}, u32[]{:S(2)}) collective-permute-start(bf16[8,96,1024]{2,1,0:T(8,128)(2,1)S(1)} %all-to-all-done.refs_0_), channel_id=1, source_target_pairs={{0,1},{1,2},{2,3},{3,0},{4,7},{5,4},{6,5},{7,6},{8,9},{9,10},{10,1... | collective-permute-start | bytes 4718600 | tf_op jit(solution)/shard_map/behind/ppermute | solution.py:55
  36.1 21.5 %collective-permute-start.2 = (bf16[8,96,1024]{2,1,0:T(8,128)(2,1)S(1)}, bf16[8,96,1024]{2,1,0:T(8,128)(2,1)S(1)}, u32[]{:S(2)}, u32[]{:S(2)}) collective-permute-start(bf16[8,96,1024]{2,1,0:T(8,128)(2,1)S(1)} %all-to-all-done.refs_0_), channel_id=1, source_target_pairs={{4,0},{0,4},{12,8},{8,12},{20,16},{16,20},{28,24},{24,28},{36,32},... | collective-permute-start | bytes 4718600 | tf_op jit(solution)/shard_map/twin_here/from_shard/ppermute | solution.py:38
  36.2 20.2 %collective-permute-start.3 = (bf16[64,6272]{1,0:T(8,128)(2,1)S(1)}, bf16[64,6272]{1,0:T(8,128)(2,1)S(1)}, u32[]{:S(2)}, u32[]{:S(2)}) collective-permute-start(bf16[64,6272]{1,0:T(8,128)(2,1)S(1)} %copy-done.15), channel_id=1, source_target_pairs={{8,0},{12,4},{0,8},{4,12},{24,16},{28,20},{16,24},{20,28},{40,32},... | collective-permute-start | bytes 2408456 | tf_op jit(solution)/shard_map/other/ppermute | solution.py:38
  36.2 20.2 %collective-permute-start.4 = (bf16[64,6272]{1,0:T(8,128)(2,1)S(1)}, bf16[64,6272]{1,0:T(8,128)(2,1)S(1)}, u32[]{:S(2)}, u32[]{:S(2)}) collective-permute-start(bf16[64,6272]{1,0:T(8,128)(2,1)S(1)} %copy-done.15), channel_id=1, source_target_pairs={{16,0},{20,4},{24,8},{28,12},{32,16},{36,20},{40,24},{44,28},{48,3... | collective-permute-start | bytes 2408456 | tf_op jit(solution)/shard_map/plus/ppermute | solution.py:38
  36.7 21.0 %collective-permute-start.5 = (bf16[64,6272]{1,0:T(8,128)(2,1)S(1)}, bf16[64,6272]{1,0:T(8,128)(2,1)S(1)}, u32[]{:S(2)}, u32[]{:S(2)}) collective-permute-start(bf16[64,6272]{1,0:T(8,128)(2,1)S(1)} %copy-done.15), channel_id=1, source_target_pairs={{48,0},{52,4},{56,8},{60,12},{0,16},{4,20},{8,24},{12,28},{16,32},... | collective-permute-start | bytes 2408456 | tf_op jit(solution)/shard_map/minus/ppermute | solution.py:38
  57.9 24.4 %collective-permute-start.11 = (bf16[3,64,6272]{2,1,0:T(8,128)(2,1)S(1)}, bf16[3,64,6272]{2,1,0:T(8,128)(2,1)S(1)}, u32[]{:S(2)}, u32[]{:S(2)}) collective-permute-start(bf16[3,64,6272]{2,1,0:T(8,128)(2,1)S(1)} %stacked.2.refs_0_), channel_id=1, source_target_pairs={{4,0},{0,4},{12,8},{8,12},{20,16},{16,20},{28,24},{24,28},{36,32},... | collective-permute-start | bytes 7225352 | tf_op jit(solution)/shard_map/twin_first/from_shard/ppermute | solution.py:38
  58.0 24.3 %collective-permute-start.7 = (bf16[8,96,1024]{2,1,0:T(8,128)(2,1)S(1)}, bf16[8,96,1024]{2,1,0:T(8,128)(2,1)S(1)}, u32[]{:S(2)}, u32[]{:S(2)}) collective-permute-start(bf16[8,96,1024]{2,1,0:T(8,128)(2,1)S(1)} %collective-permute-done.2.refs_1_), channel_id=1, source_target_pairs={{0,1},{1,2},{2,3},{3,0},{4,7},{5,4},{6,5},{7,6},{8,9},{9,10},{10,1... | collective-permute-start | bytes 4718600 | tf_op jit(solution)/shard_map/twin_behind/ppermute | solution.py:55
  59.9 19.7 %collective-permute-start.10 = (bf16[64,6272]{1,0:T(8,128)(2,1)S(1)}, bf16[64,6272]{1,0:T(8,128)(2,1)S(1)}, u32[]{:S(2)}, u32[]{:S(2)}) collective-permute-start(bf16[64,6272]{1,0:T(8,128)(2,1)S(1)} %collective-permute-done.4.refs_1_), channel_id=1, source_target_pairs={{16,0},{20,4},{24,8},{28,12},{32,16},{36,20},{40,24},{44,28},{48,3... | collective-permute-start | bytes 2408456 | tf_op jit(solution)/shard_map/far/ppermute | solution.py:38
  61.9 20.3 %collective-permute-start.8 = (bf16[64,6272]{1,0:T(8,128)(2,1)S(1)}, bf16[64,6272]{1,0:T(8,128)(2,1)S(1)}, u32[]{:S(2)}, u32[]{:S(2)}) collective-permute-start(bf16[64,6272]{1,0:T(8,128)(2,1)S(1)} %collective-permute-done.3.refs_0_), channel_id=1, source_target_pairs={{48,0},{52,4},{56,8},{60,12},{0,16},{4,20},{8,24},{12,28},{16,32},... | collective-permute-start | bytes 2408456 | tf_op jit(solution)/shard_map/minus_other/ppermute | solution.py:38
  82.5 22.2 %collective-permute-start.15 = (bf16[3,64,6272]{2,1,0:T(8,128)(2,1)S(1)}, bf16[3,64,6272]{2,1,0:T(8,128)(2,1)S(1)}, u32[]{:S(2)}, u32[]{:S(2)}) collective-permute-start(bf16[3,64,6272]{2,1,0:T(8,128)(2,1)S(1)} %stacked.3.refs_0_), channel_id=1, source_target_pairs={{4,0},{0,4},{12,8},{8,12},{20,16},{16,20},{28,24},{24,28},{36,32},... | collective-permute-start | bytes 7225352 | tf_op jit(solution)/shard_map/twin_second/from_shard/ppermute | solution.py:38
  83.1 21.6 %collective-permute-start.6 = (bf16[8,96,1024]{2,1,0:T(8,128)(2,1)S(1)}, bf16[8,96,1024]{2,1,0:T(8,128)(2,1)S(1)}, u32[]{:S(2)}, u32[]{:S(2)}) collective-permute-start(bf16[8,96,1024]{2,1,0:T(8,128)(2,1)S(1)} %collective-permute-done.1.refs_0_), channel_id=1, source_target_pairs={{0,1},{1,2},{2,3},{3,0},{4,7},{5,4},{6,5},{7,6},{8,9},{9,10},{10,1... | collective-permute-start | bytes 4718600 | tf_op jit(solution)/shard_map/opposite/ppermute | solution.py:55
  83.7 21.1 %collective-permute-start.13 = (bf16[8,96,1024]{2,1,0:T(8,128)(2,1)S(1)}, bf16[8,96,1024]{2,1,0:T(8,128)(2,1)S(1)}, u32[]{:S(2)}, u32[]{:S(2)}) collective-permute-start(bf16[8,96,1024]{2,1,0:T(8,128)(2,1)S(1)} %collective-permute-done.7.refs_1_), channel_id=1, source_target_pairs={{4,0},{0,4},{12,8},{8,12},{20,16},{16,20},{28,24},{24,28},{36,32},... | collective-permute-start | bytes 4718600 | tf_op jit(solution)/shard_map/ahead/from_shard/ppermute | solution.py:38
  84.9 19.8 %collective-permute-start.12 = (bf16[64,6272]{1,0:T(8,128)(2,1)S(1)}, bf16[64,6272]{1,0:T(8,128)(2,1)S(1)}, u32[]{:S(2)}, u32[]{:S(2)}) collective-permute-start(bf16[64,6272]{1,0:T(8,128)(2,1)S(1)} %collective-permute-done.10.refs_2_), channel_id=1, source_target_pairs={{8,0},{12,4},{0,8},{4,12},{24,16},{28,20},{16,24},{20,28},{40,32},... | collective-permute-start | bytes 2408456 | tf_op jit(solution)/shard_map/far_other/ppermute | solution.py:38
  151.2 34.1 %collective-permute-start.20 = (bf16[3584,256]{1,0:T(8,128)(2,1)S(1)}, bf16[3584,256]{1,0:T(8,128)(2,1)S(1)}, u32[]{:S(2)}, u32[]{:S(2)}) collective-permute-start(bf16[3584,256]{1,0:T(8,128)(2,1)S(1)} %get-tuple-element.214), channel_id=1, source_target_pairs={{4,0},{0,4},{12,8},{8,12},{20,16},{16,20},{28,24},{24,28},{36,32},... | collective-permute-start | bytes 5505032 | tf_op jit(solution)/shard_map/twin/from_shard/ppermute | solution.py:38
  223.7 25.5 %collective-permute-start.34 = (bf16[2,64,4224]{2,1,0:T(8,128)(2,1)S(1)}, bf16[2,64,4224]{2,1,0:T(8,128)(2,1)}, u32[]{:S(2)}, u32[]{:S(2)}) collective-permute-start(bf16[2,64,4224]{2,1,0:T(8,128)(2,1)S(1)} %collective-permute-done.33), channel_id=1, source_target_pairs={{0,16},{1,17},{2,18},{3,19},{4,52},{5,53},{6,54},{7,55},{8,24},{9,... | collective-permute-start | bytes 3244040 | tf_op jit(solution)/shard_map/given_c/ppermute | solution.py:55
  224.4 23.9 %collective-permute-start.27 = (bf16[8,64,1024]{2,1,0:T(8,128)(2,1)S(1)}, bf16[8,64,1024]{2,1,0:T(8,128)(2,1)S(1)}, u32[]{:S(2)}, u32[]{:S(2)}) collective-permute-start(bf16[8,64,1024]{2,1,0:T(8,128)(2,1)S(1)} %summed.10), channel_id=1, source_target_pairs={{0,1},{1,2},{2,3},{3,0},{4,7},{5,4},{6,5},{7,6},{8,9},{9,10},{10,1... | collective-permute-start | bytes 3145736 | tf_op jit(solution)/shard_map/own_2/ppermute | solution.py:55
  237.1 22.6 %collective-permute-start.39 = (bf16[8,64,1024]{2,1,0:T(8,128)(2,1)}, bf16[8,64,1024]{2,1,0:T(8,128)(2,1)}, u32[]{:S(2)}, u32[]{:S(2)}) collective-permute-start(bf16[8,64,1024]{2,1,0:T(8,128)(2,1)} %collective-permute-done.38), channel_id=1, source_target_pairs={{0,1},{1,2},{2,3},{3,0},{4,7},{5,4},{6,5},{7,6},{8,9},{9,10},{10,1... | collective-permute-start | bytes 3145736 | tf_op jit(solution)/shard_map/given_1/ppermute | solution.py:55
  237.5 33.4 %collective-permute-start.31 = (bf16[8,64,1024]{2,1,0:T(8,128)(2,1)}, bf16[8,64,1024]{2,1,0:T(8,128)(2,1)}, u32[]{:S(2)}, u32[]{:S(2)}) collective-permute-start(bf16[8,64,1024]{2,1,0:T(8,128)(2,1)} %get-tuple-element.246), channel_id=1, source_target_pairs={{0,1},{1,2},{2,3},{3,0},{4,7},{5,4},{6,5},{7,6},{8,9},{9,10},{10,1... | collective-permute-start | bytes 3145736 | tf_op jit(solution)/shard_map/far_1/ppermute | solution.py:55
  248.4 28.0 %collective-permute-start.32 = (bf16[2,64,4224]{2,1,0:T(8,128)(2,1)}, bf16[2,64,4224]{2,1,0:T(8,128)(2,1)S(1)}, u32[]{:S(2)}, u32[]{:S(2)}) collective-permute-start(bf16[2,64,4224]{2,1,0:T(8,128)(2,1)} %summed.11), channel_id=1, source_target_pairs={{0,16},{1,17},{2,18},{3,19},{4,52},{5,53},{6,54},{7,55},{8,24},{9,... | collective-permute-start | bytes 3244040 | tf_op jit(solution)/shard_map/own_c/ppermute | solution.py:55
  249.2 27.1 %collective-permute-start.35 = (bf16[2,64,4224]{2,1,0:T(8,128)(2,1)}, bf16[2,64,4224]{2,1,0:T(8,128)(2,1)}, u32[]{:S(2)}, u32[]{:S(2)}) collective-permute-start(bf16[2,64,4224]{2,1,0:T(8,128)(2,1)} %collective-permute-done.34), channel_id=1, source_target_pairs={{4,0},{0,4},{12,8},{8,12},{20,16},{16,20},{28,24},{24,28},{36,32},... | collective-permute-start | bytes 3244040 | tf_op jit(solution)/shard_map/twin_given_c/from_shard/ppermute | solution.py:38
  250.6 25.6 %all-to-all-start.1 = ((bf16[8,64,1024]{2,1,0:T(8,128)(2,1)}), bf16[8,64,1024]{2,1,0:T(8,128)(2,1)S(1)}, u32[]{:S(2)}, u32[]{:S(2)}) async-start(bf16[8,64,1024]{2,1,0:T(8,128)(2,1)} %summed.12), calls=%async_computation.1 | async-start | bytes 2097152 | tf_op jit(solution)/shard_map/swap_2/all_to_all | solution.py:701
  259.7 31.1 %collective-permute-start.40 = (bf16[8,64,1024]{2,1,0:T(8,128)(2,1)}, bf16[8,64,1024]{2,1,0:T(8,128)(2,1)}, u32[]{:S(2)}, u32[]{:S(2)}) collective-permute-start(bf16[8,64,1024]{2,1,0:T(8,128)(2,1)} %collective-permute-done.39), channel_id=1, source_target_pairs={{4,0},{0,4},{12,8},{8,12},{20,16},{16,20},{28,24},{24,28},{36,32},... | collective-permute-start | bytes 3145736 | tf_op jit(solution)/shard_map/twin_given_1/from_shard/ppermute | solution.py:38
  293.8 21.0 %all-to-all-start.2 = ((bf16[8,64,1024]{2,1,0:T(8,128)(2,1)}), bf16[8,64,1024]{2,1,0:T(8,128)(2,1)S(1)}, u32[]{:S(2)}, u32[]{:S(2)}) async-start(bf16[8,64,1024]{2,1,0:T(8,128)(2,1)} %summed.17), calls=%async_computation.2 | async-start | bytes 2097152 | tf_op jit(solution)/shard_map/swap_1/all_to_all | solution.py:701
  (49 other events, 420.3 us)

commit v6 on v5

--- a/solution.py
+++ b/solution.py
@@ -13,6 +13,7 @@
 UNIT = 4096 + 1024 * TAILS + 128
 QP = 4224
 LIMIT = 8
+HEAVY = ('attention_backward',)
 epsilon = 1e-06
 bf16, f32 = jnp.bfloat16, jnp.float32
 ANY = pl.BlockSpec(memory_space=pl.ANY)
@@ -79,7 +80,7 @@
         out_specs=list(out_kinds or [VM] * len(outs)),
         scratch_shapes=list(scratch),
         compiler_params=pltpu.CompilerParams(vmem_limit_bytes=limit * 2**20),
-        cost_estimate=pl.CostEstimate(flops=1, bytes_accessed=1, transcendentals=0),
+        cost_estimate=pl.CostEstimate(flops=3 * 10**10 if name in HEAVY else 1, bytes_accessed=1, transcendentals=0),
         name=name,
         input_output_aliases=aliases or {},
     )(*args)
@@ -114,12 +115,32 @@
     return [near(base + 4, d, size) for d in (2, -step, step, 0)]
 
 
-def pack_kernel(qkv, proj, fc1, fc2, vectors, bias, unit, pieces, small, sems):
+def pieces_kernel(fc1, fc2, pieces, sems):
     _, _, _, y = place()
-    small[...] = jnp.zeros_like(small)
-    small[0:10, 0:64] = vectors[...].astype(f32)
-    small[16:17, :] = bias[:, 0:128].astype(f32)
-    small[17:18, :] = bias[:, 128:256].astype(f32)
+    block = fc1.at[:, pl.ds(pl.multiple_of(y * 1024, 1024), 1024)]
+    rows = fc2.at[pl.ds(pl.multiple_of(y * GROWS, 16), GROWS)]
+    copies = []
+    for n in range(8):
+        copies.append(pltpu.make_async_copy(block, pieces.at[n, 0:64], sems.at[2 * n]))
+        copies.append(pltpu.make_async_copy(rows, pieces.at[n, 64 : 64 + GROWS], sems.at[2 * n + 1]))
+    start(copies)
+    wait(copies)
+
+
+def own_pieces(w_fc1, w_fc2):
+    return call(
+        pieces_kernel,
+        [((8, 64 + GROWS, 1024), bf16)],
+        (w_fc1, w_fc2),
+        [HB] * 2,
+        scratch=[pltpu.SemaphoreType.DMA((16,))],
+        moved=4 * 2**20,
+        name="own_pieces",
+        limit=56,
+    )[0]
+
+
+def unit_kernel(qkv, proj, fc2, vectors, bias, unit, small, sems):
     copies = [pltpu.make_async_copy(qkv, unit.at[:, 0:3072], sems.at[0])]
     copies.append(pltpu.make_async_copy(proj, unit.at[:, 3072:4096], sems.at[1]))
     for n in range(TAILS):
@@ -127,28 +148,26 @@
         copies.append(
             pltpu.make_async_copy(fc2.at[row : row + 64], unit.at[:, col : col + 1024], sems.at[2 + n])
         )
-    block = fc1.at[:, pl.ds(pl.multiple_of(y * 1024, 1024), 1024)]
-    rows = fc2.at[pl.ds(pl.multiple_of(y * GROWS, 16), GROWS)]
-    for n in range(8):
-        at = 2 + TAILS + 2 * n
-        copies.append(pltpu.make_async_copy(block, pieces.at[n, 0:64], sems.at[at]))
-        copies.append(pltpu.make_async_copy(rows, pieces.at[n, 64 : 64 + GROWS], sems.at[at + 1]))
     start(copies)
+    small[...] = jnp.zeros_like(small)
+    small[0:10, 0:64] = vectors[...].astype(f32)
+    small[16:17, :] = bias[:, 0:128].astype(f32)
+    small[17:18, :] = bias[:, 128:256].astype(f32)
     wait(copies)
     unit[:, UNIT - 128 : UNIT] = small[...].astype(bf16)
 
 
-def pack(w_qkv, w_proj, w_fc1, w_fc2, vectors, fc1_bias):
-    return call(
-        pack_kernel,
-        [((64, UNIT), bf16), ((8, 64 + GROWS, 1024), bf16)],
-        (w_qkv, w_proj, w_fc1, w_fc2, vectors, fc1_bias),
-        [HB] * 4 + [VM] * 2,
-        scratch=[pltpu.VMEM((64, 128), f32), pltpu.SemaphoreType.DMA((18 + TAILS,))],
+def own_unit(w_qkv, w_proj, w_fc2, vectors, fc1_bias):
+    return call(
+        unit_kernel,
+        [((64, UNIT), bf16)],
+        (w_qkv, w_proj, w_fc2, vectors, fc1_bias),
+        [HB] * 3 + [VM] * 2,
+        scratch=[pltpu.VMEM((64, 128), f32), pltpu.SemaphoreType.DMA((2 + TAILS,))],
         moved=4 * 2**20,
-        name="pack_parts",
+        name="own_unit",
         limit=56,
-    )
+    )[0]
 
 
 def start(copies):
@@ -294,10 +313,10 @@
         q, k, v = [p_out[rows, pl.ds(pl.multiple_of(h * 128 + o, 128), 128)] for o in (0, 1024, 2048)]
         s = dot(stacked_heads(q, lane), k, NT) * 0.125
         e = jnp.exp(s - jnp.max(s, axis=-1, keepdims=True))
-        soft = e / jnp.sum(e, axis=-1, keepdims=True)
+        soft = (e / jnp.sum(e, axis=-1, keepdims=True)).astype(bf16)
         if keep:
             soft_out[u] = soft
-        mixed = dot(soft.astype(bf16), v)
+        mixed = dot(soft, v)
         m_out[rows, pl.ds(pl.multiple_of(h * 128, 128), 128)] = jnp.where(lane, mixed[:128], mixed[128:]).astype(bf16)
         return 0
 
@@ -305,7 +324,7 @@
     o = dot(m_out[...], w_proj[...].reshape(D, D)) + vec[4:5, :]
     x1 = x + vec[5:6, :] * o
     if keep:
-        o_out[...] = o
+        o_out[...] = o.astype(bf16)
     x1_out[...] = x1
     hat, _ = stats(x1)
     c_out[...] = (hat * vec[6:7, :] + vec[7:8, :]).astype(bf16)
@@ -315,7 +334,7 @@
     outs = [((T, D), f32), ((T, D), bf16)]
     scratch = []
     if keep:
-        outs = [((T, D), bf16)] * 2 + [((T, 3072), bf16), ((16, 256, 128), f32), ((T, D), bf16), ((T, D), f32)] + outs
+        outs = [((T, D), bf16)] * 2 + [((T, 3072), bf16), ((16, 256, 128), bf16), ((T, D), bf16), ((T, D), bf16)] + outs
     else:
         scratch = [pltpu.VMEM((T, 3072), bf16), pltpu.VMEM((T, D), bf16)]
     return call(
@@ -327,6 +346,7 @@
         flops=2 * T * D * 4 * D,
         moved=14 * 2**20,
         name="attention_forward",
+        limit=6,
     )
 
 
@@ -357,14 +377,14 @@
         total = part if total is None else total + part
     f = total + vec[8:9, :]
     if keep:
-        f_out[...] = f
+        f_out[...] = f.astype(bf16)
     y_out[...] = (x1_ref[...] + vec[9:10, :] * f).astype(y_out.dtype)
 
 
 def feed_forward(keep, x1, c, vec, bias, weights):
     outs = [((T, D), f32 if keep else bf16)]
     if keep:
-        outs = [((T, FF), bf16), ((T, FF), bf16), ((T, D), f32)] + outs
+        outs = [((T, FF), bf16), ((T, FF), bf16), ((T, D), bf16)] + outs
     return call(
         lambda *refs: feed_forward_kernel(keep, *refs),
         outs,
@@ -373,6 +393,7 @@
         flops=4 * T * D * FF,
         moved=24 * 2**20,
         name="feed_forward",
+        limit=6,
     )
 
 
@@ -404,7 +425,7 @@
     g = g_ref[...]
     df = df_ref[...]
     small[8:9, :] = jnp.sum(df.astype(f32), axis=0, keepdims=True)
-    small[9:10, :] = jnp.sum(g * f_ref[...], axis=0, keepdims=True)
+    small[9:10, :] = jnp.sum(g * f_ref[...].astype(f32), axis=0, keepdims=True)
     small[0:4, :] = jnp.zeros((4, D), f32)
     small[14:16, :] = jnp.zeros((2, D), f32)
     total = None
@@ -424,7 +445,7 @@
     d_norm, small[6:7, :], small[7:8, :] = norm_back(total, vec[6:7, :], hat, scale)
     dx1 = g + d_norm
     dx1_out[...] = dx1
-    small[5:6, :] = jnp.sum(dx1 * o_ref[...], axis=0, keepdims=True)
+    small[5:6, :] = jnp.sum(dx1 * o_ref[...].astype(f32), axis=0, keepdims=True)
     do = (vec[5:6, :] * dx1).astype(bf16)
     do_out[...] = do
     small[4:5, :] = jnp.sum(do.astype(f32), axis=0, keepdims=True)
@@ -439,6 +460,7 @@
         flops=4 * T * D * FF,
         moved=26 * 2**20,
         name="feed_backward",
+        limit=6,
     )
 
 
@@ -455,8 +477,9 @@
         at = lambda o: pl.ds(pl.multiple_of(h * 128 + o, 128), 128)
         q, k, v = [p_ref[rows, at(o)] for o in (0, 1024, 2048)]
         dm = stacked_heads(dm_ref[rows, at(0)], lane)
-        soft = soft_ref[u]
-        dp_out[rows, at(2048)] = dot(soft.astype(bf16), dm, TN).astype(bf16)
+        low = soft_ref[u]
+        soft = low.astype(f32)
+        dp_out[rows, at(2048)] = dot(low, dm, TN).astype(bf16)
         dw = dot(dm, v, NT)
         ds = (soft * (dw - jnp.sum(soft * dw, axis=-1, keepdims=True))).astype(bf16)
         dq = dot(ds, k) * 0.125
@@ -493,6 +516,7 @@
         flops=2 * T * D * 4 * D,
         moved=18 * 2**20,
         name="attention_backward",
+        limit=6,
     )
 
 
@@ -646,42 +670,46 @@
     return out if len(outs) > 1 else out[0]
 
 
-def results_kernel(*refs):
-    fc1, fc2, columns = refs[0:4], refs[4:8], refs[8:12]
-    g_qkv, g_proj, g_fc1, g_fc2, g_vec, g_bias, fc1_all, fc2_all, cols_all, sems = refs[12:]
-    _, _, _, y = place()
-    copies = []
-    for dy in range(YS):
-        yk = near(y, dy, YS)
-        copies.append(pltpu.make_async_copy(fc1[dy], fc1_all.at[yk], sems.at[0, dy]))
-        copies.append(pltpu.make_async_copy(fc2[dy], fc2_all.at[yk], sems.at[1, dy]))
-        copies.append(pltpu.make_async_copy(columns[dy], cols_all.at[yk], sems.at[2, dy]))
+def gathered_copies(parts, target, sems):
+    y = place()[3]
+    copies = [pltpu.make_async_copy(part, target.at[near(y, dy, YS)], sems.at[dy]) for dy, part in enumerate(parts)]
     start(copies)
-    wait(copies)
+    return copies
+
+
+def fc1_results_kernel(a, b, c, d, out, held, sems):
+    wait(gathered_copies((a, b, c, d), held, sems))
     for k in range(YS):
-        g_fc1[:, k * 1024 : k * 1024 + 1024] = fc1_all[k].astype(f32)
-        g_fc2[k * 64 : k * 64 + 64, :] = fc2_all[k].astype(f32)
+        out[:, k * 1024 : k * 1024 + 1024] = held[k].astype(f32)
+
+
+def fc2_results_kernel(a, b, c, d, out, held, sems):
+    wait(gathered_copies((a, b, c, d), held, sems))
+    for k in range(YS):
+        out[k * 64 : k * 64 + 64, :] = held[k].astype(f32)
+
+
+def column_results_kernel(a, b, c, d, qkv, proj, vec, bias, held, sems):
+    wait(gathered_copies((a, b, c, d), held, sems))
+    for k in range(YS):
         line = slice(k * 16, k * 16 + 16)
-        g_qkv[line, :] = cols_all[k, :, 0:3072].astype(f32)
-        g_proj[line, :] = cols_all[k, :, 3072:4096].astype(f32)
-    g_vec[...] = cols_all[0, 0:10, 4096:4160].astype(f32)
-    g_bias[...] = cols_all[1, 0:2, 4096:4224].astype(f32)
-
-
-def results(fc1, fc2, columns):
-    return call(
-        results_kernel,
-        [((64, 3072), f32), ((64, 1024), f32), ((64, FF), f32), ((256, D), f32), ((10, 64), f32), ((2, 128), f32)],
-        list(fc1) + list(fc2) + list(columns),
-        [ANY] * 12,
-        scratch=[
-            pltpu.VMEM((4, 64, 1024), bf16),
-            pltpu.VMEM((4, 64, 1024), bf16),
-            pltpu.VMEM((4, 16, QP), bf16),
-            pltpu.SemaphoreType.DMA((3, 4)),
-        ],
+        qkv[line, :] = held[k, :, 0:3072].astype(f32)
+        proj[line, :] = held[k, :, 3072:4096].astype(f32)
+    vec[...] = held[0, 0:10, 4096:4160].astype(f32)
+    tail = held[1, 0:16, 4096:4224].astype(f32)
+    bias[:, 0:128] = tail[0:1]
+    bias[:, 128:256] = tail[1:2]
+
+
+def results(kernel, shapes, parts, name):
+    return call(
+        kernel,
+        [(shape, f32) for shape in shapes],
+        parts,
+        [ANY] * 4,
+        scratch=[pltpu.VMEM((4,) + parts[0].shape, bf16), pltpu.SemaphoreType.DMA((4,))],
         moved=10 * 2**20,
-        name="results",
+        name=name,
     )
 
 
@@ -703,8 +731,9 @@
 
 def gather(w_qkv, w_proj, w_fc1, w_fc2, vectors, fc1_bias):
     hold = lax.optimization_barrier
-    unit, pieces = pack(w_qkv, w_proj, w_fc1, w_fc2, vectors, fc1_bias)
-    here, twin_unit = swap(pieces, "here"), twin(unit, "twin_unit")
+    here = swap(own_pieces(w_fc1, w_fc2), "here")
+    unit = own_unit(w_qkv, w_proj, w_fc2, vectors, fc1_bias)
+    twin_unit = twin(unit, "twin_unit")
     unit, here, twin_unit = hold((unit, here, twin_unit))
     behind, twin_here = onward(here, "y", "behind"), twin(here, "twin_here")
     other = from_shard(unit, dz=1, name="other")
@@ -795,7 +824,11 @@
     quarters[0] = after(quarters[0], sum_1)
     column = around(summed(quarters), "around_c")
     fc1 = around(summed([got_1], "add"), "around_fc1")
-    g_qkv, g_proj, g_fc1, g_fc2, g_vec, g_bias = results(fc1, fc2, column)
+    (g_fc2,) = results(fc2_results_kernel, [(256, D)], fc2, "fc2_results")
+    g_qkv, g_proj, g_vec, g_bias = results(
+        column_results_kernel, [(64, 3072), (64, 1024), (10, 64), (1, 256)], column, "column_results"
+    )
+    (g_fc1,) = results(fc1_results_kernel, [(64, FF)], fc1, "fc1_results")
     return (
         edge.reshape(1, 2, 1, 128, D),
         g_qkv[None],
@@ -803,7 +836,7 @@
         g_fc1[None],
         g_fc2[None],
         g_vec[None],
-        g_bias.reshape(1, 256),
+        g_bias,
     )
 
 

time: 339 us -> 329 us (0.971)
  waiting for transfers between devices: 186 us -> 174 us
    ppermute x12, waiting for transfers between devices: 59.9 us -> 53 us  [onward(): return lax.ppermute(value, ('shard', 'replica'), pairs)]
    pallas_call x37 -> x40, Pallas kernels: 84 us -> 86.6 us  [call(): pl.pallas_call(kernel, out_shape=[jax.ShapeDtypeStruct(s, d) for s, d in...]
  transfers between devices with their start and end apart: 56 -> 56, of which waited for: 31 -> 29; matrix products, arithmetic and copies ran while one was open for 0% -> 0% of each run, Pallas kernels for 14% -> 18%
where the time goes in v6:
time: 329 us; the launch traced here: 323 us
  waiting for transfers between devices  174 us (53%)
  Pallas kernels  86.6 us (26%)
  starting transfers between devices  57.2 us (17%)
  local copies, waits for them, and re-layouts  3.46 us (1%)
    pallas_call x40, Pallas kernels, call(): pl.pallas_call(kernel, out_shape=[jax.ShapeDtypeStruct(s, d) for s, d in...  86.6 us
    ppermute x27, waiting for transfers between devices, from_shard(): return lax.ppermute(value, 'shard', pairs)  62.7 us
    ppermute x12, waiting for transfers between devices, onward(): return lax.ppermute(value, ('shard', 'replica'), pairs)  53 us
    ppermute x2, waiting for transfers between devices, passed_along(): return lax.ppermute(value, 'section', [(0, 1)] if steps == 1 else [(1, 0)])  27 us
    all_to_all x3, waiting for transfers between devices, swap(): lax.all_to_all(value, 'shard', split_axis=0, concat_axis=0, axis_index_gr...  19.9 us
    ppermute x12, starting transfers between devices, from_replica(): lax.ppermute(value, 'replica', [((y + dy) % YS, y) for y in range(YS)])  15.5 us
    all_to_all x3, starting transfers between devices, swap(): lax.all_to_all(value, 'shard', split_axis=0, concat_axis=0, axis_index_gr...  12.9 us
    ppermute x27, starting transfers between devices, from_shard(): return lax.ppermute(value, 'shard', pairs)  12.5 us
  transfers between devices with their start and end apart: 56, of which 29 were waited for; matrix products, arithmetic and copies ran while one was open for 0% of the time, Pallas kernels for 18%

profile of v6, /device:TPU:0, one launch (start us, length us, event | category | flops | bytes accessed | tf_op | source)
XLA Modules:
  0.0 323.2 jit_solution(1579819564934701727)
XLA Ops:
  3.7 5.7 %all-to-all-start = ((bf16[8,96,1024]{2,1,0:T(8,128)(2,1)}), bf16[8,96,1024]{2,1,0:T(8,128)(2,1)S(1)}, u32[]{:S(2)}, u32[]{:S(2)}) async-start(bf16[8,96,1024]{2,1,0:T(8,128)(2,1)} %own_pieces.1), calls=%async_computation | async-start | bytes 3145728 | tf_op jit(solution)/shard_map/here/all_to_all | solution.py:729
  14.8 18.4 %all-to-all-done.refs_0_ = bf16[8,96,1024]{2,1,0:T(8,128)(2,1)S(1)} async-done(((bf16[8,96,1024]{2,1,0:T(8,128)(2,1)}), bf16[8,96,1024]{2,1,0:T(8,128)(2,1)S(1)}, u32[]{:S(2)}, u32[]{:S(2)}) %all-to-all-start) | async-done | bytes 1572896 | tf_op jit(solution)/shard_map/here/all_to_all | solution.py:729
  37.0 18.3 %collective-permute-done.3.refs_0_ = bf16[64,6272]{1,0:T(8,128)(2,1)S(1)} collective-permute-done((bf16[64,6272]{1,0:T(8,128)(2,1)}, bf16[64,6272]{1,0:T(8,128)(2,1)S(1)}, u32[]{:S(2)}, u32[]{:S(2)}) %collective-permute-start.3) | collective-permute-done | bytes 802848 | tf_op jit(solution)/shard_map/other/ppermute | solution.py:39
  63.2 15.3 %collective-permute-done.10.refs_2_ = bf16[64,6272]{1,0:T(8,128)(2,1)S(1)} collective-permute-done((bf16[64,6272]{1,0:T(8,128)(2,1)S(1)}, bf16[64,6272]{1,0:T(8,128)(2,1)S(1)}, u32[]{:S(2)}, u32[]{:S(2)}) %collective-permute-start.10) | collective-permute-done | bytes 802848 | tf_op jit(solution)/shard_map/far/ppermute | solution.py:39
  88.4 15.3 %collective-permute-done.6.refs_0_ = bf16[8,96,1024]{2,1,0:T(8,128)(2,1)S(1)} collective-permute-done((bf16[8,96,1024]{2,1,0:T(8,128)(2,1)S(1)}, bf16[8,96,1024]{2,1,0:T(8,128)(2,1)S(1)}, u32[]{:S(2)}, u32[]{:S(2)}) %collective-permute-start.6) | collective-permute-done | bytes 1572896 | tf_op jit(solution)/shard_map/opposite/ppermute | solution.py:56
  109.4 4.3 %attention_forward.2 = (f32[256,1024]{1,0:T(8,128)S(1)}, bf16[256,1024]{1,0:T(8,128)(2,1)S(1)}) custom-call(bf16[256,1024]{1,0:T(8,128)(2,1)S(1)} %bitcast.14, f32[16,1024]{1,0:T(8,128)S(1)} %get-tuple-element.179.refs_2_.refs_1_.vec.refs_3_, bf16[8,2,64,3072]{3,2,1,0:T(8,128)(2,1)S(1)} %get-tuple-element.182.refs_2_.w_qkv, ...), custom_call_target="tpu_custom_call" | custom-call | flops 1 | bytes 1 | tf_op jit(solution)/shard_map/attention_forward/pallas_call | solution.py:76
  114.0 5.3 %feed_forward.2 = bf16[256,1024]{1,0:T(8,128)(2,1)S(1)} custom-call(f32[256,1024]{1,0:T(8,128)S(1)} %get-tuple-element.184.refs_0_, bf16[256,1024]{1,0:T(8,128)(2,1)S(1)} %get-tuple-element.185.refs_1_, f32[16,1024]{1,0:T(8,128)S(1)} %get-tuple-element.179.refs_2_.refs_1_.vec.refs_3_, f32[1,4096]{1,0:T(1,128)S(1)} %get-tuple-element.186.refs_3_, ...), custom_call_target="tpu_custom_call" | custom-call | flops 1 | bytes 1 | tf_op jit(solution)/shard_map/feed_forward/pallas_call | solution.py:76
  119.3 5.7 %collective-permute-start.18 = (bf16[256,1024]{1,0:T(8,128)(2,1)S(1)}, bf16[256,1024]{1,0:T(8,128)(2,1)S(1)}, u32[]{:S(2)}, u32[]{:S(2)}) collective-permute-start(bf16[256,1024]{1,0:T(8,128)(2,1)S(1)} %feed_forward.2), channel_id=1, source_target_pairs={{0,64},{1,65},{2,66},{3,67},{4,68},{5,69},{6,70},{7,71},{8,72},{9,... | collective-permute-start | bytes 1572872 | tf_op jit(solution)/shard_map/ppermute | solution.py:60
  125.8 10.5 %collective-permute-done.18.refs_4_ = bf16[256,1024]{1,0:T(8,128)(2,1)S(1)} collective-permute-done((bf16[256,1024]{1,0:T(8,128)(2,1)S(1)}, bf16[256,1024]{1,0:T(8,128)(2,1)S(1)}, u32[]{:S(2)}, u32[]{:S(2)}) %collective-permute-start.18) | collective-permute-done | bytes 524320 | tf_op jit(solution)/shard_map/ppermute | solution.py:60
  136.3 4.4 %attention_forward.3 = (bf16[256,1024]{1,0:T(8,128)(2,1)S(1)}, bf16[256,1024]{1,0:T(8,128)(2,1)S(1)}, bf16[256,3072]{1,0:T(8,128)(2,1)S(1)}, bf16[16,256,128]{2,...) custom-call(bf16[256,1024]{1,0:T(8,128)(2,1)S(1)} %bitcast.16, ...), custom_call_target="tpu_custom_call" | custom-call | flops 1 | bytes 1 | tf_op jit(solution)/shard_map/attention_forward/pallas_call | solution.py:76
  140.7 6.0 %feed_forward.3 = (bf16[256,4096]{1,0:T(8,128)(2,1)S(1)}, bf16[256,4096]{1,0:T(8,128)(2,1)S(1)}, bf16[256,1024]{1,0:T(8,128)(2,1)S(1)}, f32[256,1024]{1,0:T(8,128)S(1)}) custom-call(f32[256,1024]{1,0:T(8,128)S(1)} %get-tuple-element.192.refs_0_.x1_ref, bf16[256,1024]{1,0:T(8,128)(2,1)S(1)} %get-tuple-element.193.refs_1_.c_ref, ...), custom_call_target="tpu_custom_call" | custom-call | flops 1 | bytes 1 | tf_op jit(solution)/shard_map/feed_forward/pallas_call | solution.py:76
  149.7 5.5 %feed_backward.2 = (bf16[256,4096]{1,0:T(8,128)(2,1)}, f32[256,1024]{1,0:T(8,128)S(1)}, bf16[256,1024]{1,0:T(8,128)(2,1)S(1)}, f32[16,1024]{1,0:T(8,128)S(1)}) custom-call(f32[256,1024]{1,0:T(8,128)S(1)} %get-tuple-element.180.g_ref, bf16[256,1024]{1,0:T(8,128)(2,1)S(1)} %get-tuple-element.181.df_ref, bf16[256,1024]{1,0:T(8,128)(2,1)S(1)} %get-tuple-element.194.f_ref, ...), custom_call_target="tpu_custom_call" | custom-call | flops 1 | bytes 1 | tf_op jit(solution)/shard_map/feed_backward/pallas_call | solution.py:76
  155.2 9.1 %attention_backward.2 = (bf16[256,4096]{1,0:T(8,128)(2,1)}, bf16[256,1024]{1,0:T(8,128)(2,1)S(1)}, f32[16,1024]{1,0:T(8,128)}) custom-call(bf16[256,1024]{1,0:T(8,128)(2,1)S(1)} %get-tuple-element.197.do_ref, f32[256,1024]{1,0:T(8,128)S(1)} %get-tuple-element.198.dx1_ref, bf16[256,1024]{1,0:T(8,128)(2,1)S(1)} %get-tuple-element.199.x_ref, ...), custom_call_target="tpu_custom_call" | custom-call | flops 30000001024 | bytes 1 | tf_op jit(solution)/shard_map/attention_backward/pallas_call | solution.py:76
  165.6 16.5 %collective-permute-done.19.refs_2_ = bf16[256,1024]{1,0:T(8,128)(2,1)S(1)} collective-permute-done((bf16[256,1024]{1,0:T(8,128)(2,1)S(1)}, bf16[256,1024]{1,0:T(8,128)(2,1)S(1)}, u32[]{:S(2)}, u32[]{:S(2)}) %collective-permute-start.19) | collective-permute-done | bytes 524320 | tf_op jit(solution)/shard_map/ppermute | solution.py:60
  188.4 5.5 %feed_backward.3 = (bf16[256,4096]{1,0:T(8,128)(2,1)S(1)}, f32[256,1024]{1,0:T(8,128)S(1)}, bf16[256,1024]{1,0:T(8,128)(2,1)S(1)}, f32[16,1024]{1,0:T(8,128)S(1)}) custom-call(f32[256,1024]{1,0:T(8,128)S(1)} %get-tuple-element.215.g_ref, bf16[256,1024]{1,0:T(8,128)(2,1)S(1)} %get-tuple-element.213.df.df_ref, bf16[256,1024]{1,0:T(8,128)(2,1)S(1)} %get-tuple-element.194.f_ref, ...), custom_call_target="tpu_custom_call" | custom-call | flops 1 | bytes 1 | tf_op jit(solution)/shard_map/feed_backward/pallas_call | solution.py:76
  195.0 8.8 %attention_backward.3 = (bf16[256,4096]{1,0:T(8,128)(2,1)S(1)}, f32[256,1024]{1,0:T(8,128)}, f32[16,1024]{1,0:T(8,128)S(1)}) custom-call(bf16[256,1024]{1,0:T(8,128)(2,1)S(1)} %get-tuple-element.216.do_ref, f32[256,1024]{1,0:T(8,128)S(1)} %get-tuple-element.217.dx1_ref, bf16[256,1024]{1,0:T(8,128)(2,1)S(1)} %get-tuple-element.199.x_ref, ...), custom_call_target="tpu_custom_call" | custom-call | flops 30000001024 | bytes 1 | tf_op jit(solution)/shard_map/attention_backward/pallas_call | solution.py:76
  216.6 11.9 %collective-permute-done.29 = bf16[8,64,1024]{2,1,0:T(8,128)(2,1)S(1)} collective-permute-done((bf16[8,64,1024]{2,1,0:T(8,128)(2,1)S(1)}, bf16[8,64,1024]{2,1,0:T(8,128)(2,1)S(1)}, u32[]{:S(2)}, u32[]{:S(2)}) %collective-permute-start.29) | collective-permute-done | bytes 1048608 | tf_op jit(solution)/shard_map/given_2/ppermute | solution.py:56
  232.0 7.7 %collective-permute-done.27.refs_1_ = bf16[8,64,1024]{2,1,0:T(8,128)(2,1)S(1)} collective-permute-done((bf16[8,64,1024]{2,1,0:T(8,128)(2,1)S(1)}, bf16[8,64,1024]{2,1,0:T(8,128)(2,1)S(1)}, u32[]{:S(2)}, u32[]{:S(2)}) %collective-permute-start.27) | collective-permute-done | bytes 1048608 | tf_op jit(solution)/shard_map/own_2/ppermute | solution.py:56
  246.2 4.9 %collective-permute-done.39 = bf16[8,64,1024]{2,1,0:T(8,128)(2,1)} collective-permute-done((bf16[8,64,1024]{2,1,0:T(8,128)(2,1)}, bf16[8,64,1024]{2,1,0:T(8,128)(2,1)}, u32[]{:S(2)}, u32[]{:S(2)}) %collective-permute-start.39) | collective-permute-done | bytes 1048608 | tf_op jit(solution)/shard_map/given_1/ppermute | solution.py:56
  251.1 11.2 %collective-permute-done.31.refs_1_ = bf16[8,64,1024]{2,1,0:T(8,128)(2,1)} collective-permute-done((bf16[8,64,1024]{2,1,0:T(8,128)(2,1)}, bf16[8,64,1024]{2,1,0:T(8,128)(2,1)}, u32[]{:S(2)}, u32[]{:S(2)}) %collective-permute-start.31) | collective-permute-done | bytes 1048608 | tf_op jit(solution)/shard_map/far_1/ppermute | solution.py:56
  269.6 13.4 %collective-permute-done.36.refs_1_ = bf16[64,4224]{1,0:T(8,128)(2,1)S(1)} collective-permute-done((bf16[64,4224]{1,0:T(8,128)(2,1)S(1)}, bf16[64,4224]{1,0:T(8,128)(2,1)S(1)}, u32[]{:S(2)}, u32[]{:S(2)}) %collective-permute-start.36) | collective-permute-done | bytes 540704 | tf_op jit(solution)/shard_map/other_z/from_shard/ppermute | solution.py:39
  293.9 3.8 %collective-permute-done.41.refs_1_ = bf16[16,4224]{1,0:T(8,128)(2,1)S(1)} collective-permute-done((bf16[16,4224]{1,0:T(8,128)(2,1)S(1)}, bf16[16,4224]{1,0:T(8,128)(2,1)S(1)}, u32[]{:S(2)}, u32[]{:S(2)}) %collective-permute-start.41) | collective-permute-done | bytes 135200 | tf_op jit(solution)/shard_map/quarters/ppermute | solution.py:43
  303.3 4.1 %collective-permute-start.45 = (bf16[16,4224]{1,0:T(8,128)(2,1)S(1)}, bf16[16,4224]{1,0:T(8,128)(2,1)S(1)}, u32[]{:S(2)}, u32[]{:S(2)}) collective-permute-start(bf16[16,4224]{1,0:T(8,128)(2,1)S(1)} %summed.18.a), channel_id=1, source_target_pairs={{2,0},{3,1},{0,2},{1,3},{6,4},{7,5},{4,6},{5,7},{10,8},{11,9},{8,1... | collective-permute-start | bytes 405512 | tf_op jit(solution)/shard_map/around_c/ppermute | solution.py:43
  309.2 4.2 %collective-permute-start.47 = (bf16[64,1024]{1,0:T(8,128)(2,1)S(1)}, bf16[64,1024]{1,0:T(8,128)(2,1)S(1)}, u32[]{:S(2)}, u32[]{:S(2)}) collective-permute-start(bf16[64,1024]{1,0:T(8,128)(2,1)S(1)} %summed.19.a), channel_id=1, source_target_pairs={{1,0},{2,1},{3,2},{0,3},{5,4},{6,5},{7,6},{4,7},{9,8},{10,9},{11,1... | collective-permute-start | bytes 393224 | tf_op jit(solution)/shard_map/around_fc1/ppermute | solution.py:43
  (143 shorter events, 105.7 us)
Async XLA Ops:
  3.7 29.5 %all-to-all-start = ((bf16[8,96,1024]{2,1,0:T(8,128)(2,1)}), bf16[8,96,1024]{2,1,0:T(8,128)(2,1)S(1)}, u32[]{:S(2)}, u32[]{:S(2)}) async-start(bf16[8,96,1024]{2,1,0:T(8,128)(2,1)} %own_pieces.1), calls=%async_computation | async-start | bytes 3145728 | tf_op jit(solution)/shard_map/here/all_to_all | solution.py:729
  33.2 23.3 %collective-permute-start.1 = (bf16[8,96,1024]{2,1,0:T(8,128)(2,1)S(1)}, bf16[8,96,1024]{2,1,0:T(8,128)(2,1)S(1)}, u32[]{:S(2)}, u32[]{:S(2)}) collective-permute-start(bf16[8,96,1024]{2,1,0:T(8,128)(2,1)S(1)} %all-to-all-done.refs_0_), channel_id=1, source_target_pairs={{0,1},{1,2},{2,3},{3,0},{4,7},{5,4},{6,5},{7,6},{8,9},{9,10},{10,1... | collective-permute-start | bytes 4718600 | tf_op jit(solution)/shard_map/behind/ppermute | solution.py:56
  34.7 21.7 %collective-permute-start.2 = (bf16[8,96,1024]{2,1,0:T(8,128)(2,1)S(1)}, bf16[8,96,1024]{2,1,0:T(8,128)(2,1)S(1)}, u32[]{:S(2)}, u32[]{:S(2)}) collective-permute-start(bf16[8,96,1024]{2,1,0:T(8,128)(2,1)S(1)} %all-to-all-done.refs_0_), channel_id=1, source_target_pairs={{4,0},{0,4},{12,8},{8,12},{20,16},{16,20},{28,24},{24,28},{36,32},... | collective-permute-start | bytes 4718600 | tf_op jit(solution)/shard_map/twin_here/from_shard/ppermute | solution.py:39
  34.9 20.3 %collective-permute-start.3 = (bf16[64,6272]{1,0:T(8,128)(2,1)}, bf16[64,6272]{1,0:T(8,128)(2,1)S(1)}, u32[]{:S(2)}, u32[]{:S(2)}) collective-permute-start(bf16[64,6272]{1,0:T(8,128)(2,1)} %own_unit.1.refs_0_), channel_id=1, source_target_pairs={{8,0},{12,4},{0,8},{4,12},{24,16},{28,20},{16,24},{20,28},{40,32},... | collective-permute-start | bytes 2408456 | tf_op jit(solution)/shard_map/other/ppermute | solution.py:39
  34.9 20.3 %collective-permute-start.4 = (bf16[64,6272]{1,0:T(8,128)(2,1)}, bf16[64,6272]{1,0:T(8,128)(2,1)S(1)}, u32[]{:S(2)}, u32[]{:S(2)}) collective-permute-start(bf16[64,6272]{1,0:T(8,128)(2,1)} %own_unit.1.refs_0_), channel_id=1, source_target_pairs={{16,0},{20,4},{24,8},{28,12},{32,16},{36,20},{40,24},{44,28},{48,3... | collective-permute-start | bytes 2408456 | tf_op jit(solution)/shard_map/plus/ppermute | solution.py:39
  35.3 21.2 %collective-permute-start.5 = (bf16[64,6272]{1,0:T(8,128)(2,1)}, bf16[64,6272]{1,0:T(8,128)(2,1)S(1)}, u32[]{:S(2)}, u32[]{:S(2)}) collective-permute-start(bf16[64,6272]{1,0:T(8,128)(2,1)} %own_unit.1.refs_0_), channel_id=1, source_target_pairs={{48,0},{52,4},{56,8},{60,12},{0,16},{4,20},{8,24},{12,28},{16,32},... | collective-permute-start | bytes 2408456 | tf_op jit(solution)/shard_map/minus/ppermute | solution.py:39
  56.7 24.5 %collective-permute-start.11 = (bf16[3,64,6272]{2,1,0:T(8,128)(2,1)S(1)}, bf16[3,64,6272]{2,1,0:T(8,128)(2,1)S(1)}, u32[]{:S(2)}, u32[]{:S(2)}) collective-permute-start(bf16[3,64,6272]{2,1,0:T(8,128)(2,1)S(1)} %stacked.2.refs_0_), channel_id=1, source_target_pairs={{4,0},{0,4},{12,8},{8,12},{20,16},{16,20},{28,24},{24,28},{36,32},... | collective-permute-start | bytes 7225352 | tf_op jit(solution)/shard_map/twin_first/from_shard/ppermute | solution.py:39
  56.8 24.4 %collective-permute-start.7 = (bf16[8,96,1024]{2,1,0:T(8,128)(2,1)S(1)}, bf16[8,96,1024]{2,1,0:T(8,128)(2,1)S(1)}, u32[]{:S(2)}, u32[]{:S(2)}) collective-permute-start(bf16[8,96,1024]{2,1,0:T(8,128)(2,1)S(1)} %collective-permute-done.2.refs_1_), channel_id=1, source_target_pairs={{0,1},{1,2},{2,3},{3,0},{4,7},{5,4},{6,5},{7,6},{8,9},{9,10},{10,1... | collective-permute-start | bytes 4718600 | tf_op jit(solution)/shard_map/twin_behind/ppermute | solution.py:56
  58.8 19.7 %collective-permute-start.10 = (bf16[64,6272]{1,0:T(8,128)(2,1)S(1)}, bf16[64,6272]{1,0:T(8,128)(2,1)S(1)}, u32[]{:S(2)}, u32[]{:S(2)}) collective-permute-start(bf16[64,6272]{1,0:T(8,128)(2,1)S(1)} %collective-permute-done.4.refs_1_), channel_id=1, source_target_pairs={{16,0},{20,4},{24,8},{28,12},{32,16},{36,20},{40,24},{44,28},{48,3... | collective-permute-start | bytes 2408456 | tf_op jit(solution)/shard_map/far/ppermute | solution.py:39
  60.9 20.4 %collective-permute-start.8 = (bf16[64,6272]{1,0:T(8,128)(2,1)S(1)}, bf16[64,6272]{1,0:T(8,128)(2,1)S(1)}, u32[]{:S(2)}, u32[]{:S(2)}) collective-permute-start(bf16[64,6272]{1,0:T(8,128)(2,1)S(1)} %collective-permute-done.3.refs_0_), channel_id=1, source_target_pairs={{48,0},{52,4},{56,8},{60,12},{0,16},{4,20},{8,24},{12,28},{16,32},... | collective-permute-start | bytes 2408456 | tf_op jit(solution)/shard_map/minus_other/ppermute | solution.py:39
  81.5 22.2 %collective-permute-start.15 = (bf16[3,64,6272]{2,1,0:T(8,128)(2,1)S(1)}, bf16[3,64,6272]{2,1,0:T(8,128)(2,1)S(1)}, u32[]{:S(2)}, u32[]{:S(2)}) collective-permute-start(bf16[3,64,6272]{2,1,0:T(8,128)(2,1)S(1)} %stacked.3.refs_0_), channel_id=1, source_target_pairs={{4,0},{0,4},{12,8},{8,12},{20,16},{16,20},{28,24},{24,28},{36,32},... | collective-permute-start | bytes 7225352 | tf_op jit(solution)/shard_map/twin_second/from_shard/ppermute | solution.py:39
  82.1 21.6 %collective-permute-start.6 = (bf16[8,96,1024]{2,1,0:T(8,128)(2,1)S(1)}, bf16[8,96,1024]{2,1,0:T(8,128)(2,1)S(1)}, u32[]{:S(2)}, u32[]{:S(2)}) collective-permute-start(bf16[8,96,1024]{2,1,0:T(8,128)(2,1)S(1)} %collective-permute-done.1.refs_0_), channel_id=1, source_target_pairs={{0,1},{1,2},{2,3},{3,0},{4,7},{5,4},{6,5},{7,6},{8,9},{9,10},{10,1... | collective-permute-start | bytes 4718600 | tf_op jit(solution)/shard_map/opposite/ppermute | solution.py:56
  82.6 21.1 %collective-permute-start.13 = (bf16[8,96,1024]{2,1,0:T(8,128)(2,1)S(1)}, bf16[8,96,1024]{2,1,0:T(8,128)(2,1)S(1)}, u32[]{:S(2)}, u32[]{:S(2)}) collective-permute-start(bf16[8,96,1024]{2,1,0:T(8,128)(2,1)S(1)} %collective-permute-done.7.refs_1_), channel_id=1, source_target_pairs={{4,0},{0,4},{12,8},{8,12},{20,16},{16,20},{28,24},{24,28},{36,32},... | collective-permute-start | bytes 4718600 | tf_op jit(solution)/shard_map/ahead/from_shard/ppermute | solution.py:39
  83.9 19.9 %collective-permute-start.12 = (bf16[64,6272]{1,0:T(8,128)(2,1)S(1)}, bf16[64,6272]{1,0:T(8,128)(2,1)S(1)}, u32[]{:S(2)}, u32[]{:S(2)}) collective-permute-start(bf16[64,6272]{1,0:T(8,128)(2,1)S(1)} %collective-permute-done.10.refs_2_), channel_id=1, source_target_pairs={{8,0},{12,4},{0,8},{4,12},{24,16},{28,20},{16,24},{20,28},{40,32},... | collective-permute-start | bytes 2408456 | tf_op jit(solution)/shard_map/far_other/ppermute | solution.py:39
  149.2 32.9 %collective-permute-start.20 = (bf16[3584,256]{1,0:T(8,128)(2,1)S(1)}, bf16[3584,256]{1,0:T(8,128)(2,1)S(1)}, u32[]{:S(2)}, u32[]{:S(2)}) collective-permute-start(bf16[3584,256]{1,0:T(8,128)(2,1)S(1)} %get-tuple-element.208), channel_id=1, source_target_pairs={{4,0},{0,4},{12,8},{8,12},{20,16},{16,20},{28,24},{24,28},{36,32},... | collective-permute-start | bytes 5505032 | tf_op jit(solution)/shard_map/twin/from_shard/ppermute | solution.py:39
  215.1 26.1 %collective-permute-start.34 = (bf16[2,64,4224]{2,1,0:T(8,128)(2,1)S(1)}, bf16[2,64,4224]{2,1,0:T(8,128)(2,1)}, u32[]{:S(2)}, u32[]{:S(2)}) collective-permute-start(bf16[2,64,4224]{2,1,0:T(8,128)(2,1)S(1)} %collective-permute-done.33), channel_id=1, source_target_pairs={{0,16},{1,17},{2,18},{3,19},{4,52},{5,53},{6,54},{7,55},{8,24},{9,... | collective-permute-start | bytes 3244040 | tf_op jit(solution)/shard_map/given_c/ppermute | solution.py:56
  216.2 23.5 %collective-permute-start.27 = (bf16[8,64,1024]{2,1,0:T(8,128)(2,1)S(1)}, bf16[8,64,1024]{2,1,0:T(8,128)(2,1)S(1)}, u32[]{:S(2)}, u32[]{:S(2)}) collective-permute-start(bf16[8,64,1024]{2,1,0:T(8,128)(2,1)S(1)} %summed.10), channel_id=1, source_target_pairs={{0,1},{1,2},{2,3},{3,0},{4,7},{5,4},{6,5},{7,6},{8,9},{9,10},{10,1... | collective-permute-start | bytes 3145736 | tf_op jit(solution)/shard_map/own_2/ppermute | solution.py:56
  228.5 22.6 %collective-permute-start.39 = (bf16[8,64,1024]{2,1,0:T(8,128)(2,1)}, bf16[8,64,1024]{2,1,0:T(8,128)(2,1)}, u32[]{:S(2)}, u32[]{:S(2)}) collective-permute-start(bf16[8,64,1024]{2,1,0:T(8,128)(2,1)} %collective-permute-done.38), channel_id=1, source_target_pairs={{0,1},{1,2},{2,3},{3,0},{4,7},{5,4},{6,5},{7,6},{8,9},{9,10},{10,1... | collective-permute-start | bytes 3145736 | tf_op jit(solution)/shard_map/given_1/ppermute | solution.py:56
  229.5 32.8 %collective-permute-start.31 = (bf16[8,64,1024]{2,1,0:T(8,128)(2,1)}, bf16[8,64,1024]{2,1,0:T(8,128)(2,1)}, u32[]{:S(2)}, u32[]{:S(2)}) collective-permute-start(bf16[8,64,1024]{2,1,0:T(8,128)(2,1)} %get-tuple-element.240), channel_id=1, source_target_pairs={{0,1},{1,2},{2,3},{3,0},{4,7},{5,4},{6,5},{7,6},{8,9},{9,10},{10,1... | collective-permute-start | bytes 3145736 | tf_op jit(solution)/shard_map/far_1/ppermute | solution.py:56
  239.7 28.0 %collective-permute-start.32 = (bf16[2,64,4224]{2,1,0:T(8,128)(2,1)}, bf16[2,64,4224]{2,1,0:T(8,128)(2,1)S(1)}, u32[]{:S(2)}, u32[]{:S(2)}) collective-permute-start(bf16[2,64,4224]{2,1,0:T(8,128)(2,1)} %summed.11), channel_id=1, source_target_pairs={{0,16},{1,17},{2,18},{3,19},{4,52},{5,53},{6,54},{7,55},{8,24},{9,... | collective-permute-start | bytes 3244040 | tf_op jit(solution)/shard_map/own_c/ppermute | solution.py:56
  241.2 26.5 %collective-permute-start.35 = (bf16[2,64,4224]{2,1,0:T(8,128)(2,1)}, bf16[2,64,4224]{2,1,0:T(8,128)(2,1)}, u32[]{:S(2)}, u32[]{:S(2)}) collective-permute-start(bf16[2,64,4224]{2,1,0:T(8,128)(2,1)} %collective-permute-done.34), channel_id=1, source_target_pairs={{4,0},{0,4},{12,8},{8,12},{20,16},{16,20},{28,24},{24,28},{36,32},... | collective-permute-start | bytes 3244040 | tf_op jit(solution)/shard_map/twin_given_c/from_shard/ppermute | solution.py:39
  242.6 24.9 %all-to-all-start.1 = ((bf16[8,64,1024]{2,1,0:T(8,128)(2,1)}), bf16[8,64,1024]{2,1,0:T(8,128)(2,1)S(1)}, u32[]{:S(2)}, u32[]{:S(2)}) async-start(bf16[8,64,1024]{2,1,0:T(8,128)(2,1)} %summed.12), calls=%async_computation.1 | async-start | bytes 2097152 | tf_op jit(solution)/shard_map/swap_2/all_to_all | solution.py:729
  251.1 32.1 %collective-permute-start.40 = (bf16[8,64,1024]{2,1,0:T(8,128)(2,1)}, bf16[8,64,1024]{2,1,0:T(8,128)(2,1)}, u32[]{:S(2)}, u32[]{:S(2)}) collective-permute-start(bf16[8,64,1024]{2,1,0:T(8,128)(2,1)} %collective-permute-done.39), channel_id=1, source_target_pairs={{4,0},{0,4},{12,8},{8,12},{20,16},{16,20},{28,24},{24,28},{36,32},... | collective-permute-start | bytes 3145736 | tf_op jit(solution)/shard_map/twin_given_1/from_shard/ppermute | solution.py:39
  286.1 21.3 %all-to-all-start.2 = ((bf16[8,64,1024]{2,1,0:T(8,128)(2,1)}), bf16[8,64,1024]{2,1,0:T(8,128)(2,1)S(1)}, u32[]{:S(2)}, u32[]{:S(2)}) async-start(bf16[8,64,1024]{2,1,0:T(8,128)(2,1)} %summed.17), calls=%async_computation.2 | async-start | bytes 2097152 | tf_op jit(solution)/shard_map/swap_1/all_to_all | solution.py:729
  (39 other events, 418.1 us)

commit v7 on v6

--- a/solution.py
+++ b/solution.py
@@ -13,7 +13,7 @@
 UNIT = 4096 + 1024 * TAILS + 128
 QP = 4224
 LIMIT = 8
-HEAVY = ('attention_backward',)
+HEAVY = ('attention_backward', 'attention_input_grad', 'transposed_acts')
 epsilon = 1e-06
 bf16, f32 = jnp.bfloat16, jnp.float32
 ANY = pl.BlockSpec(memory_space=pl.ANY)
@@ -43,13 +43,13 @@
     return lax.ppermute(value, "replica", [((y + dy) % YS, y) for y in range(YS)])
 
 
-def onward(value, axis, name="onward"):
+def onward(value, axis, name="onward", way=1):
     pairs = []
     for x in range(XS):
         for z in range(ZS):
             for c in range(CS):
                 for y in range(YS):
-                    step = 1 - 2 * c
+                    step = way * (1 - 2 * c)
                     tx, ty = (x + step, y) if axis == "x" else (x, y + step)
                     pairs.append((shard_of(x, z, c) * YS + y, shard_of(tx, z, c) * YS + ty % YS))
     with jax.named_scope(name):
@@ -404,13 +404,13 @@
         rows = slice(m * 128, m * 128 + 128)
         g = source[rows, :].astype(f32) * jnp.where(image < counts[m], 1.0, 0.0)
         if not first:
-            g = jnp.where(lax.axis_index("section") == 1, g, refs[0][rows, :].astype(f32))
+            g = jnp.where(lax.axis_index("section") == 1, g, refs[m][...].astype(f32))
         g_out[rows, :] = g
         df_out[rows, :] = (vec[9:10, :] * g).astype(bf16)
 
 
 def upstream(counts, source, vec, received=None):
-    extra = [] if received is None else [received]
+    extra = [] if received is None else list(received)
     return call(
         lambda *refs: upstream_kernel(received is None, *refs),
         [((T, D), f32), ((T, D), bf16)],
@@ -421,13 +421,15 @@
     )
 
 
-def feed_backward_kernel(g_ref, df_ref, f_ref, gp_ref, x1_ref, o_ref, vec, w1, w2, dh_out, dx1_out, do_out, small):
+def feed_backward_kernel(keep, g_ref, df_ref, f_ref, gp_ref, x1_ref, o_ref, vec, w1, w2, dx1_out, do_out, *refs):
     g = g_ref[...]
     df = df_ref[...]
-    small[8:9, :] = jnp.sum(df.astype(f32), axis=0, keepdims=True)
-    small[9:10, :] = jnp.sum(g * f_ref[...].astype(f32), axis=0, keepdims=True)
-    small[0:4, :] = jnp.zeros((4, D), f32)
-    small[14:16, :] = jnp.zeros((2, D), f32)
+    if keep:
+        dh_out, small = refs
+        small[8:9, :] = jnp.sum(df.astype(f32), axis=0, keepdims=True)
+        small[9:10, :] = jnp.sum(g * f_ref[...].astype(f32), axis=0, keepdims=True)
+        small[0:4, :] = jnp.zeros((4, D), f32)
+        small[14:16, :] = jnp.zeros((2, D), f32)
     total = None
     ahead = dot(df, w2[0].reshape(512, D), NT)
     for t in range(8):
@@ -437,24 +439,31 @@
         if t < 7:
             ahead = dot(df, w2[t + 1].reshape(512, D), NT)
         dh = (gp_ref[:, cols].astype(f32) * du).astype(bf16)
-        dh_out[:, cols] = dh
-        small[10 + y : 11 + y, off : off + 512] = jnp.sum(dh.astype(f32), axis=0, keepdims=True)
+        if keep:
+            dh_out[:, cols] = dh
+            small[10 + y : 11 + y, off : off + 512] = jnp.sum(dh.astype(f32), axis=0, keepdims=True)
         part = dot(dh, fc1_tile(w1, t), NT)
         total = part if total is None else total + part
     hat, scale = stats(x1_ref[...])
-    d_norm, small[6:7, :], small[7:8, :] = norm_back(total, vec[6:7, :], hat, scale)
+    d_norm, d_gain, d_shift = norm_back(total, vec[6:7, :], hat, scale)
     dx1 = g + d_norm
     dx1_out[...] = dx1
-    small[5:6, :] = jnp.sum(dx1 * o_ref[...].astype(f32), axis=0, keepdims=True)
     do = (vec[5:6, :] * dx1).astype(bf16)
     do_out[...] = do
-    small[4:5, :] = jnp.sum(do.astype(f32), axis=0, keepdims=True)
-
-
-def feed_backward(g, df, f, gp, x1, o, vec, weights):
-    return call(
-        feed_backward_kernel,
-        [((T, FF), bf16), ((T, D), f32), ((T, D), bf16), ((16, D), f32)],
+    if keep:
+        small[4:5, :] = jnp.sum(do.astype(f32), axis=0, keepdims=True)
+        small[5:6, :] = jnp.sum(dx1 * o_ref[...].astype(f32), axis=0, keepdims=True)
+        small[6:7, :] = d_gain
+        small[7:8, :] = d_shift
+
+
+def feed_backward(keep, g, df, f, gp, x1, o, vec, weights):
+    outs = [((T, D), f32), ((T, D), bf16)]
+    if keep:
+        outs += [((T, FF), bf16), ((16, D), f32)]
+    return call(
+        lambda *refs: feed_backward_kernel(keep, *refs),
+        outs,
         [g, df, f, gp, x1, o, vec, weights[2], weights[3]],
         [VM] * 9,
         flops=4 * T * D * FF,
@@ -503,6 +512,50 @@
     if len(refs) > 4:
         dx = jnp.where(lax.axis_index("section") == 0, dx, refs[0][...])
     dx_out[...] = dx.astype(dx_out.dtype)
+
+
+def attention_input_grad_kernel(image, do_ref, dx1_ref, x_ref, p_ref, soft_ref, vec, w_qkv, w_proj, dx_out, dm_ref, dp_ref):
+    rows = slice(image * 128, image * 128 + 128)
+    dm_ref[...] = dot(do_ref[rows, :], w_proj[...].reshape(D, D), NT).astype(bf16)
+    lane = lax.broadcasted_iota(jnp.int32, (128, 128), 1) < 64
+
+    def unit(h, _):
+        at = lambda o: pl.ds(pl.multiple_of(h * 128 + o, 128), 128)
+        q, k, v = [p_ref[rows, at(o)] for o in (0, 1024, 2048)]
+        dm = stacked_heads(dm_ref[:, at(0)], lane)
+        low = soft_ref[image * 8 + h]
+        soft = low.astype(f32)
+        dp_ref[:, at(2048)] = dot(low, dm, TN).astype(bf16)
+        dw = dot(dm, v, NT)
+        ds = (soft * (dw - jnp.sum(soft * dw, axis=-1, keepdims=True))).astype(bf16)
+        dq = dot(ds, k) * 0.125
+        dp_ref[:, at(0)] = jnp.where(lane, dq[:128], dq[128:]).astype(bf16)
+        dp_ref[:, at(1024)] = (dot(ds, stacked_heads(q, lane), TN) * 0.125).astype(bf16)
+        return 0
+
+    lax.fori_loop(0, 8, unit, 0, unroll=8)
+    total = None
+    for j in range(6):
+        cols = slice(j * 512, j * 512 + 512)
+        part = dot(dp_ref[:, cols], w_qkv[:, :, :, cols].reshape(D, 512), NT)
+        total = part if total is None else total + part
+    hat, scale = stats(x_ref[rows, :].astype(f32))
+    d_norm, _, _ = norm_back(total, vec[0:1, :], hat, scale)
+    dx_out[...] = (dx1_ref[rows, :] + d_norm).astype(bf16)
+
+
+def attention_input_grad(image, do, dx1, x, p, soft, vec, weights):
+    return call(
+        lambda *refs: attention_input_grad_kernel(image, *refs),
+        [((128, D), bf16)],
+        [do, dx1, x, p, soft, vec, weights[0], weights[1]],
+        [VM] * 8,
+        scratch=[pltpu.VMEM((128, D), bf16), pltpu.VMEM((128, 3072), bf16)],
+        flops=T * D * 4 * D,
+        moved=10 * 2**20,
+        name="attention_input_grad",
+        limit=6,
+    )[0]
 
 
 def attention_backward(do, dx1, x, p, soft, small, vec, weights, output=None):
@@ -539,7 +592,8 @@
         chosen = jnp.where(col == there, 1.0, 0.0).astype(bf16)
         out[1024:1536, :] = dot(chosen, c_ref[...], NT).astype(bf16)
         for j in range(8):
-            block = u_ref[:, pl.ds(pl.multiple_of((2 * j + ck) * 256, 256), 256)]
+            chip = near(x, j % 4, XS) * 2 + near(z, j // 4, ZS)
+            block = u_ref[:, pl.ds(pl.multiple_of((2 * chip + ck) * 256, 256), 256)]
             turned = dot(eye, block, NT).astype(bf16)
             for k2 in range(YS):
                 out[1536 + k2 * 512 + j * 64 : 1600 + k2 * 512 + j * 64, :] = turned[k2 * 64 : k2 * 64 + 64]
@@ -634,6 +688,10 @@
     elif axis == "split":
         for n, out in enumerate(outs):
             out[...] = total[n].astype(bf16)
+    elif axis == "halves":
+        count = total.shape[0] // 2
+        outs[0][...] = total[:count].astype(bf16)
+        outs[1][...] = total[count:].astype(bf16)
     elif axis == "quarters":
         outs, held = outs[:4], outs[4]
         held[...] = total
@@ -649,6 +707,8 @@
     scratch = []
     if axis == "split":
         outs = [(shape[1:], bf16)] * shape[0]
+    elif axis == "halves":
+        outs = [((shape[0] // 2,) + shape[1:], bf16)] * 2
     elif axis == "quarters":
         outs = [((16,) + shape[1:], bf16)] * 4
         scratch = [pltpu.VMEM(shape, f32)]
@@ -780,48 +840,52 @@
     u, gp, f, output = feed_forward(True, x1, c, vec, bias, weights)
 
     g, df = upstream(image_counts, source, vec)
-    _, dx1, do, small = feed_backward(g, df, f, gp, x1, o, vec, weights)
-    _, dx, _ = attention_backward(do, dx1, inputs, p, soft, small, vec, weights)
-    received_grad = passed_along(dx, -1)
-    mine, theirs = picked(a, m, c, u)
+    dx1, do = feed_backward(False, g, df, f, gp, x1, o, vec, weights)
+    halves = [attention_input_grad(m, do, dx1, inputs, p, soft, vec, weights) for m in range(2)]
+    received_grad = [passed_along(half, -1) for half in halves]
+    mine, theirs = picked(after(a, halves[1]), m, c, u)
     received_grad, mine, theirs = lax.optimization_barrier((received_grad, mine, twin(theirs)))
 
     hold = lax.optimization_barrier
     g, df = upstream(image_counts, source, vec, received_grad)
-    opposite, behind, ahead_2, here_2 = feed_grads(fc2_grads_kernel, "fc2_grads", mine, theirs, df, twin(df, "twin_df"))
-    far_2, given_2 = onward(opposite, "y", "far_2"), onward(twin(behind, "behind_2"), "y", "given_2")
-    g = after(g, opposite)
-    dh, dx1, do, small = feed_backward(g, df, f, gp, x1, o, vec, weights)
+    parts_2 = feed_grads(fc2_grads_kernel, "fc2_grads", mine, theirs, df, twin(df, "twin_df"))
+    far_2 = onward(parts_2[0], "y", "far_2")
+    g = after(g, parts_2[0])
+    dx1, do, dh, small = feed_backward(True, g, df, f, gp, x1, o, vec, weights)
     dh2 = twin(dh, "twin_dh")
     dp, edge, small = attention_backward(do, dx1, inputs, p, soft, small, vec, weights, output)
     dh, dh2, dp, far_2 = hold((dh, dh2, dp, far_2))
     dp2, small2 = twin(dp, "twin_dp"), twin(small, "twin_small")
-    ahead_2 = summed([ahead_2, far_2])
-    own_2 = onward(ahead_2, "y", "own_2")
-    parts_1 = feed_grads(fc1_grads_kernel, "fc1_grads", mine, theirs, after(dh, ahead_2), dh2)
-    opposite, behind, ahead_1, here_1 = parts_1
-    far_1, given_1 = onward(opposite, "y", "far_1"), onward(twin(behind, "behind_1"), "y", "given_1")
-    parts_c = attention_grads(mine, theirs, after(dp, here_1), dp2, small, small2)
-    opposite, behind, ahead_c, here_c = parts_c
-    far_c, given_c = onward(opposite, "x", "far_c"), onward(twin(behind, "behind_c"), "x", "given_c")
-
-    ahead_c = summed([ahead_c, far_c])
-    own_c = onward(ahead_c, "x", "own_c")
-    sum_2 = summed([after(here_2, ahead_c), own_2, twin(given_2, "twin_given_2")])
-    got_2 = swap(sum_2, "swap_2")
-    ahead_1 = summed([after(ahead_1, sum_2), far_1])
-    own_1 = onward(ahead_1, "y", "own_1")
-    fc2 = summed([after(got_2, ahead_1)], "add")
-    same, other = summed([after(here_c, fc2), own_c, twin(given_c, "twin_given_c")], "split")
-    fc2 = around(fc2, "around_fc2")
+    relay_2 = summed([parts_2[2], far_2])
+    own_2, given_2 = onward(relay_2, "y", "own_2"), onward(after(parts_2[1], relay_2), "y", "given_2", -1)
+    parts_1 = feed_grads(fc1_grads_kernel, "fc1_grads", mine, theirs, after(dh, relay_2), dh2)
+    parts_c = attention_grads(mine, theirs, after(dp, parts_1[3]), dp2, small, small2)
+    far_c, given_c = onward(parts_c[0], "x", "far_c"), onward(parts_c[1], "x", "given_c", -1)
+    parts_1, own_2, given_2, last = hold((parts_1, own_2, given_2, parts_c[3]))
+    far_1, given_1 = onward(parts_1[0], "y", "far_1"), onward(parts_1[1], "y", "given_1", -1)
+
+    same_2, other_2 = summed([parts_2[3], own_2, given_2], "halves")
+    with jax.named_scope("other_2"):
+        other_2 = from_shard(other_2, dz=1)
+    far_c, given_c = hold((far_c, given_c))
+    relay_c = summed([after(parts_c[2], same_2), far_c])
+    own_c = onward(relay_c, "x", "own_c")
+    along = summed([after(same_2, relay_c), other_2], "split")
+    with jax.named_scope("along_2"):
+        along = [along[0]] + [from_shard(along[dx], dx=XS - dx) for dx in range(1, XS)]
+    far_1, given_1 = hold((far_1, given_1))
+    relay_1 = summed([after(parts_1[2], along[0]), far_1])
+    own_1 = onward(relay_1, "y", "own_1")
+    same, other = summed([after(last, relay_1), own_c, given_c], "split")
+    fc2 = summed([after(along[0], same)] + along[1:])
     with jax.named_scope("other_z"):
         other = from_shard(other, dz=1)
-    quarters = summed([same, other], "quarters")
+    quarters = summed([after(same, fc2), other], "quarters")
+    sum_1 = summed([after(parts_1[3], quarters[0]), own_1, given_1])
     with jax.named_scope("quarters"):
         quarters = [quarters[0]] + [from_replica(quarters[dy], YS - dy) for dy in range(1, YS)]
-    sum_1 = summed([after(here_1, quarters[0]), own_1, twin(given_1, "twin_given_1")])
+    fc2 = around(fc2, "around_fc2")
     got_1 = swap(sum_1, "swap_1")
-    quarters[0] = after(quarters[0], sum_1)
     column = around(summed(quarters), "around_c")
     fc1 = around(summed([got_1], "add"), "around_fc1")
     (g_fc2,) = results(fc2_results_kernel, [(256, D)], fc2, "fc2_results")

time: 329 us -> 317 us (0.964)
  waiting for transfers between devices: 174 us -> 166 us
  Pallas kernels: 86.6 us -> 80.9 us
  starting transfers between devices: 57.2 us -> 61.6 us
    pallas_call x40 -> x42, Pallas kernels: 86.6 us -> 80.9 us  [call(): pl.pallas_call(kernel, out_shape=[jax.ShapeDtypeStruct(s, d) for s, d in...]
    ppermute x2 -> x3, waiting for transfers between devices: 27 us -> 21.6 us  [passed_along(): return lax.ppermute(value, 'section', [(0, 1)] if steps == 1 else [(1, 0)])]
    ppermute x27 -> x25, waiting for transfers between devices: 62.7 us -> 58.4 us  [from_shard(): return lax.ppermute(value, 'shard', pairs)]
    ppermute x27 -> x25, starting transfers between devices: 12.5 us -> 16.4 us  [from_shard(): return lax.ppermute(value, 'shard', pairs)]
    all_to_all x3 -> x2, starting transfers between devices: 12.9 us -> 9.31 us  [swap(): lax.all_to_all(value, 'shard', split_axis=0, concat_axis=0, axis_index_gr...]
    all_to_all x3 -> x2, waiting for transfers between devices: 19.9 us -> 18.4 us  [swap(): lax.all_to_all(value, 'shard', split_axis=0, concat_axis=0, axis_index_gr...]
    ppermute x2 -> x3, starting transfers between devices: 7.01 us -> 8.32 us  [passed_along(): return lax.ppermute(value, 'section', [(0, 1)] if steps == 1 else [(1, 0)])]
  transfers between devices with their start and end apart: 56 -> 54, of which waited for: 29 -> 27; matrix products, arithmetic and copies ran while one was open for 0% -> 0% of each run, Pallas kernels for 18% -> 14%
where the time goes in v7:
time: 317 us; the launch traced here: 311 us
  waiting for transfers between devices  166 us (52%)
  Pallas kernels  80.9 us (26%)
  starting transfers between devices  61.6 us (19%)
    pallas_call x42, Pallas kernels, call(): pl.pallas_call(kernel, out_shape=[jax.ShapeDtypeStruct(s, d) for s, d in...  80.9 us
    ppermute x25, waiting for transfers between devices, from_shard(): return lax.ppermute(value, 'shard', pairs)  58.4 us
    ppermute x12, waiting for transfers between devices, onward(): return lax.ppermute(value, ('shard', 'replica'), pairs)  53.1 us
    ppermute x3, waiting for transfers between devices, passed_along(): return lax.ppermute(value, 'section', [(0, 1)] if steps == 1 else [(1, 0)])  21.6 us
    all_to_all x2, waiting for transfers between devices, swap(): lax.all_to_all(value, 'shard', split_axis=0, concat_axis=0, axis_index_gr...  18.4 us
    ppermute x25, starting transfers between devices, from_shard(): return lax.ppermute(value, 'shard', pairs)  16.4 us
    ppermute x12, starting transfers between devices, from_replica(): lax.ppermute(value, 'replica', [((y + dy) % YS, y) for y in range(YS)])  14.9 us
    ppermute x12, waiting for transfers between devices, from_replica(): lax.ppermute(value, 'replica', [((y + dy) % YS, y) for y in range(YS)])  14.6 us
  transfers between devices with their start and end apart: 54, of which 27 were waited for; matrix products, arithmetic and copies ran while one was open for 0% of the time, Pallas kernels for 14%

profile of v7, /device:TPU:0, one launch (start us, length us, event | category | flops | bytes accessed | tf_op | source)
XLA Modules:
  0.0 311.4 jit_solution(16255776499722381714)
XLA Ops:
  4.1 5.7 %all-to-all-start = ((bf16[8,96,1024]{2,1,0:T(8,128)(2,1)}), bf16[8,96,1024]{2,1,0:T(8,128)(2,1)S(1)}, u32[]{:S(2)}, u32[]{:S(2)}) async-start(bf16[8,96,1024]{2,1,0:T(8,128)(2,1)} %own_pieces.1), calls=%async_computation | async-start | bytes 3145728 | tf_op jit(solution)/shard_map/here/all_to_all | solution.py:789
  15.2 18.4 %all-to-all-done.refs_0_ = bf16[8,96,1024]{2,1,0:T(8,128)(2,1)S(1)} async-done(((bf16[8,96,1024]{2,1,0:T(8,128)(2,1)}), bf16[8,96,1024]{2,1,0:T(8,128)(2,1)S(1)}, u32[]{:S(2)}, u32[]{:S(2)}) %all-to-all-start) | async-done | bytes 1572896 | tf_op jit(solution)/shard_map/here/all_to_all | solution.py:789
  37.2 18.4 %collective-permute-done.3.refs_0_ = bf16[64,6272]{1,0:T(8,128)(2,1)S(1)} collective-permute-done((bf16[64,6272]{1,0:T(8,128)(2,1)}, bf16[64,6272]{1,0:T(8,128)(2,1)S(1)}, u32[]{:S(2)}, u32[]{:S(2)}) %collective-permute-start.3) | collective-permute-done | bytes 802848 | tf_op jit(solution)/shard_map/other/ppermute | solution.py:39
  62.9 15.9 %collective-permute-done.10.refs_2_ = bf16[64,6272]{1,0:T(8,128)(2,1)S(1)} collective-permute-done((bf16[64,6272]{1,0:T(8,128)(2,1)S(1)}, bf16[64,6272]{1,0:T(8,128)(2,1)S(1)}, u32[]{:S(2)}, u32[]{:S(2)}) %collective-permute-start.10) | collective-permute-done | bytes 802848 | tf_op jit(solution)/shard_map/far/ppermute | solution.py:39
  88.8 15.3 %collective-permute-done.6.refs_0_ = bf16[8,96,1024]{2,1,0:T(8,128)(2,1)S(1)} collective-permute-done((bf16[8,96,1024]{2,1,0:T(8,128)(2,1)S(1)}, bf16[8,96,1024]{2,1,0:T(8,128)(2,1)S(1)}, u32[]{:S(2)}, u32[]{:S(2)}) %collective-permute-start.6) | collective-permute-done | bytes 1572896 | tf_op jit(solution)/shard_map/opposite/ppermute | solution.py:56
  109.8 4.3 %attention_forward.2 = (f32[256,1024]{1,0:T(8,128)S(1)}, bf16[256,1024]{1,0:T(8,128)(2,1)S(1)}) custom-call(bf16[256,1024]{1,0:T(8,128)(2,1)S(1)} %bitcast.14, f32[16,1024]{1,0:T(8,128)S(1)} %get-tuple-element.198.refs_2_.refs_1_.refs_6_.refs_5_.refs_4_.vec, bf16[8,2,64,3072]{3,2,1,0:T(8,128)(2,1)S(1)} %get-tuple-element.201.refs_2_.refs_6_.w_qkv, ...), custom_call_target="tpu_custom_call" | custom-call | flops 1 | bytes 1 | tf_op jit(solution)/shard_map/attention_forward/pallas_call | solution.py:76
  114.4 5.3 %feed_forward.2 = bf16[256,1024]{1,0:T(8,128)(2,1)S(1)} custom-call(f32[256,1024]{1,0:T(8,128)S(1)} %get-tuple-element.203.refs_0_, bf16[256,1024]{1,0:T(8,128)(2,1)S(1)} %get-tuple-element.204.refs_1_, f32[16,1024]{1,0:T(8,128)S(1)} %get-tuple-element.198.refs_2_.refs_1_.refs_6_.refs_5_.refs_4_.vec, f32[1,4096]{1,0:T(1,128)S(1)} %get-tuple-element.205.refs_3_, ...), custom_call_target="tpu_custom_call" | custom-call | flops 1 | bytes 1 | tf_op jit(solution)/shard_map/feed_forward/pallas_call | solution.py:76
  119.7 5.7 %collective-permute-start.18 = (bf16[256,1024]{1,0:T(8,128)(2,1)S(1)}, bf16[256,1024]{1,0:T(8,128)(2,1)S(1)}, u32[]{:S(2)}, u32[]{:S(2)}) collective-permute-start(bf16[256,1024]{1,0:T(8,128)(2,1)S(1)} %feed_forward.2), channel_id=1, source_target_pairs={{0,64},{1,65},{2,66},{3,67},{4,68},{5,69},{6,70},{7,71},{8,72},{9,... | collective-permute-start | bytes 1572872 | tf_op jit(solution)/shard_map/ppermute | solution.py:60
  126.2 10.5 %collective-permute-done.18.refs_4_ = bf16[256,1024]{1,0:T(8,128)(2,1)S(1)} collective-permute-done((bf16[256,1024]{1,0:T(8,128)(2,1)S(1)}, bf16[256,1024]{1,0:T(8,128)(2,1)S(1)}, u32[]{:S(2)}, u32[]{:S(2)}) %collective-permute-start.18) | collective-permute-done | bytes 524320 | tf_op jit(solution)/shard_map/ppermute | solution.py:60
  136.6 4.4 %attention_forward.3 = (bf16[256,1024]{1,0:T(8,128)(2,1)S(1)}, bf16[256,1024]{1,0:T(8,128)(2,1)S(1)}, bf16[256,3072]{1,0:T(8,128)(2,1)S(1)}, bf16[16,256,128]{2,...) custom-call(bf16[256,1024]{1,0:T(8,128)(2,1)S(1)} %bitcast.16, ...), custom_call_target="tpu_custom_call" | custom-call | flops 1 | bytes 1 | tf_op jit(solution)/shard_map/attention_forward/pallas_call | solution.py:76
  141.0 6.0 %feed_forward.3 = (bf16[256,4096]{1,0:T(8,128)(2,1)S(1)}, bf16[256,4096]{1,0:T(8,128)(2,1)S(1)}, bf16[256,1024]{1,0:T(8,128)(2,1)S(1)}, f32[256,1024]{1,0:T(8,128)S(1)}) custom-call(f32[256,1024]{1,0:T(8,128)S(1)} %get-tuple-element.211.refs_0_.refs_4_, bf16[256,1024]{1,0:T(8,128)(2,1)S(1)} %get-tuple-element.212.refs_1_.c_ref, ...), custom_call_target="tpu_custom_call" | custom-call | flops 1 | bytes 1 | tf_op jit(solution)/shard_map/feed_forward/pallas_call | solution.py:76
  147.0 5.3 %feed_backward.2 = (f32[256,1024]{1,0:T(8,128)S(1)}, bf16[256,1024]{1,0:T(8,128)(2,1)S(1)}) custom-call(f32[256,1024]{1,0:T(8,128)S(1)} %get-tuple-element.199.refs_0_, bf16[256,1024]{1,0:T(8,128)(2,1)S(1)} %get-tuple-element.200.refs_1_, bf16[256,1024]{1,0:T(8,128)(2,1)S(1)} %get-tuple-element.213.refs_2_, ...), custom_call_target="tpu_custom_call" | custom-call | flops 1 | bytes 1 | tf_op jit(solution)/shard_map/feed_backward/pallas_call | solution.py:76
  152.3 5.5 %attention_input_grad.3 = bf16[128,1024]{1,0:T(8,128)(2,1)S(1)} custom-call(bf16[256,1024]{1,0:T(8,128)(2,1)S(1)} %get-tuple-element.216.refs_0_, f32[256,1024]{1,0:T(8,128)S(1)} %get-tuple-element.217.refs_1_, bf16[256,1024]{1,0:T(8,128)(2,1)S(1)} %get-tuple-element.218.refs_2_.x_ref, bf16[256,3072]{1,0:T(8,128)(2,1)S(1)} %get-tuple-element.219.refs_3_.p_ref, ...), custom_call_target="tpu_custom_call" | custom-call | flops 30000001024 | bytes 1 | tf_op jit(solution)/shard_map/attention_input_grad/pallas_call | solution.py:76
  161.7 5.5 %attention_input_grad.2 = bf16[128,1024]{1,0:T(8,128)(2,1)S(1)} custom-call(bf16[256,1024]{1,0:T(8,128)(2,1)S(1)} %get-tuple-element.216.refs_0_, f32[256,1024]{1,0:T(8,128)S(1)} %get-tuple-element.217.refs_1_, bf16[256,1024]{1,0:T(8,128)(2,1)S(1)} %get-tuple-element.218.refs_2_.x_ref, bf16[256,3072]{1,0:T(8,128)(2,1)S(1)} %get-tuple-element.219.refs_3_.p_ref, ...), custom_call_target="tpu_custom_call" | custom-call | flops 30000001024 | bytes 1 | tf_op jit(solution)/shard_map/attention_input_grad/pallas_call | solution.py:76
  168.8 10.7 %collective-permute-done.19.refs_2_ = bf16[128,1024]{1,0:T(8,128)(2,1)S(1)} collective-permute-done((bf16[128,1024]{1,0:T(8,128)(2,1)S(1)}, bf16[128,1024]{1,0:T(8,128)(2,1)S(1)}, u32[]{:S(2)}, u32[]{:S(2)}) %collective-permute-start.19) | collective-permute-done | bytes 262176 | tf_op jit(solution)/shard_map/ppermute | solution.py:60
  185.2 5.5 %feed_backward.3 = (f32[256,1024]{1,0:T(8,128)S(1)}, bf16[256,1024]{1,0:T(8,128)(2,1)S(1)}, bf16[256,4096]{1,0:T(8,128)(2,1)S(1)}, f32[16,1024]{1,0:T(8,128)S(1)}) custom-call(f32[256,1024]{1,0:T(8,128)S(1)} %get-tuple-element.234.refs_0_, bf16[256,1024]{1,0:T(8,128)(2,1)S(1)} %get-tuple-element.232.df.refs_1_, ...), custom_call_target="tpu_custom_call" | custom-call | flops 1 | bytes 1 | tf_op jit(solution)/shard_map/feed_backward/pallas_call | solution.py:76
  192.5 8.8 %attention_backward.1 = (bf16[256,4096]{1,0:T(8,128)(2,1)S(1)}, f32[256,1024]{1,0:T(8,128)}, f32[16,1024]{1,0:T(8,128)S(1)}) custom-call(bf16[256,1024]{1,0:T(8,128)(2,1)S(1)} %get-tuple-element.235.do_ref, f32[256,1024]{1,0:T(8,128)S(1)} %get-tuple-element.236.dx1_ref, bf16[256,1024]{1,0:T(8,128)(2,1)S(1)} %get-tuple-element.218.refs_2_.x_ref, ...), custom_call_target="tpu_custom_call" | custom-call | flops 30000001024 | bytes 1 | tf_op jit(solution)/shard_map/attention_backward/pallas_call | solution.py:76
  213.1 14.1 %collective-permute-done.26.refs_2_ = bf16[8,64,1024]{2,1,0:T(8,128)(2,1)S(1)} collective-permute-done((bf16[8,64,1024]{2,1,0:T(8,128)(2,1)S(1)}, bf16[8,64,1024]{2,1,0:T(8,128)(2,1)S(1)}, u32[]{:S(2)}, u32[]{:S(2)}) %collective-permute-start.26) | collective-permute-done | bytes 1048608 | tf_op jit(solution)/shard_map/given_2/ppermute | solution.py:56
  228.4 3.5 %collective-permute-start.33 = (bf16[8,64,1024]{2,1,0:T(8,128)(2,1)S(1)}, bf16[8,64,1024]{2,1,0:T(8,128)(2,1)S(1)}, u32[]{:S(2)}, u32[]{:S(2)}) collective-permute-start(bf16[8,64,1024]{2,1,0:T(8,128)(2,1)S(1)} %get-tuple-element.273), channel_id=1, source_target_pairs={{0,3},{1,0},{2,1},{3,2},{4,5},{5,6},{6,7},{7,4},{8,11},{9,8},{10,9... | collective-permute-start | bytes 3145736 | tf_op jit(solution)/shard_map/given_1/ppermute | solution.py:56
  232.3 4.7 %collective-permute-done.29.refs_1_ = bf16[2,64,4224]{2,1,0:T(8,128)(2,1)S(1)} collective-permute-done((bf16[2,64,4224]{2,1,0:T(8,128)(2,1)S(1)}, bf16[2,64,4224]{2,1,0:T(8,128)(2,1)S(1)}, u32[]{:S(2)}, u32[]{:S(2)}) %collective-permute-start.29) | collective-permute-done | bytes 1081376 | tf_op jit(solution)/shard_map/far_c/ppermute | solution.py:56
  237.4 16.5 %collective-permute-done.32.refs_1_ = bf16[8,64,1024]{2,1,0:T(8,128)(2,1)S(1)} collective-permute-done((bf16[8,64,1024]{2,1,0:T(8,128)(2,1)S(1)}, bf16[8,64,1024]{2,1,0:T(8,128)(2,1)S(1)}, u32[]{:S(2)}, u32[]{:S(2)}) %collective-permute-start.32) | collective-permute-done | bytes 1048608 | tf_op jit(solution)/shard_map/far_1/ppermute | solution.py:56
  258.9 5.3 %collective-permute-done.35.refs_1_ = bf16[64,1024]{1,0:T(8,128)(2,1)S(1)} collective-permute-done((bf16[64,1024]{1,0:T(8,128)(2,1)S(1)}, bf16[64,1024]{1,0:T(8,128)(2,1)S(1)}, u32[]{:S(2)}, u32[]{:S(2)}) %collective-permute-start.35) | collective-permute-done | bytes 131104 | tf_op jit(solution)/shard_map/along_2/from_shard/ppermute | solution.py:39
  271.8 3.6 %all-to-all-start.1 = ((bf16[8,64,1024]{2,1,0:T(8,128)(2,1)}), bf16[8,64,1024]{2,1,0:T(8,128)(2,1)S(1)}, u32[]{:S(2)}, u32[]{:S(2)}) async-start(bf16[8,64,1024]{2,1,0:T(8,128)(2,1)} %summed.20), calls=%async_computation.1 | async-start | bytes 2097152 | tf_op jit(solution)/shard_map/swap_1/all_to_all | solution.py:789
  280.7 4.2 %collective-permute-done.39.refs_1_ = bf16[16,4224]{1,0:T(8,128)(2,1)S(1)} collective-permute-done((bf16[16,4224]{1,0:T(8,128)(2,1)S(1)}, bf16[16,4224]{1,0:T(8,128)(2,1)S(1)}, u32[]{:S(2)}, u32[]{:S(2)}) %collective-permute-start.39) | collective-permute-done | bytes 135200 | tf_op jit(solution)/shard_map/quarters/ppermute | solution.py:43
  (133 shorter events, 106.6 us)
Async XLA Ops:
  4.1 29.5 %all-to-all-start = ((bf16[8,96,1024]{2,1,0:T(8,128)(2,1)}), bf16[8,96,1024]{2,1,0:T(8,128)(2,1)S(1)}, u32[]{:S(2)}, u32[]{:S(2)}) async-start(bf16[8,96,1024]{2,1,0:T(8,128)(2,1)} %own_pieces.1), calls=%async_computation | async-start | bytes 3145728 | tf_op jit(solution)/shard_map/here/all_to_all | solution.py:789
  33.5 23.3 %collective-permute-start.1 = (bf16[8,96,1024]{2,1,0:T(8,128)(2,1)S(1)}, bf16[8,96,1024]{2,1,0:T(8,128)(2,1)S(1)}, u32[]{:S(2)}, u32[]{:S(2)}) collective-permute-start(bf16[8,96,1024]{2,1,0:T(8,128)(2,1)S(1)} %all-to-all-done.refs_0_), channel_id=1, source_target_pairs={{0,1},{1,2},{2,3},{3,0},{4,7},{5,4},{6,5},{7,6},{8,9},{9,10},{10,1... | collective-permute-start | bytes 4718600 | tf_op jit(solution)/shard_map/behind/ppermute | solution.py:56
  35.1 21.7 %collective-permute-start.2 = (bf16[8,96,1024]{2,1,0:T(8,128)(2,1)S(1)}, bf16[8,96,1024]{2,1,0:T(8,128)(2,1)S(1)}, u32[]{:S(2)}, u32[]{:S(2)}) collective-permute-start(bf16[8,96,1024]{2,1,0:T(8,128)(2,1)S(1)} %all-to-all-done.refs_0_), channel_id=1, source_target_pairs={{4,0},{0,4},{12,8},{8,12},{20,16},{16,20},{28,24},{24,28},{36,32},... | collective-permute-start | bytes 4718600 | tf_op jit(solution)/shard_map/twin_here/from_shard/ppermute | solution.py:39
  35.2 20.5 %collective-permute-start.3 = (bf16[64,6272]{1,0:T(8,128)(2,1)}, bf16[64,6272]{1,0:T(8,128)(2,1)S(1)}, u32[]{:S(2)}, u32[]{:S(2)}) collective-permute-start(bf16[64,6272]{1,0:T(8,128)(2,1)} %own_unit.1.refs_0_), channel_id=1, source_target_pairs={{8,0},{12,4},{0,8},{4,12},{24,16},{28,20},{16,24},{20,28},{40,32},... | collective-permute-start | bytes 2408456 | tf_op jit(solution)/shard_map/other/ppermute | solution.py:39
  35.2 20.5 %collective-permute-start.4 = (bf16[64,6272]{1,0:T(8,128)(2,1)}, bf16[64,6272]{1,0:T(8,128)(2,1)S(1)}, u32[]{:S(2)}, u32[]{:S(2)}) collective-permute-start(bf16[64,6272]{1,0:T(8,128)(2,1)} %own_unit.1.refs_0_), channel_id=1, source_target_pairs={{16,0},{20,4},{24,8},{28,12},{32,16},{36,20},{40,24},{44,28},{48,3... | collective-permute-start | bytes 2408456 | tf_op jit(solution)/shard_map/plus/ppermute | solution.py:39
  35.6 21.2 %collective-permute-start.5 = (bf16[64,6272]{1,0:T(8,128)(2,1)}, bf16[64,6272]{1,0:T(8,128)(2,1)S(1)}, u32[]{:S(2)}, u32[]{:S(2)}) collective-permute-start(bf16[64,6272]{1,0:T(8,128)(2,1)} %own_unit.1.refs_0_), channel_id=1, source_target_pairs={{48,0},{52,4},{56,8},{60,12},{0,16},{4,20},{8,24},{12,28},{16,32},... | collective-permute-start | bytes 2408456 | tf_op jit(solution)/shard_map/minus/ppermute | solution.py:39
  57.1 24.5 %collective-permute-start.11 = (bf16[3,64,6272]{2,1,0:T(8,128)(2,1)S(1)}, bf16[3,64,6272]{2,1,0:T(8,128)(2,1)S(1)}, u32[]{:S(2)}, u32[]{:S(2)}) collective-permute-start(bf16[3,64,6272]{2,1,0:T(8,128)(2,1)S(1)} %stacked.2.refs_0_), channel_id=1, source_target_pairs={{4,0},{0,4},{12,8},{8,12},{20,16},{16,20},{28,24},{24,28},{36,32},... | collective-permute-start | bytes 7225352 | tf_op jit(solution)/shard_map/twin_first/from_shard/ppermute | solution.py:39
  57.2 24.4 %collective-permute-start.7 = (bf16[8,96,1024]{2,1,0:T(8,128)(2,1)S(1)}, bf16[8,96,1024]{2,1,0:T(8,128)(2,1)S(1)}, u32[]{:S(2)}, u32[]{:S(2)}) collective-permute-start(bf16[8,96,1024]{2,1,0:T(8,128)(2,1)S(1)} %collective-permute-done.2.refs_1_), channel_id=1, source_target_pairs={{0,1},{1,2},{2,3},{3,0},{4,7},{5,4},{6,5},{7,6},{8,9},{9,10},{10,1... | collective-permute-start | bytes 4718600 | tf_op jit(solution)/shard_map/twin_behind/ppermute | solution.py:56
  58.5 20.3 %collective-permute-start.10 = (bf16[64,6272]{1,0:T(8,128)(2,1)S(1)}, bf16[64,6272]{1,0:T(8,128)(2,1)S(1)}, u32[]{:S(2)}, u32[]{:S(2)}) collective-permute-start(bf16[64,6272]{1,0:T(8,128)(2,1)S(1)} %collective-permute-done.4.refs_1_), channel_id=1, source_target_pairs={{16,0},{20,4},{24,8},{28,12},{32,16},{36,20},{40,24},{44,28},{48,3... | collective-permute-start | bytes 2408456 | tf_op jit(solution)/shard_map/far/ppermute | solution.py:39
  58.9 20.1 %collective-permute-start.9 = (bf16[64,6272]{1,0:T(8,128)(2,1)S(1)}, bf16[64,6272]{1,0:T(8,128)(2,1)S(1)}, u32[]{:S(2)}, u32[]{:S(2)}) collective-permute-start(bf16[64,6272]{1,0:T(8,128)(2,1)S(1)} %collective-permute-done.4.refs_1_), channel_id=1, source_target_pairs={{8,0},{12,4},{0,8},{4,12},{24,16},{28,20},{16,24},{20,28},{40,32},... | collective-permute-start | bytes 2408456 | tf_op jit(solution)/shard_map/plus_other/ppermute | solution.py:39
  60.6 21.0 %collective-permute-start.8 = (bf16[64,6272]{1,0:T(8,128)(2,1)S(1)}, bf16[64,6272]{1,0:T(8,128)(2,1)S(1)}, u32[]{:S(2)}, u32[]{:S(2)}) collective-permute-start(bf16[64,6272]{1,0:T(8,128)(2,1)S(1)} %collective-permute-done.3.refs_0_), channel_id=1, source_target_pairs={{48,0},{52,4},{56,8},{60,12},{0,16},{4,20},{8,24},{12,28},{16,32},... | collective-permute-start | bytes 2408456 | tf_op jit(solution)/shard_map/minus_other/ppermute | solution.py:39
  81.9 22.2 %collective-permute-start.15 = (bf16[3,64,6272]{2,1,0:T(8,128)(2,1)S(1)}, bf16[3,64,6272]{2,1,0:T(8,128)(2,1)S(1)}, u32[]{:S(2)}, u32[]{:S(2)}) collective-permute-start(bf16[3,64,6272]{2,1,0:T(8,128)(2,1)S(1)} %stacked.3.refs_0_), channel_id=1, source_target_pairs={{4,0},{0,4},{12,8},{8,12},{20,16},{16,20},{28,24},{24,28},{36,32},... | collective-permute-start | bytes 7225352 | tf_op jit(solution)/shard_map/twin_second/from_shard/ppermute | solution.py:39
  82.4 21.6 %collective-permute-start.6 = (bf16[8,96,1024]{2,1,0:T(8,128)(2,1)S(1)}, bf16[8,96,1024]{2,1,0:T(8,128)(2,1)S(1)}, u32[]{:S(2)}, u32[]{:S(2)}) collective-permute-start(bf16[8,96,1024]{2,1,0:T(8,128)(2,1)S(1)} %collective-permute-done.1.refs_0_), channel_id=1, source_target_pairs={{0,1},{1,2},{2,3},{3,0},{4,7},{5,4},{6,5},{7,6},{8,9},{9,10},{10,1... | collective-permute-start | bytes 4718600 | tf_op jit(solution)/shard_map/opposite/ppermute | solution.py:56
  82.8 21.3 %collective-permute-start.13 = (bf16[8,96,1024]{2,1,0:T(8,128)(2,1)S(1)}, bf16[8,96,1024]{2,1,0:T(8,128)(2,1)S(1)}, u32[]{:S(2)}, u32[]{:S(2)}) collective-permute-start(bf16[8,96,1024]{2,1,0:T(8,128)(2,1)S(1)} %collective-permute-done.7.refs_1_), channel_id=1, source_target_pairs={{4,0},{0,4},{12,8},{8,12},{20,16},{16,20},{28,24},{24,28},{36,32},... | collective-permute-start | bytes 4718600 | tf_op jit(solution)/shard_map/ahead/from_shard/ppermute | solution.py:39
  84.1 20.0 %collective-permute-start.12 = (bf16[64,6272]{1,0:T(8,128)(2,1)S(1)}, bf16[64,6272]{1,0:T(8,128)(2,1)S(1)}, u32[]{:S(2)}, u32[]{:S(2)}) collective-permute-start(bf16[64,6272]{1,0:T(8,128)(2,1)S(1)} %collective-permute-done.10.refs_2_), channel_id=1, source_target_pairs={{8,0},{12,4},{0,8},{4,12},{24,16},{28,20},{16,24},{20,28},{40,32},... | collective-permute-start | bytes 2408456 | tf_op jit(solution)/shard_map/far_other/ppermute | solution.py:39
  161.6 18.0 %collective-permute-start.21 = (bf16[3584,256]{1,0:T(8,128)(2,1)S(1)}, bf16[3584,256]{1,0:T(8,128)(2,1)S(1)}, u32[]{:S(2)}, u32[]{:S(2)}) collective-permute-start(bf16[3584,256]{1,0:T(8,128)(2,1)S(1)} %get-tuple-element.226), channel_id=1, source_target_pairs={{4,0},{0,4},{12,8},{8,12},{20,16},{16,20},{28,24},{24,28},{36,32},... | collective-permute-start | bytes 5505032 | tf_op jit(solution)/shard_map/twin/from_shard/ppermute | solution.py:39
  201.5 25.7 %collective-permute-start.26 = (bf16[8,64,1024]{2,1,0:T(8,128)(2,1)S(1)}, bf16[8,64,1024]{2,1,0:T(8,128)(2,1)S(1)}, u32[]{:S(2)}, u32[]{:S(2)}) collective-permute-start(bf16[8,64,1024]{2,1,0:T(8,128)(2,1)S(1)} %get-tuple-element.252), channel_id=1, source_target_pairs={{0,3},{1,0},{2,1},{3,2},{4,5},{5,6},{6,7},{7,4},{8,11},{9,8},{10,9... | collective-permute-start | bytes 3145736 | tf_op jit(solution)/shard_map/given_2/ppermute | solution.py:56
  203.6 24.8 %collective-permute-start.25 = (bf16[8,64,1024]{2,1,0:T(8,128)(2,1)S(1)}, bf16[8,64,1024]{2,1,0:T(8,128)(2,1)S(1)}, u32[]{:S(2)}, u32[]{:S(2)}) collective-permute-start(bf16[8,64,1024]{2,1,0:T(8,128)(2,1)S(1)} %summed.11), channel_id=1, source_target_pairs={{0,1},{1,2},{2,3},{3,0},{4,7},{5,4},{6,5},{7,6},{8,9},{9,10},{10,1... | collective-permute-start | bytes 3145736 | tf_op jit(solution)/shard_map/own_2/ppermute | solution.py:56
  209.8 27.1 %collective-permute-start.29 = (bf16[2,64,4224]{2,1,0:T(8,128)(2,1)S(1)}, bf16[2,64,4224]{2,1,0:T(8,128)(2,1)S(1)}, u32[]{:S(2)}, u32[]{:S(2)}) collective-permute-start(bf16[2,64,4224]{2,1,0:T(8,128)(2,1)S(1)} %get-tuple-element.265), channel_id=1, source_target_pairs={{0,16},{1,17},{2,18},{3,19},{4,52},{5,53},{6,54},{7,55},{8,24},{9,... | collective-permute-start | bytes 3244040 | tf_op jit(solution)/shard_map/far_c/ppermute | solution.py:56
  210.4 26.6 %collective-permute-start.30 = (bf16[2,64,4224]{2,1,0:T(8,128)(2,1)S(1)}, bf16[2,64,4224]{2,1,0:T(8,128)(2,1)S(1)}, u32[]{:S(2)}, u32[]{:S(2)}) collective-permute-start(bf16[2,64,4224]{2,1,0:T(8,128)(2,1)S(1)} %get-tuple-element.266), channel_id=1, source_target_pairs={{0,48},{1,49},{2,50},{3,51},{4,20},{5,21},{6,22},{7,23},{8,56},{9,... | collective-permute-start | bytes 3244040 | tf_op jit(solution)/shard_map/given_c/ppermute | solution.py:56
  228.4 25.5 %collective-permute-start.32 = (bf16[8,64,1024]{2,1,0:T(8,128)(2,1)S(1)}, bf16[8,64,1024]{2,1,0:T(8,128)(2,1)S(1)}, u32[]{:S(2)}, u32[]{:S(2)}) collective-permute-start(bf16[8,64,1024]{2,1,0:T(8,128)(2,1)S(1)} %get-tuple-element.272), channel_id=1, source_target_pairs={{0,1},{1,2},{2,3},{3,0},{4,7},{5,4},{6,5},{7,6},{8,9},{9,10},{10,1... | collective-permute-start | bytes 3145736 | tf_op jit(solution)/shard_map/far_1/ppermute | solution.py:56
  228.4 25.5 %collective-permute-start.33 = (bf16[8,64,1024]{2,1,0:T(8,128)(2,1)S(1)}, bf16[8,64,1024]{2,1,0:T(8,128)(2,1)S(1)}, u32[]{:S(2)}, u32[]{:S(2)}) collective-permute-start(bf16[8,64,1024]{2,1,0:T(8,128)(2,1)S(1)} %get-tuple-element.273), channel_id=1, source_target_pairs={{0,3},{1,0},{2,1},{3,2},{4,5},{5,6},{6,7},{7,4},{8,11},{9,8},{10,9... | collective-permute-start | bytes 3145736 | tf_op jit(solution)/shard_map/given_1/ppermute | solution.py:56
  237.2 17.2 %collective-permute-start.34 = (bf16[2,64,4224]{2,1,0:T(8,128)(2,1)S(1)}, bf16[2,64,4224]{2,1,0:T(8,128)(2,1)S(1)}, u32[]{:S(2)}, u32[]{:S(2)}) collective-permute-start(bf16[2,64,4224]{2,1,0:T(8,128)(2,1)S(1)} %summed.13), channel_id=1, source_target_pairs={{0,16},{1,17},{2,18},{3,19},{4,52},{5,53},{6,54},{7,55},{8,24},{9,... | collective-permute-start | bytes 3244040 | tf_op jit(solution)/shard_map/own_c/ppermute | solution.py:56
  271.8 21.4 %all-to-all-start.1 = ((bf16[8,64,1024]{2,1,0:T(8,128)(2,1)}), bf16[8,64,1024]{2,1,0:T(8,128)(2,1)S(1)}, u32[]{:S(2)}, u32[]{:S(2)}) async-start(bf16[8,64,1024]{2,1,0:T(8,128)(2,1)} %summed.20), calls=%async_computation.1 | async-start | bytes 2097152 | tf_op jit(solution)/shard_map/swap_1/all_to_all | solution.py:789
  (33 other events, 364.2 us)
